TPU v7x, 32 devices: a whole 2x2x4 slice. The times are simulated.
32 devices in a mesh: seq: 4 (over y, x), batch: 8 (over z, core).
Axes of the slice: x: 2, y: 2, z: 4, core: 2. Of those that a mesh axis runs over, the one named last changes fastest.
Arguments:
- inputs: float32 [16, 1024, 768], P('batch', 'seq'), may hold values from -6 to 6
- gain_one: float32 [768], P(('seq', 'batch')), may hold values from 0.1 to 1.9
- w_in: float32 [768, 2304], P(('seq', 'batch')), may hold values from -0.21875 to 0.21875
- conv_weight: float32 [3, 2304], P(None, ('seq', 'batch')), may hold values from -3 to 3
- kernel: float32 [2, 2048, 768], P(None, 'batch', 'seq'), may hold values from -6 to 6
- w_out: float32 [768, 768], P(('seq', 'batch')), may hold values from -0.21875 to 0.21875
- gain_two: float32 [768], P(('seq', 'batch')), may hold values from 0.1 to 1.9
- w_gate: float32 [768, 3072], P(('seq', 'batch')), may hold values from -0.21875 to 0.21875
- w_up: float32 [768, 3072], P(('seq', 'batch')), may hold values from -0.21875 to 0.21875
- w_down: float32 [3072, 768], P(('seq', 'batch')), may hold values from -0.109375 to 0.109375
- mask_positions: int32 [16, 80], P('batch'), may hold values from 0 to 1023, as said below
- mask_counts: int32 [16], P('batch'), may hold values from 1 to 80, as said below
- grad_rows: float32 [16, 80, 768], P('batch'), may hold values from -6 to 6
Outputs:
- outputs: float32 [16, 1024, 768], P('batch', 'seq')
- input_grad: float32 [16, 1024, 768], P('batch', 'seq')
- gain_one_grad: float32 [768], P(('seq', 'batch'))
- w_in_grad: float32 [768, 2304], P(('seq', 'batch'))
- conv_weight_grad: float32 [3, 2304], P(None, ('seq', 'batch'))
- kernel_grad: float32 [2, 2048, 768], P(None, 'batch', 'seq')
- w_out_grad: float32 [768, 768], P(('seq', 'batch'))
- gain_two_grad: float32 [768], P(('seq', 'batch'))
- w_gate_grad: float32 [768, 3072], P(('seq', 'batch'))
- w_up_grad: float32 [768, 3072], P(('seq', 'batch'))
- w_down_grad: float32 [3072, 768], P(('seq', 'batch'))
Inputs may be any that keep to these rules, and one draw needn't show every extreme that they name: `mask_positions`: the 80 entries of a row are distinct positions of that sequence; only the first mask_counts of them are live. `mask_counts`: in each aligned block of 2 sequences one row has 4 or more live positions; some row of the batch has 80.
All inputs are finite; a program needn't handle non-finite values.
Results may differ from a plain program's by a relative error of at most 0.0003.
Values sent between devices are 32-bit elements; how exact they have to be, the bound alone decides.
No kernel may reach another device: no remote copies, remote signals or barrier semaphores. Data moves between devices by JAX's collectives and lax.ppermute only.
A program may use at most 256 MiB of HBM per device.

v0:
```python
import math

import jax
import jax.numpy as jnp
from jax import lax
from jax.sharding import PartitionSpec as P

eps = 1e-05


def extended(value, sides, width):
    for axis, dim in sides:
        devices, length = (lax.axis_size(axis), value.shape[dim])
        up = [(i, (i + 1) % devices) for i in range(devices - 1)]
        down = [(j, i) for i, j in up]
        last = lax.slice_in_dim(value, length - width, length, axis=dim)
        initial = lax.slice_in_dim(value, 0, width, axis=dim)
        before = lax.ppermute(last, axis, up)
        after = lax.ppermute(initial, axis, down)
        value = jnp.concatenate([before, value, after], axis=dim)
    return value


def contract(pattern, left_side, right_side):
    return jnp.einsum(pattern, left_side, right_side, precision=lax.Precision.HIGHEST)


def matmul(left_side, right_side):
    return contract("std,de->ste", left_side, right_side)


def layer_norm(values, norm_gain):
    centered = values - jnp.mean(values, axis=-1, keepdims=True)
    spread = jnp.mean(centered * centered, axis=-1, keepdims=True)
    return centered * lax.rsqrt(spread + eps) * norm_gain


def split_length(length):
    first_len = 1
    for factor in range(1, math.isqrt(length) + 1):
        if length % factor == 0:
            first_len = factor
    return (first_len, length // first_len)


def phase_table(row_count, col_count, multiple, length, direction):
    row_index = jnp.arange(row_count, dtype=jnp.int32)[:, None]
    col_index = jnp.arange(col_count, dtype=jnp.int32)[None, :]
    turn_count = row_index * col_index * multiple % length
    angles = turn_count.astype(jnp.float32) * (direction * 2.0 * math.pi / length)
    return (jnp.cos(angles), jnp.sin(angles))


def transform(real_part, imag_part, direction):
    seqs_count, length, channels = real_part.shape
    first_len, second_len = split_length(length)
    real_part = real_part.reshape(seqs_count, first_len, second_len, channels)
    imag_part = imag_part.reshape(seqs_count, first_len, second_len, channels)
    cos_one, sin_one = phase_table(first_len, first_len, second_len, length, direction)
    step_real = contract("ft,btsw->bfsw", cos_one, real_part) - contract(
        "ft,btsw->bfsw", sin_one, imag_part
    )
    step_imag = contract("ft,btsw->bfsw", cos_one, imag_part) + contract(
        "ft,btsw->bfsw", sin_one, real_part
    )
    cos_mid, sin_mid = phase_table(first_len, second_len, 1, length, direction)
    cos_mid = cos_mid[None, :, :, None]
    sin_mid = sin_mid[None, :, :, None]
    twist_real = step_real * cos_mid - step_imag * sin_mid
    twist_imag = step_real * sin_mid + step_imag * cos_mid
    cos_two, sin_two = phase_table(second_len, second_len, first_len, length, direction)
    final_real = contract("gs,bfsw->bgfw", cos_two, twist_real) - contract(
        "gs,bfsw->bgfw", sin_two, twist_imag
    )
    final_imag = contract("gs,bfsw->bgfw", cos_two, twist_imag) + contract(
        "gs,bfsw->bgfw", sin_two, twist_real
    )
    return (
        final_real.reshape(seqs_count, length, channels),
        final_imag.reshape(seqs_count, length, channels),
    )


def channel_mix(signal, values, kernel):
    length = signal.shape[1]
    padding = ((0, 0), (0, length), (0, 0))
    signal_long = jnp.pad(signal, padding)
    values_long = jnp.pad(values, padding)
    zero_part = jnp.zeros_like(signal_long)
    signal_real, signal_imag = transform(signal_long, zero_part, -1.0)
    values_real, values_imag = transform(values_long, zero_part, -1.0)
    shrink = 1.0 / math.sqrt(length)
    kernel_real = kernel[0] + signal_real * shrink
    kernel_imag = kernel[1] + signal_imag * shrink
    prod_real = kernel_real * values_real - kernel_imag * values_imag
    prod_imag = kernel_real * values_imag + kernel_imag * values_real
    back_real, back_imag = transform(prod_real, prod_imag, 1.0)
    return back_real[:, :length] / (2 * length)


def pre_mix(inputs, gain_one, w_in):
    return matmul(layer_norm(inputs, gain_one), w_in)


def short_conv(padded, conv_weight):
    return (
        conv_weight[0] * padded[:, :-2]
        + conv_weight[1] * padded[:, 1:-1]
        + conv_weight[2] * padded[:, 2:]
    )


def post_mix(inputs, gating, long_conv, w_out, gain_two, w_gate, w_up, w_down):
    residual = inputs + matmul(gating * long_conv, w_out)
    normed = layer_norm(residual, gain_two)
    hidden = jax.nn.gelu(matmul(normed, w_gate), approximate=True) * matmul(normed, w_up)
    return residual + matmul(hidden, w_down)


def body(
    inputs,
    gain_one,
    w_in,
    conv_weight,
    kernel,
    w_out,
    gain_two,
    w_gate,
    w_up,
    w_down,
    mask_positions,
    mask_counts,
    grad_rows,
):
    w_in, w_out, w_gate, w_up, w_down, gain_one, gain_two, conv_weight = (
        lax.all_gather(w_in, ("seq", "batch"), axis=0, tiled=True),
        lax.all_gather(w_out, ("seq", "batch"), axis=0, tiled=True),
        lax.all_gather(w_gate, ("seq", "batch"), axis=0, tiled=True),
        lax.all_gather(w_up, ("seq", "batch"), axis=0, tiled=True),
        lax.all_gather(w_down, ("seq", "batch"), axis=0, tiled=True),
        lax.all_gather(gain_one, ("seq", "batch"), axis=0, tiled=True),
        lax.all_gather(gain_two, ("seq", "batch"), axis=0, tiled=True),
        lax.all_gather(conv_weight, ("seq", "batch"), axis=1, tiled=True),
    )
    full_kernel = lax.all_gather(kernel, "batch", axis=1, tiled=True)
    tokens = inputs.shape[1]
    projected, pre_pull = jax.vjp(pre_mix, inputs, gain_one, w_in)
    padded = extended(projected, (("seq", 1),), 1)
    mixed = short_conv(padded, conv_weight)
    signal, gating, values = jnp.split(mixed, 3, axis=2)
    signal_wide, values_wide = (
        lax.all_to_all(signal, "seq", split_axis=2, concat_axis=1, tiled=True),
        lax.all_to_all(values, "seq", split_axis=2, concat_axis=1, tiled=True),
    )
    wide_out, wide_pull = jax.vjp(channel_mix, signal_wide, values_wide, full_kernel)
    long_conv = lax.all_to_all(wide_out, "seq", split_axis=1, concat_axis=2, tiled=True)
    offset = lax.axis_index("seq") * tokens
    places = offset + jnp.arange(tokens, dtype=jnp.int32)
    slot_index = jnp.arange(mask_positions.shape[1], dtype=jnp.int32)
    live_slots = slot_index[None, :] < mask_counts[:, None]
    select = (
        (mask_positions[:, :, None] == places[None, None, :]) & live_slots[:, :, None]
    ).astype(jnp.float32)
    post_weights = (w_out, gain_two, w_gate, w_up, w_down)
    outputs, post_pull = jax.vjp(post_mix, inputs, gating, long_conv, *post_weights)
    cotangent = contract("smt,smd->std", select, grad_rows)
    post_grads = post_pull(cotangent)
    input_direct, gating_grad, long_grad = (post_grads[0], post_grads[1], post_grads[2])
    w_out_grad, gain_two_grad, w_gate_grad, w_up_grad, w_down_grad = post_grads[3:]
    wide_grad = lax.all_to_all(long_grad, "seq", split_axis=2, concat_axis=1, tiled=True)
    signal_wide_grad, values_wide_grad, kernel_full_grad = wide_pull(wide_grad)
    kernel_sum = lax.psum_scatter(kernel_full_grad, "batch", scatter_dimension=1, tiled=True)
    signal_grad, values_grad = (
        lax.all_to_all(signal_wide_grad, "seq", split_axis=1, concat_axis=2, tiled=True),
        lax.all_to_all(values_wide_grad, "seq", split_axis=1, concat_axis=2, tiled=True),
    )
    mixed_grad = jnp.concatenate((signal_grad, gating_grad, values_grad), axis=2)
    mixed_padded = extended(mixed_grad, (("seq", 1),), 1)
    projected_grad = (
        conv_weight[0] * mixed_padded[:, 2:]
        + conv_weight[1] * mixed_padded[:, 1:-1]
        + conv_weight[2] * mixed_padded[:, :-2]
    )
    conv_weight_grad = jnp.stack(
        [
            jnp.sum(padded[:, :-2] * mixed_grad, axis=(0, 1)),
            jnp.sum(padded[:, 1:-1] * mixed_grad, axis=(0, 1)),
            jnp.sum(padded[:, 2:] * mixed_grad, axis=(0, 1)),
        ]
    )
    input_pre, gain_one_grad, w_in_grad = pre_pull(projected_grad)
    input_grad = input_direct + input_pre
    w_in_sum, w_out_sum, w_gate_sum, w_up_sum, w_down_sum, gain_one_sum, gain_two_sum, conv_sum = (
        lax.psum_scatter(w_in_grad, ("seq", "batch"), scatter_dimension=0, tiled=True),
        lax.psum_scatter(w_out_grad, ("seq", "batch"), scatter_dimension=0, tiled=True),
        lax.psum_scatter(w_gate_grad, ("seq", "batch"), scatter_dimension=0, tiled=True),
        lax.psum_scatter(w_up_grad, ("seq", "batch"), scatter_dimension=0, tiled=True),
        lax.psum_scatter(w_down_grad, ("seq", "batch"), scatter_dimension=0, tiled=True),
        lax.psum_scatter(gain_one_grad, ("seq", "batch"), scatter_dimension=0, tiled=True),
        lax.psum_scatter(gain_two_grad, ("seq", "batch"), scatter_dimension=0, tiled=True),
        lax.psum_scatter(conv_weight_grad, ("seq", "batch"), scatter_dimension=1, tiled=True),
    )
    return (
        outputs,
        input_grad,
        gain_one_sum,
        w_in_sum,
        conv_sum,
        kernel_sum,
        w_out_sum,
        gain_two_sum,
        w_gate_sum,
        w_up_sum,
        w_down_sum,
    )


def solution(mesh):
    placed = (
        P("batch", "seq", None),
        P(("seq", "batch")),
        P(("seq", "batch"), None),
        P(None, ("seq", "batch")),
        P(None, "batch", "seq"),
        P(("seq", "batch"), None),
        P(("seq", "batch")),
        P(("seq", "batch"), None),
        P(("seq", "batch"), None),
        P(("seq", "batch"), None),
        P("batch", None),
        P("batch"),
        P("batch", None, None),
    )
    return jax.shard_map(
        body,
        mesh=mesh,
        in_specs=placed,
        out_specs=(
            P("batch", "seq", None),
            P("batch", "seq", None),
            P(("seq", "batch")),
            P(("seq", "batch"), None),
            P(None, ("seq", "batch")),
            P(None, "batch", "seq"),
            P(("seq", "batch"), None),
            P(("seq", "batch")),
            P(("seq", "batch"), None),
            P(("seq", "batch"), None),
            P(("seq", "batch"), None),
        ),
        check_vma=False,
    )
```

profile of v0, /device:TPU:0, one launch (start us, length us, event | category | flops | bytes accessed | tf_op | source)
XLA Modules:
  0.0 1447.0 jit_solution(3896364639372092975)
XLA Ops:
  15.0 43.8 %all-gather = f32[32,72,3]{1,2,0:T(4,128)S(1)} all-gather(f32[1,72,3]{1,2,0:T(4,128)S(1)} %bitcast.438), channel_id=1, replica_groups=mesh['seq'=4,'batch'=8] {'seq','batch'}, dimensions={0}, use_global_device_ids=true | all-gather | bytes 28512 | tf_op jit(solution)/shard_map/all_gather | solution.py:143
  59.4 38.0 %all-reduce.11 = (f32[768]{0:T(1024)S(1)}, f32[768]{0:T(1024)S(1)}) all-reduce(f32[768]{0:T(1024)S(1)} %dynamic-update-slice, f32[768]{0:T(1024)S(1)} %dynamic-update-slice.1), channel_id=1, replica_groups=mesh['seq'=4,'batch'=8] {'seq','batch'}, use_global_device_ids=true, to_apply=%add.5 | all-reduce | flops 1536 | bytes 12288
  97.4 14.1 fusion.14
  135.3 14.4 all-to-all-done.1
  185.7 7.1 fusion.130
  192.8 7.2 fusion.124
  200.0 7.4 fusion.127
  207.5 14.1 fusion.57
  221.6 8.9 fusion.108
  230.5 6.7 multiply_bitcast_fusion.1
  241.7 7.1 fusion.106
  248.9 7.0 multiply_bitcast_fusion
  260.4 6.7 fusion.94
  267.2 6.8 add_bitcast_fusion.4
  276.5 6.7 fusion.96
  283.2 7.0 subtract_bitcast_fusion.1
  293.3 5.7 multiply_subtract_fusion
  299.0 6.4 fusion.88
  305.5 6.6 fusion.86
  312.1 7.0 fusion.140
  319.1 8.2 fusion.55
  327.3 6.5 fusion.73
  333.9 6.7 subtract_bitcast_fusion
  354.8 21.1 %all-to-all-done.2 = f32[2,1024,192]{2,0,1:T(2,128)S(1)} async-done(((f32[2,1024,192]{2,0,1:T(2,128)}), f32[2,1024,192]{2,0,1:T(2,128)S(1)}, u32[]{:S(2)}, u32[]{:S(2)}) %all-to-all-start.2) | async-done | bytes 1572896 | tf_op jit(solution)/shard_map/all_to_all | solution.py:156
  382.0 7.2 fusion.510
  389.5 19.2 %fusion.6 = f32[2,256,3072]{2,1,0:T(8,128)} fusion(f32[768,3072]{1,0:T(8,128)} %all-gather.16.cloned.1.call-done, f32[2,256,768]{2,1,0:T(8,128)S(1)} %get-tuple-element.98, f32[768]{0:T(1024)S(1)} %get-tuple-element.60, f32[2,256]{1,0:T(2,128)S(1)} %fusion.302, f32[2,256]{1,0:T(2,128)S(1)} %broadcast_multiply_fusion.1), kind=kOutput, calls=%fused_computation.6 | convolution fusion | flops 14496694272 | bytes 17308672 | tf_op jit(solution)/shard_map/jvp(std,de->ste)/dot_general | solution.py:25
  408.7 19.7 %fusion.10 = f32[2,256,3072]{2,1,0:T(8,128)} fusion(f32[768,3072]{1,0:T(8,128)} %all-gather.14.cloned.1.call-done, f32[2,256,768]{2,1,0:T(8,128)S(1)} %get-tuple-element.98, f32[768]{0:T(1024)S(1)} %get-tuple-element.60, f32[2,256]{1,0:T(2,128)S(1)} %fusion.302, f32[2,256]{1,0:T(2,128)S(1)} %broadcast_multiply_fusion.1), kind=kOutput, calls=%fused_computation.10 | convolution fusion | flops 14496694272 | bytes 17308672 | tf_op jit(solution)/shard_map/jvp(std,de->ste)/dot_general | solution.py:25
  428.4 18.8 %all-gather.18.cloned.1.call-done = f32[3072,768]{1,0:T(8,128)} async-done(((f32[96,768]{1,0:T(8,128)}), f32[3072,768]{1,0:T(8,128)}) %all-gather.18.cloned.1.call-update) | async-done | bytes 9437200 | tf_op jit(solution)/shard_map/all_gather | solution.py:140
  447.3 18.8 %fusion = f32[2,256,3072]{2,1,0:T(8,128)S(1)} fusion(f32[2,256,768]{2,1,0:T(8,128)} %fusion.199, f32[3072,768]{1,0:T(8,128)} %all-gather.18.cloned.1.call-done), kind=kOutput, calls=%fused_computation | convolution fusion | flops 14495514624 | bytes 17301504 | tf_op jit(solution)/shard_map/transpose(jvp(std,de->ste))/dot_general | solution.py:25
  466.1 26.1 %fusion.4 = f32[2,256,768]{2,1,0:T(8,128)} fusion(f32[768,3072]{1,0:T(8,128)} %all-gather.16.cloned.1.call-done, f32[2,256,3072]{2,1,0:T(8,128)S(1)} %fusion, f32[2,256,3072]{2,1,0:T(8,128)S(1)} %copy-done.2), kind=kOutput, calls=%fused_computation.4 | convolution fusion | flops 14509670400 | bytes 23592960 | tf_op jit(solution)/shard_map/transpose(jvp(std,de->ste))/dot_general | solution.py:25
  492.2 45.3 %multiply_reduce_fusion.6 = (f32[2,256]{1,0:T(2,128)S(1)}, f32[2,256,768]{2,1,0:T(8,128)S(1)}) fusion(f32[2,256,768]{2,1,0:T(8,128)S(1)} %get-tuple-element.98, f32[768]{0:T(1024)S(1)} %get-tuple-element.60, f32[2,256]{1,0:T(2,128)S(1)} %broadcast_multiply_fusion.1, f32[2,256,768]{2,1,0:T(8,128)} %fusion.4, f32[768,3072]{1,0:T(8,128)} %all-gather.14.cloned.1.call-done, ...), kind=kOutput, calls=%fused_computation.211 | convolution fusion | flops 14528937984 | bytes 33037312 | tf_op jit(solution)/shard_map/transpose(jvp(std,de->ste))/dot_general | solution.py:25
  540.2 7.8 fusion.509
  563.0 13.0 all-to-all-done.3
  583.8 6.7 fusion.53
  590.5 8.4 fusion.503
  598.9 6.7 fusion.71
  605.7 7.2 fusion.69
  612.9 6.7 add_bitcast_fusion.3
  626.1 18.3 %add_reduce_fusion.1 = (f32[32,64,192]{2,0,1:T(8,128)}, f32[32,64,192]{2,0,1:T(8,128)}, f32[2,32,64,192]{3,1,2,0:T(8,128)}) fusion(f32[2,32,64,192]{3,1,2,0:T(8,128)} %copy-done.15, f32[2,32,64,192]{3,2,1,0:T(8,128)S(1)} %bitcast.402, f32[2,32,64,192]{3,2,1,0:T(8,128)S(1)} %bitcast.404, f32[2,64,192,32]{2,3,1,0:T(8,128)} %fusion.69, ...), kind=kOutput, calls=%fused_computation.125 | convolution fusion | flops 309083136 | bytes 22020096 | tf_op jit(solution)/shard_map/transpose(jvp(ft,btsw->bfsw))/dot_general | solution.py:25
  644.4 6.7 copy.343
  651.2 17.1 %add_multiply_fusion.1 = (f32[2,64,32,192]{3,1,2,0:T(8,128)}, f32[2,64,32,192]{3,1,2,0:T(8,128)}, f32[2,64,32,192]{3,1,2,0:T(8,128)}, f32[2,64,32,192]{3,1,2,0:T(8,128)}) fusion(f32[2,64,32,192]{3,1,2,0:T(8,128)} %copy-done.22, f32[2,64,32,192]{3,1,2,0:T(8,128)} %copy-done.23, f32[2,64,32,192]{3,2,1,0:T(8,128)} %bitcast.418, ...), kind=kLoop, calls=%fused_computation.133 | loop fusion | flops 13369344 | bytes 34603008 | tf_op jit(solution)/shard_map/transpose(jvp())/mul | solution.py:94
  668.3 8.4 fusion.29
  676.7 6.0 fusion.31
  687.7 6.2 fusion.42
  705.0 5.6 fusion.162
  710.7 6.0 fusion.156
  716.6 12.0 fusion.38
  728.6 8.8 fusion.61
  737.4 6.4 add_bitcast_fusion
  753.9 8.8 fusion.65
  762.7 6.5 add_bitcast_fusion.1
  783.6 7.8 convolution_bitcast_fusion.4
  801.5 6.1 all-to-all-done.4
  817.8 7.7 multiply_reduce_fusion.2
  834.6 18.7 %convolution_bitcast_fusion.3 = f32[768,2304]{1,0:T(8,128)} fusion(f32[2,256,768]{2,1,0:T(8,128)S(1)} %copy-done.4, f32[768]{0:T(1024)S(1)} %copy-done.52, f32[2,256]{1,0:T(2,128)S(1)} %copy-done.60, f32[2,256]{1,0:T(2,128)S(1)} %copy-done.54, f32[2,1,2304]{2,1,0:T(1,128)S(1)} %collective-permute-done.3, f32[2,256,768]{2,1,0:T(8,128)S(1)} %copy-done.46, ...), kind=kOutput, calls=%fused_computation.28 | convolution fusion | flops 10888151040 | bytes 13441024 | tf_op jit(solution)/shard_map/transpose(jvp(std,de->ste))/dot_general | solution.py:25
  853.6 25.4 %convolution_bitcast_fusion.2 = f32[768,3072]{1,0:T(8,128)} fusion(f32[2,256,768]{2,1,0:T(8,128)S(1)} %get-tuple-element.98, f32[768]{0:T(1024)S(1)} %get-tuple-element.60, f32[2,256]{1,0:T(2,128)S(1)} %fusion.302, f32[2,256]{1,0:T(2,128)S(1)} %broadcast_multiply_fusion.1, f32[2,256,3072]{2,1,0:T(8,128)} %fusion.10, f32[2,256,3072]{2,1,0:T(8,128)} %copy-done.45, ...), kind=kOutput, calls=%fused_computation.27 | convolution fusion | flops 14528151552 | bytes 29891584 | tf_op jit(solution)/shard_map/transpose(jvp(std,de->ste))/dot_general | solution.py:25
  879.3 21.7 %convolution_bitcast_fusion.1 = f32[768,3072]{1,0:T(8,128)} fusion(f32[2,256,768]{2,1,0:T(8,128)S(1)} %get-tuple-element.98, f32[768]{0:T(1024)S(1)} %get-tuple-element.60, f32[2,256]{1,0:T(2,128)S(1)} %fusion.302, f32[2,256]{1,0:T(2,128)S(1)} %broadcast_multiply_fusion.1, f32[2,256,3072]{2,1,0:T(8,128)} %copy-done.45, f32[2,256,3072]{2,1,0:T(8,128)} %fusion.10), kind=kOutput, calls=%fused_computation.26 | convolution fusion | flops 14510850048 | bytes 23600128 | tf_op jit(solution)/shard_map/transpose(jvp(std,de->ste))/dot_general | solution.py:25
  901.6 22.4 %convolution_bitcast_fusion = f32[3072,768]{1,0:T(8,128)} fusion(f32[2,256,768]{2,1,0:T(8,128)} %fusion.199, f32[2,256,3072]{2,1,0:T(8,128)} %fusion.6, f32[2,256,3072]{2,1,0:T(8,128)} %fusion.10), kind=kOutput, calls=%fused_computation.25 | convolution fusion | flops 14509670400 | bytes 23592960 | tf_op jit(solution)/shard_map/transpose(jvp(std,de->ste))/dot_general | solution.py:25
  924.0 22.0 %fusion.184 = f32[2,256,768]{2,1,0:T(8,128)} fusion(f32[2,256,768]{2,1,0:T(8,128)S(1)} %get-tuple-element.98, f32[3072,768]{1,0:T(8,128)} %all-gather.18.cloned.1.call-done, f32[2,256,3072]{2,1,0:T(8,128)} %fusion.6, f32[2,256,3072]{2,1,0:T(8,128)} %fusion.10), kind=kOutput, calls=%fused_computation.221 | convolution fusion | flops 14510063616 | bytes 25165824 | tf_op jit(solution)/shard_map/jvp(std,de->ste)/dot_general | solution.py:25
  946.1 19.6 %multiply_reduce_fusion.5 = (f32[2,256]{1,0:T(2,128)S(1)}, f32[2,256,768]{2,1,0:T(8,128)}) fusion(f32[2,256,768]{2,1,0:T(8,128)S(1)} %copy-done.5, f32[768]{0:T(1024)S(1)} %copy-done.52, f32[2,256]{1,0:T(2,128)S(1)} %copy-done.54, f32[768,2304]{1,0:T(8,128)} %all-gather.8.cloned.1.call-done, f32[2,1,2304]{2,1,0:T(1,128)S(1)} %collective-permute-done.3, ...), kind=kOutput, calls=%fused_computation.209 | convolution fusion | flops 10888544256 | bytes 15013888 | tf_op jit(solution)/shard_map/transpose(jvp(std,de->ste))/dot_general | solution.py:25
  968.2 40.6 %all-reduce.10 = (f32[768]{0:T(1024)S(1)}, f32[3,2304]{1,0:T(4,128)S(1)}, f32[768]{0:T(1024)S(1)}) all-reduce(f32[768]{0:T(1024)S(1)} %get-tuple-element.51, f32[3,2304]{1,0:T(4,128)S(1)} %pad_maximum_fusion.9, f32[768]{0:T(1024)S(1)} %copy-done.69), channel_id=2, replica_groups=mesh['seq'=4,'batch'=8] {'seq','batch'}, use_global_device_ids=true, to_apply=%region_9.10.clone | all-reduce | flops 8448 | bytes 67584
  1016.2 140.9 %reduce-scatter.14.cloned.1.call-done = f32[24,3072]{1,0:T(8,128)} async-done(((f32[768,3072]{1,0:T(8,128)}), f32[24,3072]{1,0:T(8,128)}) %reduce-scatter.14.cloned.1.call-update) | async-done | bytes 294928 | tf_op jit(solution)/shard_map/reduce_scatter | solution.py:196
  1157.0 142.2 %reduce-scatter.16.cloned.1.call-done = f32[24,3072]{1,0:T(8,128)} async-done(((f32[768,3072]{1,0:T(8,128)}), f32[24,3072]{1,0:T(8,128)}) %reduce-scatter.16.cloned.1.call-update) | async-done | bytes 294928 | tf_op jit(solution)/shard_map/reduce_scatter | solution.py:197
  1299.2 140.7 %reduce-scatter.18.cloned.1.call-done = f32[96,768]{1,0:T(8,128)} async-done(((f32[3072,768]{1,0:T(8,128)}), f32[96,768]{1,0:T(8,128)}) %reduce-scatter.18.cloned.1.call-update) | async-done | bytes 294928 | tf_op jit(solution)/shard_map/reduce_scatter | solution.py:198
  (292 shorter events, 215.5 us)
Async XLA Ops:
  7.2 345.6 %copy-start = (f32[2,80,768]{2,1,0:T(8,128)S(1)}, f32[2,80,768]{2,1,0:T(8,128)}, u32[]{:S(2)}) copy-start(f32[2,80,768]{2,1,0:T(8,128)} %param.25) | copy-start | bytes 1474564
  7.2 6.9 copy-start.3
  7.2 7.8 copy-start.70
  7.2 51.7 %copy-start.72 = (f32[24]{0:T(128)S(1)}, f32[24]{0:T(128)}, u32[]{:S(2)}) copy-start(f32[24]{0:T(128)} %param.14) | copy-start | bytes 292
  7.2 52.0 %copy-start.73 = (f32[24]{0:T(128)S(1)}, f32[24]{0:T(128)}, u32[]{:S(2)}) copy-start(f32[24]{0:T(128)} %param.19) | copy-start | bytes 292
  7.2 90.2 %all-gather.8.cloned.1.call-start = ((), (), s32[]{:S(2)}) async-start(), calls=%async_computation.12 | async-start | bytes 7299072 | tf_op jit(solution)/shard_map/all_gather | solution.py:136
  8.0 154.1 %all-gather.10.cloned.1.call-start = ((), (), s32[]{:S(2)}) async-start(), calls=%async_computation.13 | async-start | bytes 4718592 | tf_op jit(solution)/shard_map/all_gather | solution.py:145
  10.1 371.9 %all-gather.12.cloned.1.call-start = ((), (), s32[]{:S(2)}) async-start(), calls=%async_computation.14 | async-start | bytes 2433024 | tf_op jit(solution)/shard_map/all_gather | solution.py:137
  10.8 378.7 %all-gather.16.cloned.1.call-start = ((), (), s32[]{:S(2)}) async-start(), calls=%async_computation.16 | async-start | bytes 9732096 | tf_op jit(solution)/shard_map/all_gather | solution.py:139
  11.4 397.4 %all-gather.14.cloned.1.call-start = ((), (), s32[]{:S(2)}) async-start(), calls=%async_computation.15 | async-start | bytes 9732096 | tf_op jit(solution)/shard_map/all_gather | solution.py:138
  12.0 435.3 %all-gather.18.cloned.1.call-start = ((), (), s32[]{:S(2)}) async-start(), calls=%async_computation.17 | async-start | bytes 9732096 | tf_op jit(solution)/shard_map/all_gather | solution.py:140
  14.1 97.4 %copy-start.53 = (f32[2,256]{1,0:T(2,128)}, f32[2,256]{1,0:T(2,128)S(1)}, u32[]{:S(2)}) copy-start(f32[2,256]{1,0:T(2,128)S(1)} %broadcast_multiply_fusion.2) | copy-start | bytes 6148
  14.5 97.1 %copy-start.59 = (f32[2,256]{1,0:T(2,128)}, f32[2,256]{1,0:T(2,128)S(1)}, u32[]{:S(2)}) copy-start(f32[2,256]{1,0:T(2,128)S(1)} %fusion.301) | copy-start | bytes 6148
  97.4 14.1 copy-start.51
  111.5 11.6 copy-start.7
  111.6 5.6 collective-permute-start
  115.8 5.7 collective-permute-start.1
  127.9 21.7 %all-to-all-start.1 = ((f32[2,256,768]{1,0,2:T(2,128)}), f32[2,256,768]{1,0,2:T(2,128)S(1)}, u32[]{:S(2)}, u32[]{:S(2)}) async-start(f32[2,256,768]{1,0,2:T(2,128)} %copy.290), calls=%async_computation.1 | async-start | bytes 3145728 | tf_op jit(solution)/shard_map/all_to_all | solution.py:153
  149.6 12.4 copy-start.49
  149.6 24.5 %all-to-all-start = ((f32[2,256,768]{1,0,2:T(2,128)}), f32[2,256,768]{1,0,2:T(2,128)}, u32[]{:S(2)}, u32[]{:S(2)}) async-start(f32[2,256,768]{1,0,2:T(2,128)} %copy.275), calls=%async_computation | async-start | bytes 3145728 | tf_op jit(solution)/shard_map/all_to_all | solution.py:152
  165.9 126.7 %copy-start.31 = (f32[1,2048,192]{2,1,0:T(8,128)}, f32[1,2048,192]{2,1,0:T(8,128)S(1)}, u32[]{:S(2)}) copy-start(f32[1,2048,192]{2,1,0:T(8,128)S(1)} %get-tuple-element.90) | copy-start | bytes 4718596
  181.9 10.9 copy-start.14
  192.8 7.2 copy-start.12
  276.5 16.2 %copy-start.8 = (f32[2,64,32,192]{3,2,1,0:T(8,128)}, f32[2,64,32,192]{3,2,1,0:T(8,128)S(1)}, u32[]{:S(2)}) copy-start(f32[2,64,32,192]{3,2,1,0:T(8,128)S(1)} %copy.312) | copy-start | bytes 9437188
  348.8 27.2 %all-to-all-start.2 = ((f32[2,1024,192]{2,0,1:T(2,128)}), f32[2,1024,192]{2,0,1:T(2,128)S(1)}, u32[]{:S(2)}, u32[]{:S(2)}) async-start(f32[2,1024,192]{2,0,1:T(2,128)} %copy.327), calls=%async_computation.2 | async-start | bytes 4194304 | tf_op jit(solution)/shard_map/all_to_all | solution.py:156
  447.3 18.8 %copy-start.2 = (f32[2,256,3072]{2,1,0:T(8,128)S(1)}, f32[2,256,3072]{2,1,0:T(8,128)}, u32[]{:S(2)}) copy-start(f32[2,256,3072]{2,1,0:T(8,128)} %fusion.10) | copy-start | bytes 18874372
  447.3 44.9 %slice-start = ((s8[6291456]{0:T(1024)(128)(4,1)}), s8[4194304]{0:T(1024)(128)(4,1)S(1)}, s32[]{:S(2)}) async-start(s8[6291456]{0:T(1024)(128)(4,1)} %bitcast.399), calls=%async_computation.24 | async-start | bytes 8388608
  466.1 26.1 %copy-start.45 = (f32[2,256,3072]{2,1,0:T(8,128)}, f32[2,256,3072]{2,1,0:T(8,128)S(1)}, u32[]{:S(2)}) copy-start(f32[2,256,3072]{2,1,0:T(8,128)S(1)} %fusion) | copy-start | bytes 18874372
  466.1 26.1 %slice-start.1 = ((s8[6291456]{0:T(1024)(128)(4,1)}), s8[2097152]{0:T(1024)(128)(4,1)S(1)}, s32[]{:S(2)}) async-start(s8[6291456]{0:T(1024)(128)(4,1)} %bitcast.399), calls=%async_computation.25 | async-start | bytes 4194304
  540.2 7.8 copy-start.29
  551.7 24.4 %all-to-all-start.3 = ((f32[2,256,768]{1,0,2:T(2,128)}), f32[2,256,768]{1,0,2:T(2,128)}, u32[]{:S(2)}, u32[]{:S(2)}) async-start(f32[2,256,768]{1,0,2:T(2,128)} %copy.331), calls=%async_computation.3 | async-start | bytes 3145728 | tf_op jit(solution)/shard_map/all_to_all | solution.py:170
  556.0 458.2 %reduce-scatter.10.cloned.1.call-start = ((), (), s32[]{:S(2)}) async-start(), calls=%async_computation.19 | async-start | bytes 4718592 | tf_op jit(solution)/shard_map/reduce_scatter | solution.py:172
  644.4 6.7 copy-start.20
  668.3 8.4 copy-start.25
  728.6 8.8 copy-start.38
  749.5 29.3 %all-to-all-start.5 = ((f32[2,1024,192]{2,0,1:T(2,128)}), f32[2,1024,192]{2,0,1:T(2,128)}, u32[]{:S(2)}, u32[]{:S(2)}) async-start(f32[2,1024,192]{2,0,1:T(2,128)} %copy.362), calls=%async_computation.5 | async-start | bytes 4194304 | tf_op jit(solution)/shard_map/all_to_all | solution.py:175
  753.9 8.8 copy-start.36
  778.7 28.8 %all-to-all-start.4 = ((f32[2,1024,192]{2,0,1:T(2,128)}), f32[2,1024,192]{2,0,1:T(2,128)}, u32[]{:S(2)}, u32[]{:S(2)}) async-start(f32[2,1024,192]{2,0,1:T(2,128)} %copy.350), calls=%async_computation.4 | async-start | bytes 4194304 | tf_op jit(solution)/shard_map/all_to_all | solution.py:174
  783.2 233.0 %reduce-scatter.12.cloned.1.call-start = ((), (), s32[]{:S(2)}) async-start(), calls=%async_computation.20 | async-start | bytes 2433024 | tf_op jit(solution)/shard_map/reduce_scatter | solution.py:195
  791.5 224.7 %reduce-scatter.8.cloned.1.call-start = ((), (), s32[]{:S(2)}) async-start(), calls=%async_computation.18 | async-start | bytes 7299072 | tf_op jit(solution)/shard_map/reduce_scatter | solution.py:194
  807.5 10.2 copy-start.56
  807.5 10.2 copy-start.58
  817.7 16.8 %copy-start.4 = (f32[2,256,768]{2,1,0:T(8,128)S(1)}, f32[2,256,768]{2,1,0:T(8,128)}, u32[]{:S(2)}) copy-start(f32[2,256,768]{2,1,0:T(8,128)} %param.13) | copy-start | bytes 4718596
  817.7 16.8 %copy-start.43 = (f32[2,256,768]{2,1,0:T(8,128)S(1)}, f32[2,256,768]{2,1,0:T(8,128)}, u32[]{:S(2)}) copy-start(f32[2,256,768]{2,1,0:T(8,128)} %get-tuple-element.91) | copy-start | bytes 4718596
  817.7 16.8 %copy-start.46 = (f32[2,256,768]{2,1,0:T(8,128)S(1)}, f32[2,256,768]{2,1,0:T(8,128)}, u32[]{:S(2)}) copy-start(f32[2,256,768]{2,1,0:T(8,128)} %copy.366) | copy-start | bytes 4718596
  817.7 16.8 %copy-start.48 = (f32[2,256,768]{2,1,0:T(8,128)S(1)}, f32[2,256,768]{2,1,0:T(8,128)}, u32[]{:S(2)}) copy-start(f32[2,256,768]{2,1,0:T(8,128)} %copy.365) | copy-start | bytes 4718596
  817.7 16.8 %copy-start.52 = (f32[768]{0:T(1024)S(1)}, f32[768]{0:T(1024)}, u32[]{:S(2)}) copy-start(f32[768]{0:T(1024)} %copy-done.51) | copy-start | bytes 9220
  817.7 16.8 %copy-start.54 = (f32[2,256]{1,0:T(2,128)S(1)}, f32[2,256]{1,0:T(2,128)}, u32[]{:S(2)}) copy-start(f32[2,256]{1,0:T(2,128)} %copy-done.53) | copy-start | bytes 6148
  817.8 16.8 %copy-start.60 = (f32[2,256]{1,0:T(2,128)S(1)}, f32[2,256]{1,0:T(2,128)}, u32[]{:S(2)}) copy-start(f32[2,256]{1,0:T(2,128)} %copy-done.59) | copy-start | bytes 6148
  817.8 16.8 %copy-start.62 = (f32[2304]{0:T(1024)S(1)}, f32[2304]{0:T(1024)}, u32[]{:S(2)}) copy-start(f32[2304]{0:T(1024)} %copy-done.61) | copy-start | bytes 27652
  817.8 16.8 %copy-start.64 = (f32[2304]{0:T(1024)S(1)}, f32[2304]{0:T(1024)}, u32[]{:S(2)}) copy-start(f32[2304]{0:T(1024)} %copy-done.63) | copy-start | bytes 27652
  817.8 16.8 %copy-start.66 = (f32[2304]{0:T(1024)S(1)}, f32[2304]{0:T(1024)}, u32[]{:S(2)}) copy-start(f32[2304]{0:T(1024)} %copy-done.65) | copy-start | bytes 27652
  825.6 4.8 collective-permute-start.3
  828.9 5.7 collective-permute-start.2
  853.3 303.7 %reduce-scatter.14.cloned.1.call-start = ((), (), s32[]{:S(2)}) async-start(), calls=%async_computation.21 | async-start | bytes 9732096 | tf_op jit(solution)/shard_map/reduce_scatter | solution.py:196
  879.0 420.2 %reduce-scatter.16.cloned.1.call-start = ((), (), s32[]{:S(2)}) async-start(), calls=%async_computation.22 | async-start | bytes 9732096 | tf_op jit(solution)/shard_map/reduce_scatter | solution.py:197
  901.1 538.9 %reduce-scatter.18.cloned.1.call-start = ((), (), s32[]{:S(2)}) async-start(), calls=%async_computation.23 | async-start | bytes 9732096 | tf_op jit(solution)/shard_map/reduce_scatter | solution.py:198
  924.0 22.1 %copy-start.5 = (f32[2,256,768]{2,1,0:T(8,128)S(1)}, f32[2,256,768]{2,1,0:T(8,128)}, u32[]{:S(2)}) copy-start(f32[2,256,768]{2,1,0:T(8,128)} %param.13) | copy-start | bytes 4718596
  924.0 22.1 %copy-start.44 = (f32[2,256,768]{2,1,0:T(8,128)S(1)}, f32[2,256,768]{2,1,0:T(8,128)}, u32[]{:S(2)}) copy-start(f32[2,256,768]{2,1,0:T(8,128)} %get-tuple-element.91) | copy-start | bytes 4718596
  924.0 22.1 %copy-start.47 = (f32[2,256,768]{2,1,0:T(8,128)S(1)}, f32[2,256,768]{2,1,0:T(8,128)}, u32[]{:S(2)}) copy-start(f32[2,256,768]{2,1,0:T(8,128)} %copy.366) | copy-start | bytes 4718596
  946.1 19.7 %copy-start.68 = (f32[2,256]{1,0:T(2,128)S(1)}, f32[2,256]{1,0:T(2,128)}, u32[]{:S(2)}) copy-start(f32[2,256]{1,0:T(2,128)} %copy-done.67) | copy-start | bytes 6148
  946.1 22.1 %copy-start.69 = (f32[768]{0:T(1024)S(1)}, f32[768]{0:T(1024)}, u32[]{:S(2)}) copy-start(f32[768]{0:T(1024)} %get-tuple-element.49) | copy-start | bytes 9220
  965.8 44.9 %copy-start.6 = (f32[2,256,768]{2,1,0:T(8,128)S(1)}, f32[2,256,768]{2,1,0:T(8,128)}, u32[]{:S(2)}) copy-start(f32[2,256,768]{2,1,0:T(8,128)} %param.13) | copy-start | bytes 4718596
  965.8 474.2 %copy-start.1 = (f32[2,80,768]{2,1,0:T(8,128)S(1)}, f32[2,80,768]{2,1,0:T(8,128)}, u32[]{:S(2)}) copy-start(f32[2,80,768]{2,1,0:T(8,128)} %param.25) | copy-start | bytes 1474564
  (35 other events, 152.4 us)
Sparse Core Ops, SparseCore 0:
  11.1 76.9 all-gather.7
  89.7 45.2 all-gather.9
  138.0 57.9 all-gather.11
  198.9 80.9 all-gather.15
  282.8 80.7 all-gather.13
  366.4 80.8 all-gather.17
  687.8 48.5 reduce-scatter.9
  791.6 98.9 reduce-scatter.11
  897.8 118.0 reduce-scatter.7
  1022.3 134.7 reduce-scatter.13
  1164.5 134.6 reduce-scatter.15
  1305.5 134.3 reduce-scatter.17
where the time goes:
time: 1450 us
  matrix products  579 us (40%)
  waiting for transfers between devices  517 us (36%)
  local copies, waits for them, and re-layouts  126 us (9%)
  blocking collectives  122 us (8%)
  other arithmetic  49.2 us (3%)
  starting transfers between devices  37.7 us (3%)
  between operations  15.8 us (1%)
    dot_general x54, matrix products, contract(): jnp.einsum(pattern, left_side, right_side, precision=lax.Precision.HIGHEST)  579 us
    reduce_scatter x1, waiting for transfers between devices, body(): lax.psum_scatter(w_up_grad, ('seq', 'batch'), scatter_dimension=0, tiled=...  142 us
    reduce_scatter x1, waiting for transfers between devices, body(): lax.psum_scatter(w_gate_grad, ('seq', 'batch'), scatter_dimension=0, tile...  141 us
    reduce_scatter x1, waiting for transfers between devices, body(): lax.psum_scatter(w_down_grad, ('seq', 'batch'), scatter_dimension=0, tile...  141 us
    unnamed x2, blocking collectives  78.5 us
    all_gather x1, blocking collectives, body(): lax.all_gather(conv_weight, ('seq', 'batch'), axis=1, tiled=True)  43.8 us
  transfers between devices with their start and end apart: 22, of which 12 were waited for; matrix products, arithmetic and copies ran while one was open for 37% of the time, Pallas kernels for 0%

commit v1 on v0

v1 whole, which is shorter than its diff:
```python
import math

import jax
import jax.numpy as jnp
import numpy as np
from jax import lax
from jax.sharding import PartitionSpec as P

EPS = 1e-05
HIGH = lax.Precision.HIGH
RADIX = 8
FOLDED = 5


def contract(pattern, left_side, right_side):
    return jnp.einsum(pattern, left_side, right_side, precision=HIGH)


def swap(value, axis, distance):
    devices = lax.axis_size(axis)
    return lax.ppermute(value, axis, [(i, i ^ distance) for i in range(devices)])


def gather_pieces(value, axis, dim):
    half = value.shape[dim] // 2
    first = lax.slice_in_dim(value, 0, half, axis=dim)
    second = lax.slice_in_dim(value, half, 2 * half, axis=dim)
    first_one = swap(first, axis, 1)
    second_two = swap(second, axis, 2)
    first_two = swap(first, axis, 2)
    second_one = swap(second, axis, 1)
    first_three = swap(first_one, axis, 2)
    second_three = swap(second_two, axis, 1)
    return (
        value,
        jnp.concatenate([first_one, second_one], axis=dim),
        jnp.concatenate([first_two, second_two], axis=dim),
        jnp.concatenate([first_three, second_three], axis=dim),
    )


def scatter_pieces(pieces, axis, dim):
    half = pieces[0].shape[dim] // 2
    first = [lax.slice_in_dim(p, 0, half, axis=dim) for p in pieces]
    second = [lax.slice_in_dim(p, half, 2 * half, axis=dim) for p in pieces]
    first_three = swap(first[3], axis, 2)
    second_three = swap(second[3], axis, 1)
    first_two = swap(first[2], axis, 2)
    second_one = swap(second[1], axis, 1)
    first_one = swap(first[1] + first_three, axis, 1)
    second_two = swap(second[2] + second_three, axis, 2)
    return jnp.concatenate(
        [first[0] + first_two + first_one, second[0] + second_one + second_two], axis=dim
    )


def normalize(values):
    centered = values - jnp.mean(values, axis=-1, keepdims=True)
    inverse = lax.rsqrt(jnp.mean(centered * centered, axis=-1, keepdims=True) + EPS)
    return centered * inverse, inverse


def norm_pull(normed, inverse, grad):
    along = jnp.mean(grad * normed, axis=-1, keepdims=True)
    return (grad - jnp.mean(grad, axis=-1, keepdims=True) - normed * along) * inverse


def phase_tables(length):
    block = length // RADIX
    place = np.arange(block)[:, None]
    turn = np.arange(block)[None, :]
    forward, backward = [], []
    for phase in range(FOLDED):
        angle = 2.0 * np.pi * ((RADIX * turn + phase) * place % length) / length
        cos, sin = np.cos(angle), np.sin(angle)
        forward.append(np.block([[cos, -sin], [sin, cos]]))
        backward.append(np.block([[cos.T, sin.T], [-sin.T, cos.T]]))
    as_f32 = lambda t: jnp.asarray(np.stack(t).astype(np.float32))
    return as_f32(forward), as_f32(backward)


def dft(value, tables):
    block = tables.shape[1] // 2
    x0, x1, x2, x3 = [value[..., i * block : (i + 1) * block] for i in range(4)]
    root = math.sqrt(0.5)
    even, odd = x0 + x2, x1 + x3
    diff, tail = x0 - x2, (x1 - x3)
    slant, lean = tail * root, odd * root
    parts = [
        (even + odd, None),
        (x0 + slant, -x2 - lean),
        (diff, -tail),
        (x0 - slant, x2 - lean),
        (even - odd, None),
    ]
    out = []
    for phase, (real, imag) in enumerate(parts):
        if imag is None:
            out.append(contract("bck,kf->bcf", real, tables[phase, :block]))
        else:
            both = jnp.concatenate([real, imag], axis=-1)
            out.append(contract("bck,kf->bcf", both, tables[phase]))
    return out


def inverse_dft(spectra, tables):
    block = tables.shape[1] // 2
    root = math.sqrt(0.5)
    v0 = contract("bcf,fk->bck", spectra[0], tables[0, :, :block])
    v4 = contract("bcf,fk->bck", spectra[4], tables[4, :, :block])
    reals, imags = [None], [None]
    for phase in (1, 2, 3):
        both = contract("bcf,fk->bck", spectra[phase], tables[phase])
        reals.append(both[..., :block])
        imags.append(both[..., block:])
    _, r1, r2, r3 = reals
    _, i1, i2, i3 = imags
    plus, minus = v0 + v4, v0 - v4
    return jnp.concatenate(
        [
            plus + r1 + r2 + r3,
            minus - i2 + root * ((r1 - i1) - (r3 + i3)),
            plus - r2 - i1 + i3,
            minus + i2 + root * ((r3 - i3) - (r1 + i1)),
        ],
        axis=-1,
    )


def split_complex(value):
    block = value.shape[-1] // 2
    return value[..., :block], value[..., block:]


def times(left_side, right_side, conj=False):
    a, b = split_complex(left_side)
    c, d = split_complex(right_side)
    if conj:
        d = -d
    return jnp.concatenate([a * c - b * d, a * d + b * c], axis=-1)


def shift(value, step):
    zero = jnp.zeros_like(value[..., :1])
    if step < 0:
        return jnp.concatenate([zero, value[..., :-1]], axis=-1)
    return jnp.concatenate([value[..., 1:], zero], axis=-1)


def body(
    inputs,
    gain_one,
    w_in,
    conv_weight,
    kernel,
    w_out,
    gain_two,
    w_gate,
    w_up,
    w_down,
    mask_positions,
    mask_counts,
    grad_rows,
):
    shards = lax.axis_size("seq")
    groups = lax.axis_size("batch")
    s = lax.axis_index("seq")
    seqs, tokens, width = inputs.shape
    length = tokens * shards
    freqs = 2 * length
    block = freqs // RADIX
    own = width // shards
    rows = w_in.shape[0]
    hidden_own = w_gate.shape[1] // shards
    scale = 1.0 / math.sqrt(length)
    forward, backward = phase_tables(freqs)

    def columns(shard, blocks):
        wide = shard.reshape(rows, blocks, shards, -1)
        wide = lax.all_to_all(wide, "seq", split_axis=2, concat_axis=0, tiled=True)
        wide = wide.reshape(1, shards, rows, -1)
        full = lax.all_gather(wide, "batch", axis=0, tiled=True)
        return full.transpose(1, 0, 2, 3).reshape(width, -1)

    def columns_back(grad, blocks):
        parts = grad.reshape(shards, groups, rows, -1).transpose(1, 0, 2, 3)
        mine = lax.psum_scatter(parts, "batch", scatter_dimension=0, tiled=True)
        mine = mine.reshape(shards * rows, blocks, 1, -1)
        mine = lax.all_to_all(mine, "seq", split_axis=0, concat_axis=2, tiled=True)
        return mine.reshape(rows, -1)

    x_pieces = gather_pieces(inputs, "seq", 1)
    w_pre = columns(gain_one[:, None] * w_in, 3)
    taps_all = lax.all_gather(conv_weight, ("seq", "batch"), axis=1, tiled=True)
    taps = lax.dynamic_slice_in_dim(taps_all.reshape(3, 3, shards, own), s, 1, axis=2).reshape(3, 3 * own)

    wide = kernel.reshape(2, -1, RADIX, own)
    mirror = [(i, groups - 1 - i) for i in range(groups)]
    folded = lax.ppermute(wide[:, ::-1, :4:-1], "batch", mirror)
    folded = jnp.stack([wide[0, :, 1:4] + folded[0], wide[1, :, 1:4] - folded[1]])
    folded = jnp.concatenate([wide[:, :, :1], folded, wide[:, :, 4:5]], axis=2)
    folded = folded.transpose(2, 3, 0, 1)
    base = lax.all_gather(folded, "batch", axis=3, tiled=True).reshape(FOLDED, own, 2 * block)

    w_out_rows = lax.all_gather(w_out, "batch", axis=0, tiled=True)
    w_out_rel = jnp.concatenate(gather_pieces(w_out_rows, "seq", 0), axis=0)
    w_gate_own = columns(gain_two[:, None] * w_gate, 1)
    w_up_own = columns(gain_two[:, None] * w_up, 1)
    w_down_own = lax.all_gather(w_down, "batch", axis=0, tiled=True)

    x = jnp.zeros((seqs, length, width), jnp.float32)
    for d, piece in enumerate(x_pieces):
        x = lax.dynamic_update_slice(x, piece, (0, (s ^ d) * tokens, 0))
    n_one, _ = normalize(x)
    projected = contract("btd,dc->bct", n_one, w_pre)
    tap = taps[:, None, :, None]
    mixed = tap[0] * shift(projected, -1) + tap[1] * projected + tap[2] * shift(projected, 1)
    signal, gating, values = mixed[:, :own], mixed[:, own : 2 * own], mixed[:, 2 * own :]

    signal_hat = dft(signal, forward)
    values_hat = dft(values, forward)
    spectrum = []
    for phase in range(FOLDED):
        weight = scale if phase in (0, 4) else 2.0 * scale
        spectrum.append(base[phase] + weight * signal_hat[phase])
    products = [times(a, b) for a, b in zip(spectrum, values_hat)]
    long_conv = inverse_dft(products, backward) / freqs

    gated = gating * long_conv
    gated_rel = jnp.concatenate(gather_pieces(gated, "seq", 2), axis=1)
    residual = x + contract("bct,cd->btd", gated_rel, w_out_rel)

    slot = jnp.arange(mask_positions.shape[1], dtype=jnp.int32)
    live = slot[None, :] < mask_counts[:, None]
    places = jnp.arange(length, dtype=jnp.int32)
    select = ((mask_positions[:, :, None] == places) & live[:, :, None]).astype(jnp.float32)
    d_out = jnp.where(live[:, :, None], grad_rows, 0.0)

    n_two, _ = normalize(residual)
    gate = contract("btd,df->btf", n_two, w_gate_own)
    up = contract("btd,df->btf", n_two, w_up_own)
    hidden = jax.nn.gelu(gate, approximate=True) * up
    down = contract("btf,fd->btd", hidden, w_down_own)
    down_pieces = [
        lax.dynamic_slice_in_dim(down, (s ^ d) * tokens, tokens, axis=1) for d in range(4)
    ]
    outputs = scatter_pieces(down_pieces, "seq", 1)
    outputs = outputs + lax.dynamic_slice_in_dim(residual, s * tokens, tokens, axis=1)

    n_live, inverse_live = normalize(contract("bmt,btd->bmd", select, residual))

    def gated_unit(g, u):
        return jax.nn.gelu(g, approximate=True) * u

    hidden_live, unit_pull = jax.vjp(
        gated_unit,
        contract("bmd,df->bmf", n_live, w_gate_own),
        contract("bmd,df->bmf", n_live, w_up_own),
    )
    d_hidden = contract("bmd,fd->bmf", d_out, w_down_own)
    d_gate, d_up = unit_pull(d_hidden)
    w_down_part = contract("bmf,bmd->fd", hidden_live, d_out)
    w_gate_part = contract("bmd,bmf->df", n_live, d_gate)
    w_up_part = contract("bmd,bmf->df", n_live, d_up)
    e_two = contract("bmf,df->bmd", d_gate, w_gate_own) + contract("bmf,df->bmd", d_up, w_up_own)
    e_two = e_two + swap(e_two, "seq", 1)
    e_two = e_two + swap(e_two, "seq", 2)
    d_residual = d_out + norm_pull(n_live, inverse_live, e_two)
    w_out_own = w_out_rows
    d_gated = contract("bmd,cd->bmc", d_residual, w_out_own)
    gating_live = contract("bmt,bct->bmc", select, gating)
    long_live = contract("bmt,bct->bmc", select, long_conv)
    w_out_part = contract("bmc,bmd->cd", gating_live * long_live, d_residual)
    d_gating = contract("bmt,bmc->bct", select, d_gated * long_live)
    d_long = contract("bmt,bmc->bct", select, d_gated * gating_live)

    grad_hat = [g / freqs for g in dft(d_long, forward)]
    kernel_hat = [times(g, v, conj=True) for g, v in zip(grad_hat, values_hat)]
    kernel_part = jnp.stack([jnp.sum(k, axis=0) for k in kernel_hat])
    d_signal_hat = [
        k * (scale if phase in (0, 4) else 2.0 * scale) for phase, k in enumerate(kernel_hat)
    ]
    d_values_hat = [times(g, k, conj=True) for g, k in zip(grad_hat, spectrum)]
    d_signal = inverse_dft(d_signal_hat, backward)
    d_values = inverse_dft(d_values_hat, backward)
    d_mixed = jnp.concatenate([d_signal, d_gating, d_values], axis=1)
    taps_part = jnp.stack(
        [
            jnp.sum(shift(projected, -1) * d_mixed, axis=(0, 2)),
            jnp.sum(projected * d_mixed, axis=(0, 2)),
            jnp.sum(shift(projected, 1) * d_mixed, axis=(0, 2)),
        ]
    )
    d_projected = tap[0] * shift(d_mixed, 1) + tap[1] * d_mixed + tap[2] * shift(d_mixed, -1)
    w_in_part = contract("btd,bct->dc", n_one, d_projected)
    e_one = contract("bct,dc->btd", d_projected, w_pre)
    e_pieces = [
        lax.dynamic_slice_in_dim(e_one, (s ^ d) * tokens, tokens, axis=1) for d in range(4)
    ]
    e_own = scatter_pieces(e_pieces, "seq", 1)
    n_own, inverse_own = normalize(inputs)
    select_own = lax.dynamic_slice_in_dim(select, s * tokens, tokens, axis=2)
    input_grad = norm_pull(n_own, inverse_own, e_own) + contract("bmt,bmd->btd", select_own, d_residual)

    w_down_sum = lax.psum_scatter(w_down_part, "batch", scatter_dimension=0, tiled=True)
    w_gate_sum = columns_back(w_gate_part, 1)
    w_up_sum = columns_back(w_up_part, 1)
    w_out_sum = lax.psum_scatter(w_out_part, "batch", scatter_dimension=0, tiled=True)
    w_in_sum = columns_back(w_in_part, 3)
    gain_one_sum = jnp.sum(w_in * w_in_sum, axis=1)
    gain_two_sum = jnp.sum(w_gate * w_gate_sum, axis=1) + jnp.sum(w_up * w_up_sum, axis=1)

    placed = jnp.zeros((3, 3, shards, own), jnp.float32)
    placed = lax.dynamic_update_slice(placed, taps_part.reshape(3, 3, 1, own), (0, 0, s, 0))
    taps_sum = lax.psum_scatter(
        placed.reshape(3, 3 * width), ("seq", "batch"), scatter_dimension=1, tiled=True
    )

    kernel_part = kernel_part.reshape(FOLDED, own, 2, block)
    kernel_sum = lax.psum_scatter(kernel_part, "batch", scatter_dimension=3, tiled=True)
    kernel_sum = kernel_sum.transpose(2, 3, 0, 1)
    mirrored = lax.ppermute(kernel_sum[:, ::-1, 3:0:-1], "batch", mirror)
    mirrored = jnp.stack([mirrored[0], -mirrored[1]])
    kernel_grad = jnp.concatenate([kernel_sum, mirrored], axis=2).reshape(kernel.shape)

    return (
        outputs,
        input_grad,
        gain_one_sum,
        gain_one[:, None] * w_in_sum,
        taps_sum,
        kernel_grad,
        w_out_sum,
        gain_two_sum,
        gain_two[:, None] * w_gate_sum,
        gain_two[:, None] * w_up_sum,
        w_down_sum,
    )


def solution(mesh):
    split = ("seq", "batch")
    placed = (
        P("batch", "seq", None),
        P(split),
        P(split, None),
        P(None, split),
        P(None, "batch", "seq"),
        P(split, None),
        P(split),
        P(split, None),
        P(split, None),
        P(split, None),
        P("batch", None),
        P("batch"),
        P("batch", None, None),
    )
    return jax.shard_map(
        body,
        mesh=mesh,
        in_specs=placed,
        out_specs=(
            P("batch", "seq", None),
            P("batch", "seq", None),
            P(split),
            P(split, None),
            P(None, split),
            P(None, "batch", "seq"),
            P(split, None),
            P(split),
            P(split, None),
            P(split, None),
            P(split, None),
        ),
        check_vma=False,
    )
```

time: 1450 us -> 736 us (0.51)
  matrix products: 579 us -> 147 us
  waiting for transfers between devices: 517 us -> 170 us
  blocking collectives: 122 us -> 151 us
  other arithmetic: 49.2 us -> 76 us
  starting transfers between devices: 37.7 us -> 52.4 us
    dot_general x54 -> x53, matrix products: 579 us -> 147 us  [contract(): return jnp.einsum(pattern, left_side, right_side, precision=HIGH)]
    reduce_scatter x6 -> x2, waiting for transfers between devices: 424 us -> 16.1 us  [the longest x1 16.1 us: body(): lax.psum_scatter(w_down_part, 'batch', scatter_dimension=0, tiled=True)]
    ppermute x4 -> x34, waiting for transfers between devices: 8.41 us -> 146 us  [the longest x32 134 us: swap(): lax.ppermute(value, axis, [(i, i ^ distance) for i in range(devices)])]
    all_to_all x6 -> x4, waiting for transfers between devices: 62.7 us -> 7.69 us  [the longest x3 7.69 us: columns_back(): mine = lax.all_to_all(mine, 'seq', split_axis=0, concat_axis=2, tiled=True)]
    all_to_all x11 -> x5, local copies, waits for them, and re-layouts: 30.2 us -> 0.52 us  [the longest x4 0.37 us: columns_back(): mine = lax.all_to_all(mine, 'seq', split_axis=0, concat_axis=2, tiled=True)]
    all_gather x1 -> x2, blocking collectives: 43.8 us -> 72.4 us  [the longest x1 41.7 us: body(): taps_all = lax.all_gather(conv_weight, ('seq', 'batch'), axis=1, tiled=True)]
    slice x5 -> x17, local copies, waits for them, and re-layouts: 4.18 us -> 32.6 us  [the longest x6 21.2 us: body(): spectrum.append(base[phase] + weight * signal_hat[phase])]
    ppermute x4 -> x34, starting transfers between devices: 10.2 us -> 37.6 us  [the longest x32 34.9 us: swap(): lax.ppermute(value, axis, [(i, i ^ distance) for i in range(devices)])]
  transfers between devices with their start and end apart: 22 -> 46, of which waited for: 12 -> 24; matrix products, arithmetic and copies ran while one was open for 37% -> 30% of each run, Pallas kernels for 0% -> 0%
where the time goes in v1:
time: 736 us; the launch traced here: 728 us
  waiting for transfers between devices  170 us (23%)
  blocking collectives  151 us (21%)
  matrix products  147 us (20%)
  local copies, waits for them, and re-layouts  114 us (15%)
  other arithmetic  76 us (10%)
  starting transfers between devices  52.4 us (7%)
  between operations  17.2 us (2%)
    dot_general x53, matrix products, contract(): return jnp.einsum(pattern, left_side, right_side, precision=HIGH)  147 us
    ppermute x32, waiting for transfers between devices, swap(): lax.ppermute(value, axis, [(i, i ^ distance) for i in range(devices)])  134 us
    unnamed x1, blocking collectives  57.5 us
    all_gather x1, blocking collectives, body(): taps_all = lax.all_gather(conv_weight, ('seq', 'batch'), axis=1, tiled=True)  41.7 us
    unnamed x281, local copies, waits for them, and re-layouts  40.8 us
    ppermute x32, starting transfers between devices, swap(): lax.ppermute(value, axis, [(i, i ^ distance) for i in range(devices)])  34.9 us
    all_gather x1, blocking collectives, body(): w_out_rows = lax.all_gather(w_out, 'batch', axis=0, tiled=True)  30.7 us
    slice x6, local copies, waits for them, and re-layouts, body(): spectrum.append(base[phase] + weight * signal_hat[phase])  21.2 us
  transfers between devices with their start and end apart: 46, of which 24 were waited for; matrix products, arithmetic and copies ran while one was open for 30% of the time, Pallas kernels for 0%

profile of v1, /device:TPU:0, one launch (start us, length us, event | category | flops | bytes accessed | tf_op | source)
XLA Modules:
  0.0 727.5 jit_solution(10506260014371547771)
XLA Ops:
  8.6 11.3 %all_to_all.90 = f32[24,3,4,192]{3,0,1,2:T(8,128)S(1)} all-to-all(f32[24,3,4,192]{3,0,1,2:T(8,128)S(1)} %copy.120), channel_id=1, replica_groups=mesh['seq'=4,'batch'=8] {'seq'}, dimensions={2} | all-to-all | bytes 442368 | tf_op jit(solution)/shard_map/all_to_all | solution.py:180
  24.6 8.6 %collective-permute-done.6 = f32[2,32,3,192]{3,2,1,0:T(4,128)S(1)} collective-permute-done((f32[2,32,3,192]{3,2,1,0:T(4,128)S(1)}, f32[2,32,3,192]{3,2,1,0:T(4,128)S(1)}, u32[]{:S(2)}, u32[]{:S(2)}) %collective-permute-start.6) | collective-permute-done | bytes 147488 | tf_op jit(solution)/shard_map/ppermute | solution.py:199
  35.5 9.8 %all_to_all.91 = f32[24,1,4,768]{3,0,1,2:T(8,128)} all-to-all(f32[24,1,4,768]{3,0,1,2:T(8,128)S(1)} %copy.134), channel_id=1, replica_groups=mesh['seq'=4,'batch'=8] {'seq'}, dimensions={2} | all-to-all | bytes 589824 | tf_op jit(solution)/shard_map/all_to_all | solution.py:180
  51.1 16.5 %collective-permute-done = f32[2,128,768]{1,2,0:T(8,128)} collective-permute-done((f32[2,128,768]{1,2,0:T(8,128)}, f32[2,128,768]{1,2,0:T(8,128)}, u32[]{:S(2)}, u32[]{:S(2)}) %collective-permute-start) | collective-permute-done | bytes 786464 | tf_op jit(solution)/shard_map/ppermute | solution.py:21
  70.7 3.5 all-to-all-start.2
  74.2 30.7 %all_gather.24 = f32[192,768]{1,0:T(8,128)S(1)} all-gather(f32[24,768]{1,0:T(8,128)S(1)} %copy-done.103), channel_id=1, replica_groups=mesh['seq'=4,'batch'=8] {'batch'}, dimensions={0}, use_global_device_ids=true | all-gather | bytes 663552 | tf_op jit(solution)/shard_map/all_gather | solution.py:205
  105.0 41.7 %all-gather.2 = f32[32,72,3]{1,2,0:T(4,128)S(1)} all-gather(f32[1,72,3]{1,2,0:T(4,128)S(1)} %bitcast.230), channel_id=1, replica_groups=mesh['seq'=4,'batch'=8] {'seq','batch'}, dimensions={0}, use_global_device_ids=true | all-gather | bytes 28512 | tf_op jit(solution)/shard_map/all_gather | solution.py:194
  148.3 3.5 broadcast_in_dim.12
  154.0 2.7 maximum_dynamic-update-slice_fusion
  156.7 2.7 maximum_dynamic-update-slice_fusion.1
  159.4 2.7 maximum_dynamic-update-slice_fusion.2
  162.0 3.2 reduce_sum.207
  165.3 3.6 multiply_reduce_fusion.1
  171.9 9.0 %fusion.55 = f32[2,576,1024]{2,1,0:T(8,128)S(1)} fusion(f32[768,576,1]{1,0,2:T(8,128)S(1)} %bitcast.198, f32[2,1024,768]{1,2,0:T(8,128)} %maximum_dynamic-update-slice_fusion.2, f32[2,1024]{1,0:T(2,128)S(1)} %add_rsqrt_fusion.1, f32[2,1024]{1,0:T(2,128)S(1)} %broadcast_multiply_fusion.7), kind=kOutput, calls=%fused_computation.61 | convolution fusion | flops 5438963712 | bytes 12795904 | tf_op jit(solution)/shard_map/btd,dc->bct/dot_general | solution.py:16
  196.9 11.2 %fusion.263 = (f32[1,192,2,256]{1,0,3,2:T(1,128)}, f32[1,192,2,256]{1,0,3,2:T(1,128)}, f32[1,192,2,256]{1,0,3,2:T(1,128)}, f32[1,192,2,256]{1,0,3,2:T(1,128)}, f32[1,192,2,256]{1,0,3,2:T(1,128)}) fusion(f32[5,192,2,256]{1,0,3,2:T(8,128)} %all-gather.11.cloned.1.call-done), kind=kLoop, calls=%fused_computation.417 | loop fusion | bytes 3932160 | tf_op jit(solution)/shard_map/slice | solution.py:225
  249.0 24.0 %collective-permute-done.16 = f32[96,768]{0,1:T(8,128)S(1)} collective-permute-done((f32[96,768]{0,1:T(8,128)S(1)}, f32[96,768]{0,1:T(8,128)S(1)}, u32[]{:S(2)}, u32[]{:S(2)}) %collective-permute-start.16) | collective-permute-done | bytes 294944 | tf_op jit(solution)/shard_map/ppermute | solution.py:21
  275.2 6.9 collective-permute-done.13
  284.1 5.9 collective-permute-done.18
  294.3 3.7 concatenate.158
  300.1 3.0 fusion.51
  307.0 4.2 collective-permute-done.9
  311.1 14.7 %collective-permute-done.11 = f32[2,192,512]{2,1,0:T(8,128)} collective-permute-done((f32[2,192,512]{2,1,0:T(8,128)}, f32[2,192,512]{2,1,0:T(8,128)}, u32[]{:S(2)}, u32[]{:S(2)}) %collective-permute-start.11) | collective-permute-done | bytes 786464 | tf_op jit(solution)/shard_map/ppermute | solution.py:21
  326.1 11.6 %fusion.269 = (f32[2,1024]{1,0:T(2,128)S(1)}, f32[2,1024,768]{1,2,0:T(8,128)S(1)}) fusion(f32[2,1024,768]{1,2,0:T(8,128)} %maximum_dynamic-update-slice_fusion.2, f32[768,768]{0,1:T(8,128)} %concatenate.158, f32[2,192,512]{2,1,0:T(8,128)} %collective-permute-done.12, f32[2,192,512]{2,1,0:T(8,128)} %collective-permute-done.11, ...), kind=kOutput, calls=%fused_computation.423 | convolution fusion | flops 7260338176 | bytes 21241856 | tf_op jit(solution)/shard_map/bct,cd->btd/dot_general | solution.py:16
  346.8 2.8 fusion.187
  349.5 7.3 collective-permute-done.25
  358.0 3.0 fusion.188
  361.0 6.9 collective-permute-done.26
  394.1 2.7 multiply_subtract_fusion.9
  410.8 6.9 copy.153
  417.8 2.4 fusion.129
  420.3 2.4 fusion.137
  427.9 6.4 multiply_reduce_fusion.4
  434.3 3.7 fusion.261
  438.1 3.9 multiply_add_fusion
  442.0 13.1 %fusion.28 = f32[768,576,1]{1,0,2:T(8,128)} fusion(f32[2,576,1024]{2,1,0:T(8,128)S(1)} %multiply_add_fusion, f32[2,1024,768]{1,2,0:T(8,128)} %maximum_dynamic-update-slice_fusion.2, f32[2,1024]{1,0:T(2,128)S(1)} %copy-done.114, f32[2,1024]{1,0:T(2,128)S(1)} %copy-done.105), kind=kOutput, calls=%fused_computation.30 | convolution fusion | flops 5438963712 | bytes 12795904 | tf_op jit(solution)/shard_map/btd,bct->dc/dot_general | solution.py:16
  455.8 3.7 multiply_reduce_fusion
  459.6 12.6 %fusion.24 = f32[2,1024,768]{2,1,0:T(8,128)S(1)} fusion(f32[768,768,1]{1,0,2:T(8,128)} %bitcast.193, f32[2,1024,768]{1,2,0:T(8,128)} %copy-done.6, f32[2,1024]{1,0:T(2,128)S(1)} %add_rsqrt_fusion, f32[2,1024]{1,0:T(2,128)S(1)} %copy-done.106), kind=kOutput, calls=%fused_computation.26 | convolution fusion | flops 7250903040 | bytes 14958592 | tf_op jit(solution)/shard_map/btd,df->btf/dot_general | solution.py:16
  472.3 9.7 %fusion.26 = f32[2,1024,768]{2,1,0:T(8,128)S(1)} fusion(f32[768,768,1]{1,0,2:T(8,128)S(1)} %bitcast.190, f32[2,1024,768]{1,2,0:T(8,128)S(1)} %bitcast.187, f32[2,1024]{1,0:T(2,128)S(1)} %add_rsqrt_fusion, f32[2,1024]{1,0:T(2,128)S(1)} %copy-done.106), kind=kOutput, calls=%fused_computation.28 | convolution fusion | flops 7250903040 | bytes 14958592 | tf_op jit(solution)/shard_map/btd,df->btf/dot_general | solution.py:16
  482.1 13.5 %fusion.271 = f32[2,1024,768]{2,1,0:T(8,128)S(1)} fusion(f32[2,576,1024]{2,1,0:T(8,128)S(1)} %bitcast.195, f32[768,576,1]{1,0,2:T(8,128)S(1)} %bitcast.199), kind=kOutput, calls=%fused_computation.425 | convolution fusion | flops 5435817984 | bytes 12779520 | tf_op jit(solution)/shard_map/bct,dc->btd/dot_general | solution.py:16
  495.6 2.7 copy-done.7
  500.6 9.5 %fusion.8 = f32[2,1024,768]{1,2,0:T(8,128)S(1)} fusion(f32[2,1024,768]{2,1,0:T(8,128)S(1)} %fusion.24, f32[2,1024,768]{2,1,0:T(8,128)S(1)} %fusion.26, f32[768,768]{1,0:T(8,128)S(1)} %copy-done.67), kind=kOutput, calls=%fused_computation.9 | convolution fusion | flops 7261913088 | bytes 21233664 | tf_op jit(solution)/shard_map/btf,fd->btd/dot_general | solution.py:16
  510.1 2.6 copy-done.49
  519.2 2.4 dynamic-slice_add_fusion.2
  521.6 4.0 collective-permute-start.29
  525.9 10.2 %collective-permute-done.20 = f32[2,128,768]{1,2,0:T(8,128)} collective-permute-done((f32[2,128,768]{1,2,0:T(8,128)}, f32[2,128,768]{1,2,0:T(8,128)}, u32[]{:S(2)}, u32[]{:S(2)}) %collective-permute-start.20) | collective-permute-done | bytes 786464 | tf_op jit(solution)/shard_map/ppermute | solution.py:21
  538.4 3.9 collective-permute-start.21
  542.3 3.8 convolution_bitcast_fusion
  546.1 6.8 collective-permute-done.27
  552.9 3.6 fusion.68
  556.5 4.3 collective-permute-start.31
  561.0 5.8 collective-permute-done.19
  566.8 11.2 %collective-permute-done.21 = f32[2,128,768]{1,2,0:T(8,128)} collective-permute-done((f32[2,128,768]{1,2,0:T(8,128)}, f32[2,128,768]{1,2,0:T(8,128)}, u32[]{:S(2)}, u32[]{:S(2)}) %collective-permute-start.21) | collective-permute-done | bytes 786464 | tf_op jit(solution)/shard_map/ppermute | solution.py:21
  578.0 3.9 fusion.70
  585.6 9.3 %collective-permute-done.31 = f32[2,128,768]{2,1,0:T(8,128)} collective-permute-done((f32[2,128,768]{2,1,0:T(8,128)}, f32[2,128,768]{2,1,0:T(8,128)}, u32[]{:S(2)}, u32[]{:S(2)}) %collective-permute-start.31) | collective-permute-done | bytes 786464 | tf_op jit(solution)/shard_map/ppermute | solution.py:21
  597.7 57.5 %all-reduce.5 = f32[3,2304]{1,0:T(4,128)S(1)} all-reduce(f32[3,2304]{1,0:T(4,128)S(1)} %reshape.234), channel_id=5, replica_groups=mesh['seq'=4,'batch'=8] {'seq','batch'}, use_global_device_ids=true, to_apply=%region_17.18.clone | all-reduce | flops 6912 | bytes 55296
  657.6 3.0 maximum_add_fusion
  660.6 3.0 copy.161
  671.8 3.6 all-to-all-start.3
  681.6 2.6 collective-permute-done.33
  684.2 4.0 all-to-all-start.4
  689.8 3.9 all-to-all-done.4
  693.7 3.5 all-to-all-start.5
  698.8 3.8 all-to-all-done.5
  704.4 16.1 %reduce-scatter.9.cloned.1.call-done = f32[96,768]{1,0:T(8,128)} async-done(((f32[768,768]{1,0:T(8,128)}), f32[96,768]{1,0:T(8,128)}) %reduce-scatter.9.cloned.1.call-update) | async-done | bytes 294928 | tf_op jit(solution)/shard_map/reduce_scatter | solution.py:305
  (511 shorter events, 190.1 us)
Async XLA Ops:
  7.2 28.0 %copy-start.97 = (f32[24,3072]{1,0:T(8,128)S(1)}, f32[24,3072]{1,0:T(8,128)}, u32[]{:S(2)}) copy-start(f32[24,3072]{1,0:T(8,128)} %param.23) | copy-start | bytes 884740
  7.2 28.0 %copy-start.95 = (f32[24,3072]{1,0:T(8,128)S(1)}, f32[24,3072]{1,0:T(8,128)}, u32[]{:S(2)}) copy-start(f32[24,3072]{1,0:T(8,128)} %param.22) | copy-start | bytes 884740
  7.2 28.0 %copy-start.115 = (f32[24]{0:T(128)S(1)}, f32[24]{0:T(128)}, u32[]{:S(2)}) copy-start(f32[24]{0:T(128)} %param.21) | copy-start | bytes 292
  7.2 161.7 %all-gather.9.cloned.1.call-start = ((), (), s32[]{:S(2)}) async-start(), calls=%async_computation.8 | async-start | bytes 2211840 | tf_op jit(solution)/shard_map/all_gather | solution.py:182
  19.9 25.4 %copy-start.4 = (f32[2,256,768]{2,1,0:T(8,128)S(1)}, f32[2,256,768]{2,1,0:T(8,128)}, u32[]{:S(2)}) copy-start(f32[2,256,768]{2,1,0:T(8,128)} %param.15) | copy-start | bytes 4718596
  21.0 175.9 %all-gather.11.cloned.1.call-start = ((), (), s32[]{:S(2)}) async-start(), calls=%async_computation.9 | async-start | bytes 4718592 | tf_op jit(solution)/shard_map/all_gather | solution.py:203
  22.7 10.5 %collective-permute-start.6 = (f32[2,32,3,192]{3,2,1,0:T(4,128)S(1)}, f32[2,32,3,192]{3,2,1,0:T(4,128)S(1)}, u32[]{:S(2)}, u32[]{:S(2)}) collective-permute-start(f32[2,32,3,192]{3,2,1,0:T(4,128)S(1)} %rev.6), channel_id=1, source_target_pairs={{0,7},{1,6},{2,5},{3,4},{4,3},{5,2},{6,1},{7,0},{8,15},{9,14},{10,... | collective-permute-start | bytes 442376 | tf_op jit(solution)/shard_map/ppermute | solution.py:199
  34.4 265.7 %all-gather.13.cloned.1.call-start = ((), (), s32[]{:S(2)}) async-start(), calls=%async_computation.10 | async-start | bytes 2654208 | tf_op jit(solution)/shard_map/all_gather | solution.py:209
  35.1 268.1 %all-gather.15.cloned.1.call-start = ((), (), s32[]{:S(2)}) async-start(), calls=%async_computation.13 | async-start | bytes 2654208 | tf_op jit(solution)/shard_map/all_gather | solution.py:182
  35.4 38.8 %copy-start.103 = (f32[24,768]{1,0:T(8,128)S(1)}, f32[24,768]{1,0:T(8,128)}, u32[]{:S(2)}) copy-start(f32[24,768]{1,0:T(8,128)} %param.20) | copy-start | bytes 221188
  35.5 69.4 %copy-start.117 = (f32[3,72]{1,0:T(4,128)S(1)}, f32[3,72]{1,0:T(4,128)}, u32[]{:S(2)}) copy-start(f32[3,72]{1,0:T(4,128)} %param.18) | copy-start | bytes 2596
  47.0 20.5 %collective-permute-start = (f32[2,128,768]{1,2,0:T(8,128)}, f32[2,128,768]{1,2,0:T(8,128)}, u32[]{:S(2)}, u32[]{:S(2)}) collective-permute-start(f32[2,128,768]{1,2,0:T(8,128)} %get-tuple-element.161), channel_id=1, source_target_pairs={{0,8},{8,0},{16,24},{24,16},{1,9},{9,1},{17,25},{25,17},{2,10},{10... | collective-permute-start | bytes 2359304 | tf_op jit(solution)/shard_map/ppermute | solution.py:21
  47.8 20.7 %collective-permute-start.3 = (f32[2,128,768]{1,2,0:T(8,128)}, f32[2,128,768]{1,2,0:T(8,128)}, u32[]{:S(2)}, u32[]{:S(2)}) collective-permute-start(f32[2,128,768]{1,2,0:T(8,128)} %get-tuple-element.162), channel_id=1, source_target_pairs={{0,16},{8,24},{16,0},{24,8},{1,17},{9,25},{17,1},{25,9},{2,18},{10... | collective-permute-start | bytes 2359304 | tf_op jit(solution)/shard_map/ppermute | solution.py:21
  48.2 105.7 %collective-permute-start.1 = (f32[2,128,768]{1,2,0:T(8,128)}, f32[2,128,768]{1,2,0:T(8,128)}, u32[]{:S(2)}, u32[]{:S(2)}) collective-permute-start(f32[2,128,768]{1,2,0:T(8,128)} %get-tuple-element.162), channel_id=1, source_target_pairs={{0,8},{8,0},{16,24},{24,16},{1,9},{9,1},{17,25},{25,17},{2,10},{10... | collective-permute-start | bytes 2359304 | tf_op jit(solution)/shard_map/ppermute | solution.py:21
  49.8 106.9 %collective-permute-start.2 = (f32[2,128,768]{1,2,0:T(8,128)}, f32[2,128,768]{1,2,0:T(8,128)}, u32[]{:S(2)}, u32[]{:S(2)}) collective-permute-start(f32[2,128,768]{1,2,0:T(8,128)} %get-tuple-element.161), channel_id=1, source_target_pairs={{0,16},{8,24},{16,0},{24,8},{1,17},{9,25},{17,1},{25,9},{2,18},{10... | collective-permute-start | bytes 2359304 | tf_op jit(solution)/shard_map/ppermute | solution.py:21
  67.6 91.8 %collective-permute-start.4 = (f32[2,128,768]{1,2,0:T(8,128)}, f32[2,128,768]{1,2,0:T(8,128)}, u32[]{:S(2)}, u32[]{:S(2)}) collective-permute-start(f32[2,128,768]{1,2,0:T(8,128)} %collective-permute-done), channel_id=1, source_target_pairs={{0,16},{8,24},{16,0},{24,8},{1,17},{9,25},{17,1},{25,9},{2,18},{10... | collective-permute-start | bytes 2359304 | tf_op jit(solution)/shard_map/ppermute | solution.py:21
  68.5 90.9 %collective-permute-start.5 = (f32[2,128,768]{1,2,0:T(8,128)}, f32[2,128,768]{1,2,0:T(8,128)}, u32[]{:S(2)}, u32[]{:S(2)}) collective-permute-start(f32[2,128,768]{1,2,0:T(8,128)} %collective-permute-done.3), channel_id=1, source_target_pairs={{0,8},{8,0},{16,24},{24,16},{1,9},{9,1},{17,25},{25,17},{2,10},{10... | collective-permute-start | bytes 2359304 | tf_op jit(solution)/shard_map/ppermute | solution.py:21
  70.7 82.5 %all-to-all-start.2 = ((f32[24,1,4,768]{3,0,1,2:T(8,128)}), f32[24,1,4,768]{3,0,1,2:T(8,128)S(1)}, u32[]{:S(2)}, u32[]{:S(2)}) async-start(f32[24,1,4,768]{3,0,1,2:T(8,128)} %copy.138), calls=%async_computation.2 | async-start | bytes 589824 | tf_op jit(solution)/shard_map/all_to_all | solution.py:180
  74.2 230.9 %all-gather.17.cloned.1.call-start = ((), (), s32[]{:S(2)}) async-start(), calls=%async_computation.14 | async-start | bytes 2654208 | tf_op jit(solution)/shard_map/all_gather | solution.py:182
  105.0 48.2 %copy-start.50 = (f32[192,768]{1,0:T(8,128)}, f32[192,768]{1,0:T(8,128)S(1)}, u32[]{:S(2)}) copy-start(f32[192,768]{1,0:T(8,128)S(1)} %all_gather.24) | copy-start | bytes 1769476
  153.9 514.1 %all-reduce.12.cloned.1.call-start = ((), (), s32[]{:S(2)}) async-start(), calls=%async_computation.15 | async-start | bytes 18612224
  240.0 52.5 %copy-start.119 = (s32[2]{0:T(128)S(1)}, s32[2]{0:T(128)}, u32[]{:S(2)}) copy-start(s32[2]{0:T(128)} %param.26) | copy-start | bytes 28
  243.4 54.6 %copy-start.107 = (s32[2,80]{1,0:T(2,128)S(1)}, s32[2,80]{1,0:T(2,128)}, u32[]{:S(2)}) copy-start(s32[2,80]{1,0:T(2,128)} %param.25) | copy-start | bytes 1924
  244.7 55.4 %copy-start.61 = (f32[2,80,768]{2,1,0:T(8,128)S(1)}, f32[2,80,768]{2,1,0:T(8,128)}, u32[]{:S(2)}) copy-start(f32[2,80,768]{2,1,0:T(8,128)} %param.27) | copy-start | bytes 1474564
  244.7 45.6 %collective-permute-start.7 = (f32[2,192,512]{2,1,0:T(8,128)}, f32[2,192,512]{2,1,0:T(8,128)}, u32[]{:S(2)}, u32[]{:S(2)}) collective-permute-start(f32[2,192,512]{2,1,0:T(8,128)} %get-tuple-element.149), channel_id=1, source_target_pairs={{0,8},{8,0},{16,24},{24,16},{1,9},{9,1},{17,25},{25,17},{2,10},{10... | collective-permute-start | bytes 2359304 | tf_op jit(solution)/shard_map/ppermute | solution.py:21
  244.7 46.1 %collective-permute-start.10 = (f32[2,192,512]{2,1,0:T(8,128)}, f32[2,192,512]{2,1,0:T(8,128)}, u32[]{:S(2)}, u32[]{:S(2)}) collective-permute-start(f32[2,192,512]{2,1,0:T(8,128)} %get-tuple-element.150), channel_id=1, source_target_pairs={{0,16},{8,24},{16,0},{24,8},{1,17},{9,25},{17,1},{25,9},{2,18},{10... | collective-permute-start | bytes 2359304 | tf_op jit(solution)/shard_map/ppermute | solution.py:21
  245.3 27.8 %collective-permute-start.16 = (f32[96,768]{0,1:T(8,128)S(1)}, f32[96,768]{0,1:T(8,128)S(1)}, u32[]{:S(2)}, u32[]{:S(2)}) collective-permute-start(f32[96,768]{0,1:T(8,128)S(1)} %get-tuple-element.173), channel_id=1, source_target_pairs={{0,16},{8,24},{16,0},{24,8},{1,17},{9,25},{17,1},{25,9},{2,18},{10... | collective-permute-start | bytes 884744 | tf_op jit(solution)/shard_map/ppermute | solution.py:21
  247.0 26.7 %collective-permute-start.14 = (f32[96,768]{0,1:T(8,128)S(1)}, f32[96,768]{0,1:T(8,128)S(1)}, u32[]{:S(2)}, u32[]{:S(2)}) collective-permute-start(f32[96,768]{0,1:T(8,128)S(1)} %get-tuple-element.173), channel_id=1, source_target_pairs={{0,8},{8,0},{16,24},{24,16},{1,9},{9,1},{17,25},{25,17},{2,10},{10... | collective-permute-start | bytes 884744 | tf_op jit(solution)/shard_map/ppermute | solution.py:21
  249.0 33.1 %collective-permute-start.13 = (f32[96,768]{0,1:T(8,128)S(1)}, f32[96,768]{0,1:T(8,128)S(1)}, u32[]{:S(2)}, u32[]{:S(2)}) collective-permute-start(f32[96,768]{0,1:T(8,128)S(1)} %get-tuple-element.174), channel_id=1, source_target_pairs={{0,8},{8,0},{16,24},{24,16},{1,9},{9,1},{17,25},{25,17},{2,10},{10... | collective-permute-start | bytes 884744 | tf_op jit(solution)/shard_map/ppermute | solution.py:21
  273.1 10.5 %collective-permute-start.15 = (f32[96,768]{0,1:T(8,128)S(1)}, f32[96,768]{0,1:T(8,128)S(1)}, u32[]{:S(2)}, u32[]{:S(2)}) collective-permute-start(f32[96,768]{0,1:T(8,128)S(1)} %get-tuple-element.174), channel_id=1, source_target_pairs={{0,16},{8,24},{16,0},{24,8},{1,17},{9,25},{17,1},{25,9},{2,18},{10... | collective-permute-start | bytes 884744 | tf_op jit(solution)/shard_map/ppermute | solution.py:21
  273.7 16.3 %collective-permute-start.18 = (f32[96,768]{0,1:T(8,128)S(1)}, f32[96,768]{0,1:T(8,128)}, u32[]{:S(2)}, u32[]{:S(2)}) collective-permute-start(f32[96,768]{0,1:T(8,128)S(1)} %collective-permute-done.16), channel_id=1, source_target_pairs={{0,8},{8,0},{16,24},{24,16},{1,9},{9,1},{17,25},{25,17},{2,10},{10... | collective-permute-start | bytes 884744 | tf_op jit(solution)/shard_map/ppermute | solution.py:21
  282.1 12.2 %collective-permute-start.17 = (f32[96,768]{0,1:T(8,128)S(1)}, f32[96,768]{0,1:T(8,128)}, u32[]{:S(2)}, u32[]{:S(2)}) collective-permute-start(f32[96,768]{0,1:T(8,128)S(1)} %collective-permute-done.13), channel_id=1, source_target_pairs={{0,16},{8,24},{16,0},{24,8},{1,17},{9,25},{17,1},{25,9},{2,18},{10... | collective-permute-start | bytes 884744 | tf_op jit(solution)/shard_map/ppermute | solution.py:21
  283.6 27.5 %collective-permute-start.9 = (f32[2,192,512]{2,1,0:T(8,128)}, f32[2,192,512]{2,1,0:T(8,128)}, u32[]{:S(2)}, u32[]{:S(2)}) collective-permute-start(f32[2,192,512]{2,1,0:T(8,128)} %get-tuple-element.149), channel_id=1, source_target_pairs={{0,16},{8,24},{16,0},{24,8},{1,17},{9,25},{17,1},{25,9},{2,18},{10... | collective-permute-start | bytes 2359304 | tf_op jit(solution)/shard_map/ppermute | solution.py:21
  290.0 21.1 %collective-permute-start.8 = (f32[2,192,512]{2,1,0:T(8,128)}, f32[2,192,512]{2,1,0:T(8,128)}, u32[]{:S(2)}, u32[]{:S(2)}) collective-permute-start(f32[2,192,512]{2,1,0:T(8,128)} %get-tuple-element.150), channel_id=1, source_target_pairs={{0,8},{8,0},{16,24},{24,16},{1,9},{9,1},{17,25},{25,17},{2,10},{10... | collective-permute-start | bytes 2359304 | tf_op jit(solution)/shard_map/ppermute | solution.py:21
  290.3 35.5 %collective-permute-start.11 = (f32[2,192,512]{2,1,0:T(8,128)}, f32[2,192,512]{2,1,0:T(8,128)}, u32[]{:S(2)}, u32[]{:S(2)}) collective-permute-start(f32[2,192,512]{2,1,0:T(8,128)} %collective-permute-done.7), channel_id=1, source_target_pairs={{0,16},{8,24},{16,0},{24,8},{1,17},{9,25},{17,1},{25,9},{2,18},{10... | collective-permute-start | bytes 2359304 | tf_op jit(solution)/shard_map/ppermute | solution.py:21
  290.7 35.4 %collective-permute-start.12 = (f32[2,192,512]{2,1,0:T(8,128)}, f32[2,192,512]{2,1,0:T(8,128)}, u32[]{:S(2)}, u32[]{:S(2)}) collective-permute-start(f32[2,192,512]{2,1,0:T(8,128)} %collective-permute-done.10), channel_id=1, source_target_pairs={{0,8},{8,0},{16,24},{24,16},{1,9},{9,1},{17,25},{25,17},{2,10},{10... | collective-permute-start | bytes 2359304 | tf_op jit(solution)/shard_map/ppermute | solution.py:21
  307.0 36.6 %copy-start.8 = (f32[4,8,24,768]{3,2,1,0:T(8,128)}, f32[4,8,24,768]{3,2,1,0:T(8,128)S(1)}, u32[]{:S(2)}) copy-start(f32[4,8,24,768]{3,2,1,0:T(8,128)S(1)} %copy.140) | copy-start | bytes 7077892
  344.9 11.9 %collective-permute-start.25 = (f32[2,80,768]{2,1,0:T(8,128)S(1)}, f32[2,80,768]{2,1,0:T(8,128)S(1)}, u32[]{:S(2)}, u32[]{:S(2)}) collective-permute-start(f32[2,80,768]{2,1,0:T(8,128)S(1)} %convolution_add_fusion), channel_id=1, source_target_pairs={{0,8},{8,0},{16,24},{24,16},{1,9},{9,1},{17,25},{25,17},{2,10},{10... | collective-permute-start | bytes 1474568 | tf_op jit(solution)/shard_map/ppermute | solution.py:21
  346.8 41.2 %copy-start.101 = (f32[2,80,192]{2,1,0:T(8,128)}, f32[2,80,192]{2,1,0:T(8,128)S(1)}, u32[]{:S(2)}) copy-start(f32[2,80,192]{2,1,0:T(8,128)S(1)} %fusion.66) | copy-start | bytes 368644
  356.8 11.0 %collective-permute-start.26 = (f32[2,80,768]{2,1,0:T(8,128)S(1)}, f32[2,80,768]{2,1,0:T(8,128)S(1)}, u32[]{:S(2)}, u32[]{:S(2)}) collective-permute-start(f32[2,80,768]{2,1,0:T(8,128)S(1)} %add.463), channel_id=1, source_target_pairs={{0,16},{8,24},{16,0},{24,8},{1,17},{9,25},{17,1},{25,9},{2,18},{10... | collective-permute-start | bytes 1474568 | tf_op jit(solution)/shard_map/ppermute | solution.py:21
  455.1 249.2 %reduce-scatter.7.cloned.1.call-start = ((), (), s32[]{:S(2)}) async-start(), calls=%async_computation.11 | async-start | bytes 663552 | tf_op jit(solution)/shard_map/reduce_scatter | solution.py:308
  459.6 22.4 %slice-start.6 = ((s8[4718592]{0:T(1024)(128)(4,1)}), s8[4194304]{0:T(1024)(128)(4,1)S(1)}, s32[]{:S(2)}) async-start(s8[4718592]{0:T(1024)(128)(4,1)} %bitcast.194), calls=%async_computation.22 | async-start | bytes 8388608
  499.6 19.6 %collective-permute-start.28 = (f32[2,128,768]{2,1,0:T(8,128)}, f32[2,128,768]{2,1,0:T(8,128)}, u32[]{:S(2)}, u32[]{:S(2)}) collective-permute-start(f32[2,128,768]{2,1,0:T(8,128)} %get-tuple-element.81), channel_id=1, source_target_pairs={{0,16},{8,24},{16,0},{24,8},{1,17},{9,25},{17,1},{25,9},{2,18},{10... | collective-permute-start | bytes 2359304 | tf_op jit(solution)/shard_map/ppermute | solution.py:21
  514.2 28.1 %copy-start.26 = (f32[2,80,768]{2,1,0:T(8,128)S(1)}, f32[2,80,768]{2,1,0:T(8,128)}, u32[]{:S(2)}) copy-start(f32[2,80,768]{2,1,0:T(8,128)} %copy-done.25) | copy-start | bytes 1474564
  514.2 21.8 %collective-permute-start.20 = (f32[2,128,768]{1,2,0:T(8,128)}, f32[2,128,768]{1,2,0:T(8,128)}, u32[]{:S(2)}, u32[]{:S(2)}) collective-permute-start(f32[2,128,768]{1,2,0:T(8,128)} %get-tuple-element.86), channel_id=1, source_target_pairs={{0,16},{8,24},{16,0},{24,8},{1,17},{9,25},{17,1},{25,9},{2,18},{10... | collective-permute-start | bytes 2359304 | tf_op jit(solution)/shard_map/ppermute | solution.py:21
  516.6 203.9 %reduce-scatter.9.cloned.1.call-start = ((), (), s32[]{:S(2)}) async-start(), calls=%async_computation.12 | async-start | bytes 2654208 | tf_op jit(solution)/shard_map/reduce_scatter | solution.py:305
  516.6 36.3 %collective-permute-start.27 = (f32[2,128,768]{2,1,0:T(8,128)}, f32[2,128,768]{2,1,0:T(8,128)}, u32[]{:S(2)}, u32[]{:S(2)}) collective-permute-start(f32[2,128,768]{2,1,0:T(8,128)} %get-tuple-element.80), channel_id=1, source_target_pairs={{0,16},{8,24},{16,0},{24,8},{1,17},{9,25},{17,1},{25,9},{2,18},{10... | collective-permute-start | bytes 2359304 | tf_op jit(solution)/shard_map/ppermute | solution.py:21
  521.6 31.3 %collective-permute-start.29 = (f32[2,128,768]{2,1,0:T(8,128)}, f32[2,128,768]{2,1,0:T(8,128)}, u32[]{:S(2)}, u32[]{:S(2)}) collective-permute-start(f32[2,128,768]{2,1,0:T(8,128)} %dynamic-slice_add_fusion.2), channel_id=1, source_target_pairs={{0,8},{8,0},{16,24},{24,16},{1,9},{9,1},{17,25},{25,17},{2,10},{10... | collective-permute-start | bytes 2359304 | tf_op jit(solution)/shard_map/ppermute | solution.py:21
  525.7 41.1 %collective-permute-start.19 = (f32[2,128,768]{1,2,0:T(8,128)}, f32[2,128,768]{1,2,0:T(8,128)}, u32[]{:S(2)}, u32[]{:S(2)}) collective-permute-start(f32[2,128,768]{1,2,0:T(8,128)} %get-tuple-element.85), channel_id=1, source_target_pairs={{0,16},{8,24},{16,0},{24,8},{1,17},{9,25},{17,1},{25,9},{2,18},{10... | collective-permute-start | bytes 2359304 | tf_op jit(solution)/shard_map/ppermute | solution.py:21
  525.8 41.0 %collective-permute-start.23 = (f32[2,128,768]{1,2,0:T(8,128)}, f32[2,128,768]{1,2,0:T(8,128)}, u32[]{:S(2)}, u32[]{:S(2)}) collective-permute-start(f32[2,128,768]{1,2,0:T(8,128)} %get-tuple-element.87), channel_id=1, source_target_pairs={{0,8},{8,0},{16,24},{24,16},{1,9},{9,1},{17,25},{25,17},{2,10},{10... | collective-permute-start | bytes 2359304 | tf_op jit(solution)/shard_map/ppermute | solution.py:21
  538.4 39.6 %collective-permute-start.21 = (f32[2,128,768]{1,2,0:T(8,128)}, f32[2,128,768]{1,2,0:T(8,128)}, u32[]{:S(2)}, u32[]{:S(2)}) collective-permute-start(f32[2,128,768]{1,2,0:T(8,128)} %dynamic-slice_add_fusion.6), channel_id=1, source_target_pairs={{0,8},{8,0},{16,24},{24,16},{1,9},{9,1},{17,25},{25,17},{2,10},{10... | collective-permute-start | bytes 2359304 | tf_op jit(solution)/shard_map/ppermute | solution.py:21
  556.5 27.7 %copy-start.120 = (u32[32]{0:T(128)S(1)}, u32[32]{0:T(128)}, u32[]{:S(2)}) copy-start(u32[32]{0:T(128)} %constant.122) | copy-start | bytes 388
  556.5 38.4 %collective-permute-start.31 = (f32[2,128,768]{2,1,0:T(8,128)}, f32[2,128,768]{2,1,0:T(8,128)}, u32[]{:S(2)}, u32[]{:S(2)}) collective-permute-start(f32[2,128,768]{2,1,0:T(8,128)} %get-tuple-element.78), channel_id=1, source_target_pairs={{0,8},{8,0},{16,24},{24,16},{1,9},{9,1},{17,25},{25,17},{2,10},{10... | collective-permute-start | bytes 2359304 | tf_op jit(solution)/shard_map/ppermute | solution.py:21
  561.0 36.3 %copy-start.112 = (f32[576]{0:T(1024)S(1)}, f32[576]{0:T(1024)}, u32[]{:S(2)}) copy-start(f32[576]{0:T(1024)} %get-tuple-element.55) | copy-start | bytes 6916
  561.0 36.3 %copy-start.111 = (f32[576]{0:T(1024)S(1)}, f32[576]{0:T(1024)}, u32[]{:S(2)}) copy-start(f32[576]{0:T(1024)} %get-tuple-element.56) | copy-start | bytes 6916
  561.0 36.4 %copy-start.110 = (f32[576]{0:T(1024)S(1)}, f32[576]{0:T(1024)}, u32[]{:S(2)}) copy-start(f32[576]{0:T(1024)} %get-tuple-element.57) | copy-start | bytes 6916
  581.9 73.9 %collective-permute-start.22 = (f32[2,128,768]{1,2,0:T(8,128)}, f32[2,128,768]{1,2,0:T(8,128)}, u32[]{:S(2)}, u32[]{:S(2)}) collective-permute-start(f32[2,128,768]{1,2,0:T(8,128)} %get-tuple-element.83), channel_id=1, source_target_pairs={{0,8},{8,0},{16,24},{24,16},{1,9},{9,1},{17,25},{25,17},{2,10},{10... | collective-permute-start | bytes 2359304 | tf_op jit(solution)/shard_map/ppermute | solution.py:21
  583.9 72.0 %collective-permute-start.24 = (f32[2,128,768]{1,2,0:T(8,128)}, f32[2,128,768]{1,2,0:T(8,128)}, u32[]{:S(2)}, u32[]{:S(2)}) collective-permute-start(f32[2,128,768]{1,2,0:T(8,128)} %get-tuple-element.84), channel_id=1, source_target_pairs={{0,16},{8,24},{16,0},{24,8},{1,17},{9,25},{17,1},{25,9},{2,18},{10... | collective-permute-start | bytes 2359304 | tf_op jit(solution)/shard_map/ppermute | solution.py:21
  585.4 78.1 %collective-permute-start.30 = (f32[2,128,768]{2,1,0:T(8,128)}, f32[2,128,768]{2,1,0:T(8,128)}, u32[]{:S(2)}, u32[]{:S(2)}) collective-permute-start(f32[2,128,768]{2,1,0:T(8,128)} %get-tuple-element.79), channel_id=1, source_target_pairs={{0,8},{8,0},{16,24},{24,16},{1,9},{9,1},{17,25},{25,17},{2,10},{10... | collective-permute-start | bytes 2359304 | tf_op jit(solution)/shard_map/ppermute | solution.py:21
  597.2 66.3 %collective-permute-start.32 = (f32[2,128,768]{2,1,0:T(8,128)}, f32[2,128,768]{2,1,0:T(8,128)}, u32[]{:S(2)}, u32[]{:S(2)}) collective-permute-start(f32[2,128,768]{2,1,0:T(8,128)} %dynamic-slice_add_fusion), channel_id=1, source_target_pairs={{0,16},{8,24},{16,0},{24,8},{1,17},{9,25},{17,1},{25,9},{2,18},{10... | collective-permute-start | bytes 2359304 | tf_op jit(solution)/shard_map/ppermute | solution.py:21
  671.8 12.4 %all-to-all-start.3 = ((f32[96,3,1,192]{3,2,1,0:T(1,128)}), f32[96,3,1,192]{3,2,1,0:T(1,128)S(1)}, u32[]{:S(2)}, u32[]{:S(2)}) async-start(f32[96,3,1,192]{3,2,1,0:T(1,128)} %reshape.268), calls=%async_computation.3 | async-start | bytes 589824 | tf_op jit(solution)/shard_map/all_to_all | solution.py:189
  675.5 8.7 %collective-permute-start.33 = (f32[2,32,3,192]{3,1,2,0:T(8,128)S(1)}, f32[2,32,3,192]{3,1,2,0:T(8,128)S(1)}, u32[]{:S(2)}, u32[]{:S(2)}) collective-permute-start(f32[2,32,3,192]{3,1,2,0:T(8,128)S(1)} %copy.154), channel_id=1, source_target_pairs={{0,7},{1,6},{2,5},{3,4},{4,3},{5,2},{6,1},{7,0},{8,15},{9,14},{10,... | collective-permute-start | bytes 442376 | tf_op jit(solution)/shard_map/ppermute | solution.py:322
  684.2 9.5 %all-to-all-start.4 = ((f32[96,1,1,768]{3,2,1,0:T(1,128)}), f32[96,1,1,768]{3,2,1,0:T(1,128)S(1)}, u32[]{:S(2)}, u32[]{:S(2)}) async-start(f32[96,1,1,768]{3,2,1,0:T(1,128)} %copy.157), calls=%async_computation.5 | async-start | bytes 589824 | tf_op jit(solution)/shard_map/all_to_all | solution.py:189
  693.7 8.9 %all-to-all-start.5 = ((f32[96,1,1,768]{3,2,1,0:T(1,128)}), f32[96,1,1,768]{3,2,1,0:T(1,128)S(1)}, u32[]{:S(2)}, u32[]{:S(2)}) async-start(f32[96,1,1,768]{3,2,1,0:T(1,128)} %copy.159), calls=%async_computation.6 | async-start | bytes 589824 | tf_op jit(solution)/shard_map/all_to_all | solution.py:189
  (111 other events, 620.2 us)
Sparse Core Ops, SparseCore 0:
  21.1 34.1 all-gather.8
  57.0 49.1 all-gather.10
  107.9 30.6 all-gather.12
  140.1 30.7 all-gather.14
  172.9 30.7 all-gather.16
  455.3 193.1 all-reduce.11
  651.4 31.6 reduce-scatter.6
  686.1 34.3 reduce-scatter.8

commit v2 on v0

v2 whole, which is shorter than its diff:
```python
import math

import jax
import jax.numpy as jnp
import numpy as np
from jax import lax
from jax.experimental import pallas as pl
from jax.experimental.pallas import tpu as pltpu
from jax.sharding import PartitionSpec as P

EPS = 1e-05
HIGH = lax.Precision.HIGH
RADIX = 8
FOLDED = 5
ROOT = math.sqrt(0.5)
VMEM = 56 * 1024 * 1024
COST = 20
NN = ((1,), (0,))
NT = ((1,), (1,))
TN = ((0,), (0,))
F32 = jnp.float32
BF16 = jnp.bfloat16


def contract(pattern, left_side, right_side):
    return jnp.einsum(pattern, left_side, right_side, precision=HIGH)


def swap(value, axis, distance):
    devices = lax.axis_size(axis)
    return lax.ppermute(value, axis, [(i, i ^ distance) for i in range(devices)])


def from_others(value):
    return [swap(value, "seq", d) for d in (1, 2, 3)]


def to_others(blocks):
    return [blocks[0]] + [swap(blocks[d], "seq", d) for d in (1, 2, 3)]


def to_all(value):
    return [value] + from_others(value)


def added(terms):
    return (terms[0] + terms[1]) + (terms[2] + terms[3])


def by_xor(pieces, index):
    count = len(pieces)
    out = []
    for k in range(count):
        chosen = pieces[k]
        for i in range(1, count):
            chosen = jnp.where(index == i, pieces[k ^ i], chosen)
        out.append(chosen)
    return out


def columns_out(shard, s):
    pieces = []
    for d in range(4):
        block = lax.dynamic_index_in_dim(shard, s ^ d, axis=1, keepdims=False)
        pieces.append(block if d == 0 else swap(block, "seq", d))
    return jnp.stack(by_xor(pieces, s))


def columns_there(own, s):
    pieces = []
    for d in range(4):
        block = lax.dynamic_index_in_dim(own, s ^ d, axis=0, keepdims=False)
        pieces.append(block if d == 0 else swap(block, "seq", d))
    return pieces


def over_batch(value):
    full = lax.all_gather(value, "batch", axis=0, tiled=True)
    return full.reshape((-1,) + value.shape)


def sum_over_batch(parts):
    flat = parts.reshape(-1, parts.shape[2])
    return lax.psum_scatter(flat, "batch", scatter_dimension=0, tiled=True)


def halves(value):
    high = value.astype(BF16)
    return high, (value - high.astype(F32)).astype(BF16)


def dot(left_side, right_side, dims):
    (a, b), (c, d) = left_side, right_side

    def product(x, y):
        return lax.dot_general(x, y, (dims, ((), ())), preferred_element_type=F32)

    return product(a, c) + (product(a, d) + product(b, c))


def chosen_rows(chosen, both, dims):
    high, low = both

    def product(x):
        return lax.dot_general(chosen, x, (dims, ((), ())), preferred_element_type=F32)

    return product(high) + product(low)


def normed(x):
    centered = x - jnp.mean(x, axis=-1, keepdims=True)
    inverse = lax.rsqrt(jnp.mean(centered * centered, axis=-1, keepdims=True) + EPS)
    return centered * inverse, inverse


def call(kernel, name, flops, moved, inputs, in_specs, outs, out_specs, grid=(1,), scratch=(), scalars=(), after=()):
    taken = len(scalars) + len(inputs)

    def run(*refs):
        kernel(*refs[:taken], *refs[taken + len(after) :])

    return pl.pallas_call(
        run,
        name=name,
        out_shape=tuple(outs),
        grid_spec=pltpu.PrefetchScalarGridSpec(
            num_scalar_prefetch=len(scalars),
            grid=grid,
            in_specs=list(in_specs) + [pl.BlockSpec(memory_space=pl.ANY)] * len(after),
            out_specs=tuple(out_specs),
            scratch_shapes=list(scratch),
        ),
        compiler_params=pltpu.CompilerParams(vmem_limit_bytes=VMEM),
        cost_estimate=pl.CostEstimate(flops=int(flops) // COST, bytes_accessed=int(moved) // COST, transcendentals=0),
    )(*scalars, *inputs, *after)


def shaped(*shape, dtype=F32):
    return jax.ShapeDtypeStruct(shape, dtype)


def whole(*shape):
    return pl.BlockSpec(shape, lambda *_: (0,) * len(shape))


def first(work):
    pl.when(pl.program_id(0) == 0)(work)


def fold_base(kernel, mirrored, w_out, after=()):
    _, turns, kept, own = mirrored.shape
    rows, width = w_out.shape
    wide = 2 * own

    def run(k_ref, m_ref, w_ref, out_ref):
        for phase in range(FOLDED):
            for part in range(2):
                value = k_ref[part, :, phase]
                if 0 < phase <= kept:
                    other = m_ref[part, :, phase - 1]
                    value = value + other if part == 0 else value - other
                out_ref[phase * turns : (phase + 1) * turns, part * own : (part + 1) * own] = value
        for k in range(width // wide):
            at = FOLDED * turns + k * rows
            out_ref[at : at + rows] = w_ref[:, k * wide : (k + 1) * wide]

    count = FOLDED * turns + width // wide * rows
    (out,) = call(
        run, "fold_base", 0, 12 * count * wide, [kernel, mirrored, w_out],
        [whole(*kernel.shape), whole(*mirrored.shape), whole(rows, width)],
        [shaped(count, wide)], [whole(count, wide)], after=after,
    )
    return out


def turn_in(gathered, channels):
    groups, shards, rows, columns = gathered.shape
    width = groups * shards * rows
    wide = -(-columns // 128) * 128

    def kernel(w_ref, high_ref, low_ref, flat_ref):
        flat_ref[:, channels // 128 * 128 :] = jnp.zeros((width, wide - channels // 128 * 128), F32)
        for k in range(shards):
            for j in range(groups):
                at = (k * groups + j) * rows
                flat_ref[at : at + rows, :channels] = w_ref[j, k, :, :channels]
        turned = flat_ref[...].T
        high_ref[...], low_ref[...] = halves(turned[:channels])

    return call(
        kernel, "turn_in", 0, 4 * 2 * width * wide, [gathered], [whole(*gathered.shape)],
        [shaped(channels, width, dtype=BF16)] * 2, [whole(channels, width)] * 2,
        scratch=[pltpu.VMEM((width, wide), F32)],
    )


def split_units(gathered, w_down, after=()):
    groups, shards, rows, columns = gathered.shape
    width = groups * shards * rows
    units = w_down.shape[0]

    def kernel(w_ref, d_ref, high_ref, low_ref, dh_ref, dl_ref, flat_ref):
        k = pl.program_id(0)
        for j in range(groups):
            flat_ref[j * rows : (j + 1) * rows] = w_ref[j, 0]

        high_ref[...], low_ref[...] = halves(flat_ref[...])
        dh_ref[...], dl_ref[...] = halves(d_ref[...])

    part = pl.BlockSpec((groups * rows, columns), lambda i: (i, 0))
    down = pl.BlockSpec((units // shards, width), lambda i: (i, 0))
    return call(
        kernel, "split_units", 0, 8 * width * (columns + units), [gathered, w_down],
        [pl.BlockSpec((groups, 1, rows, columns), lambda i: (0, i, 0, 0)), down],
        [shaped(width, columns, dtype=BF16)] * 2 + [shaped(units, width, dtype=BF16)] * 2,
        [part, part, down, down], grid=(shards,),
        scratch=[pltpu.VMEM((groups * rows, columns), F32)], after=after,
    )


def arrange(pieces, s, after=()):
    tokens, width = pieces[0].shape
    length = 4 * tokens

    def kernel(s_ref, p0, p1, p2, p3, x_ref, high_ref, low_ref):
        for d, piece in enumerate((p0, p1, p2, p3)):

            @pl.when(pl.program_id(0) == d)
            def _(piece=piece):
                x = piece[...]
                x_ref[...] = x
                high_ref[...], low_ref[...] = halves(normed(x)[0])

    rows = pl.BlockSpec((tokens, width), lambda i, s_ref: (s_ref[0] ^ i, 0))
    return call(
        kernel, "arrange", 0, 12 * length * width, pieces, [whole(tokens, width)] * 4,
        [shaped(length, width), shaped(length, width, dtype=BF16), shaped(length, width, dtype=BF16)],
        [rows] * 3, grid=(4,), scalars=[s.reshape(1)], after=after,
    )


def project(w_turned, n_both, after=()):
    channels, width = w_turned[0].shape
    length = n_both[0].shape[0]
    tokens = length // 2

    def kernel(wh, wl, nh, nl, out_ref):
        out_ref[...] = dot((wh[...], wl[...]), (nh[...], nl[...]), NT)

    rows = pl.BlockSpec((tokens, width), lambda i: (i, 0))
    (out,) = call(
        kernel, "project", 6 * length * width * channels, 4 * (length * width + channels * (length + width)),
        [*w_turned, *n_both], [whole(channels, width)] * 2 + [rows] * 2,
        [shaped(channels, length)], [pl.BlockSpec((channels, tokens), lambda i: (0, i))], grid=(2,), after=after,
    )
    return out


def phase_tables(length):
    block = length // RADIX
    place = np.arange(block)[:, None]
    turn = np.arange(block)[None, :]
    tables = []
    for phase in range(FOLDED):
        angle = 2.0 * np.pi * ((RADIX * turn + phase) * place % length) / length
        cos, sin = np.cos(angle), np.sin(angle)
        tables.append(np.block([[cos, -sin], [sin, cos]]))
    table = np.stack(tables).astype(np.float32)
    high = table.astype(BF16)
    low = (table - high.astype(np.float32)).astype(BF16)
    return jnp.asarray(high), jnp.asarray(low)


def shift(value, step):
    length = value.shape[1]
    lane = lax.broadcasted_iota(jnp.int32, value.shape, 1)
    if step < 0:
        return jnp.where(lane == 0, 0.0, pltpu.roll(value, 1, 1))
    return jnp.where(lane == length - 1, 0.0, pltpu.roll(value, length - 1, 1))


def fold(value, phase, block):
    x0, x1, x2, x3 = [value[:, i * block : (i + 1) * block] for i in range(4)]
    if phase == 0:
        return (x0 + x2) + (x1 + x3)
    if phase == 4:
        return (x0 + x2) - (x1 + x3)
    if phase == 2:
        return jnp.concatenate([x0 - x2, x3 - x1], axis=1)
    slant, lean = (x1 - x3) * ROOT, (x1 + x3) * ROOT
    if phase == 1:
        return jnp.concatenate([x0 + slant, -x2 - lean], axis=1)
    return jnp.concatenate([x0 - slant, x2 - lean], axis=1)


def unfold(total_ref, value, phase, block):
    if phase == 0:
        terms = (value,) * 4
    elif phase == 4:
        terms = (value, -value, value, -value)
    else:
        real, imag = value[:, :block], value[:, block:]
        if phase == 2:
            terms = (real, -imag, -real, imag)
        elif phase == 1:
            terms = (real, ROOT * (real - imag), -imag, -ROOT * (real + imag))
        else:
            terms = (real, -ROOT * (real + imag), imag, ROOT * (real - imag))
    for i, term in enumerate(terms):
        cols = slice(i * block, (i + 1) * block)
        total_ref[:, cols] = term if phase == 0 else total_ref[:, cols] + term


def times(left_side, right_side, block, conj=False):
    a, b = left_side[:, :block], left_side[:, block:]
    c, d = right_side[:, :block], right_side[:, block:]
    if conj:
        d = -d
    return jnp.concatenate([a * c - b * d, a * d + b * c], axis=1)


def pair(phase):
    return 1.0 if phase in (0, 4) else 2.0


def depth(phase, block):
    return block if phase in (0, 4) else 2 * block


def mix(projected, taps, base, tables, after=()):
    own, length = projected.shape[1:]
    block = 2 * length // RADIX
    groups = base.shape[0]
    turns = block // groups
    if turns % 8:
        base = base[:, : FOLDED * turns].reshape(groups, FOLDED, turns, 2 * own)
        spectrum = pl.BlockSpec((groups, 1, turns, 2 * own), lambda i: (0, i, 0, 0))
    else:
        spectrum = pl.BlockSpec((groups, turns, 2 * own), lambda i: (0, i, 0))
    scale = 1.0 / math.sqrt(length)

    def kernel(p_ref, tap_ref, base_ref, th_ref, tl_ref, gated_ref, gating_ref, long_ref, vals_ref, spec_ref,
               mixed_ref, acc_ref, base_t):
        step = pl.program_id(0)

        @pl.when(step == 0)
        def _():
            for k in range(3):

                p = p_ref[k]
                tap = tap_ref[k]
                mixed = tap[:, 0:1] * shift(p, -1) + tap[:, 1:2] * p + tap[:, 2:3] * shift(p, 1)
                if k == 1:
                    gating_ref[...] = mixed
                else:
                    mixed_ref[k // 2 * own : (k // 2 + 1) * own] = mixed

        turned = base_ref[...].reshape(block, 2 * own).T
        base_t[:, :block] = turned[:own]
        base_t[:, block:] = turned[own:]

        for phase in range(FOLDED):

            @pl.when(step == phase)
            def _(phase=phase):
                deep = depth(phase, block)
                table = (th_ref[0, :deep], tl_ref[0, :deep])
                hats = dot(halves(fold(mixed_ref[...], phase, block)), table, NN)
                spec = base_t[...] + (pair(phase) * scale) * hats[:own]
                vals = hats[own:]
                spec_ref[0] = spec
                vals_ref[0] = vals
                unfold(acc_ref, dot(halves(times(spec, vals, block)), table, NT), phase, block)

        @pl.when(step == FOLDED - 1)
        def _():
            long_conv = acc_ref[...] * (0.5 / length)
            long_ref[...] = long_conv
            gated_ref[...] = gating_ref[...] * long_conv

    flat, hat = shaped(own, length), shaped(FOLDED, own, 2 * block)
    by_phase = lambda *shape: pl.BlockSpec((1,) + shape, lambda i, *_: (i,) + (0,) * len(shape))
    return call(
        kernel, "mix", 3 * 6 * own * 4 * length * length, 4 * own * length * 22,
        [projected, taps, base, *tables],
        [whole(3, own, length), whole(3, own, 3)]
        + [spectrum]
        + [by_phase(2 * block, 2 * block), by_phase(2 * block, 2 * block)],
        [flat, flat, flat, hat, hat],
        [whole(own, length)] * 3 + [by_phase(own, 2 * block)] * 2,
        grid=(FOLDED,),
        scratch=[
            pltpu.VMEM((2 * own, length), F32),
            pltpu.VMEM((own, length), F32),
            pltpu.VMEM((own, 2 * block), F32),
        ],
        after=after,
    )


def mix_back(which, places, d_gating, d_long, projected, taps, vals, spec, kernel_sum, tables, after=()):
    own, length = projected.shape[1:]
    block = vals.shape[2] // 2
    groups = lax.axis_size("batch")
    turns = block // groups
    slots = places.shape[1]
    scale = 1.0 / math.sqrt(length)

    def kernel(at_ref, dg_ref, dl_ref, p_ref, tap_ref, vals_ref, spec_ref, th_ref, tl_ref, *refs):
        sum_refs, (out_ref, ker_ref, dtap_ref, long_ref, gating_ref, acc_ref) = refs[:-6], refs[-6:]
        step = pl.program_id(0)

        @pl.when(step == 0)
        def _():
            at = lax.broadcasted_iota(jnp.int32, (slots, length), 1)
            chosen = jnp.where(at == at_ref[0], 1.0, 0.0).astype(BF16)
            for source, target in ((dg_ref, gating_ref), (dl_ref, long_ref)):
                high, low = halves(source[0])
                target[...] = lax.dot_general(high, chosen, (NN, ((), ())), preferred_element_type=F32) + (
                    lax.dot_general(low, chosen, (NN, ((), ())), preferred_element_type=F32)
                )

        for phase in range(FOLDED):

            @pl.when(step == phase)
            def _(phase=phase):
                deep = depth(phase, block)
                table = (th_ref[0, :deep], tl_ref[0, :deep])
                hat = dot(halves(fold(long_ref[...], phase, block)), table, NN) * (0.5 / length)
                ker = times(hat, vals_ref[0], block, conj=True)
                spread = jnp.concatenate([ker[:, :block], ker[:, block:]], axis=0).T.reshape(groups, turns, 2 * own)
                ker_ref[:, 0] = sum_refs[0][:, 0] + spread if sum_refs else spread
                both = jnp.concatenate(
                    [ker * (pair(phase) * scale), times(hat, spec_ref[0], block, conj=True)], axis=0
                )
                unfold(acc_ref, dot(halves(both), table, NT), phase, block)

        @pl.when(step == FOLDED - 1)
        def _():
            lane = lax.broadcasted_iota(jnp.int32, (own, 128), 1)
            for k in range(3):
                grad = gating_ref[...] if k == 1 else acc_ref[k // 2 * own : (k // 2 + 1) * own]
                p = p_ref[k]
                tap = tap_ref[k]
                out_ref[k] = tap[:, 0:1] * shift(grad, 1) + tap[:, 1:2] * grad + tap[:, 2:3] * shift(grad, -1)
                sums = jnp.zeros((own, 128), F32)
                for j, moved in enumerate((shift(p, -1), p, shift(p, 1))):
                    sums = jnp.where(lane == j, jnp.sum(moved * grad, axis=1, keepdims=True), sums)
                dtap_ref[k] = sums

    by_phase = lambda *shape: pl.BlockSpec((1,) + shape, lambda i, *_: (i,) + (0,) * len(shape))
    spectrum = pl.BlockSpec((groups, 1, turns, 2 * own), lambda i, *_: (0, i, 0, 0))
    return call(
        kernel, "mix_back", 3 * 6 * own * 4 * length * length, 4 * own * length * 22,
        [places, d_gating, d_long, projected, taps, vals, spec, *tables, *kernel_sum],
        [
            pl.BlockSpec((1, slots, 1), lambda i: (which, 0, 0)),
            pl.BlockSpec((1, own, slots), lambda i: (which, 0, 0)),
            pl.BlockSpec((1, own, slots), lambda i: (which, 0, 0)),
            whole(3, own, length),
            whole(3, own, 3),
            by_phase(own, 2 * block),
            by_phase(own, 2 * block),
            by_phase(2 * block, 2 * block),
            by_phase(2 * block, 2 * block),
        ] + [spectrum] * len(kernel_sum),
        [shaped(3, own, length), shaped(groups, FOLDED, turns, 2 * own), shaped(3, own, 128)],
        [whole(3, own, length), spectrum, whole(3, own, 128)],
        grid=(FOLDED,),
        scratch=[
            pltpu.VMEM((own, length), F32),
            pltpu.VMEM((own, length), F32),
            pltpu.VMEM((2 * own, length), F32),
        ],
        after=after,
    )


def add_mixer(x, gated, w_out, after=()):
    length, width = x.shape
    own = gated[0].shape[0]
    tokens = length // 2

    def kernel(x_ref, g0, g1, g2, g3, w0, w1, w2, w3, out_ref, wh, wl, gh, gl):
        @first
        def _():
            for d, ref in enumerate((w0, w1, w2, w3)):
                wh[d * own : (d + 1) * own], wl[d * own : (d + 1) * own] = halves(ref[...])

        for d, ref in enumerate((g0, g1, g2, g3)):
            gh[d * own : (d + 1) * own], gl[d * own : (d + 1) * own] = halves(ref[...])
        out_ref[...] = x_ref[...] + dot((gh[...], gl[...]), (wh[...], wl[...]), TN)

    rows = pl.BlockSpec((tokens, width), lambda i: (i, 0))
    (out,) = call(
        kernel, "add_mixer", 6 * length * width * width, 4 * (3 * length * width + width * width),
        [x, *gated, *w_out],
        [rows] + [pl.BlockSpec((own, tokens), lambda i: (0, i))] * 4 + [whole(own, width)] * 4,
        [shaped(length, width)], [rows], grid=(2,),
        scratch=[pltpu.VMEM((width, width), BF16)] * 2 + [pltpu.VMEM((width, tokens), BF16)] * 2,
        after=after,
    )
    return out


def gelu_parts(u):
    inner = math.sqrt(2.0 / math.pi) * (u + 0.044715 * (u * u * u))
    return 0.5 * (1.0 + jnp.tanh(inner))


def deal(low, value, out_refs):
    tokens = value.shape[0] // 2
    for step in range(2):
        for crossed in range(2):

            @pl.when((pl.program_id(0) == step) & (low == crossed))
            def _(step=step, crossed=crossed):
                out_refs[2 * step + crossed][...] = value[:tokens]
                out_refs[2 * step + 1 - crossed][...] = value[tokens:]


def feed_forward(residual, w_units, w_down, s, after=()):
    length, width = residual.shape
    units = w_down[0].shape[0]
    tokens = length // 4

    def kernel(s_ref, r_ref, wh, wl, dh, dl, *out_refs):
        both = halves(normed(r_ref[...])[0])
        gate_up = dot(both, (wh[...], wl[...]), NN)
        gate, up = gate_up[:, :units], gate_up[:, units:]
        out = dot(halves(gate * gelu_parts(gate) * up), (dh[...], dl[...]), NN)
        deal(s_ref[0] & 1, out, out_refs)

    return call(
        kernel, "feed_forward", 18 * length * width * units, 4 * (2 * length * width + 3 * width * units),
        [residual, *w_units, *w_down],
        [pl.BlockSpec((2 * tokens, width), lambda i, s_ref: ((s_ref[0] >> 1) ^ i, 0))]
        + [whole(width, 2 * units)] * 2 + [whole(units, width)] * 2,
        [shaped(tokens, width)] * 4, [whole(tokens, width)] * 4,
        grid=(2,), scalars=[s.reshape(1)], after=after,
    )


def chosen(at_ref, slots, length):
    lane = lax.broadcasted_iota(jnp.int32, (slots, length), 1)
    return jnp.where(lane == at_ref[...], 1.0, 0.0).astype(BF16)


def live_back(residual, places, d_out, w_units, w_down, used, after=()):
    seqs = len(residual)
    length, width = residual[0].shape
    slots = places.shape[1]
    units = w_down[0].shape[0]
    rows = seqs * slots

    def kernel(r_refs, at_ref, o_ref, wh, wl, dh, dl, live_ref, n_ref, hid_ref, du_ref, e_ref):
        for i, ref in enumerate(r_refs):
            pick = chosen(at_ref.at[i], slots, length)
            live_ref[i * slots : (i + 1) * slots] = chosen_rows(pick, halves(ref[...]), NN)
        n = normed(live_ref[...])[0]
        n_ref[...] = n
        gate_up = dot(halves(n), (wh[...], wl[...]), NN)
        d_hidden = dot(halves(o_ref[...]), (dh[...], dl[...]), NT)
        gate, up = gate_up[:, :units], gate_up[:, units:]
        half = gelu_parts(gate)
        slope = half + gate * 2.0 * half * (1.0 - half) * math.sqrt(2.0 / math.pi) * (1.0 + 0.134145 * (gate * gate))
        hid_ref[...] = gate * half * up
        d_units = jnp.concatenate([d_hidden * up * slope, d_hidden * (gate * half)], axis=1)
        du_ref[...] = d_units
        e = dot(halves(d_units), (wh[...], wl[...]), NT)
        for i in range(seqs):
            e_ref[i * used : (i + 1) * used] = e[i * slots : i * slots + used]

    def spread(*refs):
        kernel(refs[:seqs], *refs[seqs:])

    return call(
        spread, "live_back", 30 * rows * width * units, 4 * (2 * length * width + 4 * width * units),
        [*residual, places, d_out, *w_units, *w_down],
        [whole(length, width)] * seqs + [whole(seqs, slots, 1), whole(rows, width)]
        + [whole(width, 2 * units)] * 2 + [whole(units, width)] * 2,
        [shaped(rows, width), shaped(rows, width), shaped(rows, units), shaped(rows, 2 * units), shaped(seqs * used, width)],
        [whole(rows, width), whole(rows, width), whole(rows, units), whole(rows, 2 * units), whole(seqs * used, width)],
        after=after,
    )


def unit_grads(normed_live, d_units, hidden, d_out, shards, after=()):
    slots, width = normed_live.shape
    units = hidden.shape[1]
    groups = lax.axis_size("batch")
    rows = width // groups // shards
    down = units // groups

    def kernel(n_ref, u_ref, h_ref, o_ref, out_ref):
        @pl.when(pl.program_id(0) < 2)
        def _():
            part = dot(halves(n_ref[...]), halves(u_ref[...]), TN)
            for j in range(groups):
                for k in range(shards):
                    at = (k * groups + j) * rows
                    out_ref[j, k * rows : (k + 1) * rows] = part[at : at + rows]

        @pl.when(pl.program_id(0) == 2)
        def _():
            part = dot(halves(h_ref[...]), halves(o_ref[...]), TN)
            for j in range(groups):
                out_ref[j] = part[j * down : (j + 1) * down]

    (out,) = call(
        kernel, "unit_grads", 18 * slots * width * units, 4 * 3 * width * units,
        [normed_live, d_units, hidden, d_out],
        [
            whole(slots, width),
            pl.BlockSpec((slots, units), lambda i: (0, jnp.minimum(i, 1))),
            whole(slots, units),
            whole(slots, width),
        ],
        [shaped(groups, shards * rows, 2 * units + width)],
        [pl.BlockSpec((groups, shards * rows, width), lambda i: (0, 0, i))],
        grid=(3,), after=after,
    )
    return out


def live_mix(live, d_out, e_terms, w_out, gating, long_conv, places, after=()):
    seqs = len(gating)
    own, length = gating[0].shape
    rows, width = live.shape
    slots = rows // seqs
    used = e_terms[0].shape[0]

    def kernel(live_ref, o_ref, *refs):
        e_refs, w_ref, refs = refs[: 2 * seqs], refs[2 * seqs], refs[2 * seqs + 1 :]
        g_refs, l_refs, refs = refs[:seqs], refs[seqs : 2 * seqs], refs[2 * seqs :]
        at_ref, res_ref, dw_ref, dg_ref, dl_ref, e_all, pick_ref = refs
        e_all[...] = jnp.zeros((rows, width), F32)
        for i in range(seqs):
            e_all[i * slots : i * slots + used] = e_refs[i][...] + e_refs[seqs + i][...]
        n, inverse = normed(live_ref[...])
        e = e_all[...]
        along = jnp.mean(e * n, axis=-1, keepdims=True)
        res_ref[...] = o_ref[...] + (e - jnp.mean(e, axis=-1, keepdims=True) - n * along) * inverse
        d_res = halves(res_ref[...])
        d_gated = dot(halves(w_ref[...]), d_res, NT)
        for i in range(seqs):
            pick = chosen(at_ref.at[i], slots, length)
            at = slice(i * slots, (i + 1) * slots)
            gate = [lax.dot_general(v, pick, (NT, ((), ())), preferred_element_type=F32) for v in halves(g_refs[i][...])]
            lng = [lax.dot_general(v, pick, (NT, ((), ())), preferred_element_type=F32) for v in halves(l_refs[i][...])]
            gate, lng = gate[0] + gate[1], lng[0] + lng[1]
            dg_ref[i] = d_gated[:, at] * lng
            dl_ref[i] = d_gated[:, at] * gate
            pick_ref[:, at] = gate * lng
        dw_ref[...] = dot(halves(pick_ref[...]), d_res, NN)

    return call(
        kernel, "live_mix", 20 * rows * width * own, 4 * (4 * own * length + 4 * rows * width),
        [live, d_out, *e_terms, w_out, *gating, *long_conv, places],
        [whole(rows, width)] * 2 + [whole(used, width)] * (2 * seqs) + [whole(own, width)]
        + [whole(own, length)] * (2 * seqs) + [whole(seqs, slots, 1)],
        [shaped(rows, width), shaped(own, width), shaped(seqs, own, slots), shaped(seqs, own, slots)],
        [whole(rows, width), whole(own, width), whole(seqs, own, slots), whole(seqs, own, slots)],
        scratch=[pltpu.VMEM((rows, width), F32), pltpu.VMEM((own, rows), F32)],
        after=after,
    )


def project_back(d_projected, n_both, w_turned, w_sum, s, after=()):
    channels, length = d_projected.shape
    width = n_both[0].shape[1]
    tokens = length // 4

    def kernel(s_ref, d_ref, nh, nl, wh, wl, *refs):
        sum_refs, e_refs, dw_ref = refs[:-5], refs[-5:-1], refs[-1]
        both = halves(d_ref[...])
        deal(s_ref[0] & 1, dot(both, (wh[...], wl[...]), TN), e_refs)
        part = dot(both, (nh[...], nl[...]), NN)

        @pl.when(pl.program_id(0) == 0)
        def _():
            dw_ref[...] = sum_refs[0][...] + part if sum_refs else part

        @pl.when(pl.program_id(0) == 1)
        def _():
            dw_ref[...] += part

    at = lambda i, s_ref: ((s_ref[0] >> 1) ^ i, 0)
    return call(
        kernel, "project_back", 12 * length * width * channels,
        4 * (2 * length * width + channels * (length + 3 * width)),
        [d_projected, *n_both, *w_turned, *w_sum],
        [pl.BlockSpec((channels, 2 * tokens), lambda i, s_ref: (0, (s_ref[0] >> 1) ^ i))]
        + [pl.BlockSpec((2 * tokens, width), at)] * 2 + [whole(channels, width)] * (2 + len(w_sum)),
        [shaped(tokens, width)] * 4 + [shaped(channels, width)],
        [whole(tokens, width)] * 4 + [whole(channels, width)],
        grid=(2,), scalars=[s.reshape(1)], after=after,
    )


def turn_back(turned, placed, w_out_part, after=()):
    channels, width = turned.shape
    own = w_out_part.shape[0]
    groups = lax.axis_size("batch")
    shards = width // own
    rows = own // groups
    wide = -(-(channels + 1) // 128) * 128

    def kernel(w_ref, p_ref, o_ref, out_ref, flat_ref):
        flat_ref[:channels] = w_ref[...]
        flat_ref[channels:] = jnp.zeros((wide - channels, width), F32)
        back = flat_ref[...].T
        for j in range(groups):
            for k in range(shards):
                at = (k * groups + j) * rows
                to = slice(k * rows, (k + 1) * rows)
                out_ref[j, to, : wide - 128] = back[at : at + rows, : wide - 128]
                out_ref[j, to, wide - 128 : wide] = back[at : at + rows, wide - 128 :] + p_ref[at : at + rows]
                out_ref[j, to, wide:] = o_ref[j * rows : (j + 1) * rows, k * own : (k + 1) * own]

    shape = (groups, shards * rows, wide + own)
    (out,) = call(
        kernel, "turn_back", 0, 8 * width * wide, [turned, placed, w_out_part],
        [whole(channels, width), whole(width, 128), whole(own, width)], [shaped(*shape)], [whole(*shape)],
        scratch=[pltpu.VMEM((wide, width), F32)], after=after,
    )
    return out


def norm_pull(n, inverse, grad):
    along = jnp.mean(grad * n, axis=-1, keepdims=True)
    return (grad - jnp.mean(grad, axis=-1, keepdims=True) - n * along) * inverse


def together(*values):
    return lax.optimization_barrier(values)


def body(
    inputs,
    gain_one,
    w_in,
    conv_weight,
    kernel,
    w_out,
    gain_two,
    w_gate,
    w_up,
    w_down,
    mask_positions,
    mask_counts,
    grad_rows,
):
    shards = lax.axis_size("seq")
    groups = lax.axis_size("batch")
    s = lax.axis_index("seq")
    seqs, tokens, width = inputs.shape
    length = tokens * shards
    freqs = 2 * length
    own = width // shards
    rows = w_in.shape[0]
    units = w_gate.shape[1] // shards
    count = conv_weight.shape[1]
    extra = 3 * count // rows
    tables = phase_tables(freqs)

    w_pre = (gain_one[:, None] * w_in).reshape(rows, 3, shards, own).transpose(0, 2, 1, 3)
    w_pre = w_pre.reshape(rows, shards, 3 * own)
    carried = jnp.broadcast_to(conv_weight.reshape(rows, 1, extra), (rows, shards, extra))
    split = 3 * own + extra
    sent = columns_out(jnp.concatenate([w_pre, carried], axis=2), s)
    wide = kernel.reshape(2, -1, RADIX, own)
    mirror = [(i, groups - 1 - i) for i in range(groups)]
    folded = lax.ppermute(wide[:, ::-1, :4:-1], "batch", mirror)
    sent, folded, inputs_now = together(sent, folded, inputs)
    w_pre = over_batch(sent.reshape(shards * rows, split)).reshape(groups, shards, rows, split)

    folded = fold_base(wide, folded, w_out)
    spectra = folded.shape[0] - rows * shards // 2
    near = [(swap(inputs_now[i], "seq", 1), swap(inputs_now[i], "seq", 2)) for i in range(seqs)]
    near, folded, w_pre, w_gate_now, w_up_now = together(near, folded, w_pre, w_gate, w_up)
    base = over_batch(folded)

    far = [swap(near[i][i % 2], "seq", 2 - i % 2) for i in range(seqs)]
    w_units = jnp.stack([gain_two[:, None] * w_gate_now, gain_two[:, None] * w_up_now], axis=1)
    w_units = w_units.reshape(rows, 2, shards, units).transpose(0, 2, 1, 3).reshape(rows, shards, 2 * units)
    w_turned = turn_in(w_pre, 3 * own)
    taps = w_pre[..., 3 * own :].reshape(groups, shards, 3, count).transpose(2, 1, 0, 3)
    taps = lax.dynamic_index_in_dim(taps.reshape(3, 3, shards, own), s, axis=2, keepdims=False)
    taps = taps.transpose(1, 2, 0)
    far, w_units, w_down_now, w_turned, taps = together(far, columns_out(w_units, s), w_down, w_turned, taps)
    x_pieces = [(inputs[i], *near[i], far[i]) for i in range(seqs)]
    w_units = over_batch(w_units.reshape(shards * rows, 2 * units))
    w_down_own = over_batch(w_down_now).reshape(units, width)

    slots = mask_positions.shape[1]
    pad = -slots % 128
    live = jnp.arange(slots, dtype=jnp.int32) < mask_counts[:, None]
    places = jnp.pad(jnp.where(live, mask_positions, -1), ((0, 0), (0, pad)), constant_values=-1)
    d_out = jnp.pad(jnp.where(live[:, :, None], grad_rows, 0.0), ((0, 0), (0, pad), (0, 0)))
    d_out = d_out.reshape(-1, width)
    places = places[:, :, None]

    def first_half(i, after):
        x_i, *n_i = arrange(x_pieces[i], s, after=after)
        return x_i, n_i, project(w_turned, n_i).reshape(3, own, length)

    first_0 = first_half(0, ())
    (x_0, n_0, p_0), base = together(first_0, base)

    w_out_own = base[:, spectra:].reshape(groups, shards // 2, rows, 2 * own).transpose(0, 2, 1, 3).reshape(own, width)
    w_out_there, (gated_0, *mixed_0) = together(from_others(w_out_own), mix(p_0, taps, base, tables))

    first_1 = first_half(1, (gated_0,))
    there_0, first_1, (gated_1, *mixed_1) = together(
        from_others(gated_0), first_1, mix(first_1[2], taps, base, tables, after=(gated_0,))
    )
    x_1, n_1, p_1 = first_1
    n_one, projected = (n_0, n_1), (p_0, p_1)
    gating, long_conv, vals, spec = zip(mixed_0, mixed_1)
    w_out_pieces = (w_out_own, *w_out_there)

    residual_0 = add_mixer(x_0, (gated_0, *there_0), w_out_pieces, after=(gated_1,))
    w_units = split_units(w_units.reshape(groups, shards, rows, 2 * units), w_down_own, after=(residual_0,))
    w_units, w_down_own = w_units[:2], w_units[2:]
    down_0 = feed_forward(residual_0, w_units, w_down_own, s)
    there_1, down_0, residual_0, w_units, w_down_own = together(
        from_others(gated_1), down_0, residual_0, w_units, w_down_own
    )

    residual_1 = add_mixer(x_1, (gated_1, *there_1), w_out_pieces, after=(down_0[0],))
    lived = live_back((residual_0, residual_1), places, d_out, w_units, w_down_own, slots)
    out_0 = [down_0[0], swap(down_0[1], "seq", 1), swap(down_0[2], "seq", 2)]
    lived, residual_1, out_0 = together(lived, residual_1, out_0)
    live_rows, n_live, hidden, d_units, e_two = lived
    residual = (residual_0, residual_1)

    e_two = [e_two[:slots], e_two[slots:]]
    unit_part = unit_grads(n_live, d_units, hidden, d_out, shards)
    e_there, unit_part = together([swap(e, "seq", 1 + i) for i, e in enumerate(e_two)], unit_part)
    unit_sums = sum_over_batch(unit_part)

    e_two = [e + there for e, there in zip(e_two, e_there)]
    down_1 = feed_forward(residual_1, w_units, w_down_own, s, after=(unit_part,))
    e_there, down_1 = together([swap(e, "seq", 2 - i) for i, e in enumerate(e_two)], down_1)
    e_terms = [*e_two, *e_there]

    d_residual, w_out_part, d_gating, d_long = live_mix(live_rows, d_out, e_terms, w_out_own, gating, long_conv, places)
    kernel_part, taps_part, d_projected = (), 0.0, []
    for i in range(seqs):
        d_p, *kernel_part, d_taps = mix_back(
            i, places, d_gating, d_long, projected[i], taps, vals[i], spec[i], kernel_part, tables,
            after=d_projected[-1:],
        )
        taps_part = taps_part + d_taps[:, :, :3]
        d_projected.append(d_p)
    out_0 += [swap(down_0[3], "seq", 3)]
    out_1 = [down_1[0], swap(down_1[1], "seq", 1), swap(down_1[2], "seq", 2)]
    d_projected, (kernel_part,), taps_part, d_residual, w_out_part, out_0, out_1 = together(
        d_projected, kernel_part, taps_part, d_residual, w_out_part, out_0, out_1
    )

    e_0 = project_back(d_projected[0].reshape(3 * own, length), n_0, w_turned, (), s)
    out_1 += [swap(down_1[3], "seq", 3)]
    (*e_0, w_in_part), out_1, unit_sums, kernel_part = together(e_0, out_1, unit_sums, kernel_part)
    kernel_sum = sum_over_batch(kernel_part.reshape(groups, -1, 2 * own))

    e_1 = project_back(d_projected[1].reshape(3 * own, length), n_1, w_turned, (w_in_part,), s)
    placed = jnp.zeros((3, 3, shards, own), F32)
    taps_part = taps_part.transpose(2, 0, 1)[:, :, None]
    placed = lax.dynamic_update_slice(placed, taps_part, (0, 0, s, 0))
    placed = placed.reshape(3, shards, groups, count).transpose(1, 2, 0, 3).reshape(width, extra)
    free = 3 * own % 128
    placed = jnp.pad(placed, ((0, 0), (free, 128 - free - extra)))
    w_in_part = turn_back(e_1[4], placed, w_out_part)
    e_there = [swap(e_0[1], "seq", 1), swap(e_0[2], "seq", 2)]
    outputs = [
        added(out) + lax.dynamic_slice_in_dim(residual[i], s * tokens, tokens, axis=0)
        for i, out in enumerate((out_0, out_1))
    ]
    e_there, e_1, w_in_part = together(e_there, e_1[:4], w_in_part)
    w_in_sum = sum_over_batch(w_in_part)

    e_one = ([e_0[0], *e_there, swap(e_0[3], "seq", 3)], to_others(e_1))
    outputs = jnp.stack(
        [
            added(out) + lax.dynamic_slice_in_dim(residual[i], s * tokens, tokens, axis=0)
            for i, out in enumerate((out_0, out_1))
        ]
    )
    e_one, w_in_sum, kernel_sum, outputs = together(e_one, w_in_sum, kernel_sum, outputs)

    kernel_sum = kernel_sum.reshape(FOLDED, -1, 2, own).transpose(2, 1, 0, 3)
    mirrored = lax.ppermute(kernel_sum[:, ::-1, 3:0:-1], "batch", mirror)
    w_back = jnp.concatenate([w_in_sum[:, :-own], unit_sums[:, : 2 * units]], axis=1)
    w_back = columns_there(w_back.reshape(shards, rows, -1), s)

    e_own = jnp.stack([added(e) for e in e_one])
    n_own, inverse_own = normed(inputs)
    here = s * tokens + jnp.arange(tokens, dtype=jnp.int32)
    select_own = (places == here).astype(F32)
    direct = contract("bmt,bmd->btd", select_own, d_residual.reshape(seqs, slots + pad, width))
    input_grad = norm_pull(n_own, inverse_own, e_own) + direct
    mirrored = jnp.stack([mirrored[0], -mirrored[1]])
    kernel_grad = jnp.concatenate([kernel_sum, mirrored], axis=2).reshape(kernel.shape)
    w_out_sum = w_in_sum[:, -own:].reshape(shards, rows, own).transpose(1, 0, 2).reshape(w_out.shape)
    w_back = by_xor(w_back, s)
    w_in_sum = w_back
    taps_sum = sum(p[:, 3 * own : split] for p in w_in_sum).reshape(conv_weight.shape)
    w_in_sum = jnp.stack([p[:, : 3 * own].reshape(rows, 3, own) for p in w_in_sum], axis=2)
    w_in_sum = w_in_sum.reshape(w_in.shape)
    w_down_sum = unit_sums[:, 2 * units :].reshape(w_down.shape)
    w_units_sum = [p[:, -2 * units :] for p in w_back]
    w_gate_sum = jnp.concatenate([p[:, :units] for p in w_units_sum], axis=1)
    w_up_sum = jnp.concatenate([p[:, units:] for p in w_units_sum], axis=1)
    gain_one_sum = jnp.sum(w_in * w_in_sum, axis=1)
    gain_two_sum = jnp.sum(w_gate * w_gate_sum, axis=1) + jnp.sum(w_up * w_up_sum, axis=1)

    return (
        outputs,
        input_grad,
        gain_one_sum,
        gain_one[:, None] * w_in_sum,
        taps_sum,
        kernel_grad,
        w_out_sum,
        gain_two_sum,
        gain_two[:, None] * w_gate_sum,
        gain_two[:, None] * w_up_sum,
        w_down_sum,
    )


def solution(mesh):
    split = ("seq", "batch")
    placed = (
        P("batch", "seq", None),
        P(split),
        P(split, None),
        P(None, split),
        P(None, "batch", "seq"),
        P(split, None),
        P(split),
        P(split, None),
        P(split, None),
        P(split, None),
        P("batch", None),
        P("batch"),
        P("batch", None, None),
    )
    return jax.shard_map(
        body,
        mesh=mesh,
        in_specs=placed,
        out_specs=(
            P("batch", "seq", None),
            P("batch", "seq", None),
            P(split),
            P(split, None),
            P(None, split),
            P(None, "batch", "seq"),
            P(split, None),
            P(split),
            P(split, None),
            P(split, None),
            P(split, None),
        ),
        check_vma=False,
    )
```

time: 1450 us -> 452 us (0.31)
  matrix products: 579 us -> 3.24 us
  waiting for transfers between devices: 517 us -> 114 us
  Pallas kernels: 0 us -> 211 us
  blocking collectives: 122 us -> 0 us
  local copies, waits for them, and re-layouts: 126 us -> 28.2 us
  other arithmetic: 49.2 us -> 22.4 us
    dot_general x54 -> x1, matrix products: 579 us -> 3.24 us  [contract(): return jnp.einsum(pattern, left_side, right_side, precision=HIGH)]
    reduce_scatter x6 -> x3, waiting for transfers between devices: 424 us -> 0.02 us  [sum_over_batch(): return lax.psum_scatter(flat, 'batch', scatter_dimension=0, tiled=True)]
    pallas_call x0 -> x21, Pallas kernels: none -> 211 us  [call(): pl.pallas_call(run, name=name, out_shape=tuple(outs), grid_spec=pltpu.Pre...]
    ppermute x4 -> x42, waiting for transfers between devices: 8.41 us -> 111 us  [the longest x40 102 us: swap(): lax.ppermute(value, axis, [(i, i ^ distance) for i in range(devices)])]
    unnamed x2 -> x0, blocking collectives: 78.5 us -> none
    all_to_all x6 -> x0, waiting for transfers between devices: 62.7 us -> none  [the longest x1 21.1 us: body(): lax.all_to_all(wide_out, 'seq', split_axis=1, concat_axis=2, tiled=True)]
    all_gather x1 -> x0, blocking collectives: 43.8 us -> none  [body(): lax.all_gather(conv_weight, ('seq', 'batch'), axis=1, tiled=True)]
    ppermute x4 -> x42, starting transfers between devices: 10.2 us -> 50.2 us  [the longest x40 47.3 us: swap(): lax.ppermute(value, axis, [(i, i ^ distance) for i in range(devices)])]
  transfers between devices with their start and end apart: 22 -> 49, of which waited for: 12 -> 17; matrix products, arithmetic and copies ran while one was open for 37% -> 8% of each run, Pallas kernels for 0% -> 48%
where the time goes in v2:
time: 452 us; the launch traced here: 445 us
  Pallas kernels  211 us (47%)
  waiting for transfers between devices  114 us (25%)
  starting transfers between devices  50.7 us (11%)
  local copies, waits for them, and re-layouts  28.2 us (6%)
  other arithmetic  22.4 us (5%)
  between operations  15.3 us (3%)
    pallas_call x21, Pallas kernels, call(): pl.pallas_call(run, name=name, out_shape=tuple(outs), grid_spec=pltpu.Pre...  211 us
    ppermute x40, waiting for transfers between devices, swap(): lax.ppermute(value, axis, [(i, i ^ distance) for i in range(devices)])  102 us
    ppermute x40, starting transfers between devices, swap(): lax.ppermute(value, axis, [(i, i ^ distance) for i in range(devices)])  47.3 us
  transfers between devices with their start and end apart: 49, of which 17 were waited for; matrix products, arithmetic and copies ran while one was open for 8% of the time, Pallas kernels for 48%

profile of v2, /device:TPU:0, one launch (start us, length us, event | category | flops | bytes accessed | tf_op | source)
XLA Modules:
  0.0 444.7 jit_solution(17544929196375024096)
XLA Ops:
  9.1 4.0 collective-permute-start
  14.4 2.7 collective-permute-start.3
  18.6 5.6 %collective-permute-done.3.refs_1_ = f32[2,32,3,192]{3,2,1,0:T(4,128)S(1)} collective-permute-done((f32[2,32,3,192]{3,2,1,0:T(4,128)S(1)}, f32[2,32,3,192]{3,2,1,0:T(4,128)S(1)}, u32[]{:S(2)}, u32[]{:S(2)}) %collective-permute-start.3) | collective-permute-done | bytes 147488 | tf_op jit(solution)/shard_map/ppermute | solution.py:774
  26.3 2.3 collective-permute-start.4
  28.6 1.5 collective-permute-start.5
  30.7 2.0 fold_base.1
  32.7 14.6 %collective-permute-done.4.refs_2_ = f32[256,768]{1,0:T(8,128)} collective-permute-done((f32[256,768]{1,0:T(8,128)}, f32[256,768]{1,0:T(8,128)}, u32[]{:S(2)}, u32[]{:S(2)}) %collective-permute-start.4) | collective-permute-done | bytes 786464 | tf_op jit(solution)/shard_map/ppermute | solution.py:31
  47.3 2.1 collective-permute-done.5.refs_3_
  49.4 14.1 %collective-permute-done.6.refs_2_ = f32[256,768]{1,0:T(8,128)S(1)} collective-permute-done((f32[256,768]{1,0:T(8,128)}, f32[256,768]{1,0:T(8,128)S(1)}, u32[]{:S(2)}, u32[]{:S(2)}) %collective-permute-start.6) | collective-permute-done | bytes 786464 | tf_op jit(solution)/shard_map/ppermute | solution.py:31
  63.5 1.6 collective-permute-done.7.refs_3_
  68.0 1.9 collective-permute-start.10
  71.5 3.3 turn_in.1
  76.1 1.5 collective-permute-start.8
  81.8 12.2 %collective-permute-done.8.refs_4_ = f32[256,768]{1,0:T(8,128)} collective-permute-done((f32[256,768]{1,0:T(8,128)}, f32[256,768]{1,0:T(8,128)}, u32[]{:S(2)}, u32[]{:S(2)}) %collective-permute-start.8) | collective-permute-done | bytes 786464 | tf_op jit(solution)/shard_map/ppermute | solution.py:31
  97.1 5.3 %arrange.2 = (f32[1024,768]{1,0:T(8,128)}, bf16[1024,768]{1,0:T(8,128)(2,1)}, bf16[1024,768]{1,0:T(8,128)(2,1)}) custom-call(s32[1]{0:T(128)} %bitcast.refs_0_, f32[256,768]{1,0:T(8,128)} %get-tuple-element.376.refs_1_, f32[256,768]{1,0:T(8,128)} %collective-permute-done.4.refs_2_, f32[256,768]{1,0:T(8,128)} %collective-permute-done.5.refs_3_, ...), custom_call_target="tpu_custom_call" | custom-call | bytes 471859 | tf_op jit(solution)/shard_map/arrange/pallas_call | solution.py:122
  102.4 6.2 %project.2 = f32[576,1024]{1,0:T(8,128)} custom-call(bf16[576,768]{1,0:T(8,128)(2,1)} %get-tuple-element.196.refs_0_.refs_4_, bf16[576,768]{1,0:T(8,128)(2,1)} %get-tuple-element.197.refs_1_.refs_5_, bf16[1024,768]{1,0:T(8,128)(2,1)} %get-tuple-element.295.refs_2_, bf16[1024,768]{1,0:T(8,128)(2,1)} %get-tuple-element.296.refs_3_), custom_call_target="tpu_custom_call" | custom-call | flops 135895456 | bytes 363724 | tf_op jit(solution)/shard_map/project/pallas_call | solution.py:122
  110.1 1.5 collective-permute-start.13
  112.1 1.5 collective-permute-start.15
  113.6 13.5 %mix.2 = (f32[192,1024]{1,0:T(8,128)}, f32[192,1024]{1,0:T(8,128)}, f32[192,1024]{1,0:T(8,128)}, f32[5,192,512]{2,1,0:T(8,128)}, f32[5,192,512]{2,1,0:T(8,128)}) custom-call(f32[3,192,1024]{2,1,0:T(8,128)} %bitcast.152, f32[3,192,3]{2,1,0:T(8,128)} %bitcast.170, f32[8,208,384]{2,1,0:T(8,128)} %bitcast.157, ...), custom_call_target="tpu_custom_call" | custom-call | flops 724775744 | bytes 865075 | tf_op jit(solution)/shard_map/mix/pallas_call | solution.py:122
  127.2 10.0 %collective-permute-done.14.refs_7_ = f32[192,768]{1,0:T(8,128)S(1)} collective-permute-done((f32[192,768]{1,0:T(8,128)S(1)}, f32[192,768]{1,0:T(8,128)S(1)}, u32[]{:S(2)}, u32[]{:S(2)}) %collective-permute-start.14) | collective-permute-done | bytes 589856 | tf_op jit(solution)/shard_map/ppermute | solution.py:31
  137.2 1.7 collective-permute-start.17
  138.9 1.8 collective-permute-start.18
  140.7 5.6 %arrange.3 = (f32[1024,768]{1,0:T(8,128)}, bf16[1024,768]{1,0:T(8,128)(2,1)}, bf16[1024,768]{1,0:T(8,128)(2,1)}) custom-call(s32[1]{0:T(128)} %bitcast.refs_0_, f32[256,768]{1,0:T(8,128)} %get-tuple-element.375.refs_1_, f32[256,768]{1,0:T(8,128)} %copy-done.31, f32[256,768]{1,0:T(8,128)} %collective-permute-done.7.refs_3_, f32[256,768]{1,0:T(8,128)} %copy-done.32, ...), custom_call_target="tpu_custom_call" | custom-call | bytes 471859 | tf_op jit(solution)/shard_map/arrange/pallas_call | solution.py:122
  146.3 6.2 %project.3 = f32[576,1024]{1,0:T(8,128)} custom-call(bf16[576,768]{1,0:T(8,128)(2,1)} %get-tuple-element.196.refs_0_.refs_4_, bf16[576,768]{1,0:T(8,128)(2,1)} %get-tuple-element.197.refs_1_.refs_5_, bf16[1024,768]{1,0:T(8,128)(2,1)} %get-tuple-element.311.refs_2_, bf16[1024,768]{1,0:T(8,128)(2,1)} %get-tuple-element.312.refs_3_), custom_call_target="tpu_custom_call" | custom-call | flops 135895456 | bytes 363724 | tf_op jit(solution)/shard_map/project/pallas_call | solution.py:122
  152.5 13.8 %mix.3 = (f32[192,1024]{1,0:T(8,128)}, f32[192,1024]{1,0:T(8,128)}, f32[192,1024]{1,0:T(8,128)}, f32[5,192,512]{2,1,0:T(8,128)}, f32[5,192,512]{2,1,0:T(8,128)}) custom-call(f32[3,192,1024]{2,1,0:T(8,128)} %bitcast.154, f32[3,192,3]{2,1,0:T(8,128)} %bitcast.171, f32[8,208,384]{2,1,0:T(8,128)} %bitcast.158, ...), custom_call_target="tpu_custom_call" | custom-call | flops 724775744 | bytes 865075 | tf_op jit(solution)/shard_map/mix/pallas_call | solution.py:122
  166.3 4.9 %collective-permute-done.17.refs_3_ = f32[192,1024]{1,0:T(8,128)S(1)} collective-permute-done((f32[192,1024]{1,0:T(8,128)}, f32[192,1024]{1,0:T(8,128)S(1)}, u32[]{:S(2)}, u32[]{:S(2)}) %collective-permute-start.17) | collective-permute-done | bytes 786464 | tf_op jit(solution)/shard_map/ppermute | solution.py:31
  171.4 2.5 collective-permute-start.20
  174.8 8.7 %add_mixer.2.refs_2_.refs_1_.refs_0_ = f32[1024,768]{1,0:T(8,128)} custom-call(f32[1024,768]{1,0:T(8,128)} %get-tuple-element.219.refs_0_, f32[192,1024]{1,0:T(8,128)} %get-tuple-element.207.refs_5_.refs_1_, f32[192,1024]{1,0:T(8,128)} %copy-done.28, f32[192,1024]{1,0:T(8,128)} %copy-done.29, f32[192,1024]{1,0:T(8,128)} %copy-done.30, f32[192,768]{1,0:T(8,128)} %bitcast.166, ...), custom_call_target="tpu_custom_call" | custom-call | flops 181193936 | bytes 589824 | tf_op jit(solution)/shard_map/add_mixer/pallas_call | solution.py:122
  183.5 1.9 all-gather.9.cloned.1.call-done
  185.4 6.3 %split_units.1 = (bf16[768,1536]{1,0:T(8,128)(2,1)}, bf16[768,1536]{1,0:T(8,128)(2,1)}, bf16[768,768]{1,0:T(8,128)(2,1)}, bf16[768,768]{1,0:T(8,128)(2,1)}) custom-call(f32[8,4,24,1536]{3,2,1,0:T(8,128)} %bitcast.174, f32[768,768]{1,0:T(8,128)} %all-gather.11.cloned.1.call-done.refs_1_, f32[1024,768]{1,0:T(8,128)} %add_mixer.2.refs_2_.refs_1_.refs_0_), custom_call_target="tpu_custom_call" | custom-call | bytes 707788 | tf_op jit(solution)/shard_map/split_units/pallas_call | solution.py:122
  191.7 19.7 %feed_forward.2 = (f32[256,768]{1,0:T(8,128)}, f32[256,768]{1,0:T(8,128)}, f32[256,768]{1,0:T(8,128)}, f32[256,768]{1,0:T(8,128)}) custom-call(s32[1]{0:T(128)} %bitcast.refs_0_, f32[1024,768]{1,0:T(8,128)} %add_mixer.2.refs_2_.refs_1_.refs_0_, bf16[768,1536]{1,0:T(8,128)(2,1)} %get-tuple-element.242.refs_2_.refs_4_, ...), custom_call_target="tpu_custom_call" | custom-call | flops 543581824 | bytes 668467 | tf_op jit(solution)/shard_map/feed_forward/pallas_call | solution.py:122
  212.6 1.5 collective-permute-start.22
  214.1 1.5 collective-permute-start.23
  218.6 8.7 %add_mixer.3.refs_1_ = f32[1024,768]{1,0:T(8,128)} custom-call(f32[1024,768]{1,0:T(8,128)} %get-tuple-element.237.refs_0_, f32[192,1024]{1,0:T(8,128)} %get-tuple-element.218.refs_9_.refs_1_, f32[192,1024]{1,0:T(8,128)} %copy-done.26, f32[192,1024]{1,0:T(8,128)} %copy-done.27, f32[192,1024]{1,0:T(8,128)} %collective-permute-done.21.refs_4_, ...), custom_call_target="tpu_custom_call" | custom-call | flops 181193936 | bytes 589824 | tf_op jit(solution)/shard_map/add_mixer/pallas_call | solution.py:122
  227.3 13.1 %live_back.1 = (f32[256,768]{1,0:T(8,128)}, f32[256,768]{1,0:T(8,128)}, f32[256,768]{1,0:T(8,128)}, f32[256,1536]{1,0:T(8,128)}, f32[160,768]{1,0:T(8,128)}) custom-call(f32[1024,768]{1,0:T(8,128)} %add_mixer.2.refs_2_.refs_1_.refs_0_, f32[1024,768]{1,0:T(8,128)} %add_mixer.3.refs_1_, s32[2,128,1]{2,1,0:T(8,128)} %copy.55.refs_2_.refs_11_.refs_0_, ...), custom_call_target="tpu_custom_call" | custom-call | flops 226492416 | bytes 786432 | tf_op jit(solution)/shard_map/live_back/pallas_call | solution.py:122
  240.4 1.4 fusion.28
  243.0 7.0 %unit_grads.1.refs_6_ = f32[8,96,2304]{2,1,0:T(8,128)} custom-call(f32[256,768]{1,0:T(8,128)} %get-tuple-element.255.refs_0_, f32[256,1536]{1,0:T(8,128)} %get-tuple-element.256.refs_1_, f32[256,768]{1,0:T(8,128)} %get-tuple-element.257.refs_2_, f32[256,768]{1,0:T(8,128)} %bitcast.160), custom_call_target="tpu_custom_call" | custom-call | flops 135895456 | bytes 353894 | tf_op jit(solution)/shard_map/unit_grads/pallas_call | solution.py:122
  252.1 1.5 collective-permute-start.26
  253.6 1.5 collective-permute-start.27
  255.6 20.1 %feed_forward.3 = (f32[256,768]{1,0:T(8,128)}, f32[256,768]{1,0:T(8,128)}, f32[256,768]{1,0:T(8,128)}, f32[256,768]{1,0:T(8,128)}) custom-call(s32[1]{0:T(128)} %bitcast.refs_0_, f32[1024,768]{1,0:T(8,128)} %add_mixer.3.refs_1_, bf16[768,1536]{1,0:T(8,128)(2,1)} %get-tuple-element.242.refs_2_.refs_4_, bf16[768,1536]{1,0:T(8,128)(2,1)} %get-tuple-element.243.refs_3_.refs_5_, ...), custom_call_target="tpu_custom_call" | custom-call | flops 543581824 | bytes 668467 | tf_op jit(solution)/shard_map/feed_forward/pallas_call | solution.py:122
  275.7 1.6 collective-permute-start.29
  277.3 1.5 collective-permute-start.30
  279.3 6.2 %live_mix.1 = (f32[256,768]{1,0:T(8,128)}, f32[192,768]{1,0:T(8,128)}, f32[2,192,128]{2,1,0:T(8,128)}, f32[2,192,128]{2,1,0:T(8,128)}) custom-call(f32[256,768]{1,0:T(8,128)} %get-tuple-element.253.refs_0_, f32[256,768]{1,0:T(8,128)} %bitcast.161, f32[80,768]{1,0:T(8,128)} %copy-done.15, f32[80,768]{1,0:T(8,128)} %copy-done.14, f32[80,768]{1,0:T(8,128)} %copy-done.36, ...), custom_call_target="tpu_custom_call" | custom-call | flops 37748736 | bytes 314572 | tf_op jit(solution)/shard_map/live_mix/pallas_call | solution.py:122
  285.5 15.0 %mix_back.2 = (f32[3,192,1024]{2,1,0:T(8,128)}, f32[8,5,32,384]{3,2,1,0:T(8,128)}, f32[3,192,128]{2,1,0:T(8,128)}) custom-call(s32[2,128,1]{2,1,0:T(8,128)} %copy.55.refs_2_.refs_11_.refs_0_, f32[2,192,128]{2,1,0:T(8,128)} %get-tuple-element.272.refs_1_, f32[2,192,128]{2,1,0:T(8,128)} %get-tuple-element.273.refs_2_, f32[3,192,1024]{2,1,0:T(8,128)} %bitcast.153, ...), custom_call_target="tpu_custom_call" | custom-call | flops 724775744 | bytes 865075 | tf_op jit(solution)/shard_map/mix_back/pallas_call | solution.py:122
  300.5 15.1 %mix_back.3 = (f32[3,192,1024]{2,1,0:T(8,128)}, f32[8,5,32,384]{3,2,1,0:T(8,128)}, f32[3,192,128]{2,1,0:T(8,128)}) custom-call(s32[2,128,1]{2,1,0:T(8,128)} %copy.55.refs_2_.refs_11_.refs_0_, f32[2,192,128]{2,1,0:T(8,128)} %get-tuple-element.272.refs_1_, f32[2,192,128]{2,1,0:T(8,128)} %get-tuple-element.273.refs_2_, f32[3,192,1024]{2,1,0:T(8,128)} %bitcast.155, ...), custom_call_target="tpu_custom_call" | custom-call | flops 724775744 | bytes 865075 | tf_op jit(solution)/shard_map/mix_back/pallas_call | solution.py:122
  316.7 15.8 %project_back.2 = (f32[256,768]{1,0:T(8,128)}, f32[256,768]{1,0:T(8,128)}, f32[256,768]{1,0:T(8,128)}, f32[256,768]{1,0:T(8,128)}, f32[576,768]{1,0:T(8,128)}) custom-call(s32[1]{0:T(128)} %bitcast.refs_0_, f32[576,1024]{1,0:T(8,128)} %bitcast.169, bf16[1024,768]{1,0:T(8,128)(2,1)} %get-tuple-element.295.refs_2_, ...), custom_call_target="tpu_custom_call" | custom-call | flops 271790912 | bytes 697958 | tf_op jit(solution)/shard_map/project_back/pallas_call | solution.py:122
  332.6 1.6 collective-permute-start.32
  334.2 1.5 collective-permute-start.33
  337.2 15.7 %project_back.3 = (f32[256,768]{1,0:T(8,128)}, f32[256,768]{1,0:T(8,128)}, f32[256,768]{1,0:T(8,128)}, f32[256,768]{1,0:T(8,128)}, f32[576,768]{1,0:T(8,128)}) custom-call(s32[1]{0:T(128)} %bitcast.refs_0_, f32[576,1024]{1,0:T(8,128)} %bitcast.181, bf16[1024,768]{1,0:T(8,128)(2,1)} %get-tuple-element.311.refs_2_, ...), custom_call_target="tpu_custom_call" | custom-call | flops 271790912 | bytes 697958 | tf_op jit(solution)/shard_map/project_back/pallas_call | solution.py:122
  352.9 4.0 turn_back.1
  357.8 1.6 collective-permute-start.35
  359.4 1.6 collective-permute-start.36
  361.3 1.5 add_bitcast_fusion.3
  364.3 1.6 add_bitcast_fusion.2
  367.2 12.1 %collective-permute-done.34 = f32[256,768]{1,0:T(8,128)} collective-permute-done((f32[256,768]{1,0:T(8,128)}, f32[256,768]{1,0:T(8,128)}, u32[]{:S(2)}, u32[]{:S(2)}) %collective-permute-start.34) | collective-permute-done | bytes 786464 | tf_op jit(solution)/shard_map/ppermute | solution.py:31
  379.2 15.8 %collective-permute-done.35 = f32[256,768]{1,0:T(8,128)} collective-permute-done((f32[256,768]{1,0:T(8,128)}, f32[256,768]{1,0:T(8,128)}, u32[]{:S(2)}, u32[]{:S(2)}) %collective-permute-start.35) | collective-permute-done | bytes 786464 | tf_op jit(solution)/shard_map/ppermute | solution.py:31
  396.0 12.1 %collective-permute-done.37 = f32[256,768]{1,0:T(8,128)} collective-permute-done((f32[256,768]{1,0:T(8,128)}, f32[256,768]{1,0:T(8,128)}, u32[]{:S(2)}, u32[]{:S(2)}) %collective-permute-start.37) | collective-permute-done | bytes 786464 | tf_op jit(solution)/shard_map/ppermute | solution.py:31
  408.2 3.2 add_bitcast_fusion
  414.3 2.0 collective-permute-start.38
  419.6 1.6 rev.7
  421.5 3.2 multiply_add_fusion
  425.5 3.0 collective-permute-done.41
  431.4 1.3 fusion.3
  434.0 1.4 broadcast_multiply_fusion.2
  (249 shorter events, 52.4 us)
Async XLA Ops:
  7.2 57.9 %all-gather.5.cloned.1.call-start = ((), (), s32[]{:S(2)}) async-start(), calls=%async_computation.3 | async-start | bytes 2211840 | tf_op jit(solution)/shard_map/all_gather | solution.py:78
  9.1 8.0 %collective-permute-start = (f32[24,585]{1,0:T(8,128)S(1)}, f32[24,585]{1,0:T(8,128)S(1)}, u32[]{:S(2)}, u32[]{:S(2)}) collective-permute-start(f32[24,585]{1,0:T(8,128)S(1)} %get-tuple-element.405), channel_id=1, source_target_pairs={{0,24},{8,16},{16,8},{24,0},{1,25},{9,17},{17,9},{25,1},{2,26},{10... | collective-permute-start | bytes 168488 | tf_op jit(solution)/shard_map/ppermute | solution.py:31
  13.0 4.2 collective-permute-start.1
  13.5 11.5 %copy-start = (f32[2,256,768]{2,1,0:T(8,128)S(1)}, f32[2,256,768]{2,1,0:T(8,128)}, u32[]{:S(2)}) copy-start(f32[2,256,768]{2,1,0:T(8,128)} %param.15) | copy-start | bytes 4718596
  13.5 4.2 collective-permute-start.2
  13.9 12.4 %copy-start.3 = (f32[2,256,192]{2,1,0:T(8,128)}, f32[2,256,192]{2,1,0:T(8,128)S(1)}, u32[]{:S(2)}) copy-start(f32[2,256,192]{2,1,0:T(8,128)S(1)} %copy.47) | copy-start | bytes 1179652
  14.4 9.8 %collective-permute-start.3 = (f32[2,32,3,192]{3,2,1,0:T(4,128)S(1)}, f32[2,32,3,192]{3,2,1,0:T(4,128)S(1)}, u32[]{:S(2)}, u32[]{:S(2)}) collective-permute-start(f32[2,32,3,192]{3,2,1,0:T(4,128)S(1)} %rev.6), channel_id=1, source_target_pairs={{0,7},{1,6},{2,5},{3,4},{4,3},{5,2},{6,1},{7,0},{8,15},{9,14},{10,... | collective-permute-start | bytes 442376 | tf_op jit(solution)/shard_map/ppermute | solution.py:774
  24.9 40.2 %copy-start.10 = (f32[24,3072]{1,0:T(8,128)S(1)}, f32[24,3072]{1,0:T(8,128)}, u32[]{:S(2)}) copy-start(f32[24,3072]{1,0:T(8,128)} %param.22) | copy-start | bytes 884740
  25.0 40.2 %copy-start.12 = (f32[24,3072]{1,0:T(8,128)S(1)}, f32[24,3072]{1,0:T(8,128)}, u32[]{:S(2)}) copy-start(f32[24,3072]{1,0:T(8,128)} %param.23) | copy-start | bytes 884740
  25.0 40.2 %copy-start.38 = (f32[24]{0:T(128)S(1)}, f32[24]{0:T(128)}, u32[]{:S(2)}) copy-start(f32[24]{0:T(128)} %param.21) | copy-start | bytes 292
  25.0 83.6 %all-gather.7.cloned.1.call-start = ((), (), s32[]{:S(2)}) async-start(), calls=%async_computation.4 | async-start | bytes 2875392 | tf_op jit(solution)/shard_map/all_gather | solution.py:78
  26.3 21.0 %collective-permute-start.4 = (f32[256,768]{1,0:T(8,128)}, f32[256,768]{1,0:T(8,128)}, u32[]{:S(2)}, u32[]{:S(2)}) collective-permute-start(f32[256,768]{1,0:T(8,128)} %get-tuple-element.378), channel_id=1, source_target_pairs={{0,8},{8,0},{16,24},{24,16},{1,9},{9,1},{17,25},{25,17},{2,10},{10... | collective-permute-start | bytes 2359304 | tf_op jit(solution)/shard_map/ppermute | solution.py:31
  28.6 20.7 %collective-permute-start.5 = (f32[256,768]{1,0:T(8,128)}, f32[256,768]{1,0:T(8,128)}, u32[]{:S(2)}, u32[]{:S(2)}) collective-permute-start(f32[256,768]{1,0:T(8,128)} %get-tuple-element.378), channel_id=1, source_target_pairs={{0,16},{8,24},{16,0},{24,8},{1,17},{9,25},{17,1},{25,9},{2,18},{10... | collective-permute-start | bytes 2359304 | tf_op jit(solution)/shard_map/ppermute | solution.py:31
  30.1 33.3 %collective-permute-start.6 = (f32[256,768]{1,0:T(8,128)}, f32[256,768]{1,0:T(8,128)S(1)}, u32[]{:S(2)}, u32[]{:S(2)}) collective-permute-start(f32[256,768]{1,0:T(8,128)} %get-tuple-element.377), channel_id=1, source_target_pairs={{0,8},{8,0},{16,24},{24,16},{1,9},{9,1},{17,25},{25,17},{2,10},{10... | collective-permute-start | bytes 2359304 | tf_op jit(solution)/shard_map/ppermute | solution.py:31
  30.7 34.4 %collective-permute-start.7 = (f32[256,768]{1,0:T(8,128)}, f32[256,768]{1,0:T(8,128)}, u32[]{:S(2)}, u32[]{:S(2)}) collective-permute-start(f32[256,768]{1,0:T(8,128)} %get-tuple-element.377), channel_id=1, source_target_pairs={{0,16},{8,24},{16,0},{24,8},{1,17},{9,25},{17,1},{25,9},{2,18},{10... | collective-permute-start | bytes 2359304 | tf_op jit(solution)/shard_map/ppermute | solution.py:31
  65.1 118.4 %all-gather.11.cloned.1.call-start = ((), (), s32[]{:S(2)}) async-start(), calls=%async_computation.6 | async-start | bytes 2654208 | tf_op jit(solution)/shard_map/all_gather | solution.py:78
  68.0 11.8 %collective-permute-start.10 = (f32[24,1536]{1,0:T(8,128)}, f32[24,1536]{1,0:T(8,128)S(1)}, u32[]{:S(2)}, u32[]{:S(2)}) collective-permute-start(f32[24,1536]{1,0:T(8,128)} %get-tuple-element.390), channel_id=1, source_target_pairs={{0,24},{8,16},{16,8},{24,0},{1,25},{9,17},{17,9},{25,1},{2,26},{10... | collective-permute-start | bytes 442376 | tf_op jit(solution)/shard_map/ppermute | solution.py:31
  70.0 9.9 %collective-permute-start.11 = (f32[24,1536]{1,0:T(8,128)}, f32[24,1536]{1,0:T(8,128)}, u32[]{:S(2)}, u32[]{:S(2)}) collective-permute-start(f32[24,1536]{1,0:T(8,128)} %get-tuple-element.392), channel_id=1, source_target_pairs={{0,16},{8,24},{16,0},{24,8},{1,17},{9,25},{17,1},{25,9},{2,18},{10... | collective-permute-start | bytes 442376 | tf_op jit(solution)/shard_map/ppermute | solution.py:31
  70.5 9.3 %collective-permute-start.12 = (f32[24,1536]{1,0:T(8,128)}, f32[24,1536]{1,0:T(8,128)}, u32[]{:S(2)}, u32[]{:S(2)}) collective-permute-start(f32[24,1536]{1,0:T(8,128)} %get-tuple-element.391), channel_id=1, source_target_pairs={{0,8},{8,0},{16,24},{24,16},{1,9},{9,1},{17,25},{25,17},{2,10},{10... | collective-permute-start | bytes 442376 | tf_op jit(solution)/shard_map/ppermute | solution.py:31
  76.1 17.9 %collective-permute-start.8 = (f32[256,768]{1,0:T(8,128)}, f32[256,768]{1,0:T(8,128)}, u32[]{:S(2)}, u32[]{:S(2)}) collective-permute-start(f32[256,768]{1,0:T(8,128)} %collective-permute-done.4.refs_2_), channel_id=1, source_target_pairs={{0,16},{8,24},{16,0},{24,8},{1,17},{9,25},{17,1},{25,9},{2,18},{10... | collective-permute-start | bytes 2359304 | tf_op jit(solution)/shard_map/ppermute | solution.py:31
  77.6 17.4 %collective-permute-start.9 = (f32[256,768]{1,0:T(8,128)}, f32[256,768]{1,0:T(8,128)S(1)}, u32[]{:S(2)}, u32[]{:S(2)}) collective-permute-start(f32[256,768]{1,0:T(8,128)} %collective-permute-done.7.refs_3_), channel_id=1, source_target_pairs={{0,8},{8,0},{16,24},{24,16},{1,9},{9,1},{17,25},{25,17},{2,10},{10... | collective-permute-start | bytes 2359304 | tf_op jit(solution)/shard_map/ppermute | solution.py:31
  95.1 90.3 %all-gather.9.cloned.1.call-start = ((), (), s32[]{:S(2)}) async-start(), calls=%async_computation.5 | async-start | bytes 5308416 | tf_op jit(solution)/shard_map/all_gather | solution.py:78
  95.7 236.9 %reduce-scatter.4.cloned.1.call-start = ((), (), s32[]{:S(2)}) async-start(), calls=%async_computation.7 | async-start | bytes 7962624 | tf_op jit(solution)/shard_map/reduce_scatter | solution.py:84
  110.0 17.1 %copy-start.1 = (f32[24,8,2,384]{3,1,2,0:T(8,128)}, f32[24,8,2,384]{3,1,2,0:T(8,128)S(1)}, u32[]{:S(2)}) copy-start(f32[24,8,2,384]{3,1,2,0:T(8,128)S(1)} %copy.63) | copy-start | bytes 1769476
  110.1 17.1 %collective-permute-start.13 = (f32[192,768]{1,0:T(8,128)S(1)}, f32[192,768]{1,0:T(8,128)S(1)}, u32[]{:S(2)}, u32[]{:S(2)}) collective-permute-start(f32[192,768]{1,0:T(8,128)S(1)} %bitcast.163), channel_id=1, source_target_pairs={{0,8},{8,0},{16,24},{24,16},{1,9},{9,1},{17,25},{25,17},{2,10},{10... | collective-permute-start | bytes 1769480 | tf_op jit(solution)/shard_map/ppermute | solution.py:31
  111.6 25.6 %collective-permute-start.14 = (f32[192,768]{1,0:T(8,128)S(1)}, f32[192,768]{1,0:T(8,128)S(1)}, u32[]{:S(2)}, u32[]{:S(2)}) collective-permute-start(f32[192,768]{1,0:T(8,128)S(1)} %bitcast.164), channel_id=1, source_target_pairs={{0,16},{8,24},{16,0},{24,8},{1,17},{9,25},{17,1},{25,9},{2,18},{10... | collective-permute-start | bytes 1769480 | tf_op jit(solution)/shard_map/ppermute | solution.py:31
  112.1 25.0 %collective-permute-start.15 = (f32[192,768]{1,0:T(8,128)S(1)}, f32[192,768]{1,0:T(8,128)S(1)}, u32[]{:S(2)}, u32[]{:S(2)}) collective-permute-start(f32[192,768]{1,0:T(8,128)S(1)} %bitcast.165), channel_id=1, source_target_pairs={{0,24},{8,16},{16,8},{24,0},{1,25},{9,17},{17,9},{25,1},{2,26},{10... | collective-permute-start | bytes 1769480 | tf_op jit(solution)/shard_map/ppermute | solution.py:31
  127.2 19.2 %copy-start.5 = (f32[192,768]{1,0:T(8,128)}, f32[192,768]{1,0:T(8,128)S(1)}, u32[]{:S(2)}) copy-start(f32[192,768]{1,0:T(8,128)S(1)} %collective-permute-done.13.refs_6_) | copy-start | bytes 1769476
  137.2 29.2 %collective-permute-start.16 = (f32[192,1024]{1,0:T(8,128)}, f32[192,1024]{1,0:T(8,128)S(1)}, u32[]{:S(2)}, u32[]{:S(2)}) collective-permute-start(f32[192,1024]{1,0:T(8,128)} %get-tuple-element.207.refs_5_.refs_1_), channel_id=1, source_target_pairs={{0,8},{8,0},{16,24},{24,16},{1,9},{9,1},{17,25},{25,17},{2,10},{10... | collective-permute-start | bytes 2359304 | tf_op jit(solution)/shard_map/ppermute | solution.py:31
  137.2 34.0 %collective-permute-start.17 = (f32[192,1024]{1,0:T(8,128)}, f32[192,1024]{1,0:T(8,128)S(1)}, u32[]{:S(2)}, u32[]{:S(2)}) collective-permute-start(f32[192,1024]{1,0:T(8,128)} %get-tuple-element.207.refs_5_.refs_1_), channel_id=1, source_target_pairs={{0,16},{8,24},{16,0},{24,8},{1,17},{9,25},{17,1},{25,9},{2,18},{10... | collective-permute-start | bytes 2359304 | tf_op jit(solution)/shard_map/ppermute | solution.py:31
  138.9 32.4 %collective-permute-start.18 = (f32[192,1024]{1,0:T(8,128)}, f32[192,1024]{1,0:T(8,128)S(1)}, u32[]{:S(2)}, u32[]{:S(2)}) collective-permute-start(f32[192,1024]{1,0:T(8,128)} %get-tuple-element.207.refs_5_.refs_1_), channel_id=1, source_target_pairs={{0,24},{8,16},{16,8},{24,0},{1,25},{9,17},{17,9},{25,1},{2,26},{10... | collective-permute-start | bytes 2359304 | tf_op jit(solution)/shard_map/ppermute | solution.py:31
  171.3 40.1 %collective-permute-start.19 = (f32[192,1024]{1,0:T(8,128)}, f32[192,1024]{1,0:T(8,128)S(1)}, u32[]{:S(2)}, u32[]{:S(2)}) collective-permute-start(f32[192,1024]{1,0:T(8,128)} %get-tuple-element.218.refs_9_.refs_1_), channel_id=1, source_target_pairs={{0,8},{8,0},{16,24},{24,16},{1,9},{9,1},{17,25},{25,17},{2,10},{10... | collective-permute-start | bytes 2359304 | tf_op jit(solution)/shard_map/ppermute | solution.py:31
  171.4 40.1 %collective-permute-start.20 = (f32[192,1024]{1,0:T(8,128)}, f32[192,1024]{1,0:T(8,128)S(1)}, u32[]{:S(2)}, u32[]{:S(2)}) collective-permute-start(f32[192,1024]{1,0:T(8,128)} %get-tuple-element.218.refs_9_.refs_1_), channel_id=1, source_target_pairs={{0,16},{8,24},{16,0},{24,8},{1,17},{9,25},{17,1},{25,9},{2,18},{10... | collective-permute-start | bytes 2359304 | tf_op jit(solution)/shard_map/ppermute | solution.py:31
  173.9 37.6 %collective-permute-start.21 = (f32[192,1024]{1,0:T(8,128)}, f32[192,1024]{1,0:T(8,128)}, u32[]{:S(2)}, u32[]{:S(2)}) collective-permute-start(f32[192,1024]{1,0:T(8,128)} %get-tuple-element.218.refs_9_.refs_1_), channel_id=1, source_target_pairs={{0,24},{8,16},{16,8},{24,0},{1,25},{9,17},{17,9},{25,1},{2,26},{10... | collective-permute-start | bytes 2359304 | tf_op jit(solution)/shard_map/ppermute | solution.py:31
  191.7 23.8 %copy-start.42 = (s32[2,80]{1,0:T(2,128)S(1)}, s32[2,80]{1,0:T(2,128)}, u32[]{:S(2)}) copy-start(s32[2,80]{1,0:T(2,128)} %param.25) | copy-start | bytes 1924
  191.7 23.8 %copy-start.43 = (s32[2]{0:T(128)S(1)}, s32[2]{0:T(128)}, u32[]{:S(2)}) copy-start(s32[2]{0:T(128)} %param.26) | copy-start | bytes 28
  212.6 27.8 %collective-permute-start.22 = (f32[256,768]{1,0:T(8,128)}, f32[256,768]{1,0:T(8,128)S(1)}, u32[]{:S(2)}, u32[]{:S(2)}) collective-permute-start(f32[256,768]{1,0:T(8,128)} %get-tuple-element.251), channel_id=1, source_target_pairs={{0,8},{8,0},{16,24},{24,16},{1,9},{9,1},{17,25},{25,17},{2,10},{10... | collective-permute-start | bytes 2359304 | tf_op jit(solution)/shard_map/ppermute | solution.py:31
  214.1 26.3 %collective-permute-start.23 = (f32[256,768]{1,0:T(8,128)}, f32[256,768]{1,0:T(8,128)S(1)}, u32[]{:S(2)}, u32[]{:S(2)}) collective-permute-start(f32[256,768]{1,0:T(8,128)} %get-tuple-element.252), channel_id=1, source_target_pairs={{0,16},{8,24},{16,0},{24,8},{1,17},{9,25},{17,1},{25,9},{2,18},{10... | collective-permute-start | bytes 2359304 | tf_op jit(solution)/shard_map/ppermute | solution.py:31
  241.8 8.2 %collective-permute-start.24 = (f32[80,768]{1,0:T(8,128)S(1)}, f32[80,768]{1,0:T(8,128)S(1)}, u32[]{:S(2)}, u32[]{:S(2)}) collective-permute-start(f32[80,768]{1,0:T(8,128)S(1)} %get-tuple-element.396), channel_id=1, source_target_pairs={{0,8},{8,0},{16,24},{24,16},{1,9},{9,1},{17,25},{25,17},{2,10},{10... | collective-permute-start | bytes 737288 | tf_op jit(solution)/shard_map/ppermute | solution.py:31
  242.4 7.6 %collective-permute-start.25 = (f32[80,768]{1,0:T(8,128)S(1)}, f32[80,768]{1,0:T(8,128)}, u32[]{:S(2)}, u32[]{:S(2)}) collective-permute-start(f32[80,768]{1,0:T(8,128)S(1)} %get-tuple-element.395), channel_id=1, source_target_pairs={{0,16},{8,24},{16,0},{24,8},{1,17},{9,25},{17,1},{25,9},{2,18},{10... | collective-permute-start | bytes 737288 | tf_op jit(solution)/shard_map/ppermute | solution.py:31
  250.0 158.1 %reduce-scatter.8.cloned.1.call-start = ((), (), s32[]{:S(2)}) async-start(), calls=%async_computation.9 | async-start | bytes 2211840 | tf_op jit(solution)/shard_map/reduce_scatter | solution.py:84
  252.0 23.7 %copy-start.14 = (f32[80,768]{1,0:T(8,128)}, f32[80,768]{1,0:T(8,128)S(1)}, u32[]{:S(2)}) copy-start(f32[80,768]{1,0:T(8,128)S(1)} %get-tuple-element.393.refs_3_) | copy-start | bytes 737284
  252.0 23.7 %copy-start.15 = (f32[80,768]{1,0:T(8,128)}, f32[80,768]{1,0:T(8,128)S(1)}, u32[]{:S(2)}) copy-start(f32[80,768]{1,0:T(8,128)S(1)} %get-tuple-element.394.refs_2_) | copy-start | bytes 737284
  252.1 23.7 %collective-permute-start.26 = (f32[80,768]{1,0:T(8,128)S(1)}, f32[80,768]{1,0:T(8,128)S(1)}, u32[]{:S(2)}, u32[]{:S(2)}) collective-permute-start(f32[80,768]{1,0:T(8,128)S(1)} %get-tuple-element.394.refs_2_), channel_id=1, source_target_pairs={{0,16},{8,24},{16,0},{24,8},{1,17},{9,25},{17,1},{25,9},{2,18},{10... | collective-permute-start | bytes 737288 | tf_op jit(solution)/shard_map/ppermute | solution.py:31
  253.6 22.1 %collective-permute-start.27 = (f32[80,768]{1,0:T(8,128)S(1)}, f32[80,768]{1,0:T(8,128)S(1)}, u32[]{:S(2)}, u32[]{:S(2)}) collective-permute-start(f32[80,768]{1,0:T(8,128)S(1)} %get-tuple-element.393.refs_3_), channel_id=1, source_target_pairs={{0,8},{8,0},{16,24},{24,16},{1,9},{9,1},{17,25},{25,17},{2,10},{10... | collective-permute-start | bytes 737288 | tf_op jit(solution)/shard_map/ppermute | solution.py:31
  255.1 61.5 %collective-permute-start.28 = (f32[256,768]{1,0:T(8,128)}, f32[256,768]{1,0:T(8,128)S(1)}, u32[]{:S(2)}, u32[]{:S(2)}) collective-permute-start(f32[256,768]{1,0:T(8,128)} %get-tuple-element.290), channel_id=1, source_target_pairs={{0,24},{8,16},{16,8},{24,0},{1,25},{9,17},{17,9},{25,1},{2,26},{10... | collective-permute-start | bytes 2359304 | tf_op jit(solution)/shard_map/ppermute | solution.py:31
  275.7 40.9 %collective-permute-start.29 = (f32[256,768]{1,0:T(8,128)}, f32[256,768]{1,0:T(8,128)S(1)}, u32[]{:S(2)}, u32[]{:S(2)}) collective-permute-start(f32[256,768]{1,0:T(8,128)} %get-tuple-element.292), channel_id=1, source_target_pairs={{0,8},{8,0},{16,24},{24,16},{1,9},{9,1},{17,25},{25,17},{2,10},{10... | collective-permute-start | bytes 2359304 | tf_op jit(solution)/shard_map/ppermute | solution.py:31
  277.3 39.3 %collective-permute-start.30 = (f32[256,768]{1,0:T(8,128)}, f32[256,768]{1,0:T(8,128)S(1)}, u32[]{:S(2)}, u32[]{:S(2)}) collective-permute-start(f32[256,768]{1,0:T(8,128)} %get-tuple-element.293), channel_id=1, source_target_pairs={{0,16},{8,24},{16,0},{24,8},{1,17},{9,25},{17,1},{25,9},{2,18},{10... | collective-permute-start | bytes 2359304 | tf_op jit(solution)/shard_map/ppermute | solution.py:31
  278.8 53.7 %collective-permute-start.31 = (f32[256,768]{1,0:T(8,128)}, f32[256,768]{1,0:T(8,128)}, u32[]{:S(2)}, u32[]{:S(2)}) collective-permute-start(f32[256,768]{1,0:T(8,128)} %get-tuple-element.305), channel_id=1, source_target_pairs={{0,24},{8,16},{16,8},{24,0},{1,25},{9,17},{17,9},{25,1},{2,26},{10... | collective-permute-start | bytes 2359304 | tf_op jit(solution)/shard_map/ppermute | solution.py:31
  300.5 15.1 %copy-start.34 = (f32[3,192,128]{2,1,0:T(8,128)S(1)}, f32[3,192,128]{2,1,0:T(8,128)}, u32[]{:S(2)}) copy-start(f32[3,192,128]{2,1,0:T(8,128)} %get-tuple-element.283) | copy-start | bytes 884740
  316.6 15.8 %copy-start.20 = (f32[256,768]{1,0:T(8,128)}, f32[256,768]{1,0:T(8,128)S(1)}, u32[]{:S(2)}) copy-start(f32[256,768]{1,0:T(8,128)S(1)} %collective-permute-done.28) | copy-start | bytes 2359300
  316.6 15.8 %copy-start.22 = (f32[256,768]{1,0:T(8,128)}, f32[256,768]{1,0:T(8,128)S(1)}, u32[]{:S(2)}) copy-start(f32[256,768]{1,0:T(8,128)S(1)} %collective-permute-done.29) | copy-start | bytes 2359300
  316.7 15.8 %copy-start.24 = (f32[256,768]{1,0:T(8,128)}, f32[256,768]{1,0:T(8,128)S(1)}, u32[]{:S(2)}) copy-start(f32[256,768]{1,0:T(8,128)S(1)} %collective-permute-done.30) | copy-start | bytes 2359300
  332.5 75.6 %reduce-scatter.6.cloned.1.call-start = ((), (), s32[]{:S(2)}) async-start(), calls=%async_computation.8 | async-start | bytes 3096576 | tf_op jit(solution)/shard_map/reduce_scatter | solution.py:84
  332.6 24.3 %collective-permute-start.32 = (f32[256,768]{1,0:T(8,128)}, f32[256,768]{1,0:T(8,128)}, u32[]{:S(2)}, u32[]{:S(2)}) collective-permute-start(f32[256,768]{1,0:T(8,128)} %get-tuple-element.308), channel_id=1, source_target_pairs={{0,8},{8,0},{16,24},{24,16},{1,9},{9,1},{17,25},{25,17},{2,10},{10... | collective-permute-start | bytes 2359304 | tf_op jit(solution)/shard_map/ppermute | solution.py:31
  334.2 22.7 %collective-permute-start.33 = (f32[256,768]{1,0:T(8,128)}, f32[256,768]{1,0:T(8,128)}, u32[]{:S(2)}, u32[]{:S(2)}) collective-permute-start(f32[256,768]{1,0:T(8,128)} %get-tuple-element.309), channel_id=1, source_target_pairs={{0,16},{8,24},{16,0},{24,8},{1,17},{9,25},{17,1},{25,9},{2,18},{10... | collective-permute-start | bytes 2359304 | tf_op jit(solution)/shard_map/ppermute | solution.py:31
  357.5 21.8 %collective-permute-start.34 = (f32[256,768]{1,0:T(8,128)}, f32[256,768]{1,0:T(8,128)}, u32[]{:S(2)}, u32[]{:S(2)}) collective-permute-start(f32[256,768]{1,0:T(8,128)} %get-tuple-element.323), channel_id=1, source_target_pairs={{0,24},{8,16},{16,8},{24,0},{1,25},{9,17},{17,9},{25,1},{2,26},{10... | collective-permute-start | bytes 2359304 | tf_op jit(solution)/shard_map/ppermute | solution.py:31
  357.8 37.2 %collective-permute-start.35 = (f32[256,768]{1,0:T(8,128)}, f32[256,768]{1,0:T(8,128)}, u32[]{:S(2)}, u32[]{:S(2)}) collective-permute-start(f32[256,768]{1,0:T(8,128)} %get-tuple-element.325), channel_id=1, source_target_pairs={{0,8},{8,0},{16,24},{24,16},{1,9},{9,1},{17,25},{25,17},{2,10},{10... | collective-permute-start | bytes 2359304 | tf_op jit(solution)/shard_map/ppermute | solution.py:31
  359.4 36.6 %collective-permute-start.36 = (f32[256,768]{1,0:T(8,128)}, f32[256,768]{1,0:T(8,128)}, u32[]{:S(2)}, u32[]{:S(2)}) collective-permute-start(f32[256,768]{1,0:T(8,128)} %get-tuple-element.326), channel_id=1, source_target_pairs={{0,16},{8,24},{16,0},{24,8},{1,17},{9,25},{17,1},{25,9},{2,18},{10... | collective-permute-start | bytes 2359304 | tf_op jit(solution)/shard_map/ppermute | solution.py:31
  361.0 47.1 %collective-permute-start.37 = (f32[256,768]{1,0:T(8,128)}, f32[256,768]{1,0:T(8,128)}, u32[]{:S(2)}, u32[]{:S(2)}) collective-permute-start(f32[256,768]{1,0:T(8,128)} %get-tuple-element.327), channel_id=1, source_target_pairs={{0,24},{8,16},{16,8},{24,0},{1,25},{9,17},{17,9},{25,1},{2,26},{10... | collective-permute-start | bytes 2359304 | tf_op jit(solution)/shard_map/ppermute | solution.py:31
  414.3 17.2 %collective-permute-start.38 = (f32[24,2176]{1,0:T(8,128)}, f32[24,2176]{1,0:T(8,128)}, u32[]{:S(2)}, u32[]{:S(2)}) collective-permute-start(f32[24,2176]{1,0:T(8,128)} %get-tuple-element.387), channel_id=1, source_target_pairs={{0,24},{8,16},{16,8},{24,0},{1,25},{9,17},{17,9},{25,1},{2,26},{10... | collective-permute-start | bytes 626696 | tf_op jit(solution)/shard_map/ppermute | solution.py:31
  416.3 15.2 %collective-permute-start.39 = (f32[24,2176]{1,0:T(8,128)}, f32[24,2176]{1,0:T(8,128)}, u32[]{:S(2)}, u32[]{:S(2)}) collective-permute-start(f32[24,2176]{1,0:T(8,128)} %get-tuple-element.389), channel_id=1, source_target_pairs={{0,16},{8,24},{16,0},{24,8},{1,17},{9,25},{17,1},{25,9},{2,18},{10... | collective-permute-start | bytes 626696 | tf_op jit(solution)/shard_map/ppermute | solution.py:31
  416.9 14.5 %collective-permute-start.40 = (f32[24,2176]{1,0:T(8,128)}, f32[24,2176]{1,0:T(8,128)}, u32[]{:S(2)}, u32[]{:S(2)}) collective-permute-start(f32[24,2176]{1,0:T(8,128)} %get-tuple-element.388), channel_id=1, source_target_pairs={{0,8},{8,0},{16,24},{24,16},{1,9},{9,1},{17,25},{25,17},{2,10},{10... | collective-permute-start | bytes 626696 | tf_op jit(solution)/shard_map/ppermute | solution.py:31
  421.3 7.3 %collective-permute-start.41 = (f32[2,32,3,192]{3,0,1,2:T(2,128)}, f32[2,32,3,192]{3,0,1,2:T(2,128)}, u32[]{:S(2)}, u32[]{:S(2)}) collective-permute-start(f32[2,32,3,192]{3,0,1,2:T(2,128)} %rev.7), channel_id=1, source_target_pairs={{0,7},{1,6},{2,5},{3,4},{4,3},{5,2},{6,1},{7,0},{8,15},{9,14},{10,... | collective-permute-start | bytes 442376 | tf_op jit(solution)/shard_map/ppermute | solution.py:894
  (32 other events, 106.6 us)
Sparse Core Ops, SparseCore 0:
  25.1 32.2 all-gather.4
  65.2 35.4 all-gather.6
  102.4 30.6 all-gather.10
  134.6 50.8 all-gather.8
  250.2 78.2 reduce-scatter.3
  332.7 36.0 reduce-scatter.7
  371.2 36.3 reduce-scatter.5

commit v3 on v2

--- a/solution.py
+++ b/solution.py
@@ -147,12 +147,10 @@
     pl.when(pl.program_id(0) == 0)(work)
 
 
-def fold_base(kernel, mirrored, w_out, after=()):
+def fold_base(kernel, mirrored, after=()):
     _, turns, kept, own = mirrored.shape
-    rows, width = w_out.shape
-    wide = 2 * own
-
-    def run(k_ref, m_ref, w_ref, out_ref):
+
+    def run(k_ref, m_ref, out_ref):
         for phase in range(FOLDED):
             for part in range(2):
                 value = k_ref[part, :, phase]
@@ -160,23 +158,19 @@
                     other = m_ref[part, :, phase - 1]
                     value = value + other if part == 0 else value - other
                 out_ref[phase * turns : (phase + 1) * turns, part * own : (part + 1) * own] = value
-        for k in range(width // wide):
-            at = FOLDED * turns + k * rows
-            out_ref[at : at + rows] = w_ref[:, k * wide : (k + 1) * wide]
-
-    count = FOLDED * turns + width // wide * rows
+
+    shape = (FOLDED * turns, 2 * own)
     (out,) = call(
-        run, "fold_base", 0, 12 * count * wide, [kernel, mirrored, w_out],
-        [whole(*kernel.shape), whole(*mirrored.shape), whole(rows, width)],
-        [shaped(count, wide)], [whole(count, wide)], after=after,
+        run, "fold_base", 0, 12 * shape[0] * shape[1], [kernel, mirrored],
+        [whole(*kernel.shape), whole(*mirrored.shape)], [shaped(*shape)], [whole(*shape)], after=after,
     )
     return out
 
 
 def turn_in(gathered, channels):
-    groups, shards, rows, columns = gathered.shape
+    groups, shards, rows, _ = gathered.shape
     width = groups * shards * rows
-    wide = -(-columns // 128) * 128
+    wide = -(-channels // 128) * 128
 
     def kernel(w_ref, high_ref, low_ref, flat_ref):
         flat_ref[:, channels // 128 * 128 :] = jnp.zeros((width, wide - channels // 128 * 128), F32)
@@ -333,7 +327,7 @@
     groups = base.shape[0]
     turns = block // groups
     if turns % 8:
-        base = base[:, : FOLDED * turns].reshape(groups, FOLDED, turns, 2 * own)
+        base = base.reshape(groups, FOLDED, turns, 2 * own)
         spectrum = pl.BlockSpec((groups, 1, turns, 2 * own), lambda i: (0, i, 0, 0))
     else:
         spectrum = pl.BlockSpec((groups, turns, 2 * own), lambda i: (0, i, 0))
@@ -725,6 +719,84 @@
         scratch=[pltpu.VMEM((wide, width), F32)], after=after,
     )
     return out
+
+
+def finish(which, e_terms, x, d_residual, places, s, held, after=()):
+    tokens, width = e_terms[0].shape
+    seqs, slots, _ = places.shape
+
+    def kernel(s_ref, e0, e1, e2, e3, x_ref, d_ref, at_ref, *refs):
+        out_ref = refs[-1]
+        e = (e0[...] + e1[...]) + (e2[...] + e3[...])
+        n, inverse = normed(x_ref[0])
+        along = jnp.mean(e * n, axis=-1, keepdims=True)
+        here = lax.broadcasted_iota(jnp.int32, (slots, tokens), 1) + s_ref[0] * tokens
+        pick = jnp.where(here == at_ref[0], 1.0, 0.0).astype(BF16)
+        direct = chosen_rows(pick, halves(d_ref[...]), TN)
+        out_ref[0] = (e - jnp.mean(e, axis=-1, keepdims=True) - n * along) * inverse + direct
+
+    inputs = [*e_terms, x, d_residual, places, *held]
+    one = pl.BlockSpec((1, tokens, width), lambda i, *_: (which, 0, 0))
+    return pl.pallas_call(
+        kernel,
+        name="finish",
+        out_shape=shaped(seqs, tokens, width),
+        grid_spec=pltpu.PrefetchScalarGridSpec(
+            num_scalar_prefetch=1,
+            grid=(1,),
+            in_specs=[whole(tokens, width)] * 4
+            + [one, pl.BlockSpec((slots, width), lambda i, *_: (which, 0))]
+            + [pl.BlockSpec((1, slots, 1), lambda i, *_: (which, 0, 0))]
+            + [pl.BlockSpec(memory_space=pl.ANY)] * len(held),
+            out_specs=one,
+        ),
+        input_output_aliases={len(inputs): 0} if held else {},
+        compiler_params=pltpu.CompilerParams(vmem_limit_bytes=VMEM),
+        cost_estimate=pl.CostEstimate(flops=10**6, bytes_accessed=10**6, transcendentals=0),
+    )(s.reshape(1), *inputs)
+
+
+def weight_grads(pieces, s, gain_one, gain_two, w_in, w_gate, w_up, own, units):
+    rows, columns = pieces[0].shape
+    start = columns - 2 * units
+    shards = len(pieces)
+
+    def kernel(s_ref, *refs):
+        p_refs, refs = refs[:shards], refs[shards:]
+        one_ref, two_ref, wi_ref, wg_ref, wu_ref, di_ref, dg_ref, du_ref, g1_ref, g2_ref, tap_ref = refs
+        one, two = one_ref[...], two_ref[...]
+        lane = 3 * own // 128 * 128
+        tap_ref[...] = (p_refs[0][:, lane:start] + p_refs[1][:, lane:start]) + (
+            p_refs[2][:, lane:start] + p_refs[3][:, lane:start]
+        )
+        for index in range(shards):
+
+            @pl.when(s_ref[0] == index)
+            def _(index=index):
+                sum_one = jnp.zeros((rows, 1), F32)
+                sum_two = jnp.zeros((rows, 1), F32)
+                for d, p_ref in enumerate(p_refs):
+                    k = index ^ d
+                    for j in range(3):
+                        at = slice((j * shards + k) * own, (j * shards + k + 1) * own)
+                        part = p_ref[:, j * own : (j + 1) * own]
+                        sum_one += jnp.sum(wi_ref[:, at] * part, axis=1, keepdims=True)
+                        di_ref[:, at] = one * part
+                    at = slice(k * units, (k + 1) * units)
+                    for j, (w_ref, d_ref) in enumerate(((wg_ref, dg_ref), (wu_ref, du_ref))):
+                        part = p_ref[:, start + j * units : start + (j + 1) * units]
+                        sum_two += jnp.sum(w_ref[:, at] * part, axis=1, keepdims=True)
+                        d_ref[:, at] = two * part
+                g1_ref[...] = sum_one
+                g2_ref[...] = sum_two
+
+    inputs = [*pieces, gain_one[:, None], gain_two[:, None], w_in, w_gate, w_up]
+    wide = start - 3 * own // 128 * 128
+    outs = [w_in.shape, w_gate.shape, w_up.shape, (rows, 1), (rows, 1), (rows, wide)]
+    return call(
+        kernel, "weight_grads", 0, 0, inputs, [whole(*v.shape) for v in inputs],
+        [shaped(*v) for v in outs], [whole(*v) for v in outs], scalars=[s.reshape(1)],
+    )
 
 
 def norm_pull(n, inverse, grad):
@@ -764,35 +836,6 @@
     extra = 3 * count // rows
     tables = phase_tables(freqs)
 
-    w_pre = (gain_one[:, None] * w_in).reshape(rows, 3, shards, own).transpose(0, 2, 1, 3)
-    w_pre = w_pre.reshape(rows, shards, 3 * own)
-    carried = jnp.broadcast_to(conv_weight.reshape(rows, 1, extra), (rows, shards, extra))
-    split = 3 * own + extra
-    sent = columns_out(jnp.concatenate([w_pre, carried], axis=2), s)
-    wide = kernel.reshape(2, -1, RADIX, own)
-    mirror = [(i, groups - 1 - i) for i in range(groups)]
-    folded = lax.ppermute(wide[:, ::-1, :4:-1], "batch", mirror)
-    sent, folded, inputs_now = together(sent, folded, inputs)
-    w_pre = over_batch(sent.reshape(shards * rows, split)).reshape(groups, shards, rows, split)
-
-    folded = fold_base(wide, folded, w_out)
-    spectra = folded.shape[0] - rows * shards // 2
-    near = [(swap(inputs_now[i], "seq", 1), swap(inputs_now[i], "seq", 2)) for i in range(seqs)]
-    near, folded, w_pre, w_gate_now, w_up_now = together(near, folded, w_pre, w_gate, w_up)
-    base = over_batch(folded)
-
-    far = [swap(near[i][i % 2], "seq", 2 - i % 2) for i in range(seqs)]
-    w_units = jnp.stack([gain_two[:, None] * w_gate_now, gain_two[:, None] * w_up_now], axis=1)
-    w_units = w_units.reshape(rows, 2, shards, units).transpose(0, 2, 1, 3).reshape(rows, shards, 2 * units)
-    w_turned = turn_in(w_pre, 3 * own)
-    taps = w_pre[..., 3 * own :].reshape(groups, shards, 3, count).transpose(2, 1, 0, 3)
-    taps = lax.dynamic_index_in_dim(taps.reshape(3, 3, shards, own), s, axis=2, keepdims=False)
-    taps = taps.transpose(1, 2, 0)
-    far, w_units, w_down_now, w_turned, taps = together(far, columns_out(w_units, s), w_down, w_turned, taps)
-    x_pieces = [(inputs[i], *near[i], far[i]) for i in range(seqs)]
-    w_units = over_batch(w_units.reshape(shards * rows, 2 * units))
-    w_down_own = over_batch(w_down_now).reshape(units, width)
-
     slots = mask_positions.shape[1]
     pad = -slots % 128
     live = jnp.arange(slots, dtype=jnp.int32) < mask_counts[:, None]
@@ -801,21 +844,52 @@
     d_out = d_out.reshape(-1, width)
     places = places[:, :, None]
 
-    def first_half(i, after):
-        x_i, *n_i = arrange(x_pieces[i], s, after=after)
+    w_pre = (gain_one[:, None] * w_in).reshape(rows, 3, shards, own).transpose(0, 2, 1, 3)
+    w_pre = w_pre.reshape(rows, shards, 3 * own)
+    carried = jnp.broadcast_to(conv_weight.reshape(rows, 1, extra), (rows, shards, extra))
+    split = 3 * own + extra
+    sent = columns_out(jnp.concatenate([w_pre, carried], axis=2), s)
+    near_0 = (swap(inputs[0], "seq", 1), swap(inputs[0], "seq", 2))
+    w_down_own = over_batch(w_down).reshape(units, width)
+    sent, near_0, x_now, kernel_now, places, d_out = together(sent, near_0, inputs[1], kernel, places, d_out)
+    w_out_turned = w_out.reshape(rows, shards, own).transpose(1, 0, 2).reshape(shards * rows, own)
+    sent = jnp.concatenate([sent.reshape(shards * rows, split), w_out_turned], axis=1)
+
+    wide = kernel_now.reshape(2, -1, RADIX, own)
+    mirror = [(i, groups - 1 - i) for i in range(groups)]
+    folded = lax.ppermute(wide[:, ::-1, :4:-1], "batch", mirror)
+    near_1 = (swap(x_now, "seq", 1), swap(x_now, "seq", 2))
+    near_1, near_0, folded, sent, w_down_own, w_gate_now, w_up_now = together(
+        near_1, near_0, folded, sent, w_down_own, w_gate, w_up
+    )
+    w_pre = over_batch(sent).reshape(groups, shards, rows, split + own)
+    base = over_batch(fold_base(wide, folded))
+
+    far = (swap(near_0[0], "seq", 2), swap(near_1[1], "seq", 1))
+    w_units = jnp.stack([gain_two[:, None] * w_gate_now, gain_two[:, None] * w_up_now], axis=1)
+    w_units = w_units.reshape(rows, 2, shards, units).transpose(0, 2, 1, 3).reshape(rows, shards, 2 * units)
+    far, w_units = together(far, columns_out(w_units, s))
+    x_pieces = [(inputs[0], *near_0, far[0]), (inputs[1], *near_1, far[1])]
+    arranged_0, w_pre = together(arrange(x_pieces[0], s), w_pre)
+    w_units = over_batch(w_units.reshape(shards * rows, 2 * units))
+
+    w_out_own = w_pre[..., split:].transpose(0, 2, 1, 3).reshape(own, width)
+    w_turned = turn_in(w_pre, 3 * own)
+    taps = w_pre[..., 3 * own : split].reshape(groups, shards, 3, count).transpose(2, 1, 0, 3)
+    taps = lax.dynamic_index_in_dim(taps.reshape(3, 3, shards, own), s, axis=2, keepdims=False)
+    taps = taps.transpose(1, 2, 0)
+
+    def first_half(arranged):
+        x_i, *n_i = arranged
         return x_i, n_i, project(w_turned, n_i).reshape(3, own, length)
 
-    first_0 = first_half(0, ())
-    (x_0, n_0, p_0), base = together(first_0, base)
-
-    w_out_own = base[:, spectra:].reshape(groups, shards // 2, rows, 2 * own).transpose(0, 2, 1, 3).reshape(own, width)
-    w_out_there, (gated_0, *mixed_0) = together(from_others(w_out_own), mix(p_0, taps, base, tables))
-
-    first_1 = first_half(1, (gated_0,))
-    there_0, first_1, (gated_1, *mixed_1) = together(
-        from_others(gated_0), first_1, mix(first_1[2], taps, base, tables, after=(gated_0,))
-    )
-    x_1, n_1, p_1 = first_1
+    first_0 = first_half(arranged_0)
+    first_1 = first_half(arrange(x_pieces[1], s, after=(first_0[2],)))
+    w_out_there, (x_0, n_0, p_0), (x_1, n_1, p_1), w_turned, taps = together(
+        from_others(w_out_own), first_0, first_1, w_turned, taps
+    )
+    gated_0, *mixed_0 = mix(p_0, taps, base, tables)
+    there_0, (gated_1, *mixed_1) = together(from_others(gated_0), mix(p_1, taps, base, tables, after=(gated_0,)))
     n_one, projected = (n_0, n_1), (p_0, p_1)
     gating, long_conv, vals, spec = zip(mixed_0, mixed_1)
     w_out_pieces = (w_out_own, *w_out_there)
@@ -881,52 +955,44 @@
     e_there, e_1, w_in_part = together(e_there, e_1[:4], w_in_part)
     w_in_sum = sum_over_batch(w_in_part)
 
-    e_one = ([e_0[0], *e_there, swap(e_0[3], "seq", 3)], to_others(e_1))
+    e_0 = [e_0[0], *e_there, swap(e_0[3], "seq", 3)]
+    input_grad = finish(0, e_0, inputs, d_residual, places, s, ())
     outputs = jnp.stack(
         [
             added(out) + lax.dynamic_slice_in_dim(residual[i], s * tokens, tokens, axis=0)
             for i, out in enumerate((out_0, out_1))
         ]
     )
-    e_one, w_in_sum, kernel_sum, outputs = together(e_one, w_in_sum, kernel_sum, outputs)
-
     kernel_sum = kernel_sum.reshape(FOLDED, -1, 2, own).transpose(2, 1, 0, 3)
     mirrored = lax.ppermute(kernel_sum[:, ::-1, 3:0:-1], "batch", mirror)
+    e_1, w_in_sum, mirrored, outputs, input_grad = together(to_others(e_1), w_in_sum, mirrored, outputs, input_grad)
+
     w_back = jnp.concatenate([w_in_sum[:, :-own], unit_sums[:, : 2 * units]], axis=1)
     w_back = columns_there(w_back.reshape(shards, rows, -1), s)
-
-    e_own = jnp.stack([added(e) for e in e_one])
-    n_own, inverse_own = normed(inputs)
-    here = s * tokens + jnp.arange(tokens, dtype=jnp.int32)
-    select_own = (places == here).astype(F32)
-    direct = contract("bmt,bmd->btd", select_own, d_residual.reshape(seqs, slots + pad, width))
-    input_grad = norm_pull(n_own, inverse_own, e_own) + direct
     mirrored = jnp.stack([mirrored[0], -mirrored[1]])
     kernel_grad = jnp.concatenate([kernel_sum, mirrored], axis=2).reshape(kernel.shape)
+    input_grad = finish(1, e_1, inputs, d_residual, places, s, (input_grad,))
     w_out_sum = w_in_sum[:, -own:].reshape(shards, rows, own).transpose(1, 0, 2).reshape(w_out.shape)
-    w_back = by_xor(w_back, s)
-    w_in_sum = w_back
-    taps_sum = sum(p[:, 3 * own : split] for p in w_in_sum).reshape(conv_weight.shape)
-    w_in_sum = jnp.stack([p[:, : 3 * own].reshape(rows, 3, own) for p in w_in_sum], axis=2)
-    w_in_sum = w_in_sum.reshape(w_in.shape)
     w_down_sum = unit_sums[:, 2 * units :].reshape(w_down.shape)
-    w_units_sum = [p[:, -2 * units :] for p in w_back]
-    w_gate_sum = jnp.concatenate([p[:, :units] for p in w_units_sum], axis=1)
-    w_up_sum = jnp.concatenate([p[:, units:] for p in w_units_sum], axis=1)
-    gain_one_sum = jnp.sum(w_in * w_in_sum, axis=1)
-    gain_two_sum = jnp.sum(w_gate * w_gate_sum, axis=1) + jnp.sum(w_up * w_up_sum, axis=1)
+    w_back, kernel_grad, input_grad, w_out_sum, w_down_sum = together(
+        w_back, kernel_grad, input_grad, w_out_sum, w_down_sum
+    )
+    w_in_sum, w_gate_sum, w_up_sum, gain_one_sum, gain_two_sum, taps_sum = weight_grads(
+        w_back, s, gain_one, gain_two, w_in, w_gate, w_up, own, units
+    )
+    taps_sum = taps_sum[:, free : free + extra].reshape(conv_weight.shape)
 
     return (
         outputs,
         input_grad,
-        gain_one_sum,
-        gain_one[:, None] * w_in_sum,
+        gain_one_sum[:, 0],
+        w_in_sum,
         taps_sum,
         kernel_grad,
         w_out_sum,
-        gain_two_sum,
-        gain_two[:, None] * w_gate_sum,
-        gain_two[:, None] * w_up_sum,
+        gain_two_sum[:, 0],
+        w_gate_sum,
+        w_up_sum,
         w_down_sum,
     )
 

time: 452 us -> 437 us (0.967)
  waiting for transfers between devices: 114 us -> 101 us
  Pallas kernels: 211 us -> 222 us
  other arithmetic: 22.4 us -> 13.7 us
    ppermute x40, waiting for transfers between devices: 102 us -> 89.8 us  [swap(): lax.ppermute(value, axis, [(i, i ^ distance) for i in range(devices)])]
    pallas_call x0 -> x2, Pallas kernels: none -> 7.73 us  [finish(): pl.pallas_call(kernel, name='finish', out_shape=shaped(seqs, tokens, widt...]
    pallas_call x21 -> x22, Pallas kernels: 211 us -> 214 us  [call(): pl.pallas_call(run, name=name, out_shape=tuple(outs), grid_spec=pltpu.Pre...]
  transfers between devices with their start and end apart: 49 -> 49, of which waited for: 17 -> 20; matrix products, arithmetic and copies ran while one was open for 8% -> 7% of each run, Pallas kernels for 48% -> 51%
where the time goes in v3:
time: 437 us; the launch traced here: 431 us
  Pallas kernels  222 us (51%)
  waiting for transfers between devices  101 us (23%)
  starting transfers between devices  51.8 us (12%)
  local copies, waits for them, and re-layouts  27.6 us (6%)
  between operations  15.3 us (4%)
  other arithmetic  13.7 us (3%)
    pallas_call x22, Pallas kernels, call(): pl.pallas_call(run, name=name, out_shape=tuple(outs), grid_spec=pltpu.Pre...  214 us
    ppermute x40, waiting for transfers between devices, swap(): lax.ppermute(value, axis, [(i, i ^ distance) for i in range(devices)])  89.8 us
    ppermute x40, starting transfers between devices, swap(): lax.ppermute(value, axis, [(i, i ^ distance) for i in range(devices)])  49.1 us
  transfers between devices with their start and end apart: 49, of which 20 were waited for; matrix products, arithmetic and copies ran while one was open for 7% of the time, Pallas kernels for 51%

profile of v3, /device:TPU:0, one launch (start us, length us, event | category | flops | bytes accessed | tf_op | source)
XLA Modules:
  0.0 431.3 jit_solution(9186600251189792192)
XLA Ops:
  8.0 1.5 slice_bitcast_fusion.1
  9.5 3.0 collective-permute-start.3
  12.5 1.5 collective-permute-start.4
  15.5 2.0 collective-permute-start.1
  17.5 1.5 collective-permute-start.2
  21.3 12.0 %collective-permute-done = f32[24,585]{1,0:T(8,128)S(1)} collective-permute-done((f32[24,585]{1,0:T(8,128)}, f32[24,585]{1,0:T(8,128)S(1)}, u32[]{:S(2)}, u32[]{:S(2)}) %collective-permute-start) | collective-permute-done | bytes 56192 | tf_op jit(solution)/shard_map/ppermute | solution.py:31
  35.0 1.5 collective-permute-start.6
  38.7 1.5 collective-permute-start.7
  41.2 8.1 %collective-permute-done.7.refs_1_ = f32[2,32,3,192]{3,2,1,0:T(4,128)} collective-permute-done((f32[2,32,3,192]{3,2,1,0:T(4,128)}, f32[2,32,3,192]{3,2,1,0:T(4,128)}, u32[]{:S(2)}, u32[]{:S(2)}) %collective-permute-start.7) | collective-permute-done | bytes 147488 | tf_op jit(solution)/shard_map/ppermute | solution.py:860
  49.3 2.6 collective-permute-done.5.refs_2_
  53.1 2.0 fold_base.1
  57.3 2.5 collective-permute-start.10
  60.8 1.5 collective-permute-start.8
  62.3 1.4 collective-permute-start.9
  65.0 2.4 collective-permute-done.11
  69.2 12.4 %collective-permute-done.8.refs_4_ = f32[256,768]{1,0:T(8,128)S(1)} collective-permute-done((f32[256,768]{1,0:T(8,128)S(1)}, f32[256,768]{1,0:T(8,128)S(1)}, u32[]{:S(2)}, u32[]{:S(2)}) %collective-permute-start.8) | collective-permute-done | bytes 786464 | tf_op jit(solution)/shard_map/ppermute | solution.py:31
  82.5 5.3 %arrange.2 = (f32[1024,768]{1,0:T(8,128)}, bf16[1024,768]{1,0:T(8,128)(2,1)}, bf16[1024,768]{1,0:T(8,128)(2,1)}) custom-call(s32[1]{0:T(128)} %bitcast.refs_0_.s_ref, f32[256,768]{1,0:T(8,128)} %copy-done.4, f32[256,768]{1,0:T(8,128)} %copy-done.30, f32[256,768]{1,0:T(8,128)} %collective-permute-done.4.refs_3_, f32[256,768]{1,0:T(8,128)} %copy-done.34), custom_call_target="tpu_custom_call" | custom-call | bytes 471859 | tf_op jit(solution)/shard_map/arrange/pallas_call | solution.py:122
  87.8 1.6 all-gather.7.cloned.1.call-done
  89.4 1.5 slice_bitcast_fusion
  91.7 1.5 collective-permute-start.13
  93.3 1.5 collective-permute-start.14
  95.3 3.6 turn_in.1
  101.3 6.1 %project.2 = f32[576,1024]{1,0:T(8,128)} custom-call(bf16[576,768]{1,0:T(8,128)(2,1)} %get-tuple-element.310.refs_0_.refs_4_, bf16[576,768]{1,0:T(8,128)(2,1)} %get-tuple-element.311.refs_1_.refs_5_, bf16[1024,768]{1,0:T(8,128)(2,1)} %get-tuple-element.308.refs_2_, bf16[1024,768]{1,0:T(8,128)(2,1)} %get-tuple-element.309.refs_3_), custom_call_target="tpu_custom_call" | custom-call | flops 135895456 | bytes 363724 | tf_op jit(solution)/shard_map/project/pallas_call | solution.py:122
  107.4 5.4 %arrange.3 = (f32[1024,768]{1,0:T(8,128)}, bf16[1024,768]{1,0:T(8,128)(2,1)}, bf16[1024,768]{1,0:T(8,128)(2,1)}) custom-call(s32[1]{0:T(128)} %bitcast.refs_0_.s_ref, f32[256,768]{1,0:T(8,128)} %copy-done.3, f32[256,768]{1,0:T(8,128)} %copy-done.32, f32[256,768]{1,0:T(8,128)} %collective-permute-done.6.refs_3_, f32[256,768]{1,0:T(8,128)} %copy-done.33, ...), custom_call_target="tpu_custom_call" | custom-call | bytes 471859 | tf_op jit(solution)/shard_map/arrange/pallas_call | solution.py:122
  112.8 6.1 %project.3 = f32[576,1024]{1,0:T(8,128)} custom-call(bf16[576,768]{1,0:T(8,128)(2,1)} %get-tuple-element.310.refs_0_.refs_4_, bf16[576,768]{1,0:T(8,128)(2,1)} %get-tuple-element.311.refs_1_.refs_5_, bf16[1024,768]{1,0:T(8,128)(2,1)} %get-tuple-element.325.refs_2_, bf16[1024,768]{1,0:T(8,128)(2,1)} %get-tuple-element.326.refs_3_), custom_call_target="tpu_custom_call" | custom-call | flops 135895456 | bytes 363724 | tf_op jit(solution)/shard_map/project/pallas_call | solution.py:122
  119.0 2.1 collective-permute-done.14.refs_7_
  121.1 14.3 %mix.2 = (f32[192,1024]{1,0:T(8,128)}, f32[192,1024]{1,0:T(8,128)}, f32[192,1024]{1,0:T(8,128)}, f32[5,192,512]{2,1,0:T(8,128)}, f32[5,192,512]{2,1,0:T(8,128)}) custom-call(f32[3,192,1024]{2,1,0:T(8,128)} %bitcast.131, f32[3,192,3]{2,1,0:T(8,128)} %bitcast.142, f32[8,160,384]{2,1,0:T(8,128)} %bitcast.140, ...), custom_call_target="tpu_custom_call" | custom-call | flops 724775744 | bytes 865075 | tf_op jit(solution)/shard_map/mix/pallas_call | solution.py:122
  137.5 1.5 collective-permute-start.18
  139.0 13.7 %mix.3 = (f32[192,1024]{1,0:T(8,128)}, f32[192,1024]{1,0:T(8,128)}, f32[192,1024]{1,0:T(8,128)}, f32[5,192,512]{2,1,0:T(8,128)}, f32[5,192,512]{2,1,0:T(8,128)}) custom-call(f32[3,192,1024]{2,1,0:T(8,128)} %bitcast.133, f32[3,192,3]{2,1,0:T(8,128)} %bitcast.143, f32[8,160,384]{2,1,0:T(8,128)} %bitcast.141, ...), custom_call_target="tpu_custom_call" | custom-call | flops 724775744 | bytes 865075 | tf_op jit(solution)/shard_map/mix/pallas_call | solution.py:122
  152.7 3.5 collective-permute-done.16.refs_2_
  156.2 16.1 %collective-permute-done.17.refs_3_ = f32[192,1024]{1,0:T(8,128)S(1)} collective-permute-done((f32[192,1024]{1,0:T(8,128)}, f32[192,1024]{1,0:T(8,128)S(1)}, u32[]{:S(2)}, u32[]{:S(2)}) %collective-permute-start.17) | collective-permute-done | bytes 786464 | tf_op jit(solution)/shard_map/ppermute | solution.py:31
  172.9 1.5 collective-permute-start.20
  174.4 1.5 collective-permute-start.21
  175.9 8.6 %add_mixer.2.refs_2_.refs_1_.refs_0_ = f32[1024,768]{1,0:T(8,128)} custom-call(f32[1024,768]{1,0:T(8,128)} %get-tuple-element.232.refs_0_, f32[192,1024]{1,0:T(8,128)} %get-tuple-element.224.refs_5_.refs_1_, f32[192,1024]{1,0:T(8,128)} %copy-done.27, f32[192,1024]{1,0:T(8,128)} %copy-done.28, f32[192,1024]{1,0:T(8,128)} %copy-done.29, f32[192,768]{1,0:T(8,128)} %copy-done, ...), custom_call_target="tpu_custom_call" | custom-call | flops 181193936 | bytes 589824 | tf_op jit(solution)/shard_map/add_mixer/pallas_call | solution.py:122
  184.5 6.3 %split_units.1 = (bf16[768,1536]{1,0:T(8,128)(2,1)}, bf16[768,1536]{1,0:T(8,128)(2,1)}, bf16[768,768]{1,0:T(8,128)(2,1)}, bf16[768,768]{1,0:T(8,128)(2,1)}) custom-call(f32[8,4,24,1536]{3,2,1,0:T(8,128)} %bitcast.149, f32[768,768]{1,0:T(8,128)} %all-gather.5.cloned.1.call-done.refs_1_, f32[1024,768]{1,0:T(8,128)} %add_mixer.2.refs_2_.refs_1_.refs_0_), custom_call_target="tpu_custom_call" | custom-call | bytes 707788 | tf_op jit(solution)/shard_map/split_units/pallas_call | solution.py:122
  190.9 19.2 %feed_forward.2 = (f32[256,768]{1,0:T(8,128)}, f32[256,768]{1,0:T(8,128)}, f32[256,768]{1,0:T(8,128)}, f32[256,768]{1,0:T(8,128)}) custom-call(s32[1]{0:T(128)} %bitcast.refs_0_.s_ref, f32[1024,768]{1,0:T(8,128)} %add_mixer.2.refs_2_.refs_1_.refs_0_, bf16[768,1536]{1,0:T(8,128)(2,1)} %get-tuple-element.256.refs_2_.refs_4_, ...), custom_call_target="tpu_custom_call" | custom-call | flops 543581824 | bytes 668467 | tf_op jit(solution)/shard_map/feed_forward/pallas_call | solution.py:122
  211.6 1.5 collective-permute-start.23
  213.9 8.8 %add_mixer.3.refs_1_ = f32[1024,768]{1,0:T(8,128)} custom-call(f32[1024,768]{1,0:T(8,128)} %get-tuple-element.250.refs_0_, f32[192,1024]{1,0:T(8,128)} %get-tuple-element.231.refs_9_.refs_1_, f32[192,1024]{1,0:T(8,128)} %copy-done.24, f32[192,1024]{1,0:T(8,128)} %copy-done.25, f32[192,1024]{1,0:T(8,128)} %copy-done.26, f32[192,768]{1,0:T(8,128)} %copy-done, ...), custom_call_target="tpu_custom_call" | custom-call | flops 181193936 | bytes 589824 | tf_op jit(solution)/shard_map/add_mixer/pallas_call | solution.py:122
  222.7 13.1 %live_back.1 = (f32[256,768]{1,0:T(8,128)}, f32[256,768]{1,0:T(8,128)}, f32[256,768]{1,0:T(8,128)}, f32[256,1536]{1,0:T(8,128)}, f32[160,768]{1,0:T(8,128)}) custom-call(f32[1024,768]{1,0:T(8,128)} %add_mixer.2.refs_2_.refs_1_.refs_0_, f32[1024,768]{1,0:T(8,128)} %add_mixer.3.refs_1_, s32[2,128,1]{2,1,0:T(8,128)} %copy.64.refs_2_.refs_11_.refs_0_.at_ref, ...), custom_call_target="tpu_custom_call" | custom-call | flops 226492416 | bytes 786432 | tf_op jit(solution)/shard_map/live_back/pallas_call | solution.py:122
  235.8 1.4 fusion.17
  237.7 1.6 collective-permute-start.25
  239.3 7.0 %unit_grads.1.refs_6_ = f32[8,96,2304]{2,1,0:T(8,128)} custom-call(f32[256,768]{1,0:T(8,128)} %get-tuple-element.269.refs_0_, f32[256,1536]{1,0:T(8,128)} %get-tuple-element.270.refs_1_, f32[256,768]{1,0:T(8,128)} %get-tuple-element.271.refs_2_, f32[256,768]{1,0:T(8,128)} %bitcast.136), custom_call_target="tpu_custom_call" | custom-call | flops 135895456 | bytes 353894 | tf_op jit(solution)/shard_map/unit_grads/pallas_call | solution.py:122
  247.9 1.7 collective-permute-start.27
  249.6 1.4 collective-permute-start.28
  251.0 19.5 %feed_forward.3 = (f32[256,768]{1,0:T(8,128)}, f32[256,768]{1,0:T(8,128)}, f32[256,768]{1,0:T(8,128)}, f32[256,768]{1,0:T(8,128)}) custom-call(s32[1]{0:T(128)} %bitcast.refs_0_.s_ref, f32[1024,768]{1,0:T(8,128)} %add_mixer.3.refs_1_, bf16[768,1536]{1,0:T(8,128)(2,1)} %get-tuple-element.256.refs_2_.refs_4_, ...), custom_call_target="tpu_custom_call" | custom-call | flops 543581824 | bytes 668467 | tf_op jit(solution)/shard_map/feed_forward/pallas_call | solution.py:122
  271.8 1.5 collective-permute-start.30
  274.1 6.2 %live_mix.1 = (f32[256,768]{1,0:T(8,128)}, f32[192,768]{1,0:T(8,128)}, f32[2,192,128]{2,1,0:T(8,128)}, f32[2,192,128]{2,1,0:T(8,128)}) custom-call(f32[256,768]{1,0:T(8,128)} %get-tuple-element.267.refs_0_, f32[256,768]{1,0:T(8,128)} %bitcast.137, f32[80,768]{1,0:T(8,128)} %copy-done.13, f32[80,768]{1,0:T(8,128)} %copy-done.12, f32[80,768]{1,0:T(8,128)} %copy-done.36, ...), custom_call_target="tpu_custom_call" | custom-call | flops 37748736 | bytes 314572 | tf_op jit(solution)/shard_map/live_mix/pallas_call | solution.py:122
  280.3 15.1 %mix_back.2 = (f32[3,192,1024]{2,1,0:T(8,128)}, f32[8,5,32,384]{3,2,1,0:T(8,128)}, f32[3,192,128]{2,1,0:T(8,128)}) custom-call(s32[2,128,1]{2,1,0:T(8,128)} %copy.64.refs_2_.refs_11_.refs_0_.at_ref, f32[2,192,128]{2,1,0:T(8,128)} %get-tuple-element.286.refs_1_, f32[2,192,128]{2,1,0:T(8,128)} %get-tuple-element.287.refs_2_, f32[3,192,1024]{2,1,0:T(8,128)} %bitcast.132, ...), custom_call_target="tpu_custom_call" | custom-call | flops 724775744 | bytes 865075 | tf_op jit(solution)/shard_map/mix_back/pallas_call | solution.py:122
  295.5 15.1 %mix_back.3 = (f32[3,192,1024]{2,1,0:T(8,128)}, f32[8,5,32,384]{3,2,1,0:T(8,128)}, f32[3,192,128]{2,1,0:T(8,128)}) custom-call(s32[2,128,1]{2,1,0:T(8,128)} %copy.64.refs_2_.refs_11_.refs_0_.at_ref, f32[2,192,128]{2,1,0:T(8,128)} %get-tuple-element.286.refs_1_, f32[2,192,128]{2,1,0:T(8,128)} %get-tuple-element.287.refs_2_, f32[3,192,1024]{2,1,0:T(8,128)} %bitcast.134, ...), custom_call_target="tpu_custom_call" | custom-call | flops 724775744 | bytes 865075 | tf_op jit(solution)/shard_map/mix_back/pallas_call | solution.py:122
  311.6 15.8 %project_back.2 = (f32[256,768]{1,0:T(8,128)}, f32[256,768]{1,0:T(8,128)}, f32[256,768]{1,0:T(8,128)}, f32[256,768]{1,0:T(8,128)}, f32[576,768]{1,0:T(8,128)}) custom-call(s32[1]{0:T(128)} %bitcast.refs_0_.s_ref, f32[576,1024]{1,0:T(8,128)} %bitcast.139, bf16[1024,768]{1,0:T(8,128)(2,1)} %get-tuple-element.308.refs_2_, ...), custom_call_target="tpu_custom_call" | custom-call | flops 271790912 | bytes 697958 | tf_op jit(solution)/shard_map/project_back/pallas_call | solution.py:122
  328.8 1.5 collective-permute-start.33
  331.8 15.7 %project_back.3 = (f32[256,768]{1,0:T(8,128)}, f32[256,768]{1,0:T(8,128)}, f32[256,768]{1,0:T(8,128)}, f32[256,768]{1,0:T(8,128)}, f32[576,768]{1,0:T(8,128)}) custom-call(s32[1]{0:T(128)} %bitcast.refs_0_.s_ref, f32[576,1024]{1,0:T(8,128)} %bitcast.153, bf16[1024,768]{1,0:T(8,128)(2,1)} %get-tuple-element.325.refs_2_, ...), custom_call_target="tpu_custom_call" | custom-call | flops 271790912 | bytes 697958 | tf_op jit(solution)/shard_map/project_back/pallas_call | solution.py:122
  347.5 4.0 turn_back.1
  355.0 1.4 collective-permute-start.35
  357.2 1.9 add_bitcast_fusion.1
  360.6 1.6 add_bitcast_fusion
  365.4 9.1 %collective-permute-done.38.e3 = f32[256,768]{1,0:T(8,128)} collective-permute-done((f32[256,768]{1,0:T(8,128)}, f32[256,768]{1,0:T(8,128)}, u32[]{:S(2)}, u32[]{:S(2)}) %collective-permute-start.38) | collective-permute-done | bytes 786464 | tf_op jit(solution)/shard_map/ppermute | solution.py:31
  374.6 3.9 finish.2.refs_0_
  378.5 12.1 %collective-permute-done.34.e1 = f32[256,768]{1,0:T(8,128)} collective-permute-done((f32[256,768]{1,0:T(8,128)}, f32[256,768]{1,0:T(8,128)}, u32[]{:S(2)}, u32[]{:S(2)}) %collective-permute-start.34) | collective-permute-done | bytes 786464 | tf_op jit(solution)/shard_map/ppermute | solution.py:31
  391.3 9.6 %collective-permute-done.36.e3 = f32[256,768]{1,0:T(8,128)} collective-permute-done((f32[256,768]{1,0:T(8,128)}, f32[256,768]{1,0:T(8,128)}, u32[]{:S(2)}, u32[]{:S(2)}) %collective-permute-start.36) | collective-permute-done | bytes 786464 | tf_op jit(solution)/shard_map/ppermute | solution.py:31
  404.1 1.7 collective-permute-start.40
  408.4 3.8 finish.3
  412.3 2.8 collective-permute-done.40.refs_3_
  415.8 3.4 weight_grads.1
  (236 shorter events, 55.3 us)
Async XLA Ops:
  7.2 45.8 %all-gather.5.cloned.1.call-start = ((), (), s32[]{:S(2)}) async-start(), calls=%async_computation.3 | async-start | bytes 2654208 | tf_op jit(solution)/shard_map/all_gather | solution.py:78
  7.9 81.4 %all-gather.7.cloned.1.call-start = ((), (), s32[]{:S(2)}) async-start(), calls=%async_computation.4 | async-start | bytes 3096576 | tf_op jit(solution)/shard_map/all_gather | solution.py:78
  9.5 25.5 %copy-start.3 = (f32[256,768]{1,0:T(8,128)}, f32[256,768]{1,0:T(8,128)S(1)}, u32[]{:S(2)}) copy-start(f32[256,768]{1,0:T(8,128)S(1)} %get-tuple-element.195.refs_1_) | copy-start | bytes 2359300
  9.5 24.8 %collective-permute-start.3 = (f32[256,768]{1,0:T(8,128)S(1)}, f32[256,768]{1,0:T(8,128)S(1)}, u32[]{:S(2)}, u32[]{:S(2)}) collective-permute-start(f32[256,768]{1,0:T(8,128)S(1)} %get-tuple-element.400.refs_1_), channel_id=1, source_target_pairs={{0,8},{8,0},{16,24},{24,16},{1,9},{9,1},{17,25},{25,17},{2,10},{10... | collective-permute-start | bytes 2359304 | tf_op jit(solution)/shard_map/ppermute | solution.py:31
  12.5 21.8 %collective-permute-start.4 = (f32[256,768]{1,0:T(8,128)S(1)}, f32[256,768]{1,0:T(8,128)}, u32[]{:S(2)}, u32[]{:S(2)}) collective-permute-start(f32[256,768]{1,0:T(8,128)S(1)} %get-tuple-element.400.refs_1_), channel_id=1, source_target_pairs={{0,16},{8,24},{16,0},{24,8},{1,17},{9,25},{17,1},{25,9},{2,18},{10... | collective-permute-start | bytes 2359304 | tf_op jit(solution)/shard_map/ppermute | solution.py:31
  15.5 17.8 %collective-permute-start = (f32[24,585]{1,0:T(8,128)}, f32[24,585]{1,0:T(8,128)S(1)}, u32[]{:S(2)}, u32[]{:S(2)}) collective-permute-start(f32[24,585]{1,0:T(8,128)} %get-tuple-element.420), channel_id=1, source_target_pairs={{0,24},{8,16},{16,8},{24,0},{1,25},{9,17},{17,9},{25,1},{2,26},{10... | collective-permute-start | bytes 168488 | tf_op jit(solution)/shard_map/ppermute | solution.py:31
  15.5 18.6 %collective-permute-start.1 = (f32[24,585]{1,0:T(8,128)}, f32[24,585]{1,0:T(8,128)S(1)}, u32[]{:S(2)}, u32[]{:S(2)}) collective-permute-start(f32[24,585]{1,0:T(8,128)} %get-tuple-element.421), channel_id=1, source_target_pairs={{0,16},{8,24},{16,0},{24,8},{1,17},{9,25},{17,1},{25,9},{2,18},{10... | collective-permute-start | bytes 168488 | tf_op jit(solution)/shard_map/ppermute | solution.py:31
  17.5 16.7 %collective-permute-start.2 = (f32[24,585]{1,0:T(8,128)S(1)}, f32[24,585]{1,0:T(8,128)S(1)}, u32[]{:S(2)}, u32[]{:S(2)}) collective-permute-start(f32[24,585]{1,0:T(8,128)S(1)} %get-tuple-element.422), channel_id=1, source_target_pairs={{0,8},{8,0},{16,24},{24,16},{1,9},{9,1},{17,25},{25,17},{2,10},{10... | collective-permute-start | bytes 168488 | tf_op jit(solution)/shard_map/ppermute | solution.py:31
  20.3 19.9 %copy-start.41 = (f32[24,768]{1,0:T(8,128)S(1)}, f32[24,768]{1,0:T(8,128)}, u32[]{:S(2)}) copy-start(f32[24,768]{1,0:T(8,128)} %param.20) | copy-start | bytes 221188
  34.3 17.6 %collective-permute-start.5 = (f32[256,768]{1,0:T(8,128)S(1)}, f32[256,768]{1,0:T(8,128)S(1)}, u32[]{:S(2)}, u32[]{:S(2)}) collective-permute-start(f32[256,768]{1,0:T(8,128)S(1)} %get-tuple-element.195.refs_1_), channel_id=1, source_target_pairs={{0,8},{8,0},{16,24},{24,16},{1,9},{9,1},{17,25},{25,17},{2,10},{10... | collective-permute-start | bytes 2359304 | tf_op jit(solution)/shard_map/ppermute | solution.py:31
  35.0 18.0 %collective-permute-start.6 = (f32[256,768]{1,0:T(8,128)S(1)}, f32[256,768]{1,0:T(8,128)}, u32[]{:S(2)}, u32[]{:S(2)}) collective-permute-start(f32[256,768]{1,0:T(8,128)S(1)} %get-tuple-element.195.refs_1_), channel_id=1, source_target_pairs={{0,16},{8,24},{16,0},{24,8},{1,17},{9,25},{17,1},{25,9},{2,18},{10... | collective-permute-start | bytes 2359304 | tf_op jit(solution)/shard_map/ppermute | solution.py:31
  37.6 15.4 %copy-start.1 = (f32[2,256,192]{2,1,0:T(8,128)}, f32[2,256,192]{2,1,0:T(8,128)S(1)}, u32[]{:S(2)}) copy-start(f32[2,256,192]{2,1,0:T(8,128)S(1)} %copy.55) | copy-start | bytes 1179652
  37.6 17.5 %copy-start.10 = (f32[24,3072]{1,0:T(8,128)S(1)}, f32[24,3072]{1,0:T(8,128)}, u32[]{:S(2)}) copy-start(f32[24,3072]{1,0:T(8,128)} %refs_8_.3) | copy-start | bytes 884740
  37.7 17.5 %copy-start.11 = (f32[24,3072]{1,0:T(8,128)S(1)}, f32[24,3072]{1,0:T(8,128)}, u32[]{:S(2)}) copy-start(f32[24,3072]{1,0:T(8,128)} %refs_9_.1) | copy-start | bytes 884740
  37.7 17.5 %copy-start.42 = (f32[24]{0:T(128)S(1)}, f32[24]{0:T(128)}, u32[]{:S(2)}) copy-start(f32[24]{0:T(128)} %param.21) | copy-start | bytes 292
  38.7 10.6 %collective-permute-start.7 = (f32[2,32,3,192]{3,2,1,0:T(4,128)}, f32[2,32,3,192]{3,2,1,0:T(4,128)}, u32[]{:S(2)}, u32[]{:S(2)}) collective-permute-start(f32[2,32,3,192]{3,2,1,0:T(4,128)} %rev.6), channel_id=1, source_target_pairs={{0,7},{1,6},{2,5},{3,4},{4,3},{5,2},{6,1},{7,0},{8,15},{9,14},{10,... | collective-permute-start | bytes 442376 | tf_op jit(solution)/shard_map/ppermute | solution.py:860
  53.0 68.1 %all-gather.9.cloned.1.call-start = ((), (), s32[]{:S(2)}) async-start(), calls=%async_computation.5 | async-start | bytes 2211840 | tf_op jit(solution)/shard_map/all_gather | solution.py:78
  55.1 129.4 %all-gather.11.cloned.1.call-start = ((), (), s32[]{:S(2)}) async-start(), calls=%async_computation.6 | async-start | bytes 5308416 | tf_op jit(solution)/shard_map/all_gather | solution.py:78
  57.3 7.7 %collective-permute-start.10 = (f32[24,1536]{1,0:T(8,128)S(1)}, f32[24,1536]{1,0:T(8,128)S(1)}, u32[]{:S(2)}, u32[]{:S(2)}) collective-permute-start(f32[24,1536]{1,0:T(8,128)S(1)} %get-tuple-element.409), channel_id=1, source_target_pairs={{0,24},{8,16},{16,8},{24,0},{1,25},{9,17},{17,9},{25,1},{2,26},{10... | collective-permute-start | bytes 442376 | tf_op jit(solution)/shard_map/ppermute | solution.py:31
  59.7 7.6 %collective-permute-start.11 = (f32[24,1536]{1,0:T(8,128)S(1)}, f32[24,1536]{1,0:T(8,128)S(1)}, u32[]{:S(2)}, u32[]{:S(2)}) collective-permute-start(f32[24,1536]{1,0:T(8,128)S(1)} %get-tuple-element.411), channel_id=1, source_target_pairs={{0,16},{8,24},{16,0},{24,8},{1,17},{9,25},{17,1},{25,9},{2,18},{10... | collective-permute-start | bytes 442376 | tf_op jit(solution)/shard_map/ppermute | solution.py:31
  60.0 8.2 %collective-permute-start.12 = (f32[24,1536]{1,0:T(8,128)S(1)}, f32[24,1536]{1,0:T(8,128)S(1)}, u32[]{:S(2)}, u32[]{:S(2)}) collective-permute-start(f32[24,1536]{1,0:T(8,128)S(1)} %get-tuple-element.410), channel_id=1, source_target_pairs={{0,8},{8,0},{16,24},{24,16},{1,9},{9,1},{17,25},{25,17},{2,10},{10... | collective-permute-start | bytes 442376 | tf_op jit(solution)/shard_map/ppermute | solution.py:31
  60.8 20.7 %collective-permute-start.8 = (f32[256,768]{1,0:T(8,128)S(1)}, f32[256,768]{1,0:T(8,128)S(1)}, u32[]{:S(2)}, u32[]{:S(2)}) collective-permute-start(f32[256,768]{1,0:T(8,128)S(1)} %copy-done.31), channel_id=1, source_target_pairs={{0,16},{8,24},{16,0},{24,8},{1,17},{9,25},{17,1},{25,9},{2,18},{10... | collective-permute-start | bytes 2359304 | tf_op jit(solution)/shard_map/ppermute | solution.py:31
  62.3 19.5 %collective-permute-start.9 = (f32[256,768]{1,0:T(8,128)}, f32[256,768]{1,0:T(8,128)S(1)}, u32[]{:S(2)}, u32[]{:S(2)}) collective-permute-start(f32[256,768]{1,0:T(8,128)} %collective-permute-done.6.refs_3_), channel_id=1, source_target_pairs={{0,8},{8,0},{16,24},{24,16},{1,9},{9,1},{17,25},{25,17},{2,10},{10... | collective-permute-start | bytes 2359304 | tf_op jit(solution)/shard_map/ppermute | solution.py:31
  81.8 245.7 %reduce-scatter.4.cloned.1.call-start = ((), (), s32[]{:S(2)}) async-start(), calls=%async_computation.7 | async-start | bytes 7962624 | tf_op jit(solution)/shard_map/reduce_scatter | solution.py:84
  91.7 27.2 %collective-permute-start.13 = (f32[192,768]{1,0:T(8,128)S(1)}, f32[192,768]{1,0:T(8,128)S(1)}, u32[]{:S(2)}, u32[]{:S(2)}) collective-permute-start(f32[192,768]{1,0:T(8,128)S(1)} %reshape.152.refs_5_.refs_6_), channel_id=1, source_target_pairs={{0,8},{8,0},{16,24},{24,16},{1,9},{9,1},{17,25},{25,17},{2,10},{10... | collective-permute-start | bytes 1769480 | tf_op jit(solution)/shard_map/ppermute | solution.py:31
  93.3 27.8 %collective-permute-start.14 = (f32[192,768]{1,0:T(8,128)S(1)}, f32[192,768]{1,0:T(8,128)S(1)}, u32[]{:S(2)}, u32[]{:S(2)}) collective-permute-start(f32[192,768]{1,0:T(8,128)S(1)} %reshape.152.refs_5_.refs_6_), channel_id=1, source_target_pairs={{0,16},{8,24},{16,0},{24,8},{1,17},{9,25},{17,1},{25,9},{2,18},{10... | collective-permute-start | bytes 1769480 | tf_op jit(solution)/shard_map/ppermute | solution.py:31
  94.8 26.4 %collective-permute-start.15 = (f32[192,768]{1,0:T(8,128)S(1)}, f32[192,768]{1,0:T(8,128)S(1)}, u32[]{:S(2)}, u32[]{:S(2)}) collective-permute-start(f32[192,768]{1,0:T(8,128)S(1)} %reshape.152.refs_5_.refs_6_), channel_id=1, source_target_pairs={{0,24},{8,16},{16,8},{24,0},{1,25},{9,17},{17,9},{25,1},{2,26},{10... | collective-permute-start | bytes 1769480 | tf_op jit(solution)/shard_map/ppermute | solution.py:31
  119.0 16.5 %copy-start.5 = (f32[192,768]{1,0:T(8,128)}, f32[192,768]{1,0:T(8,128)S(1)}, u32[]{:S(2)}) copy-start(f32[192,768]{1,0:T(8,128)S(1)} %collective-permute-done.13.refs_6_) | copy-start | bytes 1769476
  135.5 20.8 %collective-permute-start.16 = (f32[192,1024]{1,0:T(8,128)}, f32[192,1024]{1,0:T(8,128)S(1)}, u32[]{:S(2)}, u32[]{:S(2)}) collective-permute-start(f32[192,1024]{1,0:T(8,128)} %get-tuple-element.224.refs_5_.refs_1_), channel_id=1, source_target_pairs={{0,8},{8,0},{16,24},{24,16},{1,9},{9,1},{17,25},{25,17},{2,10},{10... | collective-permute-start | bytes 2359304 | tf_op jit(solution)/shard_map/ppermute | solution.py:31
  136.4 35.9 %collective-permute-start.17 = (f32[192,1024]{1,0:T(8,128)}, f32[192,1024]{1,0:T(8,128)S(1)}, u32[]{:S(2)}, u32[]{:S(2)}) collective-permute-start(f32[192,1024]{1,0:T(8,128)} %get-tuple-element.224.refs_5_.refs_1_), channel_id=1, source_target_pairs={{0,16},{8,24},{16,0},{24,8},{1,17},{9,25},{17,1},{25,9},{2,18},{10... | collective-permute-start | bytes 2359304 | tf_op jit(solution)/shard_map/ppermute | solution.py:31
  137.5 34.8 %collective-permute-start.18 = (f32[192,1024]{1,0:T(8,128)}, f32[192,1024]{1,0:T(8,128)S(1)}, u32[]{:S(2)}, u32[]{:S(2)}) collective-permute-start(f32[192,1024]{1,0:T(8,128)} %get-tuple-element.224.refs_5_.refs_1_), channel_id=1, source_target_pairs={{0,24},{8,16},{16,8},{24,0},{1,25},{9,17},{17,9},{25,1},{2,26},{10... | collective-permute-start | bytes 2359304 | tf_op jit(solution)/shard_map/ppermute | solution.py:31
  156.2 19.6 %copy-start.27 = (f32[192,1024]{1,0:T(8,128)}, f32[192,1024]{1,0:T(8,128)S(1)}, u32[]{:S(2)}) copy-start(f32[192,1024]{1,0:T(8,128)S(1)} %collective-permute-done.16.refs_2_) | copy-start | bytes 2359300
  172.3 37.7 %collective-permute-start.19 = (f32[192,1024]{1,0:T(8,128)}, f32[192,1024]{1,0:T(8,128)S(1)}, u32[]{:S(2)}, u32[]{:S(2)}) collective-permute-start(f32[192,1024]{1,0:T(8,128)} %get-tuple-element.231.refs_9_.refs_1_), channel_id=1, source_target_pairs={{0,8},{8,0},{16,24},{24,16},{1,9},{9,1},{17,25},{25,17},{2,10},{10... | collective-permute-start | bytes 2359304 | tf_op jit(solution)/shard_map/ppermute | solution.py:31
  172.9 37.2 %collective-permute-start.20 = (f32[192,1024]{1,0:T(8,128)}, f32[192,1024]{1,0:T(8,128)S(1)}, u32[]{:S(2)}, u32[]{:S(2)}) collective-permute-start(f32[192,1024]{1,0:T(8,128)} %get-tuple-element.231.refs_9_.refs_1_), channel_id=1, source_target_pairs={{0,16},{8,24},{16,0},{24,8},{1,17},{9,25},{17,1},{25,9},{2,18},{10... | collective-permute-start | bytes 2359304 | tf_op jit(solution)/shard_map/ppermute | solution.py:31
  174.4 35.7 %collective-permute-start.21 = (f32[192,1024]{1,0:T(8,128)}, f32[192,1024]{1,0:T(8,128)S(1)}, u32[]{:S(2)}, u32[]{:S(2)}) collective-permute-start(f32[192,1024]{1,0:T(8,128)} %get-tuple-element.231.refs_9_.refs_1_), channel_id=1, source_target_pairs={{0,24},{8,16},{16,8},{24,0},{1,25},{9,17},{17,9},{25,1},{2,26},{10... | collective-permute-start | bytes 2359304 | tf_op jit(solution)/shard_map/ppermute | solution.py:31
  211.1 24.7 %collective-permute-start.22 = (f32[256,768]{1,0:T(8,128)}, f32[256,768]{1,0:T(8,128)S(1)}, u32[]{:S(2)}, u32[]{:S(2)}) collective-permute-start(f32[256,768]{1,0:T(8,128)} %get-tuple-element.265), channel_id=1, source_target_pairs={{0,8},{8,0},{16,24},{24,16},{1,9},{9,1},{17,25},{25,17},{2,10},{10... | collective-permute-start | bytes 2359304 | tf_op jit(solution)/shard_map/ppermute | solution.py:31
  211.6 24.2 %collective-permute-start.23 = (f32[256,768]{1,0:T(8,128)}, f32[256,768]{1,0:T(8,128)S(1)}, u32[]{:S(2)}, u32[]{:S(2)}) collective-permute-start(f32[256,768]{1,0:T(8,128)} %get-tuple-element.266), channel_id=1, source_target_pairs={{0,16},{8,24},{16,0},{24,8},{1,17},{9,25},{17,1},{25,9},{2,18},{10... | collective-permute-start | bytes 2359304 | tf_op jit(solution)/shard_map/ppermute | solution.py:31
  237.2 9.1 %collective-permute-start.24 = (f32[80,768]{1,0:T(8,128)S(1)}, f32[80,768]{1,0:T(8,128)S(1)}, u32[]{:S(2)}, u32[]{:S(2)}) collective-permute-start(f32[80,768]{1,0:T(8,128)S(1)} %get-tuple-element.415), channel_id=1, source_target_pairs={{0,8},{8,0},{16,24},{24,16},{1,9},{9,1},{17,25},{25,17},{2,10},{10... | collective-permute-start | bytes 737288 | tf_op jit(solution)/shard_map/ppermute | solution.py:31
  237.7 8.7 %collective-permute-start.25 = (f32[80,768]{1,0:T(8,128)S(1)}, f32[80,768]{1,0:T(8,128)S(1)}, u32[]{:S(2)}, u32[]{:S(2)}) collective-permute-start(f32[80,768]{1,0:T(8,128)S(1)} %get-tuple-element.414), channel_id=1, source_target_pairs={{0,16},{8,24},{16,0},{24,8},{1,17},{9,25},{17,1},{25,9},{2,18},{10... | collective-permute-start | bytes 737288 | tf_op jit(solution)/shard_map/ppermute | solution.py:31
  246.4 115.9 %reduce-scatter.8.cloned.1.call-start = ((), (), s32[]{:S(2)}) async-start(), calls=%async_computation.9 | async-start | bytes 2211840 | tf_op jit(solution)/shard_map/reduce_scatter | solution.py:84
  247.4 23.1 %copy-start.12 = (f32[80,768]{1,0:T(8,128)}, f32[80,768]{1,0:T(8,128)S(1)}, u32[]{:S(2)}) copy-start(f32[80,768]{1,0:T(8,128)S(1)} %get-tuple-element.412.refs_3_) | copy-start | bytes 737284
  247.4 23.1 %copy-start.13 = (f32[80,768]{1,0:T(8,128)}, f32[80,768]{1,0:T(8,128)S(1)}, u32[]{:S(2)}) copy-start(f32[80,768]{1,0:T(8,128)S(1)} %get-tuple-element.413.refs_2_) | copy-start | bytes 737284
  247.4 23.1 %collective-permute-start.26 = (f32[80,768]{1,0:T(8,128)S(1)}, f32[80,768]{1,0:T(8,128)S(1)}, u32[]{:S(2)}, u32[]{:S(2)}) collective-permute-start(f32[80,768]{1,0:T(8,128)S(1)} %get-tuple-element.413.refs_2_), channel_id=1, source_target_pairs={{0,16},{8,24},{16,0},{24,8},{1,17},{9,25},{17,1},{25,9},{2,18},{10... | collective-permute-start | bytes 737288 | tf_op jit(solution)/shard_map/ppermute | solution.py:31
  247.9 22.7 %collective-permute-start.27 = (f32[80,768]{1,0:T(8,128)S(1)}, f32[80,768]{1,0:T(8,128)S(1)}, u32[]{:S(2)}, u32[]{:S(2)}) collective-permute-start(f32[80,768]{1,0:T(8,128)S(1)} %get-tuple-element.412.refs_3_), channel_id=1, source_target_pairs={{0,8},{8,0},{16,24},{24,16},{1,9},{9,1},{17,25},{25,17},{2,10},{10... | collective-permute-start | bytes 737288 | tf_op jit(solution)/shard_map/ppermute | solution.py:31
  249.6 62.0 %collective-permute-start.28 = (f32[256,768]{1,0:T(8,128)}, f32[256,768]{1,0:T(8,128)S(1)}, u32[]{:S(2)}, u32[]{:S(2)}) collective-permute-start(f32[256,768]{1,0:T(8,128)} %get-tuple-element.303), channel_id=1, source_target_pairs={{0,24},{8,16},{16,8},{24,0},{1,25},{9,17},{17,9},{25,1},{2,26},{10... | collective-permute-start | bytes 2359304 | tf_op jit(solution)/shard_map/ppermute | solution.py:31
  270.6 41.0 %collective-permute-start.29 = (f32[256,768]{1,0:T(8,128)}, f32[256,768]{1,0:T(8,128)S(1)}, u32[]{:S(2)}, u32[]{:S(2)}) collective-permute-start(f32[256,768]{1,0:T(8,128)} %get-tuple-element.305), channel_id=1, source_target_pairs={{0,8},{8,0},{16,24},{24,16},{1,9},{9,1},{17,25},{25,17},{2,10},{10... | collective-permute-start | bytes 2359304 | tf_op jit(solution)/shard_map/ppermute | solution.py:31
  271.8 39.8 %collective-permute-start.30 = (f32[256,768]{1,0:T(8,128)}, f32[256,768]{1,0:T(8,128)S(1)}, u32[]{:S(2)}, u32[]{:S(2)}) collective-permute-start(f32[256,768]{1,0:T(8,128)} %get-tuple-element.306), channel_id=1, source_target_pairs={{0,16},{8,24},{16,0},{24,8},{1,17},{9,25},{17,1},{25,9},{2,18},{10... | collective-permute-start | bytes 2359304 | tf_op jit(solution)/shard_map/ppermute | solution.py:31
  273.3 54.2 %collective-permute-start.31 = (f32[256,768]{1,0:T(8,128)}, f32[256,768]{1,0:T(8,128)}, u32[]{:S(2)}, u32[]{:S(2)}) collective-permute-start(f32[256,768]{1,0:T(8,128)} %get-tuple-element.320), channel_id=1, source_target_pairs={{0,24},{8,16},{16,8},{24,0},{1,25},{9,17},{17,9},{25,1},{2,26},{10... | collective-permute-start | bytes 2359304 | tf_op jit(solution)/shard_map/ppermute | solution.py:31
  295.4 15.1 %copy-start.35 = (f32[3,192,128]{2,1,0:T(8,128)S(1)}, f32[3,192,128]{2,1,0:T(8,128)}, u32[]{:S(2)}) copy-start(f32[3,192,128]{2,1,0:T(8,128)} %get-tuple-element.296) | copy-start | bytes 884740
  311.6 15.9 %copy-start.17 = (f32[256,768]{1,0:T(8,128)}, f32[256,768]{1,0:T(8,128)S(1)}, u32[]{:S(2)}) copy-start(f32[256,768]{1,0:T(8,128)S(1)} %collective-permute-done.28) | copy-start | bytes 2359300
  311.6 15.9 %copy-start.18 = (f32[256,768]{1,0:T(8,128)}, f32[256,768]{1,0:T(8,128)S(1)}, u32[]{:S(2)}) copy-start(f32[256,768]{1,0:T(8,128)S(1)} %collective-permute-done.29) | copy-start | bytes 2359300
  311.6 15.9 %copy-start.20 = (f32[256,768]{1,0:T(8,128)}, f32[256,768]{1,0:T(8,128)S(1)}, u32[]{:S(2)}) copy-start(f32[256,768]{1,0:T(8,128)S(1)} %collective-permute-done.30) | copy-start | bytes 2359300
  327.5 73.9 %reduce-scatter.6.cloned.1.call-start = ((), (), s32[]{:S(2)}) async-start(), calls=%async_computation.8 | async-start | bytes 3096576 | tf_op jit(solution)/shard_map/reduce_scatter | solution.py:84
  327.6 23.9 %collective-permute-start.32 = (f32[256,768]{1,0:T(8,128)}, f32[256,768]{1,0:T(8,128)S(1)}, u32[]{:S(2)}, u32[]{:S(2)}) collective-permute-start(f32[256,768]{1,0:T(8,128)} %get-tuple-element.322), channel_id=1, source_target_pairs={{0,8},{8,0},{16,24},{24,16},{1,9},{9,1},{17,25},{25,17},{2,10},{10... | collective-permute-start | bytes 2359304 | tf_op jit(solution)/shard_map/ppermute | solution.py:31
  328.8 22.6 %collective-permute-start.33 = (f32[256,768]{1,0:T(8,128)}, f32[256,768]{1,0:T(8,128)S(1)}, u32[]{:S(2)}, u32[]{:S(2)}) collective-permute-start(f32[256,768]{1,0:T(8,128)} %get-tuple-element.323), channel_id=1, source_target_pairs={{0,16},{8,24},{16,0},{24,8},{1,17},{9,25},{17,1},{25,9},{2,18},{10... | collective-permute-start | bytes 2359304 | tf_op jit(solution)/shard_map/ppermute | solution.py:31
  352.9 21.7 %collective-permute-start.38 = (f32[256,768]{1,0:T(8,128)}, f32[256,768]{1,0:T(8,128)}, u32[]{:S(2)}, u32[]{:S(2)}) collective-permute-start(f32[256,768]{1,0:T(8,128)} %get-tuple-element.352), channel_id=1, source_target_pairs={{0,24},{8,16},{16,8},{24,0},{1,25},{9,17},{17,9},{25,1},{2,26},{10... | collective-permute-start | bytes 2359304 | tf_op jit(solution)/shard_map/ppermute | solution.py:31
  353.7 36.9 %collective-permute-start.34 = (f32[256,768]{1,0:T(8,128)}, f32[256,768]{1,0:T(8,128)}, u32[]{:S(2)}, u32[]{:S(2)}) collective-permute-start(f32[256,768]{1,0:T(8,128)} %get-tuple-element.336), channel_id=1, source_target_pairs={{0,8},{8,0},{16,24},{24,16},{1,9},{9,1},{17,25},{25,17},{2,10},{10... | collective-permute-start | bytes 2359304 | tf_op jit(solution)/shard_map/ppermute | solution.py:31
  355.0 36.4 %collective-permute-start.35 = (f32[256,768]{1,0:T(8,128)}, f32[256,768]{1,0:T(8,128)}, u32[]{:S(2)}, u32[]{:S(2)}) collective-permute-start(f32[256,768]{1,0:T(8,128)} %get-tuple-element.337), channel_id=1, source_target_pairs={{0,16},{8,24},{16,0},{24,8},{1,17},{9,25},{17,1},{25,9},{2,18},{10... | collective-permute-start | bytes 2359304 | tf_op jit(solution)/shard_map/ppermute | solution.py:31
  356.4 44.6 %collective-permute-start.36 = (f32[256,768]{1,0:T(8,128)}, f32[256,768]{1,0:T(8,128)}, u32[]{:S(2)}, u32[]{:S(2)}) collective-permute-start(f32[256,768]{1,0:T(8,128)} %get-tuple-element.338), channel_id=1, source_target_pairs={{0,24},{8,16},{16,8},{24,0},{1,25},{9,17},{17,9},{25,1},{2,26},{10... | collective-permute-start | bytes 2359304 | tf_op jit(solution)/shard_map/ppermute | solution.py:31
  363.5 37.4 %collective-permute-start.37 = (f32[2,32,3,192]{3,0,1,2:T(2,128)S(1)}, f32[2,32,3,192]{3,0,1,2:T(2,128)S(1)}, u32[]{:S(2)}, u32[]{:S(2)}) collective-permute-start(f32[2,32,3,192]{3,0,1,2:T(2,128)S(1)} %rev.7), channel_id=1, source_target_pairs={{0,7},{1,6},{2,5},{3,4},{4,3},{5,2},{6,1},{7,0},{8,15},{9,14},{10,... | collective-permute-start | bytes 442376 | tf_op jit(solution)/shard_map/ppermute | solution.py:967
  365.4 37.0 %slice-start = ((f32[96,2304]{1,0:T(8,128)}), f32[96,1536]{1,0:T(8,128)S(1)}, s32[]{:S(2)}) async-start(f32[96,2304]{1,0:T(8,128)} %reduce-scatter.4.cloned.1.call-done), calls=%async_computation.10 | async-start | bytes 1179648 | tf_op jit(solution)/shard_map/slice | solution.py:970
  403.3 9.0 %collective-permute-start.39 = (f32[24,2176]{1,0:T(8,128)S(1)}, f32[24,2176]{1,0:T(8,128)S(1)}, u32[]{:S(2)}, u32[]{:S(2)}) collective-permute-start(f32[24,2176]{1,0:T(8,128)S(1)} %get-tuple-element.407), channel_id=1, source_target_pairs={{0,8},{8,0},{16,24},{24,16},{1,9},{9,1},{17,25},{25,17},{2,10},{10... | collective-permute-start | bytes 626696 | tf_op jit(solution)/shard_map/ppermute | solution.py:31
  404.1 10.9 %collective-permute-start.40 = (f32[24,2176]{1,0:T(8,128)S(1)}, f32[24,2176]{1,0:T(8,128)S(1)}, u32[]{:S(2)}, u32[]{:S(2)}) collective-permute-start(f32[24,2176]{1,0:T(8,128)S(1)} %get-tuple-element.406), channel_id=1, source_target_pairs={{0,16},{8,24},{16,0},{24,8},{1,17},{9,25},{17,1},{25,9},{2,18},{10... | collective-permute-start | bytes 626696 | tf_op jit(solution)/shard_map/ppermute | solution.py:31
  405.8 9.2 %collective-permute-start.41 = (f32[24,2176]{1,0:T(8,128)S(1)}, f32[24,2176]{1,0:T(8,128)S(1)}, u32[]{:S(2)}, u32[]{:S(2)}) collective-permute-start(f32[24,2176]{1,0:T(8,128)S(1)} %get-tuple-element.405), channel_id=1, source_target_pairs={{0,24},{8,16},{16,8},{24,0},{1,25},{9,17},{17,9},{25,1},{2,26},{10... | collective-permute-start | bytes 626696 | tf_op jit(solution)/shard_map/ppermute | solution.py:31
  (34 other events, 176.4 us)
Sparse Core Ops, SparseCore 0:
  9.7 34.3 all-gather.4
  53.1 36.1 all-gather.6
  91.6 26.9 all-gather.8
  120.1 51.2 all-gather.10
  246.5 75.5 reduce-scatter.3
  327.7 34.3 reduce-scatter.7
  364.4 37.0 reduce-scatter.5

commit v4 on v3

--- a/solution.py
+++ b/solution.py
@@ -188,46 +188,54 @@
     )
 
 
-def split_units(gathered, w_down, after=()):
+def split_units(gathered, after=()):
     groups, shards, rows, columns = gathered.shape
     width = groups * shards * rows
-    units = w_down.shape[0]
-
-    def kernel(w_ref, d_ref, high_ref, low_ref, dh_ref, dl_ref, flat_ref):
-        k = pl.program_id(0)
+
+    def kernel(w_ref, high_ref, low_ref, flat_ref):
         for j in range(groups):
             flat_ref[j * rows : (j + 1) * rows] = w_ref[j, 0]
-
         high_ref[...], low_ref[...] = halves(flat_ref[...])
-        dh_ref[...], dl_ref[...] = halves(d_ref[...])
 
     part = pl.BlockSpec((groups * rows, columns), lambda i: (i, 0))
-    down = pl.BlockSpec((units // shards, width), lambda i: (i, 0))
-    return call(
-        kernel, "split_units", 0, 8 * width * (columns + units), [gathered, w_down],
-        [pl.BlockSpec((groups, 1, rows, columns), lambda i: (0, i, 0, 0)), down],
-        [shaped(width, columns, dtype=BF16)] * 2 + [shaped(units, width, dtype=BF16)] * 2,
-        [part, part, down, down], grid=(shards,),
+    return call(
+        kernel, "split_units", 0, 8 * width * columns, [gathered],
+        [pl.BlockSpec((groups, 1, rows, columns), lambda i: (0, i, 0, 0))],
+        [shaped(width, columns, dtype=BF16)] * 2, [part, part], grid=(shards,),
         scratch=[pltpu.VMEM((groups * rows, columns), F32)], after=after,
     )
 
 
-def arrange(pieces, s, after=()):
-    tokens, width = pieces[0].shape
+def split_down(weight, after=()):
+    units, width = weight.shape
+
+    def kernel(w_ref, high_ref, low_ref):
+        high_ref[...], low_ref[...] = halves(w_ref[...])
+
+    part = pl.BlockSpec((units // 2, width), lambda i: (i, 0))
+    return call(
+        kernel, "split_down", 0, 8 * units * width, [weight], [part],
+        [shaped(units, width, dtype=BF16)] * 2, [part, part], grid=(2,), after=after,
+    )
+
+
+def arrange(which, near, far, s, after=()):
+    _, tokens, width = near[0].shape
     length = 4 * tokens
 
     def kernel(s_ref, p0, p1, p2, p3, x_ref, high_ref, low_ref):
         for d, piece in enumerate((p0, p1, p2, p3)):
 
             @pl.when(pl.program_id(0) == d)
-            def _(piece=piece):
-                x = piece[...]
+            def _(d=d, piece=piece):
+                x = piece[...] if d == 3 else piece[0]
                 x_ref[...] = x
                 high_ref[...], low_ref[...] = halves(normed(x)[0])
 
     rows = pl.BlockSpec((tokens, width), lambda i, s_ref: (s_ref[0] ^ i, 0))
     return call(
-        kernel, "arrange", 0, 12 * length * width, pieces, [whole(tokens, width)] * 4,
+        kernel, "arrange", 0, 12 * length * width, [*near, far],
+        [pl.BlockSpec((1, tokens, width), lambda i, s_ref: (which, 0, 0))] * 3 + [whole(tokens, width)],
         [shaped(length, width), shaped(length, width, dtype=BF16), shaped(length, width, dtype=BF16)],
         [rows] * 3, grid=(4,), scalars=[s.reshape(1)], after=after,
     )
@@ -392,27 +400,31 @@
     )
 
 
-def mix_back(which, places, d_gating, d_long, projected, taps, vals, spec, kernel_sum, tables, after=()):
-    own, length = projected.shape[1:]
-    block = vals.shape[2] // 2
+def mix_back(places, d_gating, d_long, projected, taps, vals, spec, tables, after=()):
+    seqs = len(projected)
+    own, length = projected[0].shape[1:]
+    block = vals[0].shape[2] // 2
     groups = lax.axis_size("batch")
     turns = block // groups
     slots = places.shape[1]
     scale = 1.0 / math.sqrt(length)
 
-    def kernel(at_ref, dg_ref, dl_ref, p_ref, tap_ref, vals_ref, spec_ref, th_ref, tl_ref, *refs):
-        sum_refs, (out_ref, ker_ref, dtap_ref, long_ref, gating_ref, acc_ref) = refs[:-6], refs[-6:]
+    def kernel(at_ref, dg_ref, dl_ref, tap_ref, *refs):
+        p_refs, vals_refs, spec_refs, refs = refs[:seqs], refs[seqs : 2 * seqs], refs[2 * seqs : 3 * seqs], refs[3 * seqs :]
+        th_ref, tl_ref, *refs = refs
+        out_refs, (ker_ref, dtap_ref, long_ref, gating_ref, acc_ref) = refs[:seqs], refs[seqs:]
         step = pl.program_id(0)
 
         @pl.when(step == 0)
         def _():
             at = lax.broadcasted_iota(jnp.int32, (slots, length), 1)
-            chosen = jnp.where(at == at_ref[0], 1.0, 0.0).astype(BF16)
-            for source, target in ((dg_ref, gating_ref), (dl_ref, long_ref)):
-                high, low = halves(source[0])
-                target[...] = lax.dot_general(high, chosen, (NN, ((), ())), preferred_element_type=F32) + (
-                    lax.dot_general(low, chosen, (NN, ((), ())), preferred_element_type=F32)
-                )
+            for i in range(seqs):
+                pick = jnp.where(at == at_ref[i], 1.0, 0.0).astype(BF16)
+                for source, target in ((dg_ref, gating_ref), (dl_ref, long_ref)):
+                    high, low = halves(source[i])
+                    target[i * own : (i + 1) * own] = lax.dot_general(
+                        high, pick, (NN, ((), ())), preferred_element_type=F32
+                    ) + lax.dot_general(low, pick, (NN, ((), ())), preferred_element_type=F32)
 
         for phase in range(FOLDED):
 
@@ -420,51 +432,50 @@
             def _(phase=phase):
                 deep = depth(phase, block)
                 table = (th_ref[0, :deep], tl_ref[0, :deep])
-                hat = dot(halves(fold(long_ref[...], phase, block)), table, NN) * (0.5 / length)
-                ker = times(hat, vals_ref[0], block, conj=True)
-                spread = jnp.concatenate([ker[:, :block], ker[:, block:]], axis=0).T.reshape(groups, turns, 2 * own)
-                ker_ref[:, 0] = sum_refs[0][:, 0] + spread if sum_refs else spread
-                both = jnp.concatenate(
-                    [ker * (pair(phase) * scale), times(hat, spec_ref[0], block, conj=True)], axis=0
-                )
-                unfold(acc_ref, dot(halves(both), table, NT), phase, block)
+                hats = dot(halves(fold(long_ref[...], phase, block)), table, NN) * (0.5 / length)
+                both, kernel_sum = [], 0.0
+                for i in range(seqs):
+                    hat = hats[i * own : (i + 1) * own]
+                    ker = times(hat, vals_refs[i][0], block, conj=True)
+                    kernel_sum = kernel_sum + ker
+                    both += [ker * (pair(phase) * scale), times(hat, spec_refs[i][0], block, conj=True)]
+                turned = jnp.concatenate([kernel_sum[:, :block], kernel_sum[:, block:]], axis=0).T
+                ker_ref[:, 0] = turned.reshape(groups, turns, 2 * own)
+                unfold(acc_ref, dot(halves(jnp.concatenate(both, axis=0)), table, NT), phase, block)
 
         @pl.when(step == FOLDED - 1)
         def _():
             lane = lax.broadcasted_iota(jnp.int32, (own, 128), 1)
             for k in range(3):
-                grad = gating_ref[...] if k == 1 else acc_ref[k // 2 * own : (k // 2 + 1) * own]
-                p = p_ref[k]
                 tap = tap_ref[k]
-                out_ref[k] = tap[:, 0:1] * shift(grad, 1) + tap[:, 1:2] * grad + tap[:, 2:3] * shift(grad, -1)
                 sums = jnp.zeros((own, 128), F32)
-                for j, moved in enumerate((shift(p, -1), p, shift(p, 1))):
-                    sums = jnp.where(lane == j, jnp.sum(moved * grad, axis=1, keepdims=True), sums)
+                for i in range(seqs):
+                    if k == 1:
+                        grad = gating_ref[i * own : (i + 1) * own]
+                    else:
+                        at = 2 * i + k // 2
+                        grad = acc_ref[at * own : (at + 1) * own]
+                    p = p_refs[i][k]
+                    out_refs[i][k] = tap[:, 0:1] * shift(grad, 1) + tap[:, 1:2] * grad + tap[:, 2:3] * shift(grad, -1)
+                    for j, moved in enumerate((shift(p, -1), p, shift(p, 1))):
+                        sums += jnp.where(lane == j, jnp.sum(moved * grad, axis=1, keepdims=True), 0.0)
                 dtap_ref[k] = sums
 
-    by_phase = lambda *shape: pl.BlockSpec((1,) + shape, lambda i, *_: (i,) + (0,) * len(shape))
-    spectrum = pl.BlockSpec((groups, 1, turns, 2 * own), lambda i, *_: (0, i, 0, 0))
-    return call(
-        kernel, "mix_back", 3 * 6 * own * 4 * length * length, 4 * own * length * 22,
-        [places, d_gating, d_long, projected, taps, vals, spec, *tables, *kernel_sum],
-        [
-            pl.BlockSpec((1, slots, 1), lambda i: (which, 0, 0)),
-            pl.BlockSpec((1, own, slots), lambda i: (which, 0, 0)),
-            pl.BlockSpec((1, own, slots), lambda i: (which, 0, 0)),
-            whole(3, own, length),
-            whole(3, own, 3),
-            by_phase(own, 2 * block),
-            by_phase(own, 2 * block),
-            by_phase(2 * block, 2 * block),
-            by_phase(2 * block, 2 * block),
-        ] + [spectrum] * len(kernel_sum),
-        [shaped(3, own, length), shaped(groups, FOLDED, turns, 2 * own), shaped(3, own, 128)],
-        [whole(3, own, length), spectrum, whole(3, own, 128)],
+    by_phase = lambda *shape: pl.BlockSpec((1,) + shape, lambda i: (i,) + (0,) * len(shape))
+    flat = shaped(3, own, length)
+    return call(
+        kernel, "mix_back", seqs * 3 * 6 * own * 4 * length * length, seqs * 4 * own * length * 22,
+        [places, d_gating, d_long, taps, *projected, *vals, *spec, *tables],
+        [whole(seqs, slots, 1), whole(seqs, own, slots), whole(seqs, own, slots), whole(3, own, 3)]
+        + [whole(3, own, length)] * seqs + [by_phase(own, 2 * block)] * (2 * seqs) + [by_phase(2 * block, 2 * block)] * 2,
+        [flat] * seqs + [shaped(groups, FOLDED, turns, 2 * own), shaped(3, own, 128)],
+        [whole(3, own, length)] * seqs
+        + [pl.BlockSpec((groups, 1, turns, 2 * own), lambda i: (0, i, 0, 0)), whole(3, own, 128)],
         grid=(FOLDED,),
         scratch=[
-            pltpu.VMEM((own, length), F32),
-            pltpu.VMEM((own, length), F32),
-            pltpu.VMEM((2 * own, length), F32),
+            pltpu.VMEM((seqs * own, length), F32),
+            pltpu.VMEM((seqs * own, length), F32),
+            pltpu.VMEM((2 * seqs * own, length), F32),
         ],
         after=after,
     )
@@ -502,15 +513,43 @@
     return 0.5 * (1.0 + jnp.tanh(inner))
 
 
-def deal(low, value, out_refs):
-    tokens = value.shape[0] // 2
-    for step in range(2):
-        for crossed in range(2):
-
-            @pl.when((pl.program_id(0) == step) & (low == crossed))
-            def _(step=step, crossed=crossed):
-                out_refs[2 * step + crossed][...] = value[:tokens]
-                out_refs[2 * step + 1 - crossed][...] = value[tokens:]
+def units_of(residual, w_units, after=()):
+    length, width = residual.shape
+    units = w_units[0].shape[1] // 2
+    tokens = length // 4
+
+    def kernel(r_ref, wh, wl, high_ref, low_ref):
+        gate_up = []
+        for i in range(2):
+            rows = r_ref[i * tokens : (i + 1) * tokens]
+            gate_up.append(dot(halves(normed(rows)[0]), (wh[...], wl[...]), NN))
+        for i, v in enumerate(gate_up):
+            at = slice(i * tokens, (i + 1) * tokens)
+            high_ref[at], low_ref[at] = halves(v[:, :units] * gelu_parts(v[:, :units]) * v[:, units:])
+
+    rows = lambda columns: pl.BlockSpec((2 * tokens, columns), lambda i: (i, 0))
+    return call(
+        kernel, "units_of", 12 * length * width * units, 4 * (2 * length * width + 2 * width * units),
+        [residual, *w_units], [rows(width)] + [whole(width, 2 * units)] * 2,
+        [shaped(length, units, dtype=BF16)] * 2, [rows(units)] * 2, grid=(2,), after=after,
+    )
+
+
+def down_of(hidden, w_down, s, after=()):
+    length, units = hidden[0].shape
+    width = w_down[0].shape[1]
+    tokens = length // 4
+
+    def kernel(s_ref, hh, hl, dh, dl, *out_refs):
+        for i, out_ref in enumerate(out_refs):
+            rows = pl.ds(pl.multiple_of((s_ref[0] ^ i) * tokens, tokens), tokens)
+            out_ref[...] = dot((hh[rows], hl[rows]), (dh[...], dl[...]), NN)
+
+    return call(
+        kernel, "down_of", 6 * length * width * units, 4 * (2 * length * width + width * units),
+        [*hidden, *w_down], [whole(length, units)] * 2 + [whole(units, width)] * 2,
+        [shaped(tokens, width)] * 4, [whole(tokens, width)] * 4, scalars=[s.reshape(1)], after=after,
+    )
 
 
 def feed_forward(residual, w_units, w_down, s, after=()):
@@ -519,19 +558,20 @@
     tokens = length // 4
 
     def kernel(s_ref, r_ref, wh, wl, dh, dl, *out_refs):
-        both = halves(normed(r_ref[...])[0])
-        gate_up = dot(both, (wh[...], wl[...]), NN)
-        gate, up = gate_up[:, :units], gate_up[:, units:]
-        out = dot(halves(gate * gelu_parts(gate) * up), (dh[...], dl[...]), NN)
-        deal(s_ref[0] & 1, out, out_refs)
+        gate_up = []
+        for i in range(4):
+            rows = r_ref[pl.ds(pl.multiple_of((s_ref[0] ^ i) * tokens, tokens), tokens)]
+            gate_up.append(dot(halves(normed(rows)[0]), (wh[...], wl[...]), NN))
+        hidden = [halves(v[:, :units] * gelu_parts(v[:, :units]) * v[:, units:]) for v in gate_up]
+        for both, out_ref in zip(hidden, out_refs):
+            out_ref[...] = dot(both, (dh[...], dl[...]), NN)
 
     return call(
         kernel, "feed_forward", 18 * length * width * units, 4 * (2 * length * width + 3 * width * units),
         [residual, *w_units, *w_down],
-        [pl.BlockSpec((2 * tokens, width), lambda i, s_ref: ((s_ref[0] >> 1) ^ i, 0))]
-        + [whole(width, 2 * units)] * 2 + [whole(units, width)] * 2,
+        [whole(length, width)] + [whole(width, 2 * units)] * 2 + [whole(units, width)] * 2,
         [shaped(tokens, width)] * 4, [whole(tokens, width)] * 4,
-        grid=(2,), scalars=[s.reshape(1)], after=after,
+        scalars=[s.reshape(1)], after=after,
     )
 
 
@@ -540,17 +580,24 @@
     return jnp.where(lane == at_ref[...], 1.0, 0.0).astype(BF16)
 
 
-def live_back(residual, places, d_out, w_units, w_down, used, after=()):
-    seqs = len(residual)
-    length, width = residual[0].shape
+def live_back(residual, x, gated, w_out, places, d_out, w_units, w_down, used, after=()):
+    seqs = 1 + len(residual)
+    length, width = x.shape
+    own = gated[0].shape[0]
     slots = places.shape[1]
     units = w_down[0].shape[0]
     rows = seqs * slots
 
-    def kernel(r_refs, at_ref, o_ref, wh, wl, dh, dl, live_ref, n_ref, hid_ref, du_ref, e_ref):
-        for i, ref in enumerate(r_refs):
+    def kernel(*refs):
+        r_refs, refs = refs[: seqs - 1], refs[seqs - 1 :]
+        x_ref, g_refs, w_refs, refs = refs[0], refs[1:5], refs[5:9], refs[9:]
+        at_ref, o_ref, wh, wl, dh, dl, live_ref, n_ref, hid_ref, du_ref, e_ref = refs
+        for i, ref in enumerate((*r_refs, x_ref)):
             pick = chosen(at_ref.at[i], slots, length)
             live_ref[i * slots : (i + 1) * slots] = chosen_rows(pick, halves(ref[...]), NN)
+        mixed = jnp.concatenate([chosen_rows(pick, halves(ref[...]), NT) for ref in g_refs], axis=1)
+        weight = jnp.concatenate([ref[...] for ref in w_refs], axis=0)
+        live_ref[rows - slots :] += dot(halves(mixed), halves(weight), NN)
         n = normed(live_ref[...])[0]
         n_ref[...] = n
         gate_up = dot(halves(n), (wh[...], wl[...]), NN)
@@ -565,14 +612,11 @@
         for i in range(seqs):
             e_ref[i * used : (i + 1) * used] = e[i * slots : i * slots + used]
 
-    def spread(*refs):
-        kernel(refs[:seqs], *refs[seqs:])
-
-    return call(
-        spread, "live_back", 30 * rows * width * units, 4 * (2 * length * width + 4 * width * units),
-        [*residual, places, d_out, *w_units, *w_down],
-        [whole(length, width)] * seqs + [whole(seqs, slots, 1), whole(rows, width)]
-        + [whole(width, 2 * units)] * 2 + [whole(units, width)] * 2,
+    return call(
+        kernel, "live_back", 30 * rows * width * units, 4 * (2 * length * width + 4 * width * units),
+        [*residual, x, *gated, *w_out, places, d_out, *w_units, *w_down],
+        [whole(length, width)] * seqs + [whole(own, length)] * 4 + [whole(own, width)] * 4
+        + [whole(seqs, slots, 1), whole(rows, width)] + [whole(width, 2 * units)] * 2 + [whole(units, width)] * 2,
         [shaped(rows, width), shaped(rows, width), shaped(rows, units), shaped(rows, 2 * units), shaped(seqs * used, width)],
         [whole(rows, width), whole(rows, width), whole(rows, units), whole(rows, 2 * units), whole(seqs * used, width)],
         after=after,
@@ -666,29 +710,22 @@
     tokens = length // 4
 
     def kernel(s_ref, d_ref, nh, nl, wh, wl, *refs):
-        sum_refs, e_refs, dw_ref = refs[:-5], refs[-5:-1], refs[-1]
-        both = halves(d_ref[...])
-        deal(s_ref[0] & 1, dot(both, (wh[...], wl[...]), TN), e_refs)
-        part = dot(both, (nh[...], nl[...]), NN)
-
-        @pl.when(pl.program_id(0) == 0)
-        def _():
-            dw_ref[...] = sum_refs[0][...] + part if sum_refs else part
-
-        @pl.when(pl.program_id(0) == 1)
-        def _():
-            dw_ref[...] += part
-
-    at = lambda i, s_ref: ((s_ref[0] >> 1) ^ i, 0)
+        sum_refs, e_refs, dw_ref, ph, pl_ = refs[:-7], refs[-7:-3], refs[-3], refs[-2], refs[-1]
+        ph[...], pl_[...] = halves(d_ref[...])
+        part = dot((ph[...], pl_[...]), (nh[...], nl[...]), NN)
+        dw_ref[...] = sum_refs[0][...] + part if sum_refs else part
+        for i, e_ref in enumerate(e_refs):
+            at = pl.ds(pl.multiple_of((s_ref[0] ^ i) * tokens, tokens), tokens)
+            e_ref[...] = dot((ph[:, at], pl_[:, at]), (wh[...], wl[...]), TN)
+
     return call(
         kernel, "project_back", 12 * length * width * channels,
         4 * (2 * length * width + channels * (length + 3 * width)),
         [d_projected, *n_both, *w_turned, *w_sum],
-        [pl.BlockSpec((channels, 2 * tokens), lambda i, s_ref: (0, (s_ref[0] >> 1) ^ i))]
-        + [pl.BlockSpec((2 * tokens, width), at)] * 2 + [whole(channels, width)] * (2 + len(w_sum)),
+        [whole(channels, length)] + [whole(length, width)] * 2 + [whole(channels, width)] * (2 + len(w_sum)),
         [shaped(tokens, width)] * 4 + [shaped(channels, width)],
         [whole(tokens, width)] * 4 + [whole(channels, width)],
-        grid=(2,), scalars=[s.reshape(1)], after=after,
+        scratch=[pltpu.VMEM((channels, length), BF16)] * 2, scalars=[s.reshape(1)], after=after,
     )
 
 
@@ -849,88 +886,79 @@
     carried = jnp.broadcast_to(conv_weight.reshape(rows, 1, extra), (rows, shards, extra))
     split = 3 * own + extra
     sent = columns_out(jnp.concatenate([w_pre, carried], axis=2), s)
-    near_0 = (swap(inputs[0], "seq", 1), swap(inputs[0], "seq", 2))
-    w_down_own = over_batch(w_down).reshape(units, width)
-    sent, near_0, x_now, kernel_now, places, d_out = together(sent, near_0, inputs[1], kernel, places, d_out)
+    sent, x_now, kernel_now, places, d_out = together(sent, inputs, kernel, places, d_out)
     w_out_turned = w_out.reshape(rows, shards, own).transpose(1, 0, 2).reshape(shards * rows, own)
-    sent = jnp.concatenate([sent.reshape(shards * rows, split), w_out_turned], axis=1)
-
+    w_pre = over_batch(jnp.concatenate([sent.reshape(shards * rows, split), w_out_turned], axis=1))
+    w_pre = w_pre.reshape(groups, shards, rows, split + own)
+
+    near = [swap(x_now, "seq", 1), swap(x_now, "seq", 2)]
     wide = kernel_now.reshape(2, -1, RADIX, own)
     mirror = [(i, groups - 1 - i) for i in range(groups)]
     folded = lax.ppermute(wide[:, ::-1, :4:-1], "batch", mirror)
-    near_1 = (swap(x_now, "seq", 1), swap(x_now, "seq", 2))
-    near_1, near_0, folded, sent, w_down_own, w_gate_now, w_up_now = together(
-        near_1, near_0, folded, sent, w_down_own, w_gate, w_up
-    )
-    w_pre = over_batch(sent).reshape(groups, shards, rows, split + own)
-    base = over_batch(fold_base(wide, folded))
-
-    far = (swap(near_0[0], "seq", 2), swap(near_1[1], "seq", 1))
+    folded = fold_base(wide, folded)
+    near, folded, w_gate_now, w_up_now = together(near, folded, w_gate, w_up)
+    base = over_batch(folded)
+
+    far = [swap(near[0][0], "seq", 2), swap(near[1][1], "seq", 1)]
     w_units = jnp.stack([gain_two[:, None] * w_gate_now, gain_two[:, None] * w_up_now], axis=1)
     w_units = w_units.reshape(rows, 2, shards, units).transpose(0, 2, 1, 3).reshape(rows, shards, 2 * units)
-    far, w_units = together(far, columns_out(w_units, s))
-    x_pieces = [(inputs[0], *near_0, far[0]), (inputs[1], *near_1, far[1])]
-    arranged_0, w_pre = together(arrange(x_pieces[0], s), w_pre)
+    w_turned = turn_in(w_pre, 3 * own)
+    far, w_units, w_turned, w_pre, w_down_now = together(far, columns_out(w_units, s), w_turned, w_pre, w_down)
     w_units = over_batch(w_units.reshape(shards * rows, 2 * units))
+    w_down_own = over_batch(w_down_now).reshape(units, width)
 
     w_out_own = w_pre[..., split:].transpose(0, 2, 1, 3).reshape(own, width)
-    w_turned = turn_in(w_pre, 3 * own)
     taps = w_pre[..., 3 * own : split].reshape(groups, shards, 3, count).transpose(2, 1, 0, 3)
     taps = lax.dynamic_index_in_dim(taps.reshape(3, 3, shards, own), s, axis=2, keepdims=False)
     taps = taps.transpose(1, 2, 0)
 
-    def first_half(arranged):
-        x_i, *n_i = arranged
+    def first_half(i, after=()):
+        x_i, *n_i = arrange(i, (inputs, *near), far[i], s, after=after)
         return x_i, n_i, project(w_turned, n_i).reshape(3, own, length)
 
-    first_0 = first_half(arranged_0)
-    first_1 = first_half(arrange(x_pieces[1], s, after=(first_0[2],)))
-    w_out_there, (x_0, n_0, p_0), (x_1, n_1, p_1), w_turned, taps = together(
-        from_others(w_out_own), first_0, first_1, w_turned, taps
-    )
-    gated_0, *mixed_0 = mix(p_0, taps, base, tables)
-    there_0, (gated_1, *mixed_1) = together(from_others(gated_0), mix(p_1, taps, base, tables, after=(gated_0,)))
+    x_0, n_0, p_0 = first_half(0)
+    w_out_there, (gated_0, *mixed_0), x_0, n_0 = together(from_others(w_out_own), mix(p_0, taps, base, tables), x_0, n_0)
+    x_1, n_1, p_1 = first_half(1, (gated_0,))
+    there_0, (gated_1, *mixed_1), x_1, n_1 = together(from_others(gated_0), mix(p_1, taps, base, tables), x_1, n_1)
     n_one, projected = (n_0, n_1), (p_0, p_1)
     gating, long_conv, vals, spec = zip(mixed_0, mixed_1)
     w_out_pieces = (w_out_own, *w_out_there)
 
     residual_0 = add_mixer(x_0, (gated_0, *there_0), w_out_pieces, after=(gated_1,))
-    w_units = split_units(w_units.reshape(groups, shards, rows, 2 * units), w_down_own, after=(residual_0,))
-    w_units, w_down_own = w_units[:2], w_units[2:]
-    down_0 = feed_forward(residual_0, w_units, w_down_own, s)
+    w_units = split_units(w_units.reshape(groups, shards, rows, 2 * units), after=(residual_0,))
+    hidden_0 = units_of(residual_0, w_units)
+    w_down_own = split_down(w_down_own, after=(hidden_0[0],))
+    down_0 = down_of(hidden_0, w_down_own, s)
     there_1, down_0, residual_0, w_units, w_down_own = together(
         from_others(gated_1), down_0, residual_0, w_units, w_down_own
     )
 
-    residual_1 = add_mixer(x_1, (gated_1, *there_1), w_out_pieces, after=(down_0[0],))
-    lived = live_back((residual_0, residual_1), places, d_out, w_units, w_down_own, slots)
+    lived = live_back(
+        (residual_0,), x_1, (gated_1, *there_1), w_out_pieces, places, d_out, w_units, w_down_own, slots
+    )
+    live_rows, n_live, hidden, d_units, e_two = lived
+    unit_part = unit_grads(n_live, d_units, hidden, d_out, shards)
     out_0 = [down_0[0], swap(down_0[1], "seq", 1), swap(down_0[2], "seq", 2)]
-    lived, residual_1, out_0 = together(lived, residual_1, out_0)
-    live_rows, n_live, hidden, d_units, e_two = lived
+    live_rows, e_two, unit_part, out_0 = together(live_rows, e_two, unit_part, out_0)
+    unit_sums = sum_over_batch(unit_part)
+
+    e_two = [e_two[:slots], e_two[slots:]]
+    residual_1 = add_mixer(x_1, (gated_1, *there_1), w_out_pieces, after=(unit_part,))
+    e_there, residual_1 = together([swap(e, "seq", 1 + i) for i, e in enumerate(e_two)], residual_1)
     residual = (residual_0, residual_1)
-
-    e_two = [e_two[:slots], e_two[slots:]]
-    unit_part = unit_grads(n_live, d_units, hidden, d_out, shards)
-    e_there, unit_part = together([swap(e, "seq", 1 + i) for i, e in enumerate(e_two)], unit_part)
-    unit_sums = sum_over_batch(unit_part)
-
     e_two = [e + there for e, there in zip(e_two, e_there)]
-    down_1 = feed_forward(residual_1, w_units, w_down_own, s, after=(unit_part,))
+    down_1 = feed_forward(residual_1, w_units, w_down_own, s)
     e_there, down_1 = together([swap(e, "seq", 2 - i) for i, e in enumerate(e_two)], down_1)
     e_terms = [*e_two, *e_there]
 
     d_residual, w_out_part, d_gating, d_long = live_mix(live_rows, d_out, e_terms, w_out_own, gating, long_conv, places)
-    kernel_part, taps_part, d_projected = (), 0.0, []
-    for i in range(seqs):
-        d_p, *kernel_part, d_taps = mix_back(
-            i, places, d_gating, d_long, projected[i], taps, vals[i], spec[i], kernel_part, tables,
-            after=d_projected[-1:],
-        )
-        taps_part = taps_part + d_taps[:, :, :3]
-        d_projected.append(d_p)
+    *d_projected, kernel_part, taps_part = mix_back(
+        places, d_gating, d_long, projected, taps, vals, spec, tables
+    )
+    taps_part = taps_part[:, :, :3]
     out_0 += [swap(down_0[3], "seq", 3)]
     out_1 = [down_1[0], swap(down_1[1], "seq", 1), swap(down_1[2], "seq", 2)]
-    d_projected, (kernel_part,), taps_part, d_residual, w_out_part, out_0, out_1 = together(
+    d_projected, kernel_part, taps_part, d_residual, w_out_part, out_0, out_1 = together(
         d_projected, kernel_part, taps_part, d_residual, w_out_part, out_0, out_1
     )
 
@@ -985,12 +1013,12 @@
     return (
         outputs,
         input_grad,
-        gain_one_sum[:, 0],
+        gain_one_sum.reshape(-1),
         w_in_sum,
         taps_sum,
         kernel_grad,
         w_out_sum,
-        gain_two_sum[:, 0],
+        gain_two_sum.reshape(-1),
         w_gate_sum,
         w_up_sum,
         w_down_sum,

time: 437 us -> 418 us (0.957)
  waiting for transfers between devices: 101 us -> 91.7 us
  Pallas kernels: 222 us -> 214 us
    ppermute x40 -> x38, waiting for transfers between devices: 89.8 us -> 62.6 us  [swap(): lax.ppermute(value, axis, [(i, i ^ distance) for i in range(devices)])]
    reduce_scatter x3, waiting for transfers between devices: 0.57 us -> 13.8 us  [sum_over_batch(): return lax.psum_scatter(flat, 'batch', scatter_dimension=0, tiled=True)]
    pallas_call x22 -> x23, Pallas kernels: 214 us -> 206 us  [call(): pl.pallas_call(run, name=name, out_shape=tuple(outs), grid_spec=pltpu.Pre...]
    ppermute x1, waiting for transfers between devices: 8.11 us -> 14.7 us  [body(): folded = lax.ppermute(wide[:, ::-1, :4:-1], 'batch', mirror)]
    ppermute x40 -> x38, starting transfers between devices: 49.1 us -> 45.3 us  [swap(): lax.ppermute(value, axis, [(i, i ^ distance) for i in range(devices)])]
  transfers between devices with their start and end apart: 49 -> 47, of which waited for: 20 -> 19; matrix products, arithmetic and copies ran while one was open for 7% -> 7% of each run, Pallas kernels for 51% -> 51%
where the time goes in v4:
time: 418 us; the launch traced here: 411 us
  Pallas kernels  214 us (51%)
  waiting for transfers between devices  91.7 us (22%)
  starting transfers between devices  47.8 us (11%)
  local copies, waits for them, and re-layouts  29.3 us (7%)
  between operations  15.3 us (4%)
  other arithmetic  13 us (3%)
    pallas_call x23, Pallas kernels, call(): pl.pallas_call(run, name=name, out_shape=tuple(outs), grid_spec=pltpu.Pre...  206 us
    ppermute x38, waiting for transfers between devices, swap(): lax.ppermute(value, axis, [(i, i ^ distance) for i in range(devices)])  62.6 us
    ppermute x38, starting transfers between devices, swap(): lax.ppermute(value, axis, [(i, i ^ distance) for i in range(devices)])  45.3 us
    ppermute x1, waiting for transfers between devices, body(): folded = lax.ppermute(wide[:, ::-1, :4:-1], 'batch', mirror)  14.7 us
    reduce_scatter x3, waiting for transfers between devices, sum_over_batch(): return lax.psum_scatter(flat, 'batch', scatter_dimension=0, tiled=True)  13.8 us
  transfers between devices with their start and end apart: 47, of which 19 were waited for; matrix products, arithmetic and copies ran while one was open for 7% of the time, Pallas kernels for 51%

profile of v4, /device:TPU:0, one launch (start us, length us, event | category | flops | bytes accessed | tf_op | source)
XLA Modules:
  0.0 411.0 jit_solution(3877329743244778988)
XLA Ops:
  9.1 4.0 collective-permute-start
  15.3 2.0 collective-permute-done.1
  19.3 1.7 collective-permute-start.4
  21.0 2.0 copy.54
  23.0 1.8 slice.64
  24.8 1.8 rev.6
  26.6 1.4 collective-permute-start.5
  27.9 14.7 %collective-permute-done.5.refs_1_ = f32[2,32,3,192]{3,2,1,0:T(4,128)S(1)} collective-permute-done((f32[2,32,3,192]{3,2,1,0:T(4,128)}, f32[2,32,3,192]{3,2,1,0:T(4,128)S(1)}, u32[]{:S(2)}, u32[]{:S(2)}) %collective-permute-start.5) | collective-permute-done | bytes 147488 | tf_op jit(solution)/shard_map/ppermute | solution.py:897
  43.3 2.0 fold_base.1
  45.3 8.4 %collective-permute-done.3.refs_2_ = f32[2,256,768]{2,1,0:T(8,128)S(1)} collective-permute-done((f32[2,256,768]{2,1,0:T(8,128)S(1)}, f32[2,256,768]{2,1,0:T(8,128)S(1)}, u32[]{:S(2)}, u32[]{:S(2)}) %collective-permute-start.3) | collective-permute-done | bytes 1572896 | tf_op jit(solution)/shard_map/ppermute | solution.py:31
  58.8 1.7 collective-permute-start.8
  61.3 1.3 collective-permute-start.6
  65.1 1.6 collective-permute-done.8
  66.8 1.9 collective-permute-done.9
  69.6 3.6 turn_in.1
  73.2 10.2 %collective-permute-done.6.refs_4_ = f32[256,768]{1,0:T(8,128)} collective-permute-done((f32[256,768]{1,0:T(8,128)S(1)}, f32[256,768]{1,0:T(8,128)}, u32[]{:S(2)}, u32[]{:S(2)}) %collective-permute-start.6) | collective-permute-done | bytes 786464 | tf_op jit(solution)/shard_map/ppermute | solution.py:31
  84.0 1.5 slice_bitcast_fusion
  88.5 1.4 collective-permute-start.13
  92.3 5.5 %arrange.2 = (f32[1024,768]{1,0:T(8,128)}, bf16[1024,768]{1,0:T(8,128)(2,1)}, bf16[1024,768]{1,0:T(8,128)(2,1)}) custom-call(s32[1]{0:T(128)} %bitcast.refs_0_.s_ref, f32[2,256,768]{2,1,0:T(8,128)} %x_ref.3, f32[2,256,768]{2,1,0:T(8,128)} %copy-done.2, f32[2,256,768]{2,1,0:T(8,128)} %collective-permute-done.4.refs_3_, f32[256,768]{1,0:T(8,128)} %collective-permute-done.6.refs_4_), custom_call_target="tpu_custom_call" | custom-call | bytes 471859 | tf_op jit(solution)/shard_map/arrange/pallas_call | solution.py:122
  97.8 6.1 %project.2 = f32[576,1024]{1,0:T(8,128)} custom-call(bf16[576,768]{1,0:T(8,128)(2,1)} %get-tuple-element.196.refs_0_.refs_4_, bf16[576,768]{1,0:T(8,128)(2,1)} %get-tuple-element.197.refs_1_.refs_5_, bf16[1024,768]{1,0:T(8,128)(2,1)} %get-tuple-element.292.refs_2_, bf16[1024,768]{1,0:T(8,128)(2,1)} %get-tuple-element.293.refs_3_), custom_call_target="tpu_custom_call" | custom-call | flops 135895456 | bytes 363724 | tf_op jit(solution)/shard_map/project/pallas_call | solution.py:122
  104.0 13.4 %mix.2 = (f32[192,1024]{1,0:T(8,128)}, f32[192,1024]{1,0:T(8,128)}, f32[192,1024]{1,0:T(8,128)}, f32[5,192,512]{2,1,0:T(8,128)}, f32[5,192,512]{2,1,0:T(8,128)}) custom-call(f32[3,192,1024]{2,1,0:T(8,128)} %bitcast.131, f32[3,192,3]{2,1,0:T(8,128)} %bitcast.145, f32[8,160,384]{2,1,0:T(8,128)} %bitcast.139, ...), custom_call_target="tpu_custom_call" | custom-call | flops 724775744 | bytes 865075 | tf_op jit(solution)/shard_map/mix/pallas_call | solution.py:122
  117.5 1.5 collective-permute-start.14
  121.0 5.4 %arrange.3 = (f32[1024,768]{1,0:T(8,128)}, bf16[1024,768]{1,0:T(8,128)(2,1)}, bf16[1024,768]{1,0:T(8,128)(2,1)}) custom-call(s32[1]{0:T(128)} %bitcast.refs_0_.s_ref, f32[2,256,768]{2,1,0:T(8,128)} %x_ref.3, f32[2,256,768]{2,1,0:T(8,128)} %copy-done.2, f32[2,256,768]{2,1,0:T(8,128)} %collective-permute-done.4.refs_3_, f32[256,768]{1,0:T(8,128)} %copy-done.21, ...), custom_call_target="tpu_custom_call" | custom-call | bytes 471859 | tf_op jit(solution)/shard_map/arrange/pallas_call | solution.py:122
  126.5 6.2 %project.3 = f32[576,1024]{1,0:T(8,128)} custom-call(bf16[576,768]{1,0:T(8,128)(2,1)} %get-tuple-element.196.refs_0_.refs_4_, bf16[576,768]{1,0:T(8,128)(2,1)} %get-tuple-element.197.refs_1_.refs_5_, bf16[1024,768]{1,0:T(8,128)(2,1)} %get-tuple-element.307.refs_2_, bf16[1024,768]{1,0:T(8,128)(2,1)} %get-tuple-element.308.refs_3_), custom_call_target="tpu_custom_call" | custom-call | flops 135895456 | bytes 363724 | tf_op jit(solution)/shard_map/project/pallas_call | solution.py:122
  132.7 14.0 %mix.3 = (f32[192,1024]{1,0:T(8,128)}, f32[192,1024]{1,0:T(8,128)}, f32[192,1024]{1,0:T(8,128)}, f32[5,192,512]{2,1,0:T(8,128)}, f32[5,192,512]{2,1,0:T(8,128)}) custom-call(f32[3,192,1024]{2,1,0:T(8,128)} %bitcast.133, f32[3,192,3]{2,1,0:T(8,128)} %bitcast.146, f32[8,160,384]{2,1,0:T(8,128)} %bitcast.140, ...), custom_call_target="tpu_custom_call" | custom-call | flops 724775744 | bytes 865075 | tf_op jit(solution)/shard_map/mix/pallas_call | solution.py:122
  146.7 6.2 %collective-permute-done.16.refs_4_ = f32[192,1024]{1,0:T(8,128)S(1)} collective-permute-done((f32[192,1024]{1,0:T(8,128)}, f32[192,1024]{1,0:T(8,128)S(1)}, u32[]{:S(2)}, u32[]{:S(2)}) %collective-permute-start.16) | collective-permute-done | bytes 786464 | tf_op jit(solution)/shard_map/ppermute | solution.py:31
  153.8 1.5 collective-permute-start.18
  156.4 8.6 %add_mixer.2.refs_1_.refs_0_ = f32[1024,768]{1,0:T(8,128)} custom-call(f32[1024,768]{1,0:T(8,128)} %get-tuple-element.219.refs_0_, f32[192,1024]{1,0:T(8,128)} %get-tuple-element.208.refs_5_.refs_1_, f32[192,1024]{1,0:T(8,128)} %copy-done.23, f32[192,1024]{1,0:T(8,128)} %copy-done.24, f32[192,1024]{1,0:T(8,128)} %copy-done.25, f32[192,768]{1,0:T(8,128)} %copy-done.1, ...), custom_call_target="tpu_custom_call" | custom-call | flops 181193936 | bytes 589824 | tf_op jit(solution)/shard_map/add_mixer/pallas_call | solution.py:122
  165.0 5.1 %split_units.1 = (bf16[768,1536]{1,0:T(8,128)(2,1)}, bf16[768,1536]{1,0:T(8,128)(2,1)}) custom-call(f32[8,4,24,1536]{3,2,1,0:T(8,128)} %bitcast.144, f32[1024,768]{1,0:T(8,128)} %add_mixer.2.refs_1_.refs_0_), custom_call_target="tpu_custom_call" | custom-call | bytes 471859 | tf_op jit(solution)/shard_map/split_units/pallas_call | solution.py:122
  170.1 12.5 %units_of.1 = (bf16[1024,768]{1,0:T(8,128)(2,1)}, bf16[1024,768]{1,0:T(8,128)(2,1)}) custom-call(f32[1024,768]{1,0:T(8,128)} %add_mixer.2.refs_1_.refs_0_, bf16[768,1536]{1,0:T(8,128)(2,1)} %get-tuple-element.244.refs_1_.refs_12_.refs_2_, bf16[768,1536]{1,0:T(8,128)(2,1)} %get-tuple-element.245.refs_2_.refs_13_.refs_3_), custom_call_target="tpu_custom_call" | custom-call | flops 362387872 | bytes 550502 | tf_op jit(solution)/shard_map/units_of/pallas_call | solution.py:122
  182.6 2.9 split_down.1
  185.5 7.5 %down_of.1 = (f32[256,768]{1,0:T(8,128)}, f32[256,768]{1,0:T(8,128)}, f32[256,768]{1,0:T(8,128)}, f32[256,768]{1,0:T(8,128)}) custom-call(s32[1]{0:T(128)} %bitcast.refs_0_.s_ref, bf16[1024,768]{1,0:T(8,128)(2,1)} %get-tuple-element.229.refs_1_, bf16[1024,768]{1,0:T(8,128)(2,1)} %get-tuple-element.230.refs_2_, ...), custom_call_target="tpu_custom_call" | custom-call | flops 181193936 | bytes 432537 | tf_op jit(solution)/shard_map/down_of/pallas_call | solution.py:122
  194.0 1.5 collective-permute-start.21
  196.3 18.9 %live_back.1 = (f32[256,768]{1,0:T(8,128)}, f32[256,768]{1,0:T(8,128)}, f32[256,768]{1,0:T(8,128)}, f32[256,1536]{1,0:T(8,128)}, f32[160,768]{1,0:T(8,128)}) custom-call(f32[1024,768]{1,0:T(8,128)} %add_mixer.2.refs_1_.refs_0_, f32[1024,768]{1,0:T(8,128)} %get-tuple-element.239.refs_1_.refs_0_, f32[192,1024]{1,0:T(8,128)} %get-tuple-element.218.refs_9_.refs_2_.refs_1_, ...), custom_call_target="tpu_custom_call" | custom-call | flops 226492416 | bytes 786432 | tf_op jit(solution)/shard_map/live_back/pallas_call | solution.py:122
  215.2 7.0 %unit_grads.1.refs_9_ = f32[8,96,2304]{2,1,0:T(8,128)} custom-call(f32[256,768]{1,0:T(8,128)} %get-tuple-element.250.refs_0_, f32[256,1536]{1,0:T(8,128)} %get-tuple-element.251.refs_1_, f32[256,768]{1,0:T(8,128)} %get-tuple-element.252.refs_2_, f32[256,768]{1,0:T(8,128)} %bitcast.136), custom_call_target="tpu_custom_call" | custom-call | flops 135895456 | bytes 353894 | tf_op jit(solution)/shard_map/unit_grads/pallas_call | solution.py:122
  223.5 1.5 collective-permute-start.23
  225.1 8.9 %add_mixer.3.refs_1_ = f32[1024,768]{1,0:T(8,128)} custom-call(f32[1024,768]{1,0:T(8,128)} %get-tuple-element.239.refs_1_.refs_0_, f32[192,1024]{1,0:T(8,128)} %get-tuple-element.218.refs_9_.refs_2_.refs_1_, f32[192,1024]{1,0:T(8,128)} %copy-done.6, f32[192,1024]{1,0:T(8,128)} %copy-done.7, f32[192,1024]{1,0:T(8,128)} %copy-done.8, f32[192,768]{1,0:T(8,128)} %copy-done.1, ...), custom_call_target="tpu_custom_call" | custom-call | flops 181193936 | bytes 589824 | tf_op jit(solution)/shard_map/add_mixer/pallas_call | solution.py:122
  234.7 1.9 collective-permute-start.25
  237.7 16.4 %feed_forward.1 = (f32[256,768]{1,0:T(8,128)}, f32[256,768]{1,0:T(8,128)}, f32[256,768]{1,0:T(8,128)}, f32[256,768]{1,0:T(8,128)}) custom-call(s32[1]{0:T(128)} %bitcast.refs_0_.s_ref, f32[1024,768]{1,0:T(8,128)} %add_mixer.3.refs_1_, bf16[768,1536]{1,0:T(8,128)(2,1)} %get-tuple-element.244.refs_1_.refs_12_.refs_2_, ...), custom_call_target="tpu_custom_call" | custom-call | flops 543581824 | bytes 668467 | tf_op jit(solution)/shard_map/feed_forward/pallas_call | solution.py:122
  255.0 1.5 collective-permute-start.28
  257.7 6.2 %live_mix.1 = (f32[256,768]{1,0:T(8,128)}, f32[192,768]{1,0:T(8,128)}, f32[2,192,128]{2,1,0:T(8,128)}, f32[2,192,128]{2,1,0:T(8,128)}) custom-call(f32[256,768]{1,0:T(8,128)} %get-tuple-element.256.refs_0_, f32[256,768]{1,0:T(8,128)} %bitcast.137, f32[80,768]{1,0:T(8,128)} %copy-done.13, f32[80,768]{1,0:T(8,128)} %copy-done.12, f32[80,768]{1,0:T(8,128)} %copy-done.29, ...), custom_call_target="tpu_custom_call" | custom-call | flops 37748736 | bytes 314572 | tf_op jit(solution)/shard_map/live_mix/pallas_call | solution.py:122
  263.9 24.4 %mix_back.1 = (f32[3,192,1024]{2,1,0:T(8,128)}, f32[3,192,1024]{2,1,0:T(8,128)}, f32[8,5,32,384]{3,2,1,0:T(8,128)}, f32[3,192,128]{2,1,0:T(8,128)}) custom-call(s32[2,128,1]{2,1,0:T(8,128)} %copy.63.refs_10_.refs_11_.refs_0_.at_ref, f32[2,192,128]{2,1,0:T(8,128)} %get-tuple-element.272.refs_1_, f32[2,192,128]{2,1,0:T(8,128)} %get-tuple-element.273.refs_2_, ...), custom_call_target="tpu_custom_call" | custom-call | flops 1449551488 | bytes 1730150 | tf_op jit(solution)/shard_map/mix_back/pallas_call | solution.py:122
  289.4 11.8 %project_back.2 = (f32[256,768]{1,0:T(8,128)}, f32[256,768]{1,0:T(8,128)}, f32[256,768]{1,0:T(8,128)}, f32[256,768]{1,0:T(8,128)}, f32[576,768]{1,0:T(8,128)}) custom-call(s32[1]{0:T(128)} %bitcast.refs_0_.s_ref, f32[576,1024]{1,0:T(8,128)} %bitcast.152, bf16[1024,768]{1,0:T(8,128)(2,1)} %get-tuple-element.292.refs_2_, ...), custom_call_target="tpu_custom_call" | custom-call | flops 271790912 | bytes 697958 | tf_op jit(solution)/shard_map/project_back/pallas_call | solution.py:122
  301.2 4.1 reduce-scatter.4.cloned.1.call-done
  305.4 1.5 collective-permute-start.30
  306.9 1.5 collective-permute-start.31
  309.8 12.0 %project_back.3 = (f32[256,768]{1,0:T(8,128)}, f32[256,768]{1,0:T(8,128)}, f32[256,768]{1,0:T(8,128)}, f32[256,768]{1,0:T(8,128)}, f32[576,768]{1,0:T(8,128)}) custom-call(s32[1]{0:T(128)} %bitcast.refs_0_.s_ref, f32[576,1024]{1,0:T(8,128)} %bitcast.151, bf16[1024,768]{1,0:T(8,128)(2,1)} %get-tuple-element.307.refs_2_, ...), custom_call_target="tpu_custom_call" | custom-call | flops 271790912 | bytes 697958 | tf_op jit(solution)/shard_map/project_back/pallas_call | solution.py:122
  321.9 4.0 turn_back.1
  328.4 1.5 collective-permute-start.32
  329.8 1.5 collective-permute-start.33
  331.9 1.9 add_bitcast_fusion.1
  335.3 1.6 add_bitcast_fusion
  336.9 6.5 %reduce-scatter.8.cloned.1.call-done = f32[160,384]{1,0:T(8,128)} async-done(((f32[1280,384]{1,0:T(8,128)}), f32[160,384]{1,0:T(8,128)}) %reduce-scatter.8.cloned.1.call-update) | async-done | bytes 245776 | tf_op jit(solution)/shard_map/reduce_scatter | solution.py:84
  346.9 2.7 collective-permute-done.36.e3
  349.5 4.1 finish.2.refs_0_
  353.6 11.9 %collective-permute-done.32.e1 = f32[256,768]{1,0:T(8,128)} collective-permute-done((f32[256,768]{1,0:T(8,128)}, f32[256,768]{1,0:T(8,128)}, u32[]{:S(2)}, u32[]{:S(2)}) %collective-permute-start.32) | collective-permute-done | bytes 786464 | tf_op jit(solution)/shard_map/ppermute | solution.py:31
  366.3 13.1 %collective-permute-done.34.e3 = f32[256,768]{1,0:T(8,128)} collective-permute-done((f32[256,768]{1,0:T(8,128)}, f32[256,768]{1,0:T(8,128)}, u32[]{:S(2)}, u32[]{:S(2)}) %collective-permute-start.34) | collective-permute-done | bytes 786464 | tf_op jit(solution)/shard_map/ppermute | solution.py:31
  379.3 3.2 reduce-scatter.6.cloned.1.call-done
  384.4 1.4 collective-permute-start.37
  385.8 1.6 collective-permute-start.38
  389.5 3.8 finish.3
  395.3 3.4 weight_grads.1
  400.2 1.3 reduce
  401.5 1.3 reduce.1
  (221 shorter events, 52.2 us)
Async XLA Ops:
  7.2 62.4 %all-gather.5.cloned.1.call-start = ((), (), s32[]{:S(2)}) async-start(), calls=%async_computation.3 | async-start | bytes 3096576 | tf_op jit(solution)/shard_map/all_gather | solution.py:78
  9.1 6.2 %collective-permute-start = (f32[24,585]{1,0:T(8,128)S(1)}, f32[24,585]{1,0:T(8,128)S(1)}, u32[]{:S(2)}, u32[]{:S(2)}) collective-permute-start(f32[24,585]{1,0:T(8,128)S(1)} %get-tuple-element.400), channel_id=1, source_target_pairs={{0,24},{8,16},{16,8},{24,0},{1,25},{9,17},{17,9},{25,1},{2,26},{10... | collective-permute-start | bytes 168488 | tf_op jit(solution)/shard_map/ppermute | solution.py:31
  13.1 4.2 %collective-permute-start.1 = (f32[24,585]{1,0:T(8,128)S(1)}, f32[24,585]{1,0:T(8,128)S(1)}, u32[]{:S(2)}, u32[]{:S(2)}) collective-permute-start(f32[24,585]{1,0:T(8,128)S(1)} %get-tuple-element.401), channel_id=1, source_target_pairs={{0,16},{8,24},{16,0},{24,8},{1,17},{9,25},{17,1},{25,9},{2,18},{10... | collective-permute-start | bytes 168488 | tf_op jit(solution)/shard_map/ppermute | solution.py:31
  13.6 4.2 %collective-permute-start.2 = (f32[24,585]{1,0:T(8,128)S(1)}, f32[24,585]{1,0:T(8,128)S(1)}, u32[]{:S(2)}, u32[]{:S(2)}) collective-permute-start(f32[24,585]{1,0:T(8,128)S(1)} %get-tuple-element.402), channel_id=1, source_target_pairs={{0,8},{8,0},{16,24},{24,16},{1,9},{9,1},{17,25},{25,17},{2,10},{10... | collective-permute-start | bytes 168488 | tf_op jit(solution)/shard_map/ppermute | solution.py:31
  18.8 35.9 %copy-start.11 = (f32[24,3072]{1,0:T(8,128)S(1)}, f32[24,3072]{1,0:T(8,128)}, u32[]{:S(2)}) copy-start(f32[24,3072]{1,0:T(8,128)} %refs_8_.1) | copy-start | bytes 884740
  18.8 35.9 %copy-start.35 = (f32[24]{0:T(128)S(1)}, f32[24]{0:T(128)}, u32[]{:S(2)}) copy-start(f32[24]{0:T(128)} %param.21) | copy-start | bytes 292
  18.8 85.2 %all-gather.7.cloned.1.call-start = ((), (), s32[]{:S(2)}) async-start(), calls=%async_computation.4 | async-start | bytes 2211840 | tf_op jit(solution)/shard_map/all_gather | solution.py:78
  18.9 34.8 %collective-permute-start.3 = (f32[2,256,768]{2,1,0:T(8,128)S(1)}, f32[2,256,768]{2,1,0:T(8,128)S(1)}, u32[]{:S(2)}, u32[]{:S(2)}) collective-permute-start(f32[2,256,768]{2,1,0:T(8,128)S(1)} %copy-done), channel_id=1, source_target_pairs={{0,8},{8,0},{16,24},{24,16},{1,9},{9,1},{17,25},{25,17},{2,10},{10... | collective-permute-start | bytes 4718600 | tf_op jit(solution)/shard_map/ppermute | solution.py:31
  19.3 35.3 %collective-permute-start.4 = (f32[2,256,768]{2,1,0:T(8,128)S(1)}, f32[2,256,768]{2,1,0:T(8,128)}, u32[]{:S(2)}, u32[]{:S(2)}) collective-permute-start(f32[2,256,768]{2,1,0:T(8,128)S(1)} %copy-done), channel_id=1, source_target_pairs={{0,16},{8,24},{16,0},{24,8},{1,17},{9,25},{17,1},{25,9},{2,18},{10... | collective-permute-start | bytes 4718600 | tf_op jit(solution)/shard_map/ppermute | solution.py:31
  26.6 16.0 %collective-permute-start.5 = (f32[2,32,3,192]{3,2,1,0:T(4,128)}, f32[2,32,3,192]{3,2,1,0:T(4,128)S(1)}, u32[]{:S(2)}, u32[]{:S(2)}) collective-permute-start(f32[2,32,3,192]{3,2,1,0:T(4,128)} %rev.6), channel_id=1, source_target_pairs={{0,7},{1,6},{2,5},{3,4},{4,3},{5,2},{6,1},{7,0},{8,15},{9,14},{10,... | collective-permute-start | bytes 442376 | tf_op jit(solution)/shard_map/ppermute | solution.py:897
  53.7 7.6 %copy-start.2 = (f32[2,256,768]{2,1,0:T(8,128)}, f32[2,256,768]{2,1,0:T(8,128)S(1)}, u32[]{:S(2)}) copy-start(f32[2,256,768]{2,1,0:T(8,128)S(1)} %collective-permute-done.3.refs_2_) | copy-start | bytes 4718596
  54.6 110.4 %all-gather.9.cloned.1.call-start = ((), (), s32[]{:S(2)}) async-start(), calls=%async_computation.5 | async-start | bytes 5308416 | tf_op jit(solution)/shard_map/all_gather | solution.py:78
  57.7 7.4 %collective-permute-start.10 = (f32[24,1536]{1,0:T(8,128)S(1)}, f32[24,1536]{1,0:T(8,128)S(1)}, u32[]{:S(2)}, u32[]{:S(2)}) collective-permute-start(f32[24,1536]{1,0:T(8,128)S(1)} %get-tuple-element.390), channel_id=1, source_target_pairs={{0,8},{8,0},{16,24},{24,16},{1,9},{9,1},{17,25},{25,17},{2,10},{10... | collective-permute-start | bytes 442376 | tf_op jit(solution)/shard_map/ppermute | solution.py:31
  58.8 8.0 %collective-permute-start.8 = (f32[24,1536]{1,0:T(8,128)S(1)}, f32[24,1536]{1,0:T(8,128)S(1)}, u32[]{:S(2)}, u32[]{:S(2)}) collective-permute-start(f32[24,1536]{1,0:T(8,128)S(1)} %get-tuple-element.389), channel_id=1, source_target_pairs={{0,24},{8,16},{16,8},{24,0},{1,25},{9,17},{17,9},{25,1},{2,26},{10... | collective-permute-start | bytes 442376 | tf_op jit(solution)/shard_map/ppermute | solution.py:31
  60.5 8.1 %collective-permute-start.9 = (f32[24,1536]{1,0:T(8,128)S(1)}, f32[24,1536]{1,0:T(8,128)S(1)}, u32[]{:S(2)}, u32[]{:S(2)}) collective-permute-start(f32[24,1536]{1,0:T(8,128)S(1)} %get-tuple-element.391), channel_id=1, source_target_pairs={{0,16},{8,24},{16,0},{24,8},{1,17},{9,25},{17,1},{25,9},{2,18},{10... | collective-permute-start | bytes 442376 | tf_op jit(solution)/shard_map/ppermute | solution.py:31
  61.3 22.0 %collective-permute-start.6 = (f32[256,768]{1,0:T(8,128)S(1)}, f32[256,768]{1,0:T(8,128)}, u32[]{:S(2)}, u32[]{:S(2)}) collective-permute-start(f32[256,768]{1,0:T(8,128)S(1)} %slice_bitcast_fusion.2), channel_id=1, source_target_pairs={{0,16},{8,24},{16,0},{24,8},{1,17},{9,25},{17,1},{25,9},{2,18},{10... | collective-permute-start | bytes 2359304 | tf_op jit(solution)/shard_map/ppermute | solution.py:31
  63.9 19.5 %collective-permute-start.7 = (f32[256,768]{1,0:T(8,128)S(1)}, f32[256,768]{1,0:T(8,128)S(1)}, u32[]{:S(2)}, u32[]{:S(2)}) collective-permute-start(f32[256,768]{1,0:T(8,128)S(1)} %slice_bitcast_fusion.1), channel_id=1, source_target_pairs={{0,8},{8,0},{16,24},{24,16},{1,9},{9,1},{17,25},{25,17},{2,10},{10... | collective-permute-start | bytes 2359304 | tf_op jit(solution)/shard_map/ppermute | solution.py:31
  83.4 99.2 %all-gather.11.cloned.1.call-start = ((), (), s32[]{:S(2)}) async-start(), calls=%async_computation.6 | async-start | bytes 2654208 | tf_op jit(solution)/shard_map/all_gather | solution.py:78
  84.0 221.3 %reduce-scatter.4.cloned.1.call-start = ((), (), s32[]{:S(2)}) async-start(), calls=%async_computation.7 | async-start | bytes 7962624 | tf_op jit(solution)/shard_map/reduce_scatter | solution.py:84
  86.4 11.5 %copy-start.1 = (f32[192,768]{1,0:T(8,128)}, f32[192,768]{1,0:T(8,128)S(1)}, u32[]{:S(2)}) copy-start(f32[192,768]{1,0:T(8,128)S(1)} %reshape.158.refs_5_.refs_6_) | copy-start | bytes 1769476
  86.4 31.0 %collective-permute-start.11 = (f32[192,768]{1,0:T(8,128)S(1)}, f32[192,768]{1,0:T(8,128)S(1)}, u32[]{:S(2)}, u32[]{:S(2)}) collective-permute-start(f32[192,768]{1,0:T(8,128)S(1)} %reshape.158.refs_5_.refs_6_), channel_id=1, source_target_pairs={{0,8},{8,0},{16,24},{24,16},{1,9},{9,1},{17,25},{25,17},{2,10},{10... | collective-permute-start | bytes 1769480 | tf_op jit(solution)/shard_map/ppermute | solution.py:31
  87.5 30.0 %collective-permute-start.12 = (f32[192,768]{1,0:T(8,128)S(1)}, f32[192,768]{1,0:T(8,128)S(1)}, u32[]{:S(2)}, u32[]{:S(2)}) collective-permute-start(f32[192,768]{1,0:T(8,128)S(1)} %reshape.158.refs_5_.refs_6_), channel_id=1, source_target_pairs={{0,16},{8,24},{16,0},{24,8},{1,17},{9,25},{17,1},{25,9},{2,18},{10... | collective-permute-start | bytes 1769480 | tf_op jit(solution)/shard_map/ppermute | solution.py:31
  88.5 28.9 %collective-permute-start.13 = (f32[192,768]{1,0:T(8,128)S(1)}, f32[192,768]{1,0:T(8,128)S(1)}, u32[]{:S(2)}, u32[]{:S(2)}) collective-permute-start(f32[192,768]{1,0:T(8,128)S(1)} %reshape.158.refs_5_.refs_6_), channel_id=1, source_target_pairs={{0,24},{8,16},{16,8},{24,0},{1,25},{9,17},{17,9},{25,1},{2,26},{10... | collective-permute-start | bytes 1769480 | tf_op jit(solution)/shard_map/ppermute | solution.py:31
  117.4 9.0 %copy-start.3 = (f32[192,768]{1,0:T(8,128)}, f32[192,768]{1,0:T(8,128)S(1)}, u32[]{:S(2)}) copy-start(f32[192,768]{1,0:T(8,128)S(1)} %collective-permute-done.11.refs_6_.refs_7_) | copy-start | bytes 1769476
  117.4 9.0 %copy-start.4 = (f32[192,768]{1,0:T(8,128)}, f32[192,768]{1,0:T(8,128)S(1)}, u32[]{:S(2)}) copy-start(f32[192,768]{1,0:T(8,128)S(1)} %collective-permute-done.12.refs_7_.refs_8_) | copy-start | bytes 1769476
  117.4 9.0 %copy-start.5 = (f32[192,768]{1,0:T(8,128)}, f32[192,768]{1,0:T(8,128)S(1)}, u32[]{:S(2)}) copy-start(f32[192,768]{1,0:T(8,128)S(1)} %collective-permute-done.13.refs_8_.refs_9_) | copy-start | bytes 1769476
  117.5 29.2 %collective-permute-start.14 = (f32[192,1024]{1,0:T(8,128)}, f32[192,1024]{1,0:T(8,128)S(1)}, u32[]{:S(2)}, u32[]{:S(2)}) collective-permute-start(f32[192,1024]{1,0:T(8,128)} %get-tuple-element.208.refs_5_.refs_1_), channel_id=1, source_target_pairs={{0,8},{8,0},{16,24},{24,16},{1,9},{9,1},{17,25},{25,17},{2,10},{10... | collective-permute-start | bytes 2359304 | tf_op jit(solution)/shard_map/ppermute | solution.py:31
  118.9 27.7 %collective-permute-start.15 = (f32[192,1024]{1,0:T(8,128)}, f32[192,1024]{1,0:T(8,128)S(1)}, u32[]{:S(2)}, u32[]{:S(2)}) collective-permute-start(f32[192,1024]{1,0:T(8,128)} %get-tuple-element.208.refs_5_.refs_1_), channel_id=1, source_target_pairs={{0,16},{8,24},{16,0},{24,8},{1,17},{9,25},{17,1},{25,9},{2,18},{10... | collective-permute-start | bytes 2359304 | tf_op jit(solution)/shard_map/ppermute | solution.py:31
  120.1 32.9 %collective-permute-start.16 = (f32[192,1024]{1,0:T(8,128)}, f32[192,1024]{1,0:T(8,128)S(1)}, u32[]{:S(2)}, u32[]{:S(2)}) collective-permute-start(f32[192,1024]{1,0:T(8,128)} %get-tuple-element.208.refs_5_.refs_1_), channel_id=1, source_target_pairs={{0,24},{8,16},{16,8},{24,0},{1,25},{9,17},{17,9},{25,1},{2,26},{10... | collective-permute-start | bytes 2359304 | tf_op jit(solution)/shard_map/ppermute | solution.py:31
  146.7 9.8 %copy-start.23 = (f32[192,1024]{1,0:T(8,128)}, f32[192,1024]{1,0:T(8,128)S(1)}, u32[]{:S(2)}) copy-start(f32[192,1024]{1,0:T(8,128)S(1)} %collective-permute-done.14.refs_2_) | copy-start | bytes 2359300
  146.7 9.7 %copy-start.24 = (f32[192,1024]{1,0:T(8,128)}, f32[192,1024]{1,0:T(8,128)S(1)}, u32[]{:S(2)}) copy-start(f32[192,1024]{1,0:T(8,128)S(1)} %collective-permute-done.15.refs_3_) | copy-start | bytes 2359300
  152.9 40.1 %collective-permute-start.17 = (f32[192,1024]{1,0:T(8,128)}, f32[192,1024]{1,0:T(8,128)S(1)}, u32[]{:S(2)}, u32[]{:S(2)}) collective-permute-start(f32[192,1024]{1,0:T(8,128)} %get-tuple-element.218.refs_9_.refs_2_.refs_1_), channel_id=1, source_target_pairs={{0,8},{8,0},{16,24},{24,16},{1,9},{9,1},{17,25},{25,17},{2,10},{10... | collective-permute-start | bytes 2359304 | tf_op jit(solution)/shard_map/ppermute | solution.py:31
  153.8 39.3 %collective-permute-start.18 = (f32[192,1024]{1,0:T(8,128)}, f32[192,1024]{1,0:T(8,128)S(1)}, u32[]{:S(2)}, u32[]{:S(2)}) collective-permute-start(f32[192,1024]{1,0:T(8,128)} %get-tuple-element.218.refs_9_.refs_2_.refs_1_), channel_id=1, source_target_pairs={{0,16},{8,24},{16,0},{24,8},{1,17},{9,25},{17,1},{25,9},{2,18},{10... | collective-permute-start | bytes 2359304 | tf_op jit(solution)/shard_map/ppermute | solution.py:31
  155.3 37.8 %collective-permute-start.19 = (f32[192,1024]{1,0:T(8,128)}, f32[192,1024]{1,0:T(8,128)S(1)}, u32[]{:S(2)}, u32[]{:S(2)}) collective-permute-start(f32[192,1024]{1,0:T(8,128)} %get-tuple-element.218.refs_9_.refs_2_.refs_1_), channel_id=1, source_target_pairs={{0,24},{8,16},{16,8},{24,0},{1,25},{9,17},{17,9},{25,1},{2,26},{10... | collective-permute-start | bytes 2359304 | tf_op jit(solution)/shard_map/ppermute | solution.py:31
  193.1 29.1 %collective-permute-start.20 = (f32[256,768]{1,0:T(8,128)}, f32[256,768]{1,0:T(8,128)S(1)}, u32[]{:S(2)}, u32[]{:S(2)}) collective-permute-start(f32[256,768]{1,0:T(8,128)} %get-tuple-element.254), channel_id=1, source_target_pairs={{0,8},{8,0},{16,24},{24,16},{1,9},{9,1},{17,25},{25,17},{2,10},{10... | collective-permute-start | bytes 2359304 | tf_op jit(solution)/shard_map/ppermute | solution.py:31
  194.0 28.3 %collective-permute-start.21 = (f32[256,768]{1,0:T(8,128)}, f32[256,768]{1,0:T(8,128)}, u32[]{:S(2)}, u32[]{:S(2)}) collective-permute-start(f32[256,768]{1,0:T(8,128)} %get-tuple-element.255), channel_id=1, source_target_pairs={{0,16},{8,24},{16,0},{24,8},{1,17},{9,25},{17,1},{25,9},{2,18},{10... | collective-permute-start | bytes 2359304 | tf_op jit(solution)/shard_map/ppermute | solution.py:31
  222.3 121.1 %reduce-scatter.8.cloned.1.call-start = ((), (), s32[]{:S(2)}) async-start(), calls=%async_computation.9 | async-start | bytes 2211840 | tf_op jit(solution)/shard_map/reduce_scatter | solution.py:84
  223.3 10.7 %collective-permute-start.22 = (f32[80,768]{1,0:T(8,128)S(1)}, f32[80,768]{1,0:T(8,128)S(1)}, u32[]{:S(2)}, u32[]{:S(2)}) collective-permute-start(f32[80,768]{1,0:T(8,128)S(1)} %get-tuple-element.395), channel_id=1, source_target_pairs={{0,8},{8,0},{16,24},{24,16},{1,9},{9,1},{17,25},{25,17},{2,10},{10... | collective-permute-start | bytes 737288 | tf_op jit(solution)/shard_map/ppermute | solution.py:31
  223.5 13.0 %copy-start.40 = (f32[256,768]{1,0:T(8,128)S(1)}, f32[256,768]{1,0:T(8,128)}, u32[]{:S(2)}) copy-start(f32[256,768]{1,0:T(8,128)} %get-tuple-element.287) | copy-start | bytes 2359300
  223.5 10.5 %collective-permute-start.23 = (f32[80,768]{1,0:T(8,128)S(1)}, f32[80,768]{1,0:T(8,128)S(1)}, u32[]{:S(2)}, u32[]{:S(2)}) collective-permute-start(f32[80,768]{1,0:T(8,128)S(1)} %get-tuple-element.394), channel_id=1, source_target_pairs={{0,16},{8,24},{16,0},{24,8},{1,17},{9,25},{17,1},{25,9},{2,18},{10... | collective-permute-start | bytes 737288 | tf_op jit(solution)/shard_map/ppermute | solution.py:31
  234.1 20.0 %copy-start.12 = (f32[80,768]{1,0:T(8,128)}, f32[80,768]{1,0:T(8,128)S(1)}, u32[]{:S(2)}) copy-start(f32[80,768]{1,0:T(8,128)S(1)} %get-tuple-element.392.refs_3_) | copy-start | bytes 737284
  234.1 20.0 %copy-start.13 = (f32[80,768]{1,0:T(8,128)}, f32[80,768]{1,0:T(8,128)S(1)}, u32[]{:S(2)}) copy-start(f32[80,768]{1,0:T(8,128)S(1)} %get-tuple-element.393.refs_2_) | copy-start | bytes 737284
  234.1 20.0 %collective-permute-start.24 = (f32[80,768]{1,0:T(8,128)S(1)}, f32[80,768]{1,0:T(8,128)S(1)}, u32[]{:S(2)}, u32[]{:S(2)}) collective-permute-start(f32[80,768]{1,0:T(8,128)S(1)} %get-tuple-element.393.refs_2_), channel_id=1, source_target_pairs={{0,16},{8,24},{16,0},{24,8},{1,17},{9,25},{17,1},{25,9},{2,18},{10... | collective-permute-start | bytes 737288 | tf_op jit(solution)/shard_map/ppermute | solution.py:31
  234.7 19.5 %collective-permute-start.25 = (f32[80,768]{1,0:T(8,128)S(1)}, f32[80,768]{1,0:T(8,128)S(1)}, u32[]{:S(2)}, u32[]{:S(2)}) collective-permute-start(f32[80,768]{1,0:T(8,128)S(1)} %get-tuple-element.392.refs_3_), channel_id=1, source_target_pairs={{0,8},{8,0},{16,24},{24,16},{1,9},{9,1},{17,25},{25,17},{2,10},{10... | collective-permute-start | bytes 737288 | tf_op jit(solution)/shard_map/ppermute | solution.py:31
  236.5 51.8 %collective-permute-start.26 = (f32[256,768]{1,0:T(8,128)S(1)}, f32[256,768]{1,0:T(8,128)S(1)}, u32[]{:S(2)}, u32[]{:S(2)}) collective-permute-start(f32[256,768]{1,0:T(8,128)S(1)} %copy-done.40), channel_id=1, source_target_pairs={{0,24},{8,16},{16,8},{24,0},{1,25},{9,17},{17,9},{25,1},{2,26},{10... | collective-permute-start | bytes 2359304 | tf_op jit(solution)/shard_map/ppermute | solution.py:31
  254.2 34.2 %collective-permute-start.27 = (f32[256,768]{1,0:T(8,128)}, f32[256,768]{1,0:T(8,128)S(1)}, u32[]{:S(2)}, u32[]{:S(2)}) collective-permute-start(f32[256,768]{1,0:T(8,128)} %get-tuple-element.289), channel_id=1, source_target_pairs={{0,8},{8,0},{16,24},{24,16},{1,9},{9,1},{17,25},{25,17},{2,10},{10... | collective-permute-start | bytes 2359304 | tf_op jit(solution)/shard_map/ppermute | solution.py:31
  255.0 34.3 %collective-permute-start.28 = (f32[256,768]{1,0:T(8,128)}, f32[256,768]{1,0:T(8,128)S(1)}, u32[]{:S(2)}, u32[]{:S(2)}) collective-permute-start(f32[256,768]{1,0:T(8,128)} %get-tuple-element.290), channel_id=1, source_target_pairs={{0,16},{8,24},{16,0},{24,8},{1,17},{9,25},{17,1},{25,9},{2,18},{10... | collective-permute-start | bytes 2359304 | tf_op jit(solution)/shard_map/ppermute | solution.py:31
  256.6 44.7 %collective-permute-start.29 = (f32[256,768]{1,0:T(8,128)}, f32[256,768]{1,0:T(8,128)}, u32[]{:S(2)}, u32[]{:S(2)}) collective-permute-start(f32[256,768]{1,0:T(8,128)} %get-tuple-element.302), channel_id=1, source_target_pairs={{0,24},{8,16},{16,8},{24,0},{1,25},{9,17},{17,9},{25,1},{2,26},{10... | collective-permute-start | bytes 2359304 | tf_op jit(solution)/shard_map/ppermute | solution.py:31
  288.3 12.9 %copy-start.16 = (f32[256,768]{1,0:T(8,128)}, f32[256,768]{1,0:T(8,128)S(1)}, u32[]{:S(2)}) copy-start(f32[256,768]{1,0:T(8,128)S(1)} %collective-permute-done.26) | copy-start | bytes 2359300
  288.3 12.9 %copy-start.17 = (f32[256,768]{1,0:T(8,128)}, f32[256,768]{1,0:T(8,128)S(1)}, u32[]{:S(2)}) copy-start(f32[256,768]{1,0:T(8,128)S(1)} %collective-permute-done.27) | copy-start | bytes 2359300
  289.4 11.8 %copy-start.19 = (f32[256,768]{1,0:T(8,128)}, f32[256,768]{1,0:T(8,128)S(1)}, u32[]{:S(2)}) copy-start(f32[256,768]{1,0:T(8,128)S(1)} %collective-permute-done.28) | copy-start | bytes 2359300
  301.2 7.1 %copy-start.27 = (f32[3,192,128]{2,1,0:T(8,128)S(1)}, f32[3,192,128]{2,1,0:T(8,128)}, u32[]{:S(2)}) copy-start(f32[3,192,128]{2,1,0:T(8,128)} %get-tuple-element.281) | copy-start | bytes 884740
  305.3 77.3 %reduce-scatter.6.cloned.1.call-start = ((), (), s32[]{:S(2)}) async-start(), calls=%async_computation.8 | async-start | bytes 3096576 | tf_op jit(solution)/shard_map/reduce_scatter | solution.py:84
  305.4 20.5 %collective-permute-start.30 = (f32[256,768]{1,0:T(8,128)}, f32[256,768]{1,0:T(8,128)S(1)}, u32[]{:S(2)}, u32[]{:S(2)}) collective-permute-start(f32[256,768]{1,0:T(8,128)} %get-tuple-element.304), channel_id=1, source_target_pairs={{0,8},{8,0},{16,24},{24,16},{1,9},{9,1},{17,25},{25,17},{2,10},{10... | collective-permute-start | bytes 2359304 | tf_op jit(solution)/shard_map/ppermute | solution.py:31
  306.9 18.9 %collective-permute-start.31 = (f32[256,768]{1,0:T(8,128)}, f32[256,768]{1,0:T(8,128)}, u32[]{:S(2)}, u32[]{:S(2)}) collective-permute-start(f32[256,768]{1,0:T(8,128)} %get-tuple-element.305), channel_id=1, source_target_pairs={{0,16},{8,24},{16,0},{24,8},{1,17},{9,25},{17,1},{25,9},{2,18},{10... | collective-permute-start | bytes 2359304 | tf_op jit(solution)/shard_map/ppermute | solution.py:31
  327.8 21.7 %collective-permute-start.36 = (f32[256,768]{1,0:T(8,128)}, f32[256,768]{1,0:T(8,128)}, u32[]{:S(2)}, u32[]{:S(2)}) collective-permute-start(f32[256,768]{1,0:T(8,128)} %get-tuple-element.334), channel_id=1, source_target_pairs={{0,24},{8,16},{16,8},{24,0},{1,25},{9,17},{17,9},{25,1},{2,26},{10... | collective-permute-start | bytes 2359304 | tf_op jit(solution)/shard_map/ppermute | solution.py:31
  328.4 37.1 %collective-permute-start.32 = (f32[256,768]{1,0:T(8,128)}, f32[256,768]{1,0:T(8,128)}, u32[]{:S(2)}, u32[]{:S(2)}) collective-permute-start(f32[256,768]{1,0:T(8,128)} %get-tuple-element.318), channel_id=1, source_target_pairs={{0,8},{8,0},{16,24},{24,16},{1,9},{9,1},{17,25},{25,17},{2,10},{10... | collective-permute-start | bytes 2359304 | tf_op jit(solution)/shard_map/ppermute | solution.py:31
  329.8 36.4 %collective-permute-start.33 = (f32[256,768]{1,0:T(8,128)}, f32[256,768]{1,0:T(8,128)}, u32[]{:S(2)}, u32[]{:S(2)}) collective-permute-start(f32[256,768]{1,0:T(8,128)} %get-tuple-element.319), channel_id=1, source_target_pairs={{0,16},{8,24},{16,0},{24,8},{1,17},{9,25},{17,1},{25,9},{2,18},{10... | collective-permute-start | bytes 2359304 | tf_op jit(solution)/shard_map/ppermute | solution.py:31
  331.3 48.0 %collective-permute-start.34 = (f32[256,768]{1,0:T(8,128)}, f32[256,768]{1,0:T(8,128)}, u32[]{:S(2)}, u32[]{:S(2)}) collective-permute-start(f32[256,768]{1,0:T(8,128)} %get-tuple-element.320), channel_id=1, source_target_pairs={{0,24},{8,16},{16,8},{24,0},{1,25},{9,17},{17,9},{25,1},{2,26},{10... | collective-permute-start | bytes 2359304 | tf_op jit(solution)/shard_map/ppermute | solution.py:31
  344.7 34.7 %collective-permute-start.35 = (f32[2,32,3,192]{3,0,1,2:T(2,128)S(1)}, f32[2,32,3,192]{3,0,1,2:T(2,128)S(1)}, u32[]{:S(2)}, u32[]{:S(2)}) collective-permute-start(f32[2,32,3,192]{3,0,1,2:T(2,128)S(1)} %rev.7), channel_id=1, source_target_pairs={{0,7},{1,6},{2,5},{3,4},{4,3},{5,2},{6,1},{7,0},{8,15},{9,14},{10,... | collective-permute-start | bytes 442376 | tf_op jit(solution)/shard_map/ppermute | solution.py:995
  346.8 36.7 %slice-start = ((f32[96,2304]{1,0:T(8,128)}), f32[96,1536]{1,0:T(8,128)S(1)}, s32[]{:S(2)}) async-start(f32[96,2304]{1,0:T(8,128)} %reduce-scatter.4.cloned.1.call-done), calls=%async_computation.10 | async-start | bytes 1179648 | tf_op jit(solution)/shard_map/slice | solution.py:998
  384.4 9.0 %collective-permute-start.37 = (f32[24,2176]{1,0:T(8,128)S(1)}, f32[24,2176]{1,0:T(8,128)S(1)}, u32[]{:S(2)}, u32[]{:S(2)}) collective-permute-start(f32[24,2176]{1,0:T(8,128)S(1)} %get-tuple-element.387), channel_id=1, source_target_pairs={{0,8},{8,0},{16,24},{24,16},{1,9},{9,1},{17,25},{25,17},{2,10},{10... | collective-permute-start | bytes 626696 | tf_op jit(solution)/shard_map/ppermute | solution.py:31
  385.8 8.8 %collective-permute-start.38 = (f32[24,2176]{1,0:T(8,128)S(1)}, f32[24,2176]{1,0:T(8,128)S(1)}, u32[]{:S(2)}, u32[]{:S(2)}) collective-permute-start(f32[24,2176]{1,0:T(8,128)S(1)} %get-tuple-element.386), channel_id=1, source_target_pairs={{0,16},{8,24},{16,0},{24,8},{1,17},{9,25},{17,1},{25,9},{2,18},{10... | collective-permute-start | bytes 626696 | tf_op jit(solution)/shard_map/ppermute | solution.py:31
  387.4 7.2 %collective-permute-start.39 = (f32[24,2176]{1,0:T(8,128)S(1)}, f32[24,2176]{1,0:T(8,128)S(1)}, u32[]{:S(2)}, u32[]{:S(2)}) collective-permute-start(f32[24,2176]{1,0:T(8,128)S(1)} %get-tuple-element.385), channel_id=1, source_target_pairs={{0,24},{8,16},{16,8},{24,0},{1,25},{9,17},{17,9},{25,1},{2,26},{10... | collective-permute-start | bytes 626696 | tf_op jit(solution)/shard_map/ppermute | solution.py:31
  (26 other events, 85.8 us)
Sparse Core Ops, SparseCore 0:
  18.9 46.6 all-gather.4
  67.8 26.2 all-gather.6
  95.8 51.2 all-gather.8
  148.5 30.4 all-gather.10
  222.4 82.8 reduce-scatter.3
  307.5 35.8 reduce-scatter.7
  345.8 36.7 reduce-scatter.5

commit v5 on v4

--- a/solution.py
+++ b/solution.py
@@ -167,24 +167,27 @@
     return out
 
 
-def turn_in(gathered, channels):
-    groups, shards, rows, _ = gathered.shape
+def turn_in(gathered, channels, split, after=()):
+    groups, shards, rows, columns = gathered.shape
     width = groups * shards * rows
+    own = columns - split
     wide = -(-channels // 128) * 128
 
-    def kernel(w_ref, high_ref, low_ref, flat_ref):
+    def kernel(w_ref, high_ref, low_ref, out_ref, flat_ref):
         flat_ref[:, channels // 128 * 128 :] = jnp.zeros((width, wide - channels // 128 * 128), F32)
         for k in range(shards):
             for j in range(groups):
                 at = (k * groups + j) * rows
                 flat_ref[at : at + rows, :channels] = w_ref[j, k, :, :channels]
+                out_ref[j * rows : (j + 1) * rows, k * own : (k + 1) * own] = w_ref[j, k, :, split:]
         turned = flat_ref[...].T
         high_ref[...], low_ref[...] = halves(turned[:channels])
 
     return call(
         kernel, "turn_in", 0, 4 * 2 * width * wide, [gathered], [whole(*gathered.shape)],
-        [shaped(channels, width, dtype=BF16)] * 2, [whole(channels, width)] * 2,
-        scratch=[pltpu.VMEM((width, wide), F32)],
+        [shaped(channels, width, dtype=BF16)] * 2 + [shaped(groups * rows, width)],
+        [whole(channels, width)] * 2 + [whole(groups * rows, width)],
+        scratch=[pltpu.VMEM((width, wide), F32)], after=after,
     )
 
 
@@ -595,9 +598,12 @@
         for i, ref in enumerate((*r_refs, x_ref)):
             pick = chosen(at_ref.at[i], slots, length)
             live_ref[i * slots : (i + 1) * slots] = chosen_rows(pick, halves(ref[...]), NN)
-        mixed = jnp.concatenate([chosen_rows(pick, halves(ref[...]), NT) for ref in g_refs], axis=1)
+        mixed = []
+        for ref in g_refs:
+            parts = [lax.dot_general(v, pick, (NT, ((), ())), preferred_element_type=F32) for v in halves(ref[...])]
+            mixed.append(parts[0] + parts[1])
         weight = jnp.concatenate([ref[...] for ref in w_refs], axis=0)
-        live_ref[rows - slots :] += dot(halves(mixed), halves(weight), NN)
+        live_ref[rows - slots :] += dot(halves(jnp.concatenate(mixed, axis=0)), halves(weight), TN)
         n = normed(live_ref[...])[0]
         n_ref[...] = n
         gate_up = dot(halves(n), (wh[...], wl[...]), NN)
@@ -793,6 +799,13 @@
     )(s.reshape(1), *inputs)
 
 
+def lanes_summed(value):
+    return lax.dot_general(
+        jnp.ones((8, value.shape[1]), F32), value, (NT, ((), ())),
+        precision=lax.Precision.HIGHEST, preferred_element_type=F32,
+    )
+
+
 def weight_grads(pieces, s, gain_one, gain_two, w_in, w_gate, w_up, own, units):
     rows, columns = pieces[0].shape
     start = columns - 2 * units
@@ -810,26 +823,26 @@
 
             @pl.when(s_ref[0] == index)
             def _(index=index):
-                sum_one = jnp.zeros((rows, 1), F32)
-                sum_two = jnp.zeros((rows, 1), F32)
+                sum_one = jnp.zeros((8, rows), F32)
+                sum_two = jnp.zeros((8, rows), F32)
                 for d, p_ref in enumerate(p_refs):
                     k = index ^ d
                     for j in range(3):
                         at = slice((j * shards + k) * own, (j * shards + k + 1) * own)
                         part = p_ref[:, j * own : (j + 1) * own]
-                        sum_one += jnp.sum(wi_ref[:, at] * part, axis=1, keepdims=True)
+                        sum_one += lanes_summed(wi_ref[:, at] * part)
                         di_ref[:, at] = one * part
                     at = slice(k * units, (k + 1) * units)
                     for j, (w_ref, d_ref) in enumerate(((wg_ref, dg_ref), (wu_ref, du_ref))):
                         part = p_ref[:, start + j * units : start + (j + 1) * units]
-                        sum_two += jnp.sum(w_ref[:, at] * part, axis=1, keepdims=True)
+                        sum_two += lanes_summed(w_ref[:, at] * part)
                         d_ref[:, at] = two * part
                 g1_ref[...] = sum_one
                 g2_ref[...] = sum_two
 
     inputs = [*pieces, gain_one[:, None], gain_two[:, None], w_in, w_gate, w_up]
     wide = start - 3 * own // 128 * 128
-    outs = [w_in.shape, w_gate.shape, w_up.shape, (rows, 1), (rows, 1), (rows, wide)]
+    outs = [w_in.shape, w_gate.shape, w_up.shape, (8, rows), (8, rows), (rows, wide)]
     return call(
         kernel, "weight_grads", 0, 0, inputs, [whole(*v.shape) for v in inputs],
         [shaped(*v) for v in outs], [whole(*v) for v in outs], scalars=[s.reshape(1)],
@@ -902,13 +915,15 @@
     far = [swap(near[0][0], "seq", 2), swap(near[1][1], "seq", 1)]
     w_units = jnp.stack([gain_two[:, None] * w_gate_now, gain_two[:, None] * w_up_now], axis=1)
     w_units = w_units.reshape(rows, 2, shards, units).transpose(0, 2, 1, 3).reshape(rows, shards, 2 * units)
-    w_turned = turn_in(w_pre, 3 * own)
-    far, w_units, w_turned, w_pre, w_down_now = together(far, columns_out(w_units, s), w_turned, w_pre, w_down)
+    *w_turned, w_out_own = turn_in(w_pre, 3 * own, split)
+    taps = w_pre[..., 3 * own : split]
+    far, w_units, w_turned, w_out_own, taps, w_down_now = together(
+        far, columns_out(w_units, s), w_turned, w_out_own, taps, w_down
+    )
     w_units = over_batch(w_units.reshape(shards * rows, 2 * units))
     w_down_own = over_batch(w_down_now).reshape(units, width)
 
-    w_out_own = w_pre[..., split:].transpose(0, 2, 1, 3).reshape(own, width)
-    taps = w_pre[..., 3 * own : split].reshape(groups, shards, 3, count).transpose(2, 1, 0, 3)
+    taps = taps.reshape(groups, shards, 3, count).transpose(2, 1, 0, 3)
     taps = lax.dynamic_index_in_dim(taps.reshape(3, 3, shards, own), s, axis=2, keepdims=False)
     taps = taps.transpose(1, 2, 0)
 
@@ -1013,12 +1028,12 @@
     return (
         outputs,
         input_grad,
-        gain_one_sum.reshape(-1),
+        gain_one_sum[0],
         w_in_sum,
         taps_sum,
         kernel_grad,
         w_out_sum,
-        gain_two_sum.reshape(-1),
+        gain_two_sum[0],
         w_gate_sum,
         w_up_sum,
         w_down_sum,

time: 418 us -> 411 us (0.983)
  waiting for transfers between devices: 91.7 us -> 87.3 us
  transfers between devices with their start and end apart: 47 -> 47, of which waited for: 19 -> 18; matrix products, arithmetic and copies ran while one was open for 7% -> 7% of each run, Pallas kernels for 51% -> 52%
where the time goes in v5:
time: 411 us; the launch traced here: 405 us
  Pallas kernels  215 us (52%)
  waiting for transfers between devices  87.3 us (21%)
  starting transfers between devices  47.9 us (12%)
  local copies, waits for them, and re-layouts  29.2 us (7%)
  between operations  15.3 us (4%)
  other arithmetic  10.4 us (3%)
    pallas_call x23, Pallas kernels, call(): pl.pallas_call(run, name=name, out_shape=tuple(outs), grid_spec=pltpu.Pre...  207 us
    ppermute x38, waiting for transfers between devices, swap(): lax.ppermute(value, axis, [(i, i ^ distance) for i in range(devices)])  58.6 us
    ppermute x38, starting transfers between devices, swap(): lax.ppermute(value, axis, [(i, i ^ distance) for i in range(devices)])  45.2 us
    ppermute x1, waiting for transfers between devices, body(): folded = lax.ppermute(wide[:, ::-1, :4:-1], 'batch', mirror)  14.7 us
    reduce_scatter x3, waiting for transfers between devices, sum_over_batch(): return lax.psum_scatter(flat, 'batch', scatter_dimension=0, tiled=True)  13.3 us
  transfers between devices with their start and end apart: 47, of which 18 were waited for; matrix products, arithmetic and copies ran while one was open for 7% of the time, Pallas kernels for 52%

profile of v5, /device:TPU:0, one launch (start us, length us, event | category | flops | bytes accessed | tf_op | source)
XLA Modules:
  0.0 405.0 jit_solution(16560101112068807744)
XLA Ops:
  9.1 4.0 collective-permute-start
  15.3 2.0 collective-permute-done.1
  19.3 1.7 collective-permute-start.4
  21.0 2.0 copy.52
  23.0 1.8 slice.68
  24.8 1.8 rev.6
  26.6 1.4 collective-permute-start.5
  27.9 14.7 %collective-permute-done.5.refs_1_ = f32[2,32,3,192]{3,2,1,0:T(4,128)S(1)} collective-permute-done((f32[2,32,3,192]{3,2,1,0:T(4,128)}, f32[2,32,3,192]{3,2,1,0:T(4,128)S(1)}, u32[]{:S(2)}, u32[]{:S(2)}) %collective-permute-start.5) | collective-permute-done | bytes 147488 | tf_op jit(solution)/shard_map/ppermute | solution.py:910
  43.3 2.0 fold_base.1
  45.3 8.4 %collective-permute-done.3.refs_2_ = f32[2,256,768]{2,1,0:T(8,128)S(1)} collective-permute-done((f32[2,256,768]{2,1,0:T(8,128)S(1)}, f32[2,256,768]{2,1,0:T(8,128)S(1)}, u32[]{:S(2)}, u32[]{:S(2)}) %collective-permute-start.3) | collective-permute-done | bytes 1572896 | tf_op jit(solution)/shard_map/ppermute | solution.py:31
  58.8 1.7 collective-permute-start.8
  61.4 1.3 collective-permute-start.6
  62.7 2.1 slice_bitcast_fusion
  66.0 2.6 collective-permute-done.9
  69.5 4.1 %turn_in.1 = (bf16[576,768]{1,0:T(8,128)(2,1)}, bf16[576,768]{1,0:T(8,128)(2,1)}, f32[192,768]{1,0:T(8,128)}) custom-call(f32[8,4,24,777]{3,2,1,0:T(8,128)} %bitcast.147), custom_call_target="tpu_custom_call" | custom-call | bytes 196608 | tf_op jit(solution)/shard_map/turn_in/pallas_call | solution.py:122
  73.6 1.2 slice.69
  74.8 8.5 %collective-permute-done.6.refs_4_ = f32[256,768]{1,0:T(8,128)} collective-permute-done((f32[256,768]{1,0:T(8,128)S(1)}, f32[256,768]{1,0:T(8,128)}, u32[]{:S(2)}, u32[]{:S(2)}) %collective-permute-start.6) | collective-permute-done | bytes 786464 | tf_op jit(solution)/shard_map/ppermute | solution.py:31
  86.3 1.5 collective-permute-start.13
  89.0 5.3 %arrange.2 = (f32[1024,768]{1,0:T(8,128)}, bf16[1024,768]{1,0:T(8,128)(2,1)}, bf16[1024,768]{1,0:T(8,128)(2,1)}) custom-call(s32[1]{0:T(128)} %bitcast.refs_0_.s_ref, f32[2,256,768]{2,1,0:T(8,128)} %x_ref.3, f32[2,256,768]{2,1,0:T(8,128)} %copy-done.1, f32[2,256,768]{2,1,0:T(8,128)} %collective-permute-done.4.refs_3_, f32[256,768]{1,0:T(8,128)} %collective-permute-done.6.refs_4_), custom_call_target="tpu_custom_call" | custom-call | bytes 471859 | tf_op jit(solution)/shard_map/arrange/pallas_call | solution.py:122
  94.3 6.1 %project.2 = f32[576,1024]{1,0:T(8,128)} custom-call(bf16[576,768]{1,0:T(8,128)(2,1)} %get-tuple-element.199.refs_0_.refs_4_, bf16[576,768]{1,0:T(8,128)(2,1)} %get-tuple-element.200.refs_1_.refs_5_, bf16[1024,768]{1,0:T(8,128)(2,1)} %get-tuple-element.296.refs_2_, bf16[1024,768]{1,0:T(8,128)(2,1)} %get-tuple-element.297.refs_3_), custom_call_target="tpu_custom_call" | custom-call | flops 135895456 | bytes 363724 | tf_op jit(solution)/shard_map/project/pallas_call | solution.py:122
  100.4 13.7 %mix.2 = (f32[192,1024]{1,0:T(8,128)}, f32[192,1024]{1,0:T(8,128)}, f32[192,1024]{1,0:T(8,128)}, f32[5,192,512]{2,1,0:T(8,128)}, f32[5,192,512]{2,1,0:T(8,128)}) custom-call(f32[3,192,1024]{2,1,0:T(8,128)} %bitcast.133, f32[3,192,3]{2,1,0:T(8,128)} %bitcast.144, f32[8,160,384]{2,1,0:T(8,128)} %bitcast.141, ...), custom_call_target="tpu_custom_call" | custom-call | flops 724775744 | bytes 865075 | tf_op jit(solution)/shard_map/mix/pallas_call | solution.py:122
  116.1 1.6 collective-permute-start.16
  117.7 5.5 %arrange.3 = (f32[1024,768]{1,0:T(8,128)}, bf16[1024,768]{1,0:T(8,128)(2,1)}, bf16[1024,768]{1,0:T(8,128)(2,1)}) custom-call(s32[1]{0:T(128)} %bitcast.refs_0_.s_ref, f32[2,256,768]{2,1,0:T(8,128)} %x_ref.3, f32[2,256,768]{2,1,0:T(8,128)} %copy-done.1, f32[2,256,768]{2,1,0:T(8,128)} %collective-permute-done.4.refs_3_, f32[256,768]{1,0:T(8,128)} %copy-done.20, ...), custom_call_target="tpu_custom_call" | custom-call | bytes 471859 | tf_op jit(solution)/shard_map/arrange/pallas_call | solution.py:122
  123.2 6.2 %project.3 = f32[576,1024]{1,0:T(8,128)} custom-call(bf16[576,768]{1,0:T(8,128)(2,1)} %get-tuple-element.199.refs_0_.refs_4_, bf16[576,768]{1,0:T(8,128)(2,1)} %get-tuple-element.200.refs_1_.refs_5_, bf16[1024,768]{1,0:T(8,128)(2,1)} %get-tuple-element.311.refs_2_, bf16[1024,768]{1,0:T(8,128)(2,1)} %get-tuple-element.312.refs_3_), custom_call_target="tpu_custom_call" | custom-call | flops 135895456 | bytes 363724 | tf_op jit(solution)/shard_map/project/pallas_call | solution.py:122
  129.5 14.0 %mix.3 = (f32[192,1024]{1,0:T(8,128)}, f32[192,1024]{1,0:T(8,128)}, f32[192,1024]{1,0:T(8,128)}, f32[5,192,512]{2,1,0:T(8,128)}, f32[5,192,512]{2,1,0:T(8,128)}) custom-call(f32[3,192,1024]{2,1,0:T(8,128)} %bitcast.135, f32[3,192,3]{2,1,0:T(8,128)} %bitcast.145, f32[8,160,384]{2,1,0:T(8,128)} %bitcast.142, ...), custom_call_target="tpu_custom_call" | custom-call | flops 724775744 | bytes 865075 | tf_op jit(solution)/shard_map/mix/pallas_call | solution.py:122
  143.5 5.4 %collective-permute-done.16.refs_4_ = f32[192,1024]{1,0:T(8,128)S(1)} collective-permute-done((f32[192,1024]{1,0:T(8,128)}, f32[192,1024]{1,0:T(8,128)S(1)}, u32[]{:S(2)}, u32[]{:S(2)}) %collective-permute-start.16) | collective-permute-done | bytes 786464 | tf_op jit(solution)/shard_map/ppermute | solution.py:31
  149.0 1.3 collective-permute-start.17
  152.5 8.8 %add_mixer.2.refs_1_.refs_0_ = f32[1024,768]{1,0:T(8,128)} custom-call(f32[1024,768]{1,0:T(8,128)} %get-tuple-element.223.refs_0_, f32[192,1024]{1,0:T(8,128)} %get-tuple-element.212.refs_5_.refs_1_, f32[192,1024]{1,0:T(8,128)} %copy-done.22, f32[192,1024]{1,0:T(8,128)} %copy-done.23, f32[192,1024]{1,0:T(8,128)} %copy-done.24, ...), custom_call_target="tpu_custom_call" | custom-call | flops 181193936 | bytes 589824 | tf_op jit(solution)/shard_map/add_mixer/pallas_call | solution.py:122
  161.2 5.1 %split_units.1 = (bf16[768,1536]{1,0:T(8,128)(2,1)}, bf16[768,1536]{1,0:T(8,128)(2,1)}) custom-call(f32[8,4,24,1536]{3,2,1,0:T(8,128)} %bitcast.143, f32[1024,768]{1,0:T(8,128)} %add_mixer.2.refs_1_.refs_0_), custom_call_target="tpu_custom_call" | custom-call | bytes 471859 | tf_op jit(solution)/shard_map/split_units/pallas_call | solution.py:122
  166.4 12.5 %units_of.1 = (bf16[1024,768]{1,0:T(8,128)(2,1)}, bf16[1024,768]{1,0:T(8,128)(2,1)}) custom-call(f32[1024,768]{1,0:T(8,128)} %add_mixer.2.refs_1_.refs_0_, bf16[768,1536]{1,0:T(8,128)(2,1)} %get-tuple-element.248.refs_1_.refs_12_.refs_2_, bf16[768,1536]{1,0:T(8,128)(2,1)} %get-tuple-element.249.refs_2_.refs_13_.refs_3_), custom_call_target="tpu_custom_call" | custom-call | flops 362387872 | bytes 550502 | tf_op jit(solution)/shard_map/units_of/pallas_call | solution.py:122
  179.0 2.9 split_down.1
  181.9 7.5 %down_of.1 = (f32[256,768]{1,0:T(8,128)}, f32[256,768]{1,0:T(8,128)}, f32[256,768]{1,0:T(8,128)}, f32[256,768]{1,0:T(8,128)}) custom-call(s32[1]{0:T(128)} %bitcast.refs_0_.s_ref, bf16[1024,768]{1,0:T(8,128)(2,1)} %get-tuple-element.233.refs_1_, bf16[1024,768]{1,0:T(8,128)(2,1)} %get-tuple-element.234.refs_2_, ...), custom_call_target="tpu_custom_call" | custom-call | flops 181193936 | bytes 432537 | tf_op jit(solution)/shard_map/down_of/pallas_call | solution.py:122
  189.5 1.5 collective-permute-start.20
  191.0 1.5 collective-permute-start.21
  193.3 18.5 %live_back.1 = (f32[256,768]{1,0:T(8,128)}, f32[256,768]{1,0:T(8,128)}, f32[256,768]{1,0:T(8,128)}, f32[256,1536]{1,0:T(8,128)}, f32[160,768]{1,0:T(8,128)}) custom-call(f32[1024,768]{1,0:T(8,128)} %add_mixer.2.refs_1_.refs_0_, f32[1024,768]{1,0:T(8,128)} %get-tuple-element.243.refs_1_.refs_0_, f32[192,1024]{1,0:T(8,128)} %get-tuple-element.222.refs_9_.refs_2_.refs_1_, ...), custom_call_target="tpu_custom_call" | custom-call | flops 226492416 | bytes 786432 | tf_op jit(solution)/shard_map/live_back/pallas_call | solution.py:122
  211.8 7.0 %unit_grads.1.refs_9_ = f32[8,96,2304]{2,1,0:T(8,128)} custom-call(f32[256,768]{1,0:T(8,128)} %get-tuple-element.254.refs_0_, f32[256,1536]{1,0:T(8,128)} %get-tuple-element.255.refs_1_, f32[256,768]{1,0:T(8,128)} %get-tuple-element.256.refs_2_, f32[256,768]{1,0:T(8,128)} %bitcast.138), custom_call_target="tpu_custom_call" | custom-call | flops 135895456 | bytes 353894 | tf_op jit(solution)/shard_map/unit_grads/pallas_call | solution.py:122
  221.1 8.9 %add_mixer.3.refs_1_ = f32[1024,768]{1,0:T(8,128)} custom-call(f32[1024,768]{1,0:T(8,128)} %get-tuple-element.243.refs_1_.refs_0_, f32[192,1024]{1,0:T(8,128)} %get-tuple-element.222.refs_9_.refs_2_.refs_1_, f32[192,1024]{1,0:T(8,128)} %copy-done.5, f32[192,1024]{1,0:T(8,128)} %copy-done.6, f32[192,1024]{1,0:T(8,128)} %copy-done.7, ...), custom_call_target="tpu_custom_call" | custom-call | flops 181193936 | bytes 589824 | tf_op jit(solution)/shard_map/add_mixer/pallas_call | solution.py:122
  230.2 1.5 collective-permute-start.24
  231.7 1.5 collective-permute-start.25
  233.7 16.5 %feed_forward.1 = (f32[256,768]{1,0:T(8,128)}, f32[256,768]{1,0:T(8,128)}, f32[256,768]{1,0:T(8,128)}, f32[256,768]{1,0:T(8,128)}) custom-call(s32[1]{0:T(128)} %bitcast.refs_0_.s_ref, f32[1024,768]{1,0:T(8,128)} %add_mixer.3.refs_1_, bf16[768,1536]{1,0:T(8,128)(2,1)} %get-tuple-element.248.refs_1_.refs_12_.refs_2_, ...), custom_call_target="tpu_custom_call" | custom-call | flops 543581824 | bytes 668467 | tf_op jit(solution)/shard_map/feed_forward/pallas_call | solution.py:122
  250.3 1.5 collective-permute-start.27
  251.8 1.5 collective-permute-start.28
  253.9 6.2 %live_mix.1 = (f32[256,768]{1,0:T(8,128)}, f32[192,768]{1,0:T(8,128)}, f32[2,192,128]{2,1,0:T(8,128)}, f32[2,192,128]{2,1,0:T(8,128)}) custom-call(f32[256,768]{1,0:T(8,128)} %get-tuple-element.260.refs_0_, f32[256,768]{1,0:T(8,128)} %bitcast.139, f32[80,768]{1,0:T(8,128)} %copy-done.12, f32[80,768]{1,0:T(8,128)} %copy-done.11, f32[80,768]{1,0:T(8,128)} %copy-done.28, ...), custom_call_target="tpu_custom_call" | custom-call | flops 37748736 | bytes 314572 | tf_op jit(solution)/shard_map/live_mix/pallas_call | solution.py:122
  260.1 24.4 %mix_back.1 = (f32[3,192,1024]{2,1,0:T(8,128)}, f32[3,192,1024]{2,1,0:T(8,128)}, f32[8,5,32,384]{3,2,1,0:T(8,128)}, f32[3,192,128]{2,1,0:T(8,128)}) custom-call(s32[2,128,1]{2,1,0:T(8,128)} %copy.60.refs_10_.refs_11_.refs_0_.at_ref, f32[2,192,128]{2,1,0:T(8,128)} %get-tuple-element.276.refs_1_, f32[2,192,128]{2,1,0:T(8,128)} %get-tuple-element.277.refs_2_, ...), custom_call_target="tpu_custom_call" | custom-call | flops 1449551488 | bytes 1730150 | tf_op jit(solution)/shard_map/mix_back/pallas_call | solution.py:122
  284.6 12.3 %project_back.2 = (f32[256,768]{1,0:T(8,128)}, f32[256,768]{1,0:T(8,128)}, f32[256,768]{1,0:T(8,128)}, f32[256,768]{1,0:T(8,128)}, f32[576,768]{1,0:T(8,128)}) custom-call(s32[1]{0:T(128)} %bitcast.refs_0_.s_ref, f32[576,1024]{1,0:T(8,128)} %bitcast.153, bf16[1024,768]{1,0:T(8,128)(2,1)} %get-tuple-element.296.refs_2_, ...), custom_call_target="tpu_custom_call" | custom-call | flops 271790912 | bytes 697958 | tf_op jit(solution)/shard_map/project_back/pallas_call | solution.py:122
  296.9 4.2 %reduce-scatter.4.cloned.1.call-done = f32[96,2304]{1,0:T(8,128)} async-done(((f32[768,2304]{1,0:T(8,128)}), f32[96,2304]{1,0:T(8,128)}) %reduce-scatter.4.cloned.1.call-update) | async-done | bytes 884752 | tf_op jit(solution)/shard_map/reduce_scatter | solution.py:84
  301.2 1.5 collective-permute-start.30
  302.7 1.5 collective-permute-start.31
  305.6 12.0 %project_back.3 = (f32[256,768]{1,0:T(8,128)}, f32[256,768]{1,0:T(8,128)}, f32[256,768]{1,0:T(8,128)}, f32[256,768]{1,0:T(8,128)}, f32[576,768]{1,0:T(8,128)}) custom-call(s32[1]{0:T(128)} %bitcast.refs_0_.s_ref, f32[576,1024]{1,0:T(8,128)} %bitcast.152, bf16[1024,768]{1,0:T(8,128)(2,1)} %get-tuple-element.311.refs_2_, ...), custom_call_target="tpu_custom_call" | custom-call | flops 271790912 | bytes 697958 | tf_op jit(solution)/shard_map/project_back/pallas_call | solution.py:122
  317.7 4.0 turn_back.1
  324.2 1.5 collective-permute-start.32
  325.7 1.5 collective-permute-start.33
  327.7 1.9 add_bitcast_fusion.1
  331.1 1.6 add_bitcast_fusion
  332.8 6.2 %reduce-scatter.8.cloned.1.call-done = f32[160,384]{1,0:T(8,128)} async-done(((f32[1280,384]{1,0:T(8,128)}), f32[160,384]{1,0:T(8,128)}) %reduce-scatter.8.cloned.1.call-update) | async-done | bytes 245776 | tf_op jit(solution)/shard_map/reduce_scatter | solution.py:84
  342.3 3.0 collective-permute-done.36.e3
  345.4 3.9 finish.2.refs_0_
  349.3 12.0 %collective-permute-done.32.e1 = f32[256,768]{1,0:T(8,128)} collective-permute-done((f32[256,768]{1,0:T(8,128)}, f32[256,768]{1,0:T(8,128)}, u32[]{:S(2)}, u32[]{:S(2)}) %collective-permute-start.32) | collective-permute-done | bytes 786464 | tf_op jit(solution)/shard_map/ppermute | solution.py:31
  362.1 13.1 %collective-permute-done.34.e3 = f32[256,768]{1,0:T(8,128)} collective-permute-done((f32[256,768]{1,0:T(8,128)}, f32[256,768]{1,0:T(8,128)}, u32[]{:S(2)}, u32[]{:S(2)}) %collective-permute-start.34) | collective-permute-done | bytes 786464 | tf_op jit(solution)/shard_map/ppermute | solution.py:31
  375.2 2.9 reduce-scatter.6.cloned.1.call-done
  379.9 1.4 collective-permute-start.37
  381.3 1.4 collective-permute-start.38
  385.0 3.8 finish.3
  390.8 3.4 weight_grads.1
  (215 shorter events, 47.1 us)
Async XLA Ops:
  7.2 62.3 %all-gather.5.cloned.1.call-start = ((), (), s32[]{:S(2)}) async-start(), calls=%async_computation.3 | async-start | bytes 3096576 | tf_op jit(solution)/shard_map/all_gather | solution.py:78
  9.1 6.2 %collective-permute-start = (f32[24,585]{1,0:T(8,128)S(1)}, f32[24,585]{1,0:T(8,128)S(1)}, u32[]{:S(2)}, u32[]{:S(2)}) collective-permute-start(f32[24,585]{1,0:T(8,128)S(1)} %get-tuple-element.404), channel_id=1, source_target_pairs={{0,24},{8,16},{16,8},{24,0},{1,25},{9,17},{17,9},{25,1},{2,26},{10... | collective-permute-start | bytes 168488 | tf_op jit(solution)/shard_map/ppermute | solution.py:31
  13.1 4.2 %collective-permute-start.1 = (f32[24,585]{1,0:T(8,128)S(1)}, f32[24,585]{1,0:T(8,128)S(1)}, u32[]{:S(2)}, u32[]{:S(2)}) collective-permute-start(f32[24,585]{1,0:T(8,128)S(1)} %get-tuple-element.405), channel_id=1, source_target_pairs={{0,16},{8,24},{16,0},{24,8},{1,17},{9,25},{17,1},{25,9},{2,18},{10... | collective-permute-start | bytes 168488 | tf_op jit(solution)/shard_map/ppermute | solution.py:31
  13.6 4.2 %collective-permute-start.2 = (f32[24,585]{1,0:T(8,128)S(1)}, f32[24,585]{1,0:T(8,128)S(1)}, u32[]{:S(2)}, u32[]{:S(2)}) collective-permute-start(f32[24,585]{1,0:T(8,128)S(1)} %get-tuple-element.406), channel_id=1, source_target_pairs={{0,8},{8,0},{16,24},{24,16},{1,9},{9,1},{17,25},{25,17},{2,10},{10... | collective-permute-start | bytes 168488 | tf_op jit(solution)/shard_map/ppermute | solution.py:31
  18.8 35.9 %copy-start.10 = (f32[24,3072]{1,0:T(8,128)S(1)}, f32[24,3072]{1,0:T(8,128)}, u32[]{:S(2)}) copy-start(f32[24,3072]{1,0:T(8,128)} %refs_8_.1) | copy-start | bytes 884740
  18.8 35.9 %copy-start.34 = (f32[24]{0:T(128)S(1)}, f32[24]{0:T(128)}, u32[]{:S(2)}) copy-start(f32[24]{0:T(128)} %param.21) | copy-start | bytes 292
  18.8 81.6 %all-gather.7.cloned.1.call-start = ((), (), s32[]{:S(2)}) async-start(), calls=%async_computation.4 | async-start | bytes 2211840 | tf_op jit(solution)/shard_map/all_gather | solution.py:78
  18.9 34.8 %collective-permute-start.3 = (f32[2,256,768]{2,1,0:T(8,128)S(1)}, f32[2,256,768]{2,1,0:T(8,128)S(1)}, u32[]{:S(2)}, u32[]{:S(2)}) collective-permute-start(f32[2,256,768]{2,1,0:T(8,128)S(1)} %copy-done), channel_id=1, source_target_pairs={{0,8},{8,0},{16,24},{24,16},{1,9},{9,1},{17,25},{25,17},{2,10},{10... | collective-permute-start | bytes 4718600 | tf_op jit(solution)/shard_map/ppermute | solution.py:31
  19.3 35.3 %collective-permute-start.4 = (f32[2,256,768]{2,1,0:T(8,128)S(1)}, f32[2,256,768]{2,1,0:T(8,128)}, u32[]{:S(2)}, u32[]{:S(2)}) collective-permute-start(f32[2,256,768]{2,1,0:T(8,128)S(1)} %copy-done), channel_id=1, source_target_pairs={{0,16},{8,24},{16,0},{24,8},{1,17},{9,25},{17,1},{25,9},{2,18},{10... | collective-permute-start | bytes 4718600 | tf_op jit(solution)/shard_map/ppermute | solution.py:31
  26.6 16.0 %collective-permute-start.5 = (f32[2,32,3,192]{3,2,1,0:T(4,128)}, f32[2,32,3,192]{3,2,1,0:T(4,128)S(1)}, u32[]{:S(2)}, u32[]{:S(2)}) collective-permute-start(f32[2,32,3,192]{3,2,1,0:T(4,128)} %rev.6), channel_id=1, source_target_pairs={{0,7},{1,6},{2,5},{3,4},{4,3},{5,2},{6,1},{7,0},{8,15},{9,14},{10,... | collective-permute-start | bytes 442376 | tf_op jit(solution)/shard_map/ppermute | solution.py:910
  53.7 7.6 %copy-start.1 = (f32[2,256,768]{2,1,0:T(8,128)}, f32[2,256,768]{2,1,0:T(8,128)S(1)}, u32[]{:S(2)}) copy-start(f32[2,256,768]{2,1,0:T(8,128)S(1)} %collective-permute-done.3.refs_2_) | copy-start | bytes 4718596
  54.6 106.6 %all-gather.9.cloned.1.call-start = ((), (), s32[]{:S(2)}) async-start(), calls=%async_computation.5 | async-start | bytes 5308416 | tf_op jit(solution)/shard_map/all_gather | solution.py:78
  57.7 8.2 %collective-permute-start.10 = (f32[24,1536]{1,0:T(8,128)S(1)}, f32[24,1536]{1,0:T(8,128)S(1)}, u32[]{:S(2)}, u32[]{:S(2)}) collective-permute-start(f32[24,1536]{1,0:T(8,128)S(1)} %get-tuple-element.394), channel_id=1, source_target_pairs={{0,8},{8,0},{16,24},{24,16},{1,9},{9,1},{17,25},{25,17},{2,10},{10... | collective-permute-start | bytes 442376 | tf_op jit(solution)/shard_map/ppermute | solution.py:31
  58.8 7.2 %collective-permute-start.8 = (f32[24,1536]{1,0:T(8,128)S(1)}, f32[24,1536]{1,0:T(8,128)S(1)}, u32[]{:S(2)}, u32[]{:S(2)}) collective-permute-start(f32[24,1536]{1,0:T(8,128)S(1)} %get-tuple-element.393), channel_id=1, source_target_pairs={{0,24},{8,16},{16,8},{24,0},{1,25},{9,17},{17,9},{25,1},{2,26},{10... | collective-permute-start | bytes 442376 | tf_op jit(solution)/shard_map/ppermute | solution.py:31
  60.5 8.0 %collective-permute-start.9 = (f32[24,1536]{1,0:T(8,128)S(1)}, f32[24,1536]{1,0:T(8,128)S(1)}, u32[]{:S(2)}, u32[]{:S(2)}) collective-permute-start(f32[24,1536]{1,0:T(8,128)S(1)} %get-tuple-element.395), channel_id=1, source_target_pairs={{0,16},{8,24},{16,0},{24,8},{1,17},{9,25},{17,1},{25,9},{2,18},{10... | collective-permute-start | bytes 442376 | tf_op jit(solution)/shard_map/ppermute | solution.py:31
  61.4 22.0 %collective-permute-start.6 = (f32[256,768]{1,0:T(8,128)S(1)}, f32[256,768]{1,0:T(8,128)}, u32[]{:S(2)}, u32[]{:S(2)}) collective-permute-start(f32[256,768]{1,0:T(8,128)S(1)} %slice_bitcast_fusion.1), channel_id=1, source_target_pairs={{0,16},{8,24},{16,0},{24,8},{1,17},{9,25},{17,1},{25,9},{2,18},{10... | collective-permute-start | bytes 2359304 | tf_op jit(solution)/shard_map/ppermute | solution.py:31
  64.7 18.6 %collective-permute-start.7 = (f32[256,768]{1,0:T(8,128)}, f32[256,768]{1,0:T(8,128)S(1)}, u32[]{:S(2)}, u32[]{:S(2)}) collective-permute-start(f32[256,768]{1,0:T(8,128)} %slice_bitcast_fusion), channel_id=1, source_target_pairs={{0,8},{8,0},{16,24},{24,16},{1,9},{9,1},{17,25},{25,17},{2,10},{10... | collective-permute-start | bytes 2359304 | tf_op jit(solution)/shard_map/ppermute | solution.py:31
  83.3 11.0 %copy-start.20 = (f32[256,768]{1,0:T(8,128)}, f32[256,768]{1,0:T(8,128)S(1)}, u32[]{:S(2)}) copy-start(f32[256,768]{1,0:T(8,128)S(1)} %collective-permute-done.7.refs_4_) | copy-start | bytes 2359300
  83.4 95.6 %all-gather.11.cloned.1.call-start = ((), (), s32[]{:S(2)}) async-start(), calls=%async_computation.6 | async-start | bytes 2654208 | tf_op jit(solution)/shard_map/all_gather | solution.py:78
  84.0 217.1 %reduce-scatter.4.cloned.1.call-start = ((), (), s32[]{:S(2)}) async-start(), calls=%async_computation.7 | async-start | bytes 7962624 | tf_op jit(solution)/shard_map/reduce_scatter | solution.py:84
  84.2 29.9 %collective-permute-start.11 = (f32[192,768]{1,0:T(8,128)}, f32[192,768]{1,0:T(8,128)S(1)}, u32[]{:S(2)}, u32[]{:S(2)}) collective-permute-start(f32[192,768]{1,0:T(8,128)} %get-tuple-element.198.refs_5_.refs_6_), channel_id=1, source_target_pairs={{0,8},{8,0},{16,24},{24,16},{1,9},{9,1},{17,25},{25,17},{2,10},{10... | collective-permute-start | bytes 1769480 | tf_op jit(solution)/shard_map/ppermute | solution.py:31
  85.3 28.8 %collective-permute-start.12 = (f32[192,768]{1,0:T(8,128)}, f32[192,768]{1,0:T(8,128)S(1)}, u32[]{:S(2)}, u32[]{:S(2)}) collective-permute-start(f32[192,768]{1,0:T(8,128)} %get-tuple-element.198.refs_5_.refs_6_), channel_id=1, source_target_pairs={{0,16},{8,24},{16,0},{24,8},{1,17},{9,25},{17,1},{25,9},{2,18},{10... | collective-permute-start | bytes 1769480 | tf_op jit(solution)/shard_map/ppermute | solution.py:31
  86.3 27.8 %collective-permute-start.13 = (f32[192,768]{1,0:T(8,128)}, f32[192,768]{1,0:T(8,128)S(1)}, u32[]{:S(2)}, u32[]{:S(2)}) collective-permute-start(f32[192,768]{1,0:T(8,128)} %get-tuple-element.198.refs_5_.refs_6_), channel_id=1, source_target_pairs={{0,24},{8,16},{16,8},{24,0},{1,25},{9,17},{17,9},{25,1},{2,26},{10... | collective-permute-start | bytes 1769480 | tf_op jit(solution)/shard_map/ppermute | solution.py:31
  114.1 9.1 %copy-start.2 = (f32[192,768]{1,0:T(8,128)}, f32[192,768]{1,0:T(8,128)S(1)}, u32[]{:S(2)}) copy-start(f32[192,768]{1,0:T(8,128)S(1)} %collective-permute-done.11.refs_6_.refs_7_) | copy-start | bytes 1769476
  114.1 9.1 %copy-start.3 = (f32[192,768]{1,0:T(8,128)}, f32[192,768]{1,0:T(8,128)S(1)}, u32[]{:S(2)}) copy-start(f32[192,768]{1,0:T(8,128)S(1)} %collective-permute-done.12.refs_7_.refs_8_) | copy-start | bytes 1769476
  114.2 9.1 %copy-start.4 = (f32[192,768]{1,0:T(8,128)}, f32[192,768]{1,0:T(8,128)S(1)}, u32[]{:S(2)}) copy-start(f32[192,768]{1,0:T(8,128)S(1)} %collective-permute-done.13.refs_8_.refs_9_) | copy-start | bytes 1769476
  114.2 29.3 %collective-permute-start.14 = (f32[192,1024]{1,0:T(8,128)}, f32[192,1024]{1,0:T(8,128)S(1)}, u32[]{:S(2)}, u32[]{:S(2)}) collective-permute-start(f32[192,1024]{1,0:T(8,128)} %get-tuple-element.212.refs_5_.refs_1_), channel_id=1, source_target_pairs={{0,8},{8,0},{16,24},{24,16},{1,9},{9,1},{17,25},{25,17},{2,10},{10... | collective-permute-start | bytes 2359304 | tf_op jit(solution)/shard_map/ppermute | solution.py:31
  115.0 28.5 %collective-permute-start.15 = (f32[192,1024]{1,0:T(8,128)}, f32[192,1024]{1,0:T(8,128)S(1)}, u32[]{:S(2)}, u32[]{:S(2)}) collective-permute-start(f32[192,1024]{1,0:T(8,128)} %get-tuple-element.212.refs_5_.refs_1_), channel_id=1, source_target_pairs={{0,16},{8,24},{16,0},{24,8},{1,17},{9,25},{17,1},{25,9},{2,18},{10... | collective-permute-start | bytes 2359304 | tf_op jit(solution)/shard_map/ppermute | solution.py:31
  116.1 32.9 %collective-permute-start.16 = (f32[192,1024]{1,0:T(8,128)}, f32[192,1024]{1,0:T(8,128)S(1)}, u32[]{:S(2)}, u32[]{:S(2)}) collective-permute-start(f32[192,1024]{1,0:T(8,128)} %get-tuple-element.212.refs_5_.refs_1_), channel_id=1, source_target_pairs={{0,24},{8,16},{16,8},{24,0},{1,25},{9,17},{17,9},{25,1},{2,26},{10... | collective-permute-start | bytes 2359304 | tf_op jit(solution)/shard_map/ppermute | solution.py:31
  143.5 9.0 %copy-start.22 = (f32[192,1024]{1,0:T(8,128)}, f32[192,1024]{1,0:T(8,128)S(1)}, u32[]{:S(2)}) copy-start(f32[192,1024]{1,0:T(8,128)S(1)} %collective-permute-done.14.refs_2_) | copy-start | bytes 2359300
  143.5 8.9 %copy-start.23 = (f32[192,1024]{1,0:T(8,128)}, f32[192,1024]{1,0:T(8,128)S(1)}, u32[]{:S(2)}) copy-start(f32[192,1024]{1,0:T(8,128)S(1)} %collective-permute-done.15.refs_3_) | copy-start | bytes 2359300
  149.0 40.5 %collective-permute-start.17 = (f32[192,1024]{1,0:T(8,128)}, f32[192,1024]{1,0:T(8,128)S(1)}, u32[]{:S(2)}, u32[]{:S(2)}) collective-permute-start(f32[192,1024]{1,0:T(8,128)} %get-tuple-element.222.refs_9_.refs_2_.refs_1_), channel_id=1, source_target_pairs={{0,8},{8,0},{16,24},{24,16},{1,9},{9,1},{17,25},{25,17},{2,10},{10... | collective-permute-start | bytes 2359304 | tf_op jit(solution)/shard_map/ppermute | solution.py:31
  150.2 39.2 %collective-permute-start.18 = (f32[192,1024]{1,0:T(8,128)}, f32[192,1024]{1,0:T(8,128)S(1)}, u32[]{:S(2)}, u32[]{:S(2)}) collective-permute-start(f32[192,1024]{1,0:T(8,128)} %get-tuple-element.222.refs_9_.refs_2_.refs_1_), channel_id=1, source_target_pairs={{0,16},{8,24},{16,0},{24,8},{1,17},{9,25},{17,1},{25,9},{2,18},{10... | collective-permute-start | bytes 2359304 | tf_op jit(solution)/shard_map/ppermute | solution.py:31
  151.3 38.1 %collective-permute-start.19 = (f32[192,1024]{1,0:T(8,128)}, f32[192,1024]{1,0:T(8,128)S(1)}, u32[]{:S(2)}, u32[]{:S(2)}) collective-permute-start(f32[192,1024]{1,0:T(8,128)} %get-tuple-element.222.refs_9_.refs_2_.refs_1_), channel_id=1, source_target_pairs={{0,24},{8,16},{16,8},{24,0},{1,25},{9,17},{17,9},{25,1},{2,26},{10... | collective-permute-start | bytes 2359304 | tf_op jit(solution)/shard_map/ppermute | solution.py:31
  189.5 29.4 %collective-permute-start.20 = (f32[256,768]{1,0:T(8,128)}, f32[256,768]{1,0:T(8,128)S(1)}, u32[]{:S(2)}, u32[]{:S(2)}) collective-permute-start(f32[256,768]{1,0:T(8,128)} %get-tuple-element.258), channel_id=1, source_target_pairs={{0,8},{8,0},{16,24},{24,16},{1,9},{9,1},{17,25},{25,17},{2,10},{10... | collective-permute-start | bytes 2359304 | tf_op jit(solution)/shard_map/ppermute | solution.py:31
  191.0 27.9 %collective-permute-start.21 = (f32[256,768]{1,0:T(8,128)}, f32[256,768]{1,0:T(8,128)}, u32[]{:S(2)}, u32[]{:S(2)}) collective-permute-start(f32[256,768]{1,0:T(8,128)} %get-tuple-element.259), channel_id=1, source_target_pairs={{0,16},{8,24},{16,0},{24,8},{1,17},{9,25},{17,1},{25,9},{2,18},{10... | collective-permute-start | bytes 2359304 | tf_op jit(solution)/shard_map/ppermute | solution.py:31
  218.9 120.0 %reduce-scatter.8.cloned.1.call-start = ((), (), s32[]{:S(2)}) async-start(), calls=%async_computation.9 | async-start | bytes 2211840 | tf_op jit(solution)/shard_map/reduce_scatter | solution.py:84
  220.0 10.1 %collective-permute-start.22 = (f32[80,768]{1,0:T(8,128)S(1)}, f32[80,768]{1,0:T(8,128)S(1)}, u32[]{:S(2)}, u32[]{:S(2)}) collective-permute-start(f32[80,768]{1,0:T(8,128)S(1)} %get-tuple-element.399), channel_id=1, source_target_pairs={{0,8},{8,0},{16,24},{24,16},{1,9},{9,1},{17,25},{25,17},{2,10},{10... | collective-permute-start | bytes 737288 | tf_op jit(solution)/shard_map/ppermute | solution.py:31
  220.6 12.6 %copy-start.39 = (f32[256,768]{1,0:T(8,128)S(1)}, f32[256,768]{1,0:T(8,128)}, u32[]{:S(2)}) copy-start(f32[256,768]{1,0:T(8,128)} %get-tuple-element.291) | copy-start | bytes 2359300
  220.6 9.5 %collective-permute-start.23 = (f32[80,768]{1,0:T(8,128)S(1)}, f32[80,768]{1,0:T(8,128)S(1)}, u32[]{:S(2)}, u32[]{:S(2)}) collective-permute-start(f32[80,768]{1,0:T(8,128)S(1)} %get-tuple-element.398), channel_id=1, source_target_pairs={{0,16},{8,24},{16,0},{24,8},{1,17},{9,25},{17,1},{25,9},{2,18},{10... | collective-permute-start | bytes 737288 | tf_op jit(solution)/shard_map/ppermute | solution.py:31
  230.2 20.1 %copy-start.11 = (f32[80,768]{1,0:T(8,128)}, f32[80,768]{1,0:T(8,128)S(1)}, u32[]{:S(2)}) copy-start(f32[80,768]{1,0:T(8,128)S(1)} %get-tuple-element.396.refs_3_) | copy-start | bytes 737284
  230.2 20.1 %copy-start.12 = (f32[80,768]{1,0:T(8,128)}, f32[80,768]{1,0:T(8,128)S(1)}, u32[]{:S(2)}) copy-start(f32[80,768]{1,0:T(8,128)S(1)} %get-tuple-element.397.refs_2_) | copy-start | bytes 737284
  230.2 20.1 %collective-permute-start.24 = (f32[80,768]{1,0:T(8,128)S(1)}, f32[80,768]{1,0:T(8,128)S(1)}, u32[]{:S(2)}, u32[]{:S(2)}) collective-permute-start(f32[80,768]{1,0:T(8,128)S(1)} %get-tuple-element.397.refs_2_), channel_id=1, source_target_pairs={{0,16},{8,24},{16,0},{24,8},{1,17},{9,25},{17,1},{25,9},{2,18},{10... | collective-permute-start | bytes 737288 | tf_op jit(solution)/shard_map/ppermute | solution.py:31
  231.7 18.6 %collective-permute-start.25 = (f32[80,768]{1,0:T(8,128)S(1)}, f32[80,768]{1,0:T(8,128)S(1)}, u32[]{:S(2)}, u32[]{:S(2)}) collective-permute-start(f32[80,768]{1,0:T(8,128)S(1)} %get-tuple-element.396.refs_3_), channel_id=1, source_target_pairs={{0,8},{8,0},{16,24},{24,16},{1,9},{9,1},{17,25},{25,17},{2,10},{10... | collective-permute-start | bytes 737288 | tf_op jit(solution)/shard_map/ppermute | solution.py:31
  233.2 51.3 %collective-permute-start.26 = (f32[256,768]{1,0:T(8,128)S(1)}, f32[256,768]{1,0:T(8,128)S(1)}, u32[]{:S(2)}, u32[]{:S(2)}) collective-permute-start(f32[256,768]{1,0:T(8,128)S(1)} %copy-done.39), channel_id=1, source_target_pairs={{0,24},{8,16},{16,8},{24,0},{1,25},{9,17},{17,9},{25,1},{2,26},{10... | collective-permute-start | bytes 2359304 | tf_op jit(solution)/shard_map/ppermute | solution.py:31
  250.3 34.2 %collective-permute-start.27 = (f32[256,768]{1,0:T(8,128)}, f32[256,768]{1,0:T(8,128)S(1)}, u32[]{:S(2)}, u32[]{:S(2)}) collective-permute-start(f32[256,768]{1,0:T(8,128)} %get-tuple-element.293), channel_id=1, source_target_pairs={{0,8},{8,0},{16,24},{24,16},{1,9},{9,1},{17,25},{25,17},{2,10},{10... | collective-permute-start | bytes 2359304 | tf_op jit(solution)/shard_map/ppermute | solution.py:31
  251.8 32.7 %collective-permute-start.28 = (f32[256,768]{1,0:T(8,128)}, f32[256,768]{1,0:T(8,128)S(1)}, u32[]{:S(2)}, u32[]{:S(2)}) collective-permute-start(f32[256,768]{1,0:T(8,128)} %get-tuple-element.294), channel_id=1, source_target_pairs={{0,16},{8,24},{16,0},{24,8},{1,17},{9,25},{17,1},{25,9},{2,18},{10... | collective-permute-start | bytes 2359304 | tf_op jit(solution)/shard_map/ppermute | solution.py:31
  253.3 43.6 %collective-permute-start.29 = (f32[256,768]{1,0:T(8,128)}, f32[256,768]{1,0:T(8,128)}, u32[]{:S(2)}, u32[]{:S(2)}) collective-permute-start(f32[256,768]{1,0:T(8,128)} %get-tuple-element.306), channel_id=1, source_target_pairs={{0,24},{8,16},{16,8},{24,0},{1,25},{9,17},{17,9},{25,1},{2,26},{10... | collective-permute-start | bytes 2359304 | tf_op jit(solution)/shard_map/ppermute | solution.py:31
  284.5 12.4 %copy-start.15 = (f32[256,768]{1,0:T(8,128)}, f32[256,768]{1,0:T(8,128)S(1)}, u32[]{:S(2)}) copy-start(f32[256,768]{1,0:T(8,128)S(1)} %collective-permute-done.26) | copy-start | bytes 2359300
  284.5 12.4 %copy-start.16 = (f32[256,768]{1,0:T(8,128)}, f32[256,768]{1,0:T(8,128)S(1)}, u32[]{:S(2)}) copy-start(f32[256,768]{1,0:T(8,128)S(1)} %collective-permute-done.27) | copy-start | bytes 2359300
  284.5 12.4 %copy-start.18 = (f32[256,768]{1,0:T(8,128)}, f32[256,768]{1,0:T(8,128)S(1)}, u32[]{:S(2)}) copy-start(f32[256,768]{1,0:T(8,128)S(1)} %collective-permute-done.28) | copy-start | bytes 2359300
  296.9 7.2 %copy-start.26 = (f32[3,192,128]{2,1,0:T(8,128)S(1)}, f32[3,192,128]{2,1,0:T(8,128)}, u32[]{:S(2)}) copy-start(f32[3,192,128]{2,1,0:T(8,128)} %get-tuple-element.285) | copy-start | bytes 884740
  301.1 77.0 %reduce-scatter.6.cloned.1.call-start = ((), (), s32[]{:S(2)}) async-start(), calls=%async_computation.8 | async-start | bytes 3096576 | tf_op jit(solution)/shard_map/reduce_scatter | solution.py:84
  301.2 20.5 %collective-permute-start.30 = (f32[256,768]{1,0:T(8,128)}, f32[256,768]{1,0:T(8,128)S(1)}, u32[]{:S(2)}, u32[]{:S(2)}) collective-permute-start(f32[256,768]{1,0:T(8,128)} %get-tuple-element.308), channel_id=1, source_target_pairs={{0,8},{8,0},{16,24},{24,16},{1,9},{9,1},{17,25},{25,17},{2,10},{10... | collective-permute-start | bytes 2359304 | tf_op jit(solution)/shard_map/ppermute | solution.py:31
  302.7 19.0 %collective-permute-start.31 = (f32[256,768]{1,0:T(8,128)}, f32[256,768]{1,0:T(8,128)}, u32[]{:S(2)}, u32[]{:S(2)}) collective-permute-start(f32[256,768]{1,0:T(8,128)} %get-tuple-element.309), channel_id=1, source_target_pairs={{0,16},{8,24},{16,0},{24,8},{1,17},{9,25},{17,1},{25,9},{2,18},{10... | collective-permute-start | bytes 2359304 | tf_op jit(solution)/shard_map/ppermute | solution.py:31
  323.7 21.7 %collective-permute-start.36 = (f32[256,768]{1,0:T(8,128)}, f32[256,768]{1,0:T(8,128)}, u32[]{:S(2)}, u32[]{:S(2)}) collective-permute-start(f32[256,768]{1,0:T(8,128)} %get-tuple-element.338), channel_id=1, source_target_pairs={{0,24},{8,16},{16,8},{24,0},{1,25},{9,17},{17,9},{25,1},{2,26},{10... | collective-permute-start | bytes 2359304 | tf_op jit(solution)/shard_map/ppermute | solution.py:31
  324.2 37.1 %collective-permute-start.32 = (f32[256,768]{1,0:T(8,128)}, f32[256,768]{1,0:T(8,128)}, u32[]{:S(2)}, u32[]{:S(2)}) collective-permute-start(f32[256,768]{1,0:T(8,128)} %get-tuple-element.322), channel_id=1, source_target_pairs={{0,8},{8,0},{16,24},{24,16},{1,9},{9,1},{17,25},{25,17},{2,10},{10... | collective-permute-start | bytes 2359304 | tf_op jit(solution)/shard_map/ppermute | solution.py:31
  325.7 36.4 %collective-permute-start.33 = (f32[256,768]{1,0:T(8,128)}, f32[256,768]{1,0:T(8,128)}, u32[]{:S(2)}, u32[]{:S(2)}) collective-permute-start(f32[256,768]{1,0:T(8,128)} %get-tuple-element.323), channel_id=1, source_target_pairs={{0,16},{8,24},{16,0},{24,8},{1,17},{9,25},{17,1},{25,9},{2,18},{10... | collective-permute-start | bytes 2359304 | tf_op jit(solution)/shard_map/ppermute | solution.py:31
  327.1 48.0 %collective-permute-start.34 = (f32[256,768]{1,0:T(8,128)}, f32[256,768]{1,0:T(8,128)}, u32[]{:S(2)}, u32[]{:S(2)}) collective-permute-start(f32[256,768]{1,0:T(8,128)} %get-tuple-element.324), channel_id=1, source_target_pairs={{0,24},{8,16},{16,8},{24,0},{1,25},{9,17},{17,9},{25,1},{2,26},{10... | collective-permute-start | bytes 2359304 | tf_op jit(solution)/shard_map/ppermute | solution.py:31
  340.2 35.0 %collective-permute-start.35 = (f32[2,32,3,192]{3,0,1,2:T(2,128)S(1)}, f32[2,32,3,192]{3,0,1,2:T(2,128)S(1)}, u32[]{:S(2)}, u32[]{:S(2)}) collective-permute-start(f32[2,32,3,192]{3,0,1,2:T(2,128)S(1)} %rev.7), channel_id=1, source_target_pairs={{0,7},{1,6},{2,5},{3,4},{4,3},{5,2},{6,1},{7,0},{8,15},{9,14},{10,... | collective-permute-start | bytes 442376 | tf_op jit(solution)/shard_map/ppermute | solution.py:1010
  342.3 36.7 %slice-start = ((f32[96,2304]{1,0:T(8,128)}), f32[96,1536]{1,0:T(8,128)S(1)}, s32[]{:S(2)}) async-start(f32[96,2304]{1,0:T(8,128)} %reduce-scatter.4.cloned.1.call-done), calls=%async_computation.10 | async-start | bytes 1179648 | tf_op jit(solution)/shard_map/slice | solution.py:1013
  379.9 9.0 %collective-permute-start.37 = (f32[24,2176]{1,0:T(8,128)S(1)}, f32[24,2176]{1,0:T(8,128)S(1)}, u32[]{:S(2)}, u32[]{:S(2)}) collective-permute-start(f32[24,2176]{1,0:T(8,128)S(1)} %get-tuple-element.391), channel_id=1, source_target_pairs={{0,8},{8,0},{16,24},{24,16},{1,9},{9,1},{17,25},{25,17},{2,10},{10... | collective-permute-start | bytes 626696 | tf_op jit(solution)/shard_map/ppermute | solution.py:31
  381.3 8.7 %collective-permute-start.38 = (f32[24,2176]{1,0:T(8,128)S(1)}, f32[24,2176]{1,0:T(8,128)S(1)}, u32[]{:S(2)}, u32[]{:S(2)}) collective-permute-start(f32[24,2176]{1,0:T(8,128)S(1)} %get-tuple-element.390), channel_id=1, source_target_pairs={{0,16},{8,24},{16,0},{24,8},{1,17},{9,25},{17,1},{25,9},{2,18},{10... | collective-permute-start | bytes 626696 | tf_op jit(solution)/shard_map/ppermute | solution.py:31
  382.7 7.3 %collective-permute-start.39 = (f32[24,2176]{1,0:T(8,128)S(1)}, f32[24,2176]{1,0:T(8,128)S(1)}, u32[]{:S(2)}, u32[]{:S(2)}) collective-permute-start(f32[24,2176]{1,0:T(8,128)S(1)} %get-tuple-element.389), channel_id=1, source_target_pairs={{0,24},{8,16},{16,8},{24,0},{1,25},{9,17},{17,9},{25,1},{2,26},{10... | collective-permute-start | bytes 626696 | tf_op jit(solution)/shard_map/ppermute | solution.py:31
  (25 other events, 85.0 us)
Sparse Core Ops, SparseCore 0:
  18.9 46.6 all-gather.4
  67.8 26.2 all-gather.6
  95.8 51.2 all-gather.8
  148.5 30.4 all-gather.10
  219.1 81.9 reduce-scatter.3
  303.3 35.6 reduce-scatter.7
  341.4 36.6 reduce-scatter.5

commit v6 on v5

--- a/solution.py
+++ b/solution.py
@@ -912,7 +912,8 @@
     near, folded, w_gate_now, w_up_now = together(near, folded, w_gate, w_up)
     base = over_batch(folded)
 
-    far = [swap(near[0][0], "seq", 2), swap(near[1][1], "seq", 1)]
+    from_one, from_two, w_gate_now, w_up_now = together(near[0][0], near[1][1], w_gate_now, w_up_now)
+    far = [swap(from_one, "seq", 2), swap(from_two, "seq", 1)]
     w_units = jnp.stack([gain_two[:, None] * w_gate_now, gain_two[:, None] * w_up_now], axis=1)
     w_units = w_units.reshape(rows, 2, shards, units).transpose(0, 2, 1, 3).reshape(rows, shards, 2 * units)
     *w_turned, w_out_own = turn_in(w_pre, 3 * own, split)

time: 411 us -> 408 us (level)
    ppermute x38, waiting for transfers between devices: 58.6 us -> 67.5 us  [swap(): lax.ppermute(value, axis, [(i, i ^ distance) for i in range(devices)])]
    reduce_scatter x3, waiting for transfers between devices: 13.3 us -> 7.42 us  [sum_over_batch(): return lax.psum_scatter(flat, 'batch', scatter_dimension=0, tiled=True)]
  transfers between devices with their start and end apart: 47 -> 47, of which waited for: 18 -> 20; matrix products, arithmetic and copies ran while one was open for 7% -> 6% of each run, Pallas kernels for 52% -> 52%
where the time goes in v6:
time: 408 us; the launch traced here: 402 us
  Pallas kernels  214 us (52%)
  waiting for transfers between devices  87.6 us (21%)
  starting transfers between devices  47.7 us (12%)
  local copies, waits for them, and re-layouts  28 us (7%)
  between operations  15.3 us (4%)
  other arithmetic  9.42 us (2%)
    pallas_call x23, Pallas kernels, call(): pl.pallas_call(run, name=name, out_shape=tuple(outs), grid_spec=pltpu.Pre...  207 us
    ppermute x38, waiting for transfers between devices, swap(): lax.ppermute(value, axis, [(i, i ^ distance) for i in range(devices)])  67.5 us
    ppermute x38, starting transfers between devices, swap(): lax.ppermute(value, axis, [(i, i ^ distance) for i in range(devices)])  44.9 us
    ppermute x1, waiting for transfers between devices, body(): folded = lax.ppermute(wide[:, ::-1, :4:-1], 'batch', mirror)  12 us
  transfers between devices with their start and end apart: 47, of which 20 were waited for; matrix products, arithmetic and copies ran while one was open for 6% of the time, Pallas kernels for 52%

profile of v6, /device:TPU:0, one launch (start us, length us, event | category | flops | bytes accessed | tf_op | source)
XLA Modules:
  0.0 402.3 jit_solution(6339983207798267276)
XLA Ops:
  9.1 4.0 collective-permute-start
  15.3 2.0 collective-permute-done.1
  19.3 1.7 collective-permute-start.4
  24.1 1.4 collective-permute-start.5
  25.4 12.0 %collective-permute-done.5.refs_1_ = f32[2,32,3,192]{3,2,1,0:T(4,128)S(1)} collective-permute-done((f32[2,32,3,192]{3,2,1,0:T(4,128)}, f32[2,32,3,192]{3,2,1,0:T(4,128)S(1)}, u32[]{:S(2)}, u32[]{:S(2)}) %collective-permute-start.5) | collective-permute-done | bytes 147488 | tf_op jit(solution)/shard_map/ppermute | solution.py:910
  38.2 2.0 fold_base.1
  40.1 13.6 %collective-permute-done.3.refs_2_ = f32[2,256,768]{2,1,0:T(8,128)S(1)} collective-permute-done((f32[2,256,768]{2,1,0:T(8,128)S(1)}, f32[2,256,768]{2,1,0:T(8,128)S(1)}, u32[]{:S(2)}, u32[]{:S(2)}) %collective-permute-start.3) | collective-permute-done | bytes 1572896 | tf_op jit(solution)/shard_map/ppermute | solution.py:31
  54.6 2.4 slice_bitcast_fusion
  60.2 1.7 collective-permute-start.8
  62.8 1.2 collective-permute-start.6
  64.0 1.2 collective-permute-start.7
  66.0 3.6 collective-permute-done.8
  71.3 4.2 %turn_in.1 = (bf16[576,768]{1,0:T(8,128)(2,1)}, bf16[576,768]{1,0:T(8,128)(2,1)}, f32[192,768]{1,0:T(8,128)}) custom-call(f32[8,4,24,777]{3,2,1,0:T(8,128)} %bitcast.147), custom_call_target="tpu_custom_call" | custom-call | bytes 196608 | tf_op jit(solution)/shard_map/turn_in/pallas_call | solution.py:122
  76.6 8.1 %collective-permute-done.6.refs_4_ = f32[256,768]{1,0:T(8,128)S(1)} collective-permute-done((f32[256,768]{1,0:T(8,128)}, f32[256,768]{1,0:T(8,128)S(1)}, u32[]{:S(2)}, u32[]{:S(2)}) %collective-permute-start.6) | collective-permute-done | bytes 786464 | tf_op jit(solution)/shard_map/ppermute | solution.py:31
  86.8 1.2 collective-permute-start.12
  90.4 5.3 %arrange.2 = (f32[1024,768]{1,0:T(8,128)}, bf16[1024,768]{1,0:T(8,128)(2,1)}, bf16[1024,768]{1,0:T(8,128)(2,1)}) custom-call(s32[1]{0:T(128)} %bitcast.refs_0_.s_ref, f32[2,256,768]{2,1,0:T(8,128)} %x_ref.3, f32[2,256,768]{2,1,0:T(8,128)} %copy-done.1, f32[2,256,768]{2,1,0:T(8,128)} %collective-permute-done.4.refs_3_, f32[256,768]{1,0:T(8,128)} %copy-done.26), custom_call_target="tpu_custom_call" | custom-call | bytes 471859 | tf_op jit(solution)/shard_map/arrange/pallas_call | solution.py:122
  95.7 6.2 %project.2 = f32[576,1024]{1,0:T(8,128)} custom-call(bf16[576,768]{1,0:T(8,128)(2,1)} %get-tuple-element.207.refs_0_.refs_4_, bf16[576,768]{1,0:T(8,128)(2,1)} %get-tuple-element.208.refs_1_.refs_5_, bf16[1024,768]{1,0:T(8,128)(2,1)} %get-tuple-element.304.refs_2_, bf16[1024,768]{1,0:T(8,128)(2,1)} %get-tuple-element.305.refs_3_), custom_call_target="tpu_custom_call" | custom-call | flops 135895456 | bytes 363724 | tf_op jit(solution)/shard_map/project/pallas_call | solution.py:122
  101.8 13.5 %mix.2 = (f32[192,1024]{1,0:T(8,128)}, f32[192,1024]{1,0:T(8,128)}, f32[192,1024]{1,0:T(8,128)}, f32[5,192,512]{2,1,0:T(8,128)}, f32[5,192,512]{2,1,0:T(8,128)}) custom-call(f32[3,192,1024]{2,1,0:T(8,128)} %bitcast.133, f32[3,192,3]{2,1,0:T(8,128)} %bitcast.144, f32[8,160,384]{2,1,0:T(8,128)} %bitcast.141, ...), custom_call_target="tpu_custom_call" | custom-call | flops 724775744 | bytes 865075 | tf_op jit(solution)/shard_map/mix/pallas_call | solution.py:122
  115.4 1.2 collective-permute-start.14
  116.6 1.4 collective-permute-start.15
  118.9 5.4 %arrange.3 = (f32[1024,768]{1,0:T(8,128)}, bf16[1024,768]{1,0:T(8,128)(2,1)}, bf16[1024,768]{1,0:T(8,128)(2,1)}) custom-call(s32[1]{0:T(128)} %bitcast.refs_0_.s_ref, f32[2,256,768]{2,1,0:T(8,128)} %x_ref.3, f32[2,256,768]{2,1,0:T(8,128)} %copy-done.1, f32[2,256,768]{2,1,0:T(8,128)} %collective-permute-done.4.refs_3_, f32[256,768]{1,0:T(8,128)} %copy-done.21, ...), custom_call_target="tpu_custom_call" | custom-call | bytes 471859 | tf_op jit(solution)/shard_map/arrange/pallas_call | solution.py:122
  124.4 6.2 %project.3 = f32[576,1024]{1,0:T(8,128)} custom-call(bf16[576,768]{1,0:T(8,128)(2,1)} %get-tuple-element.207.refs_0_.refs_4_, bf16[576,768]{1,0:T(8,128)(2,1)} %get-tuple-element.208.refs_1_.refs_5_, bf16[1024,768]{1,0:T(8,128)(2,1)} %get-tuple-element.319.refs_2_, bf16[1024,768]{1,0:T(8,128)(2,1)} %get-tuple-element.320.refs_3_), custom_call_target="tpu_custom_call" | custom-call | flops 135895456 | bytes 363724 | tf_op jit(solution)/shard_map/project/pallas_call | solution.py:122
  130.6 14.0 %mix.3 = (f32[192,1024]{1,0:T(8,128)}, f32[192,1024]{1,0:T(8,128)}, f32[192,1024]{1,0:T(8,128)}, f32[5,192,512]{2,1,0:T(8,128)}, f32[5,192,512]{2,1,0:T(8,128)}) custom-call(f32[3,192,1024]{2,1,0:T(8,128)} %bitcast.135, f32[3,192,3]{2,1,0:T(8,128)} %bitcast.145, f32[8,160,384]{2,1,0:T(8,128)} %bitcast.142, ...), custom_call_target="tpu_custom_call" | custom-call | flops 724775744 | bytes 865075 | tf_op jit(solution)/shard_map/mix/pallas_call | solution.py:122
  144.6 5.6 %collective-permute-done.15.refs_3_ = f32[192,1024]{1,0:T(8,128)S(1)} collective-permute-done((f32[192,1024]{1,0:T(8,128)}, f32[192,1024]{1,0:T(8,128)S(1)}, u32[]{:S(2)}, u32[]{:S(2)}) %collective-permute-start.15) | collective-permute-done | bytes 786464 | tf_op jit(solution)/shard_map/ppermute | solution.py:31
  151.1 1.8 collective-permute-start.17
  153.3 1.3 collective-permute-start.19
  154.6 8.6 %add_mixer.2.refs_1_.refs_0_ = f32[1024,768]{1,0:T(8,128)} custom-call(f32[1024,768]{1,0:T(8,128)} %get-tuple-element.231.refs_0_, f32[192,1024]{1,0:T(8,128)} %get-tuple-element.220.refs_5_.refs_1_, f32[192,1024]{1,0:T(8,128)} %copy-done.23, f32[192,1024]{1,0:T(8,128)} %copy-done.24, f32[192,1024]{1,0:T(8,128)} %copy-done.25, ...), custom_call_target="tpu_custom_call" | custom-call | flops 181193936 | bytes 589824 | tf_op jit(solution)/shard_map/add_mixer/pallas_call | solution.py:122
  163.1 5.2 %split_units.1 = (bf16[768,1536]{1,0:T(8,128)(2,1)}, bf16[768,1536]{1,0:T(8,128)(2,1)}) custom-call(f32[8,4,24,1536]{3,2,1,0:T(8,128)} %bitcast.143, f32[1024,768]{1,0:T(8,128)} %add_mixer.2.refs_1_.refs_0_), custom_call_target="tpu_custom_call" | custom-call | bytes 471859 | tf_op jit(solution)/shard_map/split_units/pallas_call | solution.py:122
  168.3 12.5 %units_of.1 = (bf16[1024,768]{1,0:T(8,128)(2,1)}, bf16[1024,768]{1,0:T(8,128)(2,1)}) custom-call(f32[1024,768]{1,0:T(8,128)} %add_mixer.2.refs_1_.refs_0_, bf16[768,1536]{1,0:T(8,128)(2,1)} %get-tuple-element.256.refs_1_.refs_12_.refs_2_, bf16[768,1536]{1,0:T(8,128)(2,1)} %get-tuple-element.257.refs_2_.refs_13_.refs_3_), custom_call_target="tpu_custom_call" | custom-call | flops 362387872 | bytes 550502 | tf_op jit(solution)/shard_map/units_of/pallas_call | solution.py:122
  180.8 2.9 split_down.1
  183.7 7.6 %down_of.1 = (f32[256,768]{1,0:T(8,128)}, f32[256,768]{1,0:T(8,128)}, f32[256,768]{1,0:T(8,128)}, f32[256,768]{1,0:T(8,128)}) custom-call(s32[1]{0:T(128)} %bitcast.refs_0_.s_ref, bf16[1024,768]{1,0:T(8,128)(2,1)} %get-tuple-element.241.refs_1_, bf16[1024,768]{1,0:T(8,128)(2,1)} %get-tuple-element.242.refs_2_, ...), custom_call_target="tpu_custom_call" | custom-call | flops 181193936 | bytes 432537 | tf_op jit(solution)/shard_map/down_of/pallas_call | solution.py:122
  191.3 1.9 collective-permute-start.20
  194.3 18.5 %live_back.1 = (f32[256,768]{1,0:T(8,128)}, f32[256,768]{1,0:T(8,128)}, f32[256,768]{1,0:T(8,128)}, f32[256,1536]{1,0:T(8,128)}, f32[160,768]{1,0:T(8,128)}) custom-call(f32[1024,768]{1,0:T(8,128)} %add_mixer.2.refs_1_.refs_0_, f32[1024,768]{1,0:T(8,128)} %get-tuple-element.251.refs_1_.refs_0_, f32[192,1024]{1,0:T(8,128)} %get-tuple-element.230.refs_9_.refs_2_.refs_1_, ...), custom_call_target="tpu_custom_call" | custom-call | flops 226492416 | bytes 786432 | tf_op jit(solution)/shard_map/live_back/pallas_call | solution.py:122
  212.9 7.0 %unit_grads.1.refs_9_ = f32[8,96,2304]{2,1,0:T(8,128)} custom-call(f32[256,768]{1,0:T(8,128)} %get-tuple-element.262.refs_0_, f32[256,1536]{1,0:T(8,128)} %get-tuple-element.263.refs_1_, f32[256,768]{1,0:T(8,128)} %get-tuple-element.264.refs_2_, f32[256,768]{1,0:T(8,128)} %bitcast.138), custom_call_target="tpu_custom_call" | custom-call | flops 135895456 | bytes 353894 | tf_op jit(solution)/shard_map/unit_grads/pallas_call | solution.py:122
  221.0 1.5 collective-permute-start.22
  222.9 8.9 %add_mixer.3.refs_1_ = f32[1024,768]{1,0:T(8,128)} custom-call(f32[1024,768]{1,0:T(8,128)} %get-tuple-element.251.refs_1_.refs_0_, f32[192,1024]{1,0:T(8,128)} %get-tuple-element.230.refs_9_.refs_2_.refs_1_, f32[192,1024]{1,0:T(8,128)} %copy-done.5, f32[192,1024]{1,0:T(8,128)} %copy-done.6, f32[192,1024]{1,0:T(8,128)} %copy-done.7, ...), custom_call_target="tpu_custom_call" | custom-call | flops 181193936 | bytes 589824 | tf_op jit(solution)/shard_map/add_mixer/pallas_call | solution.py:122
  231.9 1.6 collective-permute-start.24
  234.2 1.3 collective-permute-start.26
  235.5 16.6 %feed_forward.1 = (f32[256,768]{1,0:T(8,128)}, f32[256,768]{1,0:T(8,128)}, f32[256,768]{1,0:T(8,128)}, f32[256,768]{1,0:T(8,128)}) custom-call(s32[1]{0:T(128)} %bitcast.refs_0_.s_ref, f32[1024,768]{1,0:T(8,128)} %add_mixer.3.refs_1_, bf16[768,1536]{1,0:T(8,128)(2,1)} %get-tuple-element.256.refs_1_.refs_12_.refs_2_, ...), custom_call_target="tpu_custom_call" | custom-call | flops 543581824 | bytes 668467 | tf_op jit(solution)/shard_map/feed_forward/pallas_call | solution.py:122
  252.1 1.8 collective-permute-start.27
  254.4 1.3 collective-permute-start.29
  255.7 6.2 %live_mix.1 = (f32[256,768]{1,0:T(8,128)}, f32[192,768]{1,0:T(8,128)}, f32[2,192,128]{2,1,0:T(8,128)}, f32[2,192,128]{2,1,0:T(8,128)}) custom-call(f32[256,768]{1,0:T(8,128)} %get-tuple-element.268.refs_0_, f32[256,768]{1,0:T(8,128)} %bitcast.139, f32[80,768]{1,0:T(8,128)} %copy-done.13, f32[80,768]{1,0:T(8,128)} %copy-done.12, f32[80,768]{1,0:T(8,128)} %copy-done.31, ...), custom_call_target="tpu_custom_call" | custom-call | flops 37748736 | bytes 314572 | tf_op jit(solution)/shard_map/live_mix/pallas_call | solution.py:122
  261.9 24.4 %mix_back.1 = (f32[3,192,1024]{2,1,0:T(8,128)}, f32[3,192,1024]{2,1,0:T(8,128)}, f32[8,5,32,384]{3,2,1,0:T(8,128)}, f32[3,192,128]{2,1,0:T(8,128)}) custom-call(s32[2,128,1]{2,1,0:T(8,128)} %copy.60.refs_10_.refs_11_.refs_0_.at_ref, f32[2,192,128]{2,1,0:T(8,128)} %get-tuple-element.284.refs_1_, f32[2,192,128]{2,1,0:T(8,128)} %get-tuple-element.285.refs_2_, ...), custom_call_target="tpu_custom_call" | custom-call | flops 1449551488 | bytes 1730150 | tf_op jit(solution)/shard_map/mix_back/pallas_call | solution.py:122
  286.6 12.0 %project_back.2 = (f32[256,768]{1,0:T(8,128)}, f32[256,768]{1,0:T(8,128)}, f32[256,768]{1,0:T(8,128)}, f32[256,768]{1,0:T(8,128)}, f32[576,768]{1,0:T(8,128)}) custom-call(s32[1]{0:T(128)} %bitcast.refs_0_.s_ref, f32[576,1024]{1,0:T(8,128)} %bitcast.153, bf16[1024,768]{1,0:T(8,128)(2,1)} %get-tuple-element.304.refs_2_, ...), custom_call_target="tpu_custom_call" | custom-call | flops 271790912 | bytes 697958 | tf_op jit(solution)/shard_map/project_back/pallas_call | solution.py:122
  298.7 1.9 collective-permute-start.30
  302.9 12.2 %project_back.3 = (f32[256,768]{1,0:T(8,128)}, f32[256,768]{1,0:T(8,128)}, f32[256,768]{1,0:T(8,128)}, f32[256,768]{1,0:T(8,128)}, f32[576,768]{1,0:T(8,128)}) custom-call(s32[1]{0:T(128)} %bitcast.refs_0_.s_ref, f32[576,1024]{1,0:T(8,128)} %bitcast.152, bf16[1024,768]{1,0:T(8,128)(2,1)} %get-tuple-element.319.refs_2_, ...), custom_call_target="tpu_custom_call" | custom-call | flops 271790912 | bytes 697958 | tf_op jit(solution)/shard_map/project_back/pallas_call | solution.py:122
  315.1 3.9 turn_back.1
  321.8 1.9 collective-permute-start.32
  325.3 1.9 add_bitcast_fusion.1
  328.7 1.6 add_bitcast_fusion
  330.4 4.8 %reduce-scatter.8.cloned.1.call-done = f32[160,384]{1,0:T(8,128)} async-done(((f32[1280,384]{1,0:T(8,128)}), f32[160,384]{1,0:T(8,128)}) %reduce-scatter.8.cloned.1.call-update) | async-done | bytes 245776 | tf_op jit(solution)/shard_map/reduce_scatter | solution.py:84
  337.4 1.2 pad_maximum_fusion
  338.6 4.2 %collective-permute-done.36.e3 = f32[256,768]{1,0:T(8,128)} collective-permute-done((f32[256,768]{1,0:T(8,128)}, f32[256,768]{1,0:T(8,128)}, u32[]{:S(2)}, u32[]{:S(2)}) %collective-permute-start.36) | collective-permute-done | bytes 786464 | tf_op jit(solution)/shard_map/ppermute | solution.py:31
  342.8 3.8 finish.2.refs_0_
  346.6 12.7 %collective-permute-done.32.e1 = f32[256,768]{1,0:T(8,128)} collective-permute-done((f32[256,768]{1,0:T(8,128)}, f32[256,768]{1,0:T(8,128)}, u32[]{:S(2)}, u32[]{:S(2)}) %collective-permute-start.32) | collective-permute-done | bytes 786464 | tf_op jit(solution)/shard_map/ppermute | solution.py:31
  359.6 11.9 %collective-permute-done.34.e3 = f32[256,768]{1,0:T(8,128)} collective-permute-done((f32[256,768]{1,0:T(8,128)}, f32[256,768]{1,0:T(8,128)}, u32[]{:S(2)}, u32[]{:S(2)}) %collective-permute-start.34) | collective-permute-done | bytes 786464 | tf_op jit(solution)/shard_map/ppermute | solution.py:31
  371.5 2.6 reduce-scatter.6.cloned.1.call-done
  375.8 1.5 collective-permute-start.37
  377.4 1.6 collective-permute-start.38
  381.0 3.8 finish.3
  384.8 1.4 collective-permute-done.38.refs_3_
  386.9 3.4 weight_grads.1
  391.7 1.2 slice_bitcast_fusion.2
  392.9 1.2 slice_bitcast_fusion.3
  (221 shorter events, 46.3 us)
Async XLA Ops:
  7.2 6.7 %copy-start.27 = (f32[2,80,768]{2,1,0:T(8,128)S(1)}, f32[2,80,768]{2,1,0:T(8,128)}, u32[]{:S(2)}) copy-start(f32[2,80,768]{2,1,0:T(8,128)} %param.27) | copy-start | bytes 1474564
  7.2 6.8 %copy-start.36 = (f32[24,768]{1,0:T(8,128)S(1)}, f32[24,768]{1,0:T(8,128)}, u32[]{:S(2)}) copy-start(f32[24,768]{1,0:T(8,128)} %param.20) | copy-start | bytes 221188
  7.2 64.0 %all-gather.5.cloned.1.call-start = ((), (), s32[]{:S(2)}) async-start(), calls=%async_computation.3 | async-start | bytes 3096576 | tf_op jit(solution)/shard_map/all_gather | solution.py:78
  9.1 6.2 %collective-permute-start = (f32[24,585]{1,0:T(8,128)S(1)}, f32[24,585]{1,0:T(8,128)S(1)}, u32[]{:S(2)}, u32[]{:S(2)}) collective-permute-start(f32[24,585]{1,0:T(8,128)S(1)} %get-tuple-element.412), channel_id=1, source_target_pairs={{0,24},{8,16},{16,8},{24,0},{1,25},{9,17},{17,9},{25,1},{2,26},{10... | collective-permute-start | bytes 168488 | tf_op jit(solution)/shard_map/ppermute | solution.py:31
  13.1 4.2 %collective-permute-start.1 = (f32[24,585]{1,0:T(8,128)S(1)}, f32[24,585]{1,0:T(8,128)S(1)}, u32[]{:S(2)}, u32[]{:S(2)}) collective-permute-start(f32[24,585]{1,0:T(8,128)S(1)} %get-tuple-element.413), channel_id=1, source_target_pairs={{0,16},{8,24},{16,0},{24,8},{1,17},{9,25},{17,1},{25,9},{2,18},{10... | collective-permute-start | bytes 168488 | tf_op jit(solution)/shard_map/ppermute | solution.py:31
  13.6 4.2 %collective-permute-start.2 = (f32[24,585]{1,0:T(8,128)S(1)}, f32[24,585]{1,0:T(8,128)S(1)}, u32[]{:S(2)}, u32[]{:S(2)}) collective-permute-start(f32[24,585]{1,0:T(8,128)S(1)} %get-tuple-element.414), channel_id=1, source_target_pairs={{0,8},{8,0},{16,24},{24,16},{1,9},{9,1},{17,25},{25,17},{2,10},{10... | collective-permute-start | bytes 168488 | tf_op jit(solution)/shard_map/ppermute | solution.py:31
  14.0 7.0 %copy-start.28 = (f32[2,256,192]{1,2,0:T(8,128)S(1)}, f32[2,256,192]{1,2,0:T(8,128)}, u32[]{:S(2)}) copy-start(f32[2,256,192]{1,2,0:T(8,128)} %param.19) | copy-start | bytes 1179652
  18.8 83.1 %all-gather.7.cloned.1.call-start = ((), (), s32[]{:S(2)}) async-start(), calls=%async_computation.4 | async-start | bytes 2211840 | tf_op jit(solution)/shard_map/all_gather | solution.py:78
  18.8 34.8 %collective-permute-start.3 = (f32[2,256,768]{2,1,0:T(8,128)S(1)}, f32[2,256,768]{2,1,0:T(8,128)S(1)}, u32[]{:S(2)}, u32[]{:S(2)}) collective-permute-start(f32[2,256,768]{2,1,0:T(8,128)S(1)} %copy-done), channel_id=1, source_target_pairs={{0,8},{8,0},{16,24},{24,16},{1,9},{9,1},{17,25},{25,17},{2,10},{10... | collective-permute-start | bytes 4718600 | tf_op jit(solution)/shard_map/ppermute | solution.py:31
  19.3 35.3 %collective-permute-start.4 = (f32[2,256,768]{2,1,0:T(8,128)S(1)}, f32[2,256,768]{2,1,0:T(8,128)}, u32[]{:S(2)}, u32[]{:S(2)}) collective-permute-start(f32[2,256,768]{2,1,0:T(8,128)S(1)} %copy-done), channel_id=1, source_target_pairs={{0,16},{8,24},{16,0},{24,8},{1,17},{9,25},{17,1},{25,9},{2,18},{10... | collective-permute-start | bytes 4718600 | tf_op jit(solution)/shard_map/ppermute | solution.py:31
  24.1 33.0 %copy-start.10 = (f32[24,3072]{1,0:T(8,128)S(1)}, f32[24,3072]{1,0:T(8,128)}, u32[]{:S(2)}) copy-start(f32[24,3072]{1,0:T(8,128)} %refs_8_.1) | copy-start | bytes 884740
  24.1 33.0 %copy-start.37 = (f32[24]{0:T(128)S(1)}, f32[24]{0:T(128)}, u32[]{:S(2)}) copy-start(f32[24]{0:T(128)} %param.21) | copy-start | bytes 292
  24.1 13.4 %collective-permute-start.5 = (f32[2,32,3,192]{3,2,1,0:T(4,128)}, f32[2,32,3,192]{3,2,1,0:T(4,128)S(1)}, u32[]{:S(2)}, u32[]{:S(2)}) collective-permute-start(f32[2,32,3,192]{3,2,1,0:T(4,128)} %rev.6), channel_id=1, source_target_pairs={{0,7},{1,6},{2,5},{3,4},{4,3},{5,2},{6,1},{7,0},{8,15},{9,14},{10,... | collective-permute-start | bytes 442376 | tf_op jit(solution)/shard_map/ppermute | solution.py:910
  54.6 108.5 %all-gather.9.cloned.1.call-start = ((), (), s32[]{:S(2)}) async-start(), calls=%async_computation.5 | async-start | bytes 5308416 | tf_op jit(solution)/shard_map/all_gather | solution.py:78
  59.2 6.8 %collective-permute-start.10 = (f32[24,1536]{1,0:T(8,128)S(1)}, f32[24,1536]{1,0:T(8,128)S(1)}, u32[]{:S(2)}, u32[]{:S(2)}) collective-permute-start(f32[24,1536]{1,0:T(8,128)S(1)} %get-tuple-element.402), channel_id=1, source_target_pairs={{0,8},{8,0},{16,24},{24,16},{1,9},{9,1},{17,25},{25,17},{2,10},{10... | collective-permute-start | bytes 442376 | tf_op jit(solution)/shard_map/ppermute | solution.py:31
  60.2 9.3 %collective-permute-start.8 = (f32[24,1536]{1,0:T(8,128)S(1)}, f32[24,1536]{1,0:T(8,128)S(1)}, u32[]{:S(2)}, u32[]{:S(2)}) collective-permute-start(f32[24,1536]{1,0:T(8,128)S(1)} %get-tuple-element.401), channel_id=1, source_target_pairs={{0,24},{8,16},{16,8},{24,0},{1,25},{9,17},{17,9},{25,1},{2,26},{10... | collective-permute-start | bytes 442376 | tf_op jit(solution)/shard_map/ppermute | solution.py:31
  62.0 8.4 %collective-permute-start.9 = (f32[24,1536]{1,0:T(8,128)S(1)}, f32[24,1536]{1,0:T(8,128)S(1)}, u32[]{:S(2)}, u32[]{:S(2)}) collective-permute-start(f32[24,1536]{1,0:T(8,128)S(1)} %get-tuple-element.403), channel_id=1, source_target_pairs={{0,16},{8,24},{16,0},{24,8},{1,17},{9,25},{17,1},{25,9},{2,18},{10... | collective-permute-start | bytes 442376 | tf_op jit(solution)/shard_map/ppermute | solution.py:31
  62.8 22.0 %collective-permute-start.6 = (f32[256,768]{1,0:T(8,128)}, f32[256,768]{1,0:T(8,128)S(1)}, u32[]{:S(2)}, u32[]{:S(2)}) collective-permute-start(f32[256,768]{1,0:T(8,128)} %get-tuple-element.198), channel_id=1, source_target_pairs={{0,16},{8,24},{16,0},{24,8},{1,17},{9,25},{17,1},{25,9},{2,18},{10... | collective-permute-start | bytes 2359304 | tf_op jit(solution)/shard_map/ppermute | solution.py:31
  64.0 20.7 %collective-permute-start.7 = (f32[256,768]{1,0:T(8,128)}, f32[256,768]{1,0:T(8,128)S(1)}, u32[]{:S(2)}, u32[]{:S(2)}) collective-permute-start(f32[256,768]{1,0:T(8,128)} %get-tuple-element.199), channel_id=1, source_target_pairs={{0,8},{8,0},{16,24},{24,16},{1,9},{9,1},{17,25},{25,17},{2,10},{10... | collective-permute-start | bytes 2359304 | tf_op jit(solution)/shard_map/ppermute | solution.py:31
  84.7 11.0 %copy-start.21 = (f32[256,768]{1,0:T(8,128)}, f32[256,768]{1,0:T(8,128)S(1)}, u32[]{:S(2)}) copy-start(f32[256,768]{1,0:T(8,128)S(1)} %collective-permute-done.7.refs_4_) | copy-start | bytes 2359300
  84.8 96.0 %all-gather.11.cloned.1.call-start = ((), (), s32[]{:S(2)}) async-start(), calls=%async_computation.6 | async-start | bytes 2654208 | tf_op jit(solution)/shard_map/all_gather | solution.py:78
  85.3 213.3 %reduce-scatter.4.cloned.1.call-start = ((), (), s32[]{:S(2)}) async-start(), calls=%async_computation.7 | async-start | bytes 7962624 | tf_op jit(solution)/shard_map/reduce_scatter | solution.py:84
  85.6 29.7 %collective-permute-start.11 = (f32[192,768]{1,0:T(8,128)}, f32[192,768]{1,0:T(8,128)S(1)}, u32[]{:S(2)}, u32[]{:S(2)}) collective-permute-start(f32[192,768]{1,0:T(8,128)} %get-tuple-element.206.refs_5_.refs_6_), channel_id=1, source_target_pairs={{0,8},{8,0},{16,24},{24,16},{1,9},{9,1},{17,25},{25,17},{2,10},{10... | collective-permute-start | bytes 1769480 | tf_op jit(solution)/shard_map/ppermute | solution.py:31
  86.8 28.6 %collective-permute-start.12 = (f32[192,768]{1,0:T(8,128)}, f32[192,768]{1,0:T(8,128)S(1)}, u32[]{:S(2)}, u32[]{:S(2)}) collective-permute-start(f32[192,768]{1,0:T(8,128)} %get-tuple-element.206.refs_5_.refs_6_), channel_id=1, source_target_pairs={{0,16},{8,24},{16,0},{24,8},{1,17},{9,25},{17,1},{25,9},{2,18},{10... | collective-permute-start | bytes 1769480 | tf_op jit(solution)/shard_map/ppermute | solution.py:31
  88.0 27.4 %collective-permute-start.13 = (f32[192,768]{1,0:T(8,128)}, f32[192,768]{1,0:T(8,128)S(1)}, u32[]{:S(2)}, u32[]{:S(2)}) collective-permute-start(f32[192,768]{1,0:T(8,128)} %get-tuple-element.206.refs_5_.refs_6_), channel_id=1, source_target_pairs={{0,24},{8,16},{16,8},{24,0},{1,25},{9,17},{17,9},{25,1},{2,26},{10... | collective-permute-start | bytes 1769480 | tf_op jit(solution)/shard_map/ppermute | solution.py:31
  115.3 9.0 %copy-start.2 = (f32[192,768]{1,0:T(8,128)}, f32[192,768]{1,0:T(8,128)S(1)}, u32[]{:S(2)}) copy-start(f32[192,768]{1,0:T(8,128)S(1)} %collective-permute-done.11.refs_6_.refs_7_) | copy-start | bytes 1769476
  115.3 9.0 %copy-start.3 = (f32[192,768]{1,0:T(8,128)}, f32[192,768]{1,0:T(8,128)S(1)}, u32[]{:S(2)}) copy-start(f32[192,768]{1,0:T(8,128)S(1)} %collective-permute-done.12.refs_7_.refs_8_) | copy-start | bytes 1769476
  115.4 9.0 %copy-start.4 = (f32[192,768]{1,0:T(8,128)}, f32[192,768]{1,0:T(8,128)S(1)}, u32[]{:S(2)}) copy-start(f32[192,768]{1,0:T(8,128)S(1)} %collective-permute-done.13.refs_8_.refs_9_) | copy-start | bytes 1769476
  115.4 29.2 %collective-permute-start.14 = (f32[192,1024]{1,0:T(8,128)}, f32[192,1024]{1,0:T(8,128)S(1)}, u32[]{:S(2)}, u32[]{:S(2)}) collective-permute-start(f32[192,1024]{1,0:T(8,128)} %get-tuple-element.220.refs_5_.refs_1_), channel_id=1, source_target_pairs={{0,8},{8,0},{16,24},{24,16},{1,9},{9,1},{17,25},{25,17},{2,10},{10... | collective-permute-start | bytes 2359304 | tf_op jit(solution)/shard_map/ppermute | solution.py:31
  116.6 33.6 %collective-permute-start.15 = (f32[192,1024]{1,0:T(8,128)}, f32[192,1024]{1,0:T(8,128)S(1)}, u32[]{:S(2)}, u32[]{:S(2)}) collective-permute-start(f32[192,1024]{1,0:T(8,128)} %get-tuple-element.220.refs_5_.refs_1_), channel_id=1, source_target_pairs={{0,16},{8,24},{16,0},{24,8},{1,17},{9,25},{17,1},{25,9},{2,18},{10... | collective-permute-start | bytes 2359304 | tf_op jit(solution)/shard_map/ppermute | solution.py:31
  118.0 33.1 %collective-permute-start.16 = (f32[192,1024]{1,0:T(8,128)}, f32[192,1024]{1,0:T(8,128)S(1)}, u32[]{:S(2)}, u32[]{:S(2)}) collective-permute-start(f32[192,1024]{1,0:T(8,128)} %get-tuple-element.220.refs_5_.refs_1_), channel_id=1, source_target_pairs={{0,24},{8,16},{16,8},{24,0},{1,25},{9,17},{17,9},{25,1},{2,26},{10... | collective-permute-start | bytes 2359304 | tf_op jit(solution)/shard_map/ppermute | solution.py:31
  144.6 10.0 %copy-start.23 = (f32[192,1024]{1,0:T(8,128)}, f32[192,1024]{1,0:T(8,128)S(1)}, u32[]{:S(2)}) copy-start(f32[192,1024]{1,0:T(8,128)S(1)} %collective-permute-done.14.refs_2_) | copy-start | bytes 2359300
  151.1 40.2 %collective-permute-start.17 = (f32[192,1024]{1,0:T(8,128)}, f32[192,1024]{1,0:T(8,128)S(1)}, u32[]{:S(2)}, u32[]{:S(2)}) collective-permute-start(f32[192,1024]{1,0:T(8,128)} %get-tuple-element.230.refs_9_.refs_2_.refs_1_), channel_id=1, source_target_pairs={{0,8},{8,0},{16,24},{24,16},{1,9},{9,1},{17,25},{25,17},{2,10},{10... | collective-permute-start | bytes 2359304 | tf_op jit(solution)/shard_map/ppermute | solution.py:31
  152.9 38.4 %collective-permute-start.18 = (f32[192,1024]{1,0:T(8,128)}, f32[192,1024]{1,0:T(8,128)S(1)}, u32[]{:S(2)}, u32[]{:S(2)}) collective-permute-start(f32[192,1024]{1,0:T(8,128)} %get-tuple-element.230.refs_9_.refs_2_.refs_1_), channel_id=1, source_target_pairs={{0,16},{8,24},{16,0},{24,8},{1,17},{9,25},{17,1},{25,9},{2,18},{10... | collective-permute-start | bytes 2359304 | tf_op jit(solution)/shard_map/ppermute | solution.py:31
  153.3 38.0 %collective-permute-start.19 = (f32[192,1024]{1,0:T(8,128)}, f32[192,1024]{1,0:T(8,128)S(1)}, u32[]{:S(2)}, u32[]{:S(2)}) collective-permute-start(f32[192,1024]{1,0:T(8,128)} %get-tuple-element.230.refs_9_.refs_2_.refs_1_), channel_id=1, source_target_pairs={{0,24},{8,16},{16,8},{24,0},{1,25},{9,17},{17,9},{25,1},{2,26},{10... | collective-permute-start | bytes 2359304 | tf_op jit(solution)/shard_map/ppermute | solution.py:31
  191.3 28.6 %collective-permute-start.20 = (f32[256,768]{1,0:T(8,128)}, f32[256,768]{1,0:T(8,128)S(1)}, u32[]{:S(2)}, u32[]{:S(2)}) collective-permute-start(f32[256,768]{1,0:T(8,128)} %get-tuple-element.266), channel_id=1, source_target_pairs={{0,8},{8,0},{16,24},{24,16},{1,9},{9,1},{17,25},{25,17},{2,10},{10... | collective-permute-start | bytes 2359304 | tf_op jit(solution)/shard_map/ppermute | solution.py:31
  193.2 26.7 %collective-permute-start.21 = (f32[256,768]{1,0:T(8,128)}, f32[256,768]{1,0:T(8,128)}, u32[]{:S(2)}, u32[]{:S(2)}) collective-permute-start(f32[256,768]{1,0:T(8,128)} %get-tuple-element.267), channel_id=1, source_target_pairs={{0,16},{8,24},{16,0},{24,8},{1,17},{9,25},{17,1},{25,9},{2,18},{10... | collective-permute-start | bytes 2359304 | tf_op jit(solution)/shard_map/ppermute | solution.py:31
  219.9 115.3 %reduce-scatter.8.cloned.1.call-start = ((), (), s32[]{:S(2)}) async-start(), calls=%async_computation.9 | async-start | bytes 2211840 | tf_op jit(solution)/shard_map/reduce_scatter | solution.py:84
  221.0 10.9 %collective-permute-start.22 = (f32[80,768]{1,0:T(8,128)S(1)}, f32[80,768]{1,0:T(8,128)S(1)}, u32[]{:S(2)}, u32[]{:S(2)}) collective-permute-start(f32[80,768]{1,0:T(8,128)S(1)} %get-tuple-element.407), channel_id=1, source_target_pairs={{0,8},{8,0},{16,24},{24,16},{1,9},{9,1},{17,25},{25,17},{2,10},{10... | collective-permute-start | bytes 737288 | tf_op jit(solution)/shard_map/ppermute | solution.py:31
  222.4 11.7 %copy-start.42 = (f32[256,768]{1,0:T(8,128)S(1)}, f32[256,768]{1,0:T(8,128)}, u32[]{:S(2)}) copy-start(f32[256,768]{1,0:T(8,128)} %get-tuple-element.299) | copy-start | bytes 2359300
  222.4 9.4 %collective-permute-start.23 = (f32[80,768]{1,0:T(8,128)S(1)}, f32[80,768]{1,0:T(8,128)S(1)}, u32[]{:S(2)}, u32[]{:S(2)}) collective-permute-start(f32[80,768]{1,0:T(8,128)S(1)} %get-tuple-element.406), channel_id=1, source_target_pairs={{0,16},{8,24},{16,0},{24,8},{1,17},{9,25},{17,1},{25,9},{2,18},{10... | collective-permute-start | bytes 737288 | tf_op jit(solution)/shard_map/ppermute | solution.py:31
  231.9 20.2 %copy-start.12 = (f32[80,768]{1,0:T(8,128)}, f32[80,768]{1,0:T(8,128)S(1)}, u32[]{:S(2)}) copy-start(f32[80,768]{1,0:T(8,128)S(1)} %get-tuple-element.404.refs_3_) | copy-start | bytes 737284
  231.9 20.2 %copy-start.13 = (f32[80,768]{1,0:T(8,128)}, f32[80,768]{1,0:T(8,128)S(1)}, u32[]{:S(2)}) copy-start(f32[80,768]{1,0:T(8,128)S(1)} %get-tuple-element.405.refs_2_) | copy-start | bytes 737284
  231.9 20.2 %collective-permute-start.24 = (f32[80,768]{1,0:T(8,128)S(1)}, f32[80,768]{1,0:T(8,128)S(1)}, u32[]{:S(2)}, u32[]{:S(2)}) collective-permute-start(f32[80,768]{1,0:T(8,128)S(1)} %get-tuple-element.405.refs_2_), channel_id=1, source_target_pairs={{0,16},{8,24},{16,0},{24,8},{1,17},{9,25},{17,1},{25,9},{2,18},{10... | collective-permute-start | bytes 737288 | tf_op jit(solution)/shard_map/ppermute | solution.py:31
  233.5 18.6 %collective-permute-start.25 = (f32[80,768]{1,0:T(8,128)S(1)}, f32[80,768]{1,0:T(8,128)S(1)}, u32[]{:S(2)}, u32[]{:S(2)}) collective-permute-start(f32[80,768]{1,0:T(8,128)S(1)} %get-tuple-element.404.refs_3_), channel_id=1, source_target_pairs={{0,8},{8,0},{16,24},{24,16},{1,9},{9,1},{17,25},{25,17},{2,10},{10... | collective-permute-start | bytes 737288 | tf_op jit(solution)/shard_map/ppermute | solution.py:31
  234.2 52.1 %collective-permute-start.26 = (f32[256,768]{1,0:T(8,128)S(1)}, f32[256,768]{1,0:T(8,128)S(1)}, u32[]{:S(2)}, u32[]{:S(2)}) collective-permute-start(f32[256,768]{1,0:T(8,128)S(1)} %copy-done.42), channel_id=1, source_target_pairs={{0,24},{8,16},{16,8},{24,0},{1,25},{9,17},{17,9},{25,1},{2,26},{10... | collective-permute-start | bytes 2359304 | tf_op jit(solution)/shard_map/ppermute | solution.py:31
  252.1 34.2 %collective-permute-start.27 = (f32[256,768]{1,0:T(8,128)}, f32[256,768]{1,0:T(8,128)S(1)}, u32[]{:S(2)}, u32[]{:S(2)}) collective-permute-start(f32[256,768]{1,0:T(8,128)} %get-tuple-element.301), channel_id=1, source_target_pairs={{0,8},{8,0},{16,24},{24,16},{1,9},{9,1},{17,25},{25,17},{2,10},{10... | collective-permute-start | bytes 2359304 | tf_op jit(solution)/shard_map/ppermute | solution.py:31
  254.0 32.6 %collective-permute-start.28 = (f32[256,768]{1,0:T(8,128)}, f32[256,768]{1,0:T(8,128)S(1)}, u32[]{:S(2)}, u32[]{:S(2)}) collective-permute-start(f32[256,768]{1,0:T(8,128)} %get-tuple-element.302), channel_id=1, source_target_pairs={{0,16},{8,24},{16,0},{24,8},{1,17},{9,25},{17,1},{25,9},{2,18},{10... | collective-permute-start | bytes 2359304 | tf_op jit(solution)/shard_map/ppermute | solution.py:31
  254.4 44.2 %collective-permute-start.29 = (f32[256,768]{1,0:T(8,128)}, f32[256,768]{1,0:T(8,128)}, u32[]{:S(2)}, u32[]{:S(2)}) collective-permute-start(f32[256,768]{1,0:T(8,128)} %get-tuple-element.314), channel_id=1, source_target_pairs={{0,24},{8,16},{16,8},{24,0},{1,25},{9,17},{17,9},{25,1},{2,26},{10... | collective-permute-start | bytes 2359304 | tf_op jit(solution)/shard_map/ppermute | solution.py:31
  286.3 12.3 %copy-start.16 = (f32[256,768]{1,0:T(8,128)}, f32[256,768]{1,0:T(8,128)S(1)}, u32[]{:S(2)}) copy-start(f32[256,768]{1,0:T(8,128)S(1)} %collective-permute-done.26) | copy-start | bytes 2359300
  286.3 12.3 %copy-start.17 = (f32[256,768]{1,0:T(8,128)}, f32[256,768]{1,0:T(8,128)S(1)}, u32[]{:S(2)}) copy-start(f32[256,768]{1,0:T(8,128)S(1)} %collective-permute-done.27) | copy-start | bytes 2359300
  286.6 12.0 %copy-start.19 = (f32[256,768]{1,0:T(8,128)}, f32[256,768]{1,0:T(8,128)S(1)}, u32[]{:S(2)}) copy-start(f32[256,768]{1,0:T(8,128)S(1)} %collective-permute-done.28) | copy-start | bytes 2359300
  298.7 75.3 %reduce-scatter.6.cloned.1.call-start = ((), (), s32[]{:S(2)}) async-start(), calls=%async_computation.8 | async-start | bytes 3096576 | tf_op jit(solution)/shard_map/reduce_scatter | solution.py:84
  298.7 20.4 %collective-permute-start.30 = (f32[256,768]{1,0:T(8,128)}, f32[256,768]{1,0:T(8,128)S(1)}, u32[]{:S(2)}, u32[]{:S(2)}) collective-permute-start(f32[256,768]{1,0:T(8,128)} %get-tuple-element.316), channel_id=1, source_target_pairs={{0,8},{8,0},{16,24},{24,16},{1,9},{9,1},{17,25},{25,17},{2,10},{10... | collective-permute-start | bytes 2359304 | tf_op jit(solution)/shard_map/ppermute | solution.py:31
  300.6 18.5 %collective-permute-start.31 = (f32[256,768]{1,0:T(8,128)}, f32[256,768]{1,0:T(8,128)}, u32[]{:S(2)}, u32[]{:S(2)}) collective-permute-start(f32[256,768]{1,0:T(8,128)} %get-tuple-element.317), channel_id=1, source_target_pairs={{0,16},{8,24},{16,0},{24,8},{1,17},{9,25},{17,1},{25,9},{2,18},{10... | collective-permute-start | bytes 2359304 | tf_op jit(solution)/shard_map/ppermute | solution.py:31
  321.1 21.7 %collective-permute-start.36 = (f32[256,768]{1,0:T(8,128)}, f32[256,768]{1,0:T(8,128)}, u32[]{:S(2)}, u32[]{:S(2)}) collective-permute-start(f32[256,768]{1,0:T(8,128)} %get-tuple-element.346), channel_id=1, source_target_pairs={{0,24},{8,16},{16,8},{24,0},{1,25},{9,17},{17,9},{25,1},{2,26},{10... | collective-permute-start | bytes 2359304 | tf_op jit(solution)/shard_map/ppermute | solution.py:31
  321.8 37.5 %collective-permute-start.32 = (f32[256,768]{1,0:T(8,128)}, f32[256,768]{1,0:T(8,128)}, u32[]{:S(2)}, u32[]{:S(2)}) collective-permute-start(f32[256,768]{1,0:T(8,128)} %get-tuple-element.330), channel_id=1, source_target_pairs={{0,8},{8,0},{16,24},{24,16},{1,9},{9,1},{17,25},{25,17},{2,10},{10... | collective-permute-start | bytes 2359304 | tf_op jit(solution)/shard_map/ppermute | solution.py:31
  323.7 35.9 %collective-permute-start.33 = (f32[256,768]{1,0:T(8,128)}, f32[256,768]{1,0:T(8,128)}, u32[]{:S(2)}, u32[]{:S(2)}) collective-permute-start(f32[256,768]{1,0:T(8,128)} %get-tuple-element.331), channel_id=1, source_target_pairs={{0,16},{8,24},{16,0},{24,8},{1,17},{9,25},{17,1},{25,9},{2,18},{10... | collective-permute-start | bytes 2359304 | tf_op jit(solution)/shard_map/ppermute | solution.py:31
  324.6 46.9 %collective-permute-start.34 = (f32[256,768]{1,0:T(8,128)}, f32[256,768]{1,0:T(8,128)}, u32[]{:S(2)}, u32[]{:S(2)}) collective-permute-start(f32[256,768]{1,0:T(8,128)} %get-tuple-element.332), channel_id=1, source_target_pairs={{0,24},{8,16},{16,8},{24,0},{1,25},{9,17},{17,9},{25,1},{2,26},{10... | collective-permute-start | bytes 2359304 | tf_op jit(solution)/shard_map/ppermute | solution.py:31
  336.5 35.0 %collective-permute-start.35 = (f32[2,32,3,192]{3,0,1,2:T(2,128)S(1)}, f32[2,32,3,192]{3,0,1,2:T(2,128)S(1)}, u32[]{:S(2)}, u32[]{:S(2)}) collective-permute-start(f32[2,32,3,192]{3,0,1,2:T(2,128)S(1)} %rev.7), channel_id=1, source_target_pairs={{0,7},{1,6},{2,5},{3,4},{4,3},{5,2},{6,1},{7,0},{8,15},{9,14},{10,... | collective-permute-start | bytes 442376 | tf_op jit(solution)/shard_map/ppermute | solution.py:1011
  338.6 36.4 %slice-start = ((f32[96,2304]{1,0:T(8,128)}), f32[96,1536]{1,0:T(8,128)S(1)}, s32[]{:S(2)}) async-start(f32[96,2304]{1,0:T(8,128)} %reduce-scatter.4.cloned.1.call-done), calls=%async_computation.10 | async-start | bytes 1179648 | tf_op jit(solution)/shard_map/slice | solution.py:1014
  375.8 9.0 %collective-permute-start.37 = (f32[24,2176]{1,0:T(8,128)S(1)}, f32[24,2176]{1,0:T(8,128)S(1)}, u32[]{:S(2)}, u32[]{:S(2)}) collective-permute-start(f32[24,2176]{1,0:T(8,128)S(1)} %get-tuple-element.399), channel_id=1, source_target_pairs={{0,8},{8,0},{16,24},{24,16},{1,9},{9,1},{17,25},{25,17},{2,10},{10... | collective-permute-start | bytes 626696 | tf_op jit(solution)/shard_map/ppermute | solution.py:31
  377.4 8.8 %collective-permute-start.38 = (f32[24,2176]{1,0:T(8,128)S(1)}, f32[24,2176]{1,0:T(8,128)S(1)}, u32[]{:S(2)}, u32[]{:S(2)}) collective-permute-start(f32[24,2176]{1,0:T(8,128)S(1)} %get-tuple-element.398), channel_id=1, source_target_pairs={{0,16},{8,24},{16,0},{24,8},{1,17},{9,25},{17,1},{25,9},{2,18},{10... | collective-permute-start | bytes 626696 | tf_op jit(solution)/shard_map/ppermute | solution.py:31
  379.0 7.2 %collective-permute-start.39 = (f32[24,2176]{1,0:T(8,128)S(1)}, f32[24,2176]{1,0:T(8,128)S(1)}, u32[]{:S(2)}, u32[]{:S(2)}) collective-permute-start(f32[24,2176]{1,0:T(8,128)S(1)} %get-tuple-element.397), channel_id=1, source_target_pairs={{0,24},{8,16},{16,8},{24,0},{1,25},{9,17},{17,9},{25,1},{2,26},{10... | collective-permute-start | bytes 626696 | tf_op jit(solution)/shard_map/ppermute | solution.py:31
  (28 other events, 83.8 us)
Sparse Core Ops, SparseCore 0:
  18.9 44.2 all-gather.4
  65.4 26.2 all-gather.6
  93.3 51.2 all-gather.8
  146.1 30.4 all-gather.10
  220.0 77.2 reduce-scatter.3
  299.6 35.6 reduce-scatter.7
  337.6 36.3 reduce-scatter.5

commit v7 on v6

--- a/solution.py
+++ b/solution.py
@@ -583,7 +583,7 @@
     return jnp.where(lane == at_ref[...], 1.0, 0.0).astype(BF16)
 
 
-def live_back(residual, x, gated, w_out, places, d_out, w_units, w_down, used, after=()):
+def live_back(residual, x, gated, w_out, places, d_out, w_units, w_down, after=()):
     seqs = 1 + len(residual)
     length, width = x.shape
     own = gated[0].shape[0]
@@ -594,7 +594,7 @@
     def kernel(*refs):
         r_refs, refs = refs[: seqs - 1], refs[seqs - 1 :]
         x_ref, g_refs, w_refs, refs = refs[0], refs[1:5], refs[5:9], refs[9:]
-        at_ref, o_ref, wh, wl, dh, dl, live_ref, n_ref, hid_ref, du_ref, e_ref = refs
+        at_ref, o_ref, wh, wl, dh, dl, live_ref, n_ref, hid_ref, du_ref = refs
         for i, ref in enumerate((*r_refs, x_ref)):
             pick = chosen(at_ref.at[i], slots, length)
             live_ref[i * slots : (i + 1) * slots] = chosen_rows(pick, halves(ref[...]), NN)
@@ -614,18 +614,32 @@
         hid_ref[...] = gate * half * up
         d_units = jnp.concatenate([d_hidden * up * slope, d_hidden * (gate * half)], axis=1)
         du_ref[...] = d_units
-        e = dot(halves(d_units), (wh[...], wl[...]), NT)
-        for i in range(seqs):
-            e_ref[i * used : (i + 1) * used] = e[i * slots : i * slots + used]
 
     return call(
         kernel, "live_back", 30 * rows * width * units, 4 * (2 * length * width + 4 * width * units),
         [*residual, x, *gated, *w_out, places, d_out, *w_units, *w_down],
         [whole(length, width)] * seqs + [whole(own, length)] * 4 + [whole(own, width)] * 4
         + [whole(seqs, slots, 1), whole(rows, width)] + [whole(width, 2 * units)] * 2 + [whole(units, width)] * 2,
-        [shaped(rows, width), shaped(rows, width), shaped(rows, units), shaped(rows, 2 * units), shaped(seqs * used, width)],
-        [whole(rows, width), whole(rows, width), whole(rows, units), whole(rows, 2 * units), whole(seqs * used, width)],
+        [shaped(rows, width), shaped(rows, width), shaped(rows, units), shaped(rows, 2 * units)],
+        [whole(rows, width), whole(rows, width), whole(rows, units), whole(rows, 2 * units)],
         after=after,
+    )
+
+
+def through_units(d_units, w_units, seqs, used, after=()):
+    rows = d_units.shape[0]
+    width, wide = w_units[0].shape
+    slots = rows // seqs
+
+    def kernel(u_ref, wh, wl, *out_refs):
+        e = dot(halves(u_ref[...]), (wh[...], wl[...]), NT)
+        for i, out_ref in enumerate(out_refs):
+            out_ref[...] = e[i * slots : i * slots + used]
+
+    return call(
+        kernel, "through_units", 6 * rows * width * wide, 4 * (rows * wide + width * wide),
+        [d_units, *w_units], [whole(rows, wide)] + [whole(width, wide)] * 2,
+        [shaped(used, width)] * seqs, [whole(used, width)] * seqs, after=after,
     )
 
 
@@ -950,16 +964,16 @@
     )
 
     lived = live_back(
-        (residual_0,), x_1, (gated_1, *there_1), w_out_pieces, places, d_out, w_units, w_down_own, slots
-    )
-    live_rows, n_live, hidden, d_units, e_two = lived
+        (residual_0,), x_1, (gated_1, *there_1), w_out_pieces, places, d_out, w_units, w_down_own
+    )
+    live_rows, n_live, hidden, d_units = lived
     unit_part = unit_grads(n_live, d_units, hidden, d_out, shards)
     out_0 = [down_0[0], swap(down_0[1], "seq", 1), swap(down_0[2], "seq", 2)]
-    live_rows, e_two, unit_part, out_0 = together(live_rows, e_two, unit_part, out_0)
+    live_rows, d_units, unit_part, out_0 = together(live_rows, d_units, unit_part, out_0)
     unit_sums = sum_over_batch(unit_part)
 
-    e_two = [e_two[:slots], e_two[slots:]]
-    residual_1 = add_mixer(x_1, (gated_1, *there_1), w_out_pieces, after=(unit_part,))
+    e_two = through_units(d_units, w_units, seqs, slots, after=(unit_part,))
+    residual_1 = add_mixer(x_1, (gated_1, *there_1), w_out_pieces, after=(e_two[0],))
     e_there, residual_1 = together([swap(e, "seq", 1 + i) for i, e in enumerate(e_two)], residual_1)
     residual = (residual_0, residual_1)
     e_two = [e + there for e, there in zip(e_two, e_there)]

time: 408 us -> 409 us (level)
    reduce_scatter x3, waiting for transfers between devices: 7.42 us -> 14.2 us  [sum_over_batch(): return lax.psum_scatter(flat, 'batch', scatter_dimension=0, tiled=True)]
    ppermute x38, waiting for transfers between devices: 67.5 us -> 62.1 us  [swap(): lax.ppermute(value, axis, [(i, i ^ distance) for i in range(devices)])]
    pallas_call x23 -> x24, Pallas kernels: 207 us -> 209 us  [call(): pl.pallas_call(run, name=name, out_shape=tuple(outs), grid_spec=pltpu.Pre...]
  transfers between devices with their start and end apart: 47 -> 47, of which waited for: 20 -> 19; matrix products, arithmetic and copies ran while one was open for 6% -> 6% of each run, Pallas kernels for 52% -> 53%
where the time goes in v7:
time: 409 us; the launch traced here: 404 us
  Pallas kernels  216 us (53%)
  waiting for transfers between devices  88.9 us (22%)
  starting transfers between devices  47.1 us (12%)
  local copies, waits for them, and re-layouts  26.5 us (6%)
  between operations  15.3 us (4%)
  other arithmetic  9.35 us (2%)
    pallas_call x24, Pallas kernels, call(): pl.pallas_call(run, name=name, out_shape=tuple(outs), grid_spec=pltpu.Pre...  209 us
    ppermute x38, waiting for transfers between devices, swap(): lax.ppermute(value, axis, [(i, i ^ distance) for i in range(devices)])  62.1 us
    ppermute x38, starting transfers between devices, swap(): lax.ppermute(value, axis, [(i, i ^ distance) for i in range(devices)])  44.2 us
    reduce_scatter x3, waiting for transfers between devices, sum_over_batch(): return lax.psum_scatter(flat, 'batch', scatter_dimension=0, tiled=True)  14.2 us
    ppermute x1, waiting for transfers between devices, body(): folded = lax.ppermute(wide[:, ::-1, :4:-1], 'batch', mirror)  12 us
  transfers between devices with their start and end apart: 47, of which 19 were waited for; matrix products, arithmetic and copies ran while one was open for 6% of the time, Pallas kernels for 53%

profile of v7, /device:TPU:0, one launch (start us, length us, event | category | flops | bytes accessed | tf_op | source)
XLA Modules:
  0.0 403.5 jit_solution(17962290048408214627)
XLA Ops:
  9.8 4.0 collective-permute-start
  16.0 2.0 collective-permute-done.1
  19.5 1.6 collective-permute-start.4
  24.7 1.4 collective-permute-start.5
  26.1 12.0 %collective-permute-done.5.refs_1_ = f32[2,32,3,192]{3,2,1,0:T(4,128)S(1)} collective-permute-done((f32[2,32,3,192]{3,2,1,0:T(4,128)}, f32[2,32,3,192]{3,2,1,0:T(4,128)S(1)}, u32[]{:S(2)}, u32[]{:S(2)}) %collective-permute-start.5) | collective-permute-done | bytes 147488 | tf_op jit(solution)/shard_map/ppermute | solution.py:924
  38.8 2.0 fold_base.1
  40.8 13.6 %collective-permute-done.4.refs_3_ = f32[2,256,768]{2,1,0:T(8,128)S(1)} collective-permute-done((f32[2,256,768]{2,1,0:T(8,128)S(1)}, f32[2,256,768]{2,1,0:T(8,128)S(1)}, u32[]{:S(2)}, u32[]{:S(2)}) %collective-permute-start.4) | collective-permute-done | bytes 1572896 | tf_op jit(solution)/shard_map/ppermute | solution.py:31
  54.4 1.3 collective-permute-done.3.refs_2_
  55.7 2.4 slice_bitcast_fusion
  61.4 1.2 collective-permute-start.10
  62.6 1.3 collective-permute-start.9
  65.4 2.6 collective-permute-done.8
  68.0 2.4 collective-permute-done.10
  71.5 1.2 slice.61
  72.6 4.1 %turn_in.1 = (bf16[576,768]{1,0:T(8,128)(2,1)}, bf16[576,768]{1,0:T(8,128)(2,1)}, f32[192,768]{1,0:T(8,128)}) custom-call(f32[8,4,24,777]{3,2,1,0:T(8,128)} %bitcast.148), custom_call_target="tpu_custom_call" | custom-call | bytes 196608 | tf_op jit(solution)/shard_map/turn_in/pallas_call | solution.py:122
  76.8 7.5 %collective-permute-done.6.refs_4_ = f32[256,768]{1,0:T(8,128)S(1)} collective-permute-done((f32[256,768]{1,0:T(8,128)}, f32[256,768]{1,0:T(8,128)S(1)}, u32[]{:S(2)}, u32[]{:S(2)}) %collective-permute-start.6) | collective-permute-done | bytes 786464 | tf_op jit(solution)/shard_map/ppermute | solution.py:31
  85.1 1.9 collective-permute-start.13
  89.9 5.3 %arrange.2 = (f32[1024,768]{1,0:T(8,128)}, bf16[1024,768]{1,0:T(8,128)(2,1)}, bf16[1024,768]{1,0:T(8,128)(2,1)}) custom-call(s32[1]{0:T(128)} %bitcast.refs_0_.s_ref, f32[2,256,768]{2,1,0:T(8,128)} %x_ref.3, f32[2,256,768]{2,1,0:T(8,128)} %collective-permute-done.3.refs_2_, f32[2,256,768]{2,1,0:T(8,128)} %copy-done.1, f32[256,768]{1,0:T(8,128)} %copy-done.26), custom_call_target="tpu_custom_call" | custom-call | bytes 471859 | tf_op jit(solution)/shard_map/arrange/pallas_call | solution.py:122
  95.2 6.1 %project.2 = f32[576,1024]{1,0:T(8,128)} custom-call(bf16[576,768]{1,0:T(8,128)(2,1)} %get-tuple-element.208.refs_0_.refs_4_, bf16[576,768]{1,0:T(8,128)(2,1)} %get-tuple-element.209.refs_1_.refs_5_, bf16[1024,768]{1,0:T(8,128)(2,1)} %get-tuple-element.306.refs_2_, bf16[1024,768]{1,0:T(8,128)(2,1)} %get-tuple-element.307.refs_3_), custom_call_target="tpu_custom_call" | custom-call | flops 135895456 | bytes 363724 | tf_op jit(solution)/shard_map/project/pallas_call | solution.py:122
  101.4 13.8 %mix.2 = (f32[192,1024]{1,0:T(8,128)}, f32[192,1024]{1,0:T(8,128)}, f32[192,1024]{1,0:T(8,128)}, f32[5,192,512]{2,1,0:T(8,128)}, f32[5,192,512]{2,1,0:T(8,128)}) custom-call(f32[3,192,1024]{2,1,0:T(8,128)} %bitcast.133, f32[3,192,3]{2,1,0:T(8,128)} %bitcast.144, f32[8,160,384]{2,1,0:T(8,128)} %bitcast.141, ...), custom_call_target="tpu_custom_call" | custom-call | flops 724775744 | bytes 865075 | tf_op jit(solution)/shard_map/mix/pallas_call | solution.py:122
  115.2 1.9 collective-permute-start.16
  118.8 5.5 %arrange.3 = (f32[1024,768]{1,0:T(8,128)}, bf16[1024,768]{1,0:T(8,128)(2,1)}, bf16[1024,768]{1,0:T(8,128)(2,1)}) custom-call(s32[1]{0:T(128)} %bitcast.refs_0_.s_ref, f32[2,256,768]{2,1,0:T(8,128)} %x_ref.3, f32[2,256,768]{2,1,0:T(8,128)} %collective-permute-done.3.refs_2_, f32[2,256,768]{2,1,0:T(8,128)} %copy-done.1, f32[256,768]{1,0:T(8,128)} %copy-done.21, ...), custom_call_target="tpu_custom_call" | custom-call | bytes 471859 | tf_op jit(solution)/shard_map/arrange/pallas_call | solution.py:122
  124.3 6.2 %project.3 = f32[576,1024]{1,0:T(8,128)} custom-call(bf16[576,768]{1,0:T(8,128)(2,1)} %get-tuple-element.208.refs_0_.refs_4_, bf16[576,768]{1,0:T(8,128)(2,1)} %get-tuple-element.209.refs_1_.refs_5_, bf16[1024,768]{1,0:T(8,128)(2,1)} %get-tuple-element.321.refs_2_, bf16[1024,768]{1,0:T(8,128)(2,1)} %get-tuple-element.322.refs_3_), custom_call_target="tpu_custom_call" | custom-call | flops 135895456 | bytes 363724 | tf_op jit(solution)/shard_map/project/pallas_call | solution.py:122
  130.5 14.0 %mix.3 = (f32[192,1024]{1,0:T(8,128)}, f32[192,1024]{1,0:T(8,128)}, f32[192,1024]{1,0:T(8,128)}, f32[5,192,512]{2,1,0:T(8,128)}, f32[5,192,512]{2,1,0:T(8,128)}) custom-call(f32[3,192,1024]{2,1,0:T(8,128)} %bitcast.135, f32[3,192,3]{2,1,0:T(8,128)} %bitcast.145, f32[8,160,384]{2,1,0:T(8,128)} %bitcast.142, ...), custom_call_target="tpu_custom_call" | custom-call | flops 724775744 | bytes 865075 | tf_op jit(solution)/shard_map/mix/pallas_call | solution.py:122
  144.5 4.7 %collective-permute-done.15.refs_3_ = f32[192,1024]{1,0:T(8,128)S(1)} collective-permute-done((f32[192,1024]{1,0:T(8,128)}, f32[192,1024]{1,0:T(8,128)S(1)}, u32[]{:S(2)}, u32[]{:S(2)}) %collective-permute-start.15) | collective-permute-done | bytes 786464 | tf_op jit(solution)/shard_map/ppermute | solution.py:31
  149.2 1.8 collective-permute-start.19
  151.0 1.2 collective-permute-start.18
  152.7 8.8 %add_mixer.2.refs_1_.refs_0_ = f32[1024,768]{1,0:T(8,128)} custom-call(f32[1024,768]{1,0:T(8,128)} %get-tuple-element.232.refs_0_, f32[192,1024]{1,0:T(8,128)} %get-tuple-element.221.refs_5_.refs_1_, f32[192,1024]{1,0:T(8,128)} %copy-done.25, f32[192,1024]{1,0:T(8,128)} %copy-done.24, f32[192,1024]{1,0:T(8,128)} %copy-done.23, ...), custom_call_target="tpu_custom_call" | custom-call | flops 181193936 | bytes 589824 | tf_op jit(solution)/shard_map/add_mixer/pallas_call | solution.py:122
  161.5 5.1 %split_units.1 = (bf16[768,1536]{1,0:T(8,128)(2,1)}, bf16[768,1536]{1,0:T(8,128)(2,1)}) custom-call(f32[8,4,24,1536]{3,2,1,0:T(8,128)} %bitcast.143, f32[1024,768]{1,0:T(8,128)} %add_mixer.2.refs_1_.refs_0_), custom_call_target="tpu_custom_call" | custom-call | bytes 471859 | tf_op jit(solution)/shard_map/split_units/pallas_call | solution.py:122
  166.6 12.5 %units_of.1 = (bf16[1024,768]{1,0:T(8,128)(2,1)}, bf16[1024,768]{1,0:T(8,128)(2,1)}) custom-call(f32[1024,768]{1,0:T(8,128)} %add_mixer.2.refs_1_.refs_0_, bf16[768,1536]{1,0:T(8,128)(2,1)} %get-tuple-element.257.refs_1_.refs_12_.refs_2_, bf16[768,1536]{1,0:T(8,128)(2,1)} %get-tuple-element.258.refs_2_.refs_13_.refs_3_), custom_call_target="tpu_custom_call" | custom-call | flops 362387872 | bytes 550502 | tf_op jit(solution)/shard_map/units_of/pallas_call | solution.py:122
  179.1 2.9 split_down.1
  182.1 7.6 %down_of.1 = (f32[256,768]{1,0:T(8,128)}, f32[256,768]{1,0:T(8,128)}, f32[256,768]{1,0:T(8,128)}, f32[256,768]{1,0:T(8,128)}) custom-call(s32[1]{0:T(128)} %bitcast.refs_0_.s_ref, bf16[1024,768]{1,0:T(8,128)(2,1)} %get-tuple-element.242.refs_1_, bf16[1024,768]{1,0:T(8,128)(2,1)} %get-tuple-element.243.refs_2_, ...), custom_call_target="tpu_custom_call" | custom-call | flops 181193936 | bytes 432537 | tf_op jit(solution)/shard_map/down_of/pallas_call | solution.py:122
  189.7 1.6 collective-permute-start.20
  193.0 14.1 %live_back.1 = (f32[256,768]{1,0:T(8,128)}, f32[256,768]{1,0:T(8,128)}, f32[256,768]{1,0:T(8,128)}, f32[256,1536]{1,0:T(8,128)}) custom-call(f32[1024,768]{1,0:T(8,128)} %add_mixer.2.refs_1_.refs_0_, f32[1024,768]{1,0:T(8,128)} %get-tuple-element.252.refs_1_.refs_0_, f32[192,1024]{1,0:T(8,128)} %get-tuple-element.231.refs_9_.refs_2_.refs_1_, ...), custom_call_target="tpu_custom_call" | custom-call | flops 226492416 | bytes 786432 | tf_op jit(solution)/shard_map/live_back/pallas_call | solution.py:122
  207.0 7.0 %unit_grads.1.refs_3_ = f32[8,96,2304]{2,1,0:T(8,128)} custom-call(f32[256,768]{1,0:T(8,128)} %get-tuple-element.263.refs_0_, f32[256,1536]{1,0:T(8,128)} %get-tuple-element.269.refs_1_.refs_0_, f32[256,768]{1,0:T(8,128)} %get-tuple-element.264.refs_2_, f32[256,768]{1,0:T(8,128)} %bitcast.138), custom_call_target="tpu_custom_call" | custom-call | flops 135895456 | bytes 353894 | tf_op jit(solution)/shard_map/unit_grads/pallas_call | solution.py:122
  214.1 5.6 %through_units.1 = (f32[80,768]{1,0:T(8,128)}, f32[80,768]{1,0:T(8,128)}) custom-call(f32[256,1536]{1,0:T(8,128)} %get-tuple-element.269.refs_1_.refs_0_, bf16[768,1536]{1,0:T(8,128)(2,1)} %get-tuple-element.257.refs_1_.refs_12_.refs_2_, bf16[768,1536]{1,0:T(8,128)(2,1)} %get-tuple-element.258.refs_2_.refs_13_.refs_3_, f32[8,96,2304]{2,1,0:T(8,128)} %unit_grads.1.refs_3_), custom_call_target="tpu_custom_call" | custom-call | flops 90596968 | bytes 314572 | tf_op jit(solution)/shard_map/through_units/pallas_call | solution.py:122
  221.4 9.5 %add_mixer.3.refs_1_ = f32[1024,768]{1,0:T(8,128)} custom-call(f32[1024,768]{1,0:T(8,128)} %get-tuple-element.252.refs_1_.refs_0_, f32[192,1024]{1,0:T(8,128)} %get-tuple-element.231.refs_9_.refs_2_.refs_1_, f32[192,1024]{1,0:T(8,128)} %copy-done.7, f32[192,1024]{1,0:T(8,128)} %copy-done.6, f32[192,1024]{1,0:T(8,128)} %copy-done.5, ...), custom_call_target="tpu_custom_call" | custom-call | flops 181193936 | bytes 589824 | tf_op jit(solution)/shard_map/add_mixer/pallas_call | solution.py:122
  231.1 1.6 collective-permute-start.25
  234.6 16.5 %feed_forward.1 = (f32[256,768]{1,0:T(8,128)}, f32[256,768]{1,0:T(8,128)}, f32[256,768]{1,0:T(8,128)}, f32[256,768]{1,0:T(8,128)}) custom-call(s32[1]{0:T(128)} %bitcast.refs_0_.s_ref, f32[1024,768]{1,0:T(8,128)} %add_mixer.3.refs_1_, bf16[768,1536]{1,0:T(8,128)(2,1)} %get-tuple-element.257.refs_1_.refs_12_.refs_2_, ...), custom_call_target="tpu_custom_call" | custom-call | flops 543581824 | bytes 668467 | tf_op jit(solution)/shard_map/feed_forward/pallas_call | solution.py:122
  251.2 1.2 collective-permute-done.24.refs_4_
  254.2 1.6 collective-permute-start.29
  255.9 6.2 %live_mix.1 = (f32[256,768]{1,0:T(8,128)}, f32[192,768]{1,0:T(8,128)}, f32[2,192,128]{2,1,0:T(8,128)}, f32[2,192,128]{2,1,0:T(8,128)}) custom-call(f32[256,768]{1,0:T(8,128)} %get-tuple-element.268.refs_0_, f32[256,768]{1,0:T(8,128)} %bitcast.139, f32[80,768]{1,0:T(8,128)} %copy-done.11, f32[80,768]{1,0:T(8,128)} %copy-done.12, f32[80,768]{1,0:T(8,128)} %copy-done.32, ...), custom_call_target="tpu_custom_call" | custom-call | flops 37748736 | bytes 314572 | tf_op jit(solution)/shard_map/live_mix/pallas_call | solution.py:122
  262.1 24.4 %mix_back.1 = (f32[3,192,1024]{2,1,0:T(8,128)}, f32[3,192,1024]{2,1,0:T(8,128)}, f32[8,5,32,384]{3,2,1,0:T(8,128)}, f32[3,192,128]{2,1,0:T(8,128)}) custom-call(s32[2,128,1]{2,1,0:T(8,128)} %copy.60.refs_10_.refs_11_.refs_0_.at_ref, f32[2,192,128]{2,1,0:T(8,128)} %get-tuple-element.286.refs_1_, f32[2,192,128]{2,1,0:T(8,128)} %get-tuple-element.287.refs_2_, ...), custom_call_target="tpu_custom_call" | custom-call | flops 1449551488 | bytes 1730150 | tf_op jit(solution)/shard_map/mix_back/pallas_call | solution.py:122
  286.5 1.5 collective-permute-done.28
  288.1 11.8 %project_back.2 = (f32[256,768]{1,0:T(8,128)}, f32[256,768]{1,0:T(8,128)}, f32[256,768]{1,0:T(8,128)}, f32[256,768]{1,0:T(8,128)}, f32[576,768]{1,0:T(8,128)}) custom-call(s32[1]{0:T(128)} %bitcast.refs_0_.s_ref, f32[576,1024]{1,0:T(8,128)} %bitcast.153, bf16[1024,768]{1,0:T(8,128)(2,1)} %get-tuple-element.306.refs_2_, ...), custom_call_target="tpu_custom_call" | custom-call | flops 271790912 | bytes 697958 | tf_op jit(solution)/shard_map/project_back/pallas_call | solution.py:122
  303.5 12.0 %project_back.3 = (f32[256,768]{1,0:T(8,128)}, f32[256,768]{1,0:T(8,128)}, f32[256,768]{1,0:T(8,128)}, f32[256,768]{1,0:T(8,128)}, f32[576,768]{1,0:T(8,128)}) custom-call(s32[1]{0:T(128)} %bitcast.refs_0_.s_ref, f32[576,1024]{1,0:T(8,128)} %bitcast.152, bf16[1024,768]{1,0:T(8,128)(2,1)} %get-tuple-element.321.refs_2_, ...), custom_call_target="tpu_custom_call" | custom-call | flops 271790912 | bytes 697958 | tf_op jit(solution)/shard_map/project_back/pallas_call | solution.py:122
  315.6 4.0 turn_back.1
  321.0 1.5 collective-permute-start.36
  324.5 1.5 collective-permute-start.34
  326.0 1.9 add_bitcast_fusion.1
  329.4 1.6 add_bitcast_fusion
  331.1 6.3 %reduce-scatter.8.cloned.1.call-done = f32[160,384]{1,0:T(8,128)} async-done(((f32[1280,384]{1,0:T(8,128)}), f32[160,384]{1,0:T(8,128)}) %reduce-scatter.8.cloned.1.call-update) | async-done | bytes 245776 | tf_op jit(solution)/shard_map/reduce_scatter | solution.py:84
  337.4 1.2 reshape.161
  339.6 1.2 pad_maximum_fusion
  340.9 1.8 collective-permute-done.36.e3
  342.7 4.1 %finish.2.refs_0_ = f32[2,256,768]{2,1,0:T(8,128)} custom-call(s32[1]{0:T(128)} %bitcast.refs_0_.s_ref, f32[256,768]{1,0:T(8,128)} %get-tuple-element.345.e0, f32[256,768]{1,0:T(8,128)} %copy-done.22, f32[256,768]{1,0:T(8,128)} %collective-permute-done.31.e2, f32[256,768]{1,0:T(8,128)} %collective-permute-done.36.e3, f32[2,256,768]{2,1,0:T(8,128)} %x_ref.3, ...), custom_call_target="tpu_custom_call" | custom-call | flops 1000000 | bytes 1000000 | tf_op jit(solution)/shard_map/finish/pallas_call | solution.py:797
  346.7 12.3 %collective-permute-done.32.e1 = f32[256,768]{1,0:T(8,128)} collective-permute-done((f32[256,768]{1,0:T(8,128)}, f32[256,768]{1,0:T(8,128)}, u32[]{:S(2)}, u32[]{:S(2)}) %collective-permute-start.32) | collective-permute-done | bytes 786464 | tf_op jit(solution)/shard_map/ppermute | solution.py:31
  359.4 9.2 %collective-permute-done.34.e3 = f32[256,768]{1,0:T(8,128)} collective-permute-done((f32[256,768]{1,0:T(8,128)}, f32[256,768]{1,0:T(8,128)}, u32[]{:S(2)}, u32[]{:S(2)}) %collective-permute-start.34) | collective-permute-done | bytes 786464 | tf_op jit(solution)/shard_map/ppermute | solution.py:31
  368.6 7.9 %reduce-scatter.6.cloned.1.call-done = f32[96,832]{1,0:T(8,128)} async-done(((f32[768,832]{1,0:T(8,128)}), f32[96,832]{1,0:T(8,128)}) %reduce-scatter.6.cloned.1.call-update) | async-done | bytes 319504 | tf_op jit(solution)/shard_map/reduce_scatter | solution.py:84
  378.3 2.3 collective-permute-start.39
  383.4 3.8 finish.3
  389.1 3.4 weight_grads.1
  392.5 1.2 slice_bitcast_fusion.3
  393.7 1.2 slice_bitcast_fusion.2
  (222 shorter events, 47.2 us)
Async XLA Ops:
  7.2 7.5 %copy-start.37 = (f32[24,768]{1,0:T(8,128)S(1)}, f32[24,768]{1,0:T(8,128)}, u32[]{:S(2)}) copy-start(f32[24,768]{1,0:T(8,128)} %param.20) | copy-start | bytes 221188
  7.2 64.2 %all-gather.5.cloned.1.call-start = ((), (), s32[]{:S(2)}) async-start(), calls=%async_computation.3 | async-start | bytes 3096576 | tf_op jit(solution)/shard_map/all_gather | solution.py:78
  9.8 6.2 %collective-permute-start = (f32[24,585]{1,0:T(8,128)S(1)}, f32[24,585]{1,0:T(8,128)S(1)}, u32[]{:S(2)}, u32[]{:S(2)}) collective-permute-start(f32[24,585]{1,0:T(8,128)S(1)} %get-tuple-element.410), channel_id=1, source_target_pairs={{0,24},{8,16},{16,8},{24,0},{1,25},{9,17},{17,9},{25,1},{2,26},{10... | collective-permute-start | bytes 168488 | tf_op jit(solution)/shard_map/ppermute | solution.py:31
  13.8 4.2 %collective-permute-start.1 = (f32[24,585]{1,0:T(8,128)S(1)}, f32[24,585]{1,0:T(8,128)S(1)}, u32[]{:S(2)}, u32[]{:S(2)}) collective-permute-start(f32[24,585]{1,0:T(8,128)S(1)} %get-tuple-element.411), channel_id=1, source_target_pairs={{0,16},{8,24},{16,0},{24,8},{1,17},{9,25},{17,1},{25,9},{2,18},{10... | collective-permute-start | bytes 168488 | tf_op jit(solution)/shard_map/ppermute | solution.py:31
  14.3 4.2 %collective-permute-start.2 = (f32[24,585]{1,0:T(8,128)S(1)}, f32[24,585]{1,0:T(8,128)S(1)}, u32[]{:S(2)}, u32[]{:S(2)}) collective-permute-start(f32[24,585]{1,0:T(8,128)S(1)} %get-tuple-element.412), channel_id=1, source_target_pairs={{0,8},{8,0},{16,24},{24,16},{1,9},{9,1},{17,25},{25,17},{2,10},{10... | collective-permute-start | bytes 168488 | tf_op jit(solution)/shard_map/ppermute | solution.py:31
  19.5 81.9 %all-gather.7.cloned.1.call-start = ((), (), s32[]{:S(2)}) async-start(), calls=%async_computation.4 | async-start | bytes 2211840 | tf_op jit(solution)/shard_map/all_gather | solution.py:78
  19.5 34.8 %collective-permute-start.4 = (f32[2,256,768]{2,1,0:T(8,128)S(1)}, f32[2,256,768]{2,1,0:T(8,128)S(1)}, u32[]{:S(2)}, u32[]{:S(2)}) collective-permute-start(f32[2,256,768]{2,1,0:T(8,128)S(1)} %copy-done), channel_id=1, source_target_pairs={{0,16},{8,24},{16,0},{24,8},{1,17},{9,25},{17,1},{25,9},{2,18},{10... | collective-permute-start | bytes 4718600 | tf_op jit(solution)/shard_map/ppermute | solution.py:31
  21.1 34.5 %collective-permute-start.3 = (f32[2,256,768]{2,1,0:T(8,128)S(1)}, f32[2,256,768]{2,1,0:T(8,128)}, u32[]{:S(2)}, u32[]{:S(2)}) collective-permute-start(f32[2,256,768]{2,1,0:T(8,128)S(1)} %copy-done), channel_id=1, source_target_pairs={{0,8},{8,0},{16,24},{24,16},{1,9},{9,1},{17,25},{25,17},{2,10},{10... | collective-permute-start | bytes 4718600 | tf_op jit(solution)/shard_map/ppermute | solution.py:31
  24.7 33.4 %copy-start.9 = (f32[24,3072]{1,0:T(8,128)S(1)}, f32[24,3072]{1,0:T(8,128)}, u32[]{:S(2)}) copy-start(f32[24,3072]{1,0:T(8,128)} %refs_8_.1) | copy-start | bytes 884740
  24.7 33.4 %copy-start.38 = (f32[24]{0:T(128)S(1)}, f32[24]{0:T(128)}, u32[]{:S(2)}) copy-start(f32[24]{0:T(128)} %param.21) | copy-start | bytes 292
  24.7 13.4 %collective-permute-start.5 = (f32[2,32,3,192]{3,2,1,0:T(4,128)}, f32[2,32,3,192]{3,2,1,0:T(4,128)S(1)}, u32[]{:S(2)}, u32[]{:S(2)}) collective-permute-start(f32[2,32,3,192]{3,2,1,0:T(4,128)} %rev.6), channel_id=1, source_target_pairs={{0,7},{1,6},{2,5},{3,4},{4,3},{5,2},{6,1},{7,0},{8,15},{9,14},{10,... | collective-permute-start | bytes 442376 | tf_op jit(solution)/shard_map/ppermute | solution.py:924
  55.7 105.8 %all-gather.9.cloned.1.call-start = ((), (), s32[]{:S(2)}) async-start(), calls=%async_computation.5 | async-start | bytes 5308416 | tf_op jit(solution)/shard_map/all_gather | solution.py:78
  60.3 7.7 %collective-permute-start.8 = (f32[24,1536]{1,0:T(8,128)S(1)}, f32[24,1536]{1,0:T(8,128)S(1)}, u32[]{:S(2)}, u32[]{:S(2)}) collective-permute-start(f32[24,1536]{1,0:T(8,128)S(1)} %get-tuple-element.403), channel_id=1, source_target_pairs={{0,24},{8,16},{16,8},{24,0},{1,25},{9,17},{17,9},{25,1},{2,26},{10... | collective-permute-start | bytes 442376 | tf_op jit(solution)/shard_map/ppermute | solution.py:31
  61.4 9.1 %collective-permute-start.10 = (f32[24,1536]{1,0:T(8,128)S(1)}, f32[24,1536]{1,0:T(8,128)S(1)}, u32[]{:S(2)}, u32[]{:S(2)}) collective-permute-start(f32[24,1536]{1,0:T(8,128)S(1)} %get-tuple-element.404), channel_id=1, source_target_pairs={{0,8},{8,0},{16,24},{24,16},{1,9},{9,1},{17,25},{25,17},{2,10},{10... | collective-permute-start | bytes 442376 | tf_op jit(solution)/shard_map/ppermute | solution.py:31
  62.6 7.9 %collective-permute-start.9 = (f32[24,1536]{1,0:T(8,128)S(1)}, f32[24,1536]{1,0:T(8,128)S(1)}, u32[]{:S(2)}, u32[]{:S(2)}) collective-permute-start(f32[24,1536]{1,0:T(8,128)S(1)} %get-tuple-element.405), channel_id=1, source_target_pairs={{0,16},{8,24},{16,0},{24,8},{1,17},{9,25},{17,1},{25,9},{2,18},{10... | collective-permute-start | bytes 442376 | tf_op jit(solution)/shard_map/ppermute | solution.py:31
  63.9 20.4 %collective-permute-start.6 = (f32[256,768]{1,0:T(8,128)}, f32[256,768]{1,0:T(8,128)S(1)}, u32[]{:S(2)}, u32[]{:S(2)}) collective-permute-start(f32[256,768]{1,0:T(8,128)} %get-tuple-element.199), channel_id=1, source_target_pairs={{0,16},{8,24},{16,0},{24,8},{1,17},{9,25},{17,1},{25,9},{2,18},{10... | collective-permute-start | bytes 2359304 | tf_op jit(solution)/shard_map/ppermute | solution.py:31
  64.6 19.6 %collective-permute-start.7 = (f32[256,768]{1,0:T(8,128)}, f32[256,768]{1,0:T(8,128)S(1)}, u32[]{:S(2)}, u32[]{:S(2)}) collective-permute-start(f32[256,768]{1,0:T(8,128)} %get-tuple-element.200), channel_id=1, source_target_pairs={{0,8},{8,0},{16,24},{24,16},{1,9},{9,1},{17,25},{25,17},{2,10},{10... | collective-permute-start | bytes 2359304 | tf_op jit(solution)/shard_map/ppermute | solution.py:31
  84.2 11.0 %copy-start.21 = (f32[256,768]{1,0:T(8,128)}, f32[256,768]{1,0:T(8,128)S(1)}, u32[]{:S(2)}) copy-start(f32[256,768]{1,0:T(8,128)S(1)} %collective-permute-done.7.refs_4_) | copy-start | bytes 2359300
  84.3 94.9 %all-gather.11.cloned.1.call-start = ((), (), s32[]{:S(2)}) async-start(), calls=%async_computation.6 | async-start | bytes 2654208 | tf_op jit(solution)/shard_map/all_gather | solution.py:78
  84.8 215.1 %reduce-scatter.4.cloned.1.call-start = ((), (), s32[]{:S(2)}) async-start(), calls=%async_computation.7 | async-start | bytes 7962624 | tf_op jit(solution)/shard_map/reduce_scatter | solution.py:84
  85.1 30.1 %collective-permute-start.13 = (f32[192,768]{1,0:T(8,128)}, f32[192,768]{1,0:T(8,128)S(1)}, u32[]{:S(2)}, u32[]{:S(2)}) collective-permute-start(f32[192,768]{1,0:T(8,128)} %get-tuple-element.207.refs_5_.refs_6_), channel_id=1, source_target_pairs={{0,24},{8,16},{16,8},{24,0},{1,25},{9,17},{17,9},{25,1},{2,26},{10... | collective-permute-start | bytes 1769480 | tf_op jit(solution)/shard_map/ppermute | solution.py:31
  87.0 28.2 %collective-permute-start.12 = (f32[192,768]{1,0:T(8,128)}, f32[192,768]{1,0:T(8,128)S(1)}, u32[]{:S(2)}, u32[]{:S(2)}) collective-permute-start(f32[192,768]{1,0:T(8,128)} %get-tuple-element.207.refs_5_.refs_6_), channel_id=1, source_target_pairs={{0,16},{8,24},{16,0},{24,8},{1,17},{9,25},{17,1},{25,9},{2,18},{10... | collective-permute-start | bytes 1769480 | tf_op jit(solution)/shard_map/ppermute | solution.py:31
  88.1 27.1 %collective-permute-start.11 = (f32[192,768]{1,0:T(8,128)}, f32[192,768]{1,0:T(8,128)S(1)}, u32[]{:S(2)}, u32[]{:S(2)}) collective-permute-start(f32[192,768]{1,0:T(8,128)} %get-tuple-element.207.refs_5_.refs_6_), channel_id=1, source_target_pairs={{0,8},{8,0},{16,24},{24,16},{1,9},{9,1},{17,25},{25,17},{2,10},{10... | collective-permute-start | bytes 1769480 | tf_op jit(solution)/shard_map/ppermute | solution.py:31
  115.2 9.1 %copy-start.2 = (f32[192,768]{1,0:T(8,128)}, f32[192,768]{1,0:T(8,128)S(1)}, u32[]{:S(2)}) copy-start(f32[192,768]{1,0:T(8,128)S(1)} %collective-permute-done.13.refs_8_.refs_9_) | copy-start | bytes 1769476
  115.2 9.0 %copy-start.3 = (f32[192,768]{1,0:T(8,128)}, f32[192,768]{1,0:T(8,128)S(1)}, u32[]{:S(2)}) copy-start(f32[192,768]{1,0:T(8,128)S(1)} %collective-permute-done.12.refs_7_.refs_8_) | copy-start | bytes 1769476
  115.2 9.0 %copy-start.4 = (f32[192,768]{1,0:T(8,128)}, f32[192,768]{1,0:T(8,128)S(1)}, u32[]{:S(2)}) copy-start(f32[192,768]{1,0:T(8,128)S(1)} %collective-permute-done.11.refs_6_.refs_7_) | copy-start | bytes 1769476
  115.2 29.2 %collective-permute-start.16 = (f32[192,1024]{1,0:T(8,128)}, f32[192,1024]{1,0:T(8,128)S(1)}, u32[]{:S(2)}, u32[]{:S(2)}) collective-permute-start(f32[192,1024]{1,0:T(8,128)} %get-tuple-element.221.refs_5_.refs_1_), channel_id=1, source_target_pairs={{0,24},{8,16},{16,8},{24,0},{1,25},{9,17},{17,9},{25,1},{2,26},{10... | collective-permute-start | bytes 2359304 | tf_op jit(solution)/shard_map/ppermute | solution.py:31
  117.2 32.0 %collective-permute-start.15 = (f32[192,1024]{1,0:T(8,128)}, f32[192,1024]{1,0:T(8,128)S(1)}, u32[]{:S(2)}, u32[]{:S(2)}) collective-permute-start(f32[192,1024]{1,0:T(8,128)} %get-tuple-element.221.refs_5_.refs_1_), channel_id=1, source_target_pairs={{0,16},{8,24},{16,0},{24,8},{1,17},{9,25},{17,1},{25,9},{2,18},{10... | collective-permute-start | bytes 2359304 | tf_op jit(solution)/shard_map/ppermute | solution.py:31
  118.3 30.9 %collective-permute-start.14 = (f32[192,1024]{1,0:T(8,128)}, f32[192,1024]{1,0:T(8,128)S(1)}, u32[]{:S(2)}, u32[]{:S(2)}) collective-permute-start(f32[192,1024]{1,0:T(8,128)} %get-tuple-element.221.refs_5_.refs_1_), channel_id=1, source_target_pairs={{0,8},{8,0},{16,24},{24,16},{1,9},{9,1},{17,25},{25,17},{2,10},{10... | collective-permute-start | bytes 2359304 | tf_op jit(solution)/shard_map/ppermute | solution.py:31
  144.5 8.2 %copy-start.23 = (f32[192,1024]{1,0:T(8,128)}, f32[192,1024]{1,0:T(8,128)S(1)}, u32[]{:S(2)}) copy-start(f32[192,1024]{1,0:T(8,128)S(1)} %collective-permute-done.16.refs_4_) | copy-start | bytes 2359300
  149.2 40.5 %collective-permute-start.19 = (f32[192,1024]{1,0:T(8,128)}, f32[192,1024]{1,0:T(8,128)S(1)}, u32[]{:S(2)}, u32[]{:S(2)}) collective-permute-start(f32[192,1024]{1,0:T(8,128)} %get-tuple-element.231.refs_9_.refs_2_.refs_1_), channel_id=1, source_target_pairs={{0,24},{8,16},{16,8},{24,0},{1,25},{9,17},{17,9},{25,1},{2,26},{10... | collective-permute-start | bytes 2359304 | tf_op jit(solution)/shard_map/ppermute | solution.py:31
  151.0 38.7 %collective-permute-start.18 = (f32[192,1024]{1,0:T(8,128)}, f32[192,1024]{1,0:T(8,128)S(1)}, u32[]{:S(2)}, u32[]{:S(2)}) collective-permute-start(f32[192,1024]{1,0:T(8,128)} %get-tuple-element.231.refs_9_.refs_2_.refs_1_), channel_id=1, source_target_pairs={{0,16},{8,24},{16,0},{24,8},{1,17},{9,25},{17,1},{25,9},{2,18},{10... | collective-permute-start | bytes 2359304 | tf_op jit(solution)/shard_map/ppermute | solution.py:31
  152.2 37.5 %collective-permute-start.17 = (f32[192,1024]{1,0:T(8,128)}, f32[192,1024]{1,0:T(8,128)S(1)}, u32[]{:S(2)}, u32[]{:S(2)}) collective-permute-start(f32[192,1024]{1,0:T(8,128)} %get-tuple-element.231.refs_9_.refs_2_.refs_1_), channel_id=1, source_target_pairs={{0,8},{8,0},{16,24},{24,16},{1,9},{9,1},{17,25},{25,17},{2,10},{10... | collective-permute-start | bytes 2359304 | tf_op jit(solution)/shard_map/ppermute | solution.py:31
  189.7 24.4 %collective-permute-start.20 = (f32[256,768]{1,0:T(8,128)}, f32[256,768]{1,0:T(8,128)S(1)}, u32[]{:S(2)}, u32[]{:S(2)}) collective-permute-start(f32[256,768]{1,0:T(8,128)} %get-tuple-element.266), channel_id=1, source_target_pairs={{0,8},{8,0},{16,24},{24,16},{1,9},{9,1},{17,25},{25,17},{2,10},{10... | collective-permute-start | bytes 2359304 | tf_op jit(solution)/shard_map/ppermute | solution.py:31
  191.3 22.8 %collective-permute-start.21 = (f32[256,768]{1,0:T(8,128)}, f32[256,768]{1,0:T(8,128)}, u32[]{:S(2)}, u32[]{:S(2)}) collective-permute-start(f32[256,768]{1,0:T(8,128)} %get-tuple-element.267), channel_id=1, source_target_pairs={{0,16},{8,24},{16,0},{24,8},{1,17},{9,25},{17,1},{25,9},{2,18},{10... | collective-permute-start | bytes 2359304 | tf_op jit(solution)/shard_map/ppermute | solution.py:31
  214.1 123.3 %reduce-scatter.8.cloned.1.call-start = ((), (), s32[]{:S(2)}) async-start(), calls=%async_computation.9 | async-start | bytes 2211840 | tf_op jit(solution)/shard_map/reduce_scatter | solution.py:84
  219.8 11.1 %collective-permute-start.23 = (f32[80,768]{1,0:T(8,128)}, f32[80,768]{1,0:T(8,128)S(1)}, u32[]{:S(2)}, u32[]{:S(2)}) collective-permute-start(f32[80,768]{1,0:T(8,128)} %get-tuple-element.272), channel_id=1, source_target_pairs={{0,16},{8,24},{16,0},{24,8},{1,17},{9,25},{17,1},{25,9},{2,18},{10... | collective-permute-start | bytes 737288 | tf_op jit(solution)/shard_map/ppermute | solution.py:31
  220.9 10.1 %copy-start.13 = (f32[80,768]{1,0:T(8,128)S(1)}, f32[80,768]{1,0:T(8,128)}, u32[]{:S(2)}) copy-start(f32[80,768]{1,0:T(8,128)} %get-tuple-element.271.refs_9_) | copy-start | bytes 737284
  220.9 10.1 %copy-start.33 = (f32[80,768]{1,0:T(8,128)S(1)}, f32[80,768]{1,0:T(8,128)}, u32[]{:S(2)}) copy-start(f32[80,768]{1,0:T(8,128)} %get-tuple-element.272) | copy-start | bytes 737284
  220.9 12.7 %copy-start.42 = (f32[256,768]{1,0:T(8,128)S(1)}, f32[256,768]{1,0:T(8,128)}, u32[]{:S(2)}) copy-start(f32[256,768]{1,0:T(8,128)} %get-tuple-element.301) | copy-start | bytes 2359300
  220.9 10.0 %collective-permute-start.22 = (f32[80,768]{1,0:T(8,128)}, f32[80,768]{1,0:T(8,128)S(1)}, u32[]{:S(2)}, u32[]{:S(2)}) collective-permute-start(f32[80,768]{1,0:T(8,128)} %get-tuple-element.271.refs_9_), channel_id=1, source_target_pairs={{0,8},{8,0},{16,24},{24,16},{1,9},{9,1},{17,25},{25,17},{2,10},{10... | collective-permute-start | bytes 737288 | tf_op jit(solution)/shard_map/ppermute | solution.py:31
  231.0 20.2 %copy-start.11 = (f32[80,768]{1,0:T(8,128)}, f32[80,768]{1,0:T(8,128)S(1)}, u32[]{:S(2)}) copy-start(f32[80,768]{1,0:T(8,128)S(1)} %add.76.refs_2_) | copy-start | bytes 737284
  231.0 20.1 %copy-start.12 = (f32[80,768]{1,0:T(8,128)}, f32[80,768]{1,0:T(8,128)S(1)}, u32[]{:S(2)}) copy-start(f32[80,768]{1,0:T(8,128)S(1)} %add.77.refs_3_) | copy-start | bytes 737284
  231.1 20.1 %collective-permute-start.25 = (f32[80,768]{1,0:T(8,128)S(1)}, f32[80,768]{1,0:T(8,128)S(1)}, u32[]{:S(2)}, u32[]{:S(2)}) collective-permute-start(f32[80,768]{1,0:T(8,128)S(1)} %add.77.refs_3_), channel_id=1, source_target_pairs={{0,8},{8,0},{16,24},{24,16},{1,9},{9,1},{17,25},{25,17},{2,10},{10... | collective-permute-start | bytes 737288 | tf_op jit(solution)/shard_map/ppermute | solution.py:31
  232.6 19.7 %collective-permute-start.24 = (f32[80,768]{1,0:T(8,128)S(1)}, f32[80,768]{1,0:T(8,128)S(1)}, u32[]{:S(2)}, u32[]{:S(2)}) collective-permute-start(f32[80,768]{1,0:T(8,128)S(1)} %add.76.refs_2_), channel_id=1, source_target_pairs={{0,16},{8,24},{16,0},{24,8},{1,17},{9,25},{17,1},{25,9},{2,18},{10... | collective-permute-start | bytes 737288 | tf_op jit(solution)/shard_map/ppermute | solution.py:31
  233.6 52.9 %collective-permute-start.26 = (f32[256,768]{1,0:T(8,128)S(1)}, f32[256,768]{1,0:T(8,128)S(1)}, u32[]{:S(2)}, u32[]{:S(2)}) collective-permute-start(f32[256,768]{1,0:T(8,128)S(1)} %copy-done.42), channel_id=1, source_target_pairs={{0,24},{8,16},{16,8},{24,0},{1,25},{9,17},{17,9},{25,1},{2,26},{10... | collective-permute-start | bytes 2359304 | tf_op jit(solution)/shard_map/ppermute | solution.py:31
  252.4 34.2 %collective-permute-start.27 = (f32[256,768]{1,0:T(8,128)}, f32[256,768]{1,0:T(8,128)S(1)}, u32[]{:S(2)}, u32[]{:S(2)}) collective-permute-start(f32[256,768]{1,0:T(8,128)} %get-tuple-element.303), channel_id=1, source_target_pairs={{0,8},{8,0},{16,24},{24,16},{1,9},{9,1},{17,25},{25,17},{2,10},{10... | collective-permute-start | bytes 2359304 | tf_op jit(solution)/shard_map/ppermute | solution.py:31
  253.4 34.7 %collective-permute-start.28 = (f32[256,768]{1,0:T(8,128)}, f32[256,768]{1,0:T(8,128)S(1)}, u32[]{:S(2)}, u32[]{:S(2)}) collective-permute-start(f32[256,768]{1,0:T(8,128)} %get-tuple-element.304), channel_id=1, source_target_pairs={{0,16},{8,24},{16,0},{24,8},{1,17},{9,25},{17,1},{25,9},{2,18},{10... | collective-permute-start | bytes 2359304 | tf_op jit(solution)/shard_map/ppermute | solution.py:31
  254.2 45.7 %collective-permute-start.29 = (f32[256,768]{1,0:T(8,128)}, f32[256,768]{1,0:T(8,128)}, u32[]{:S(2)}, u32[]{:S(2)}) collective-permute-start(f32[256,768]{1,0:T(8,128)} %get-tuple-element.316), channel_id=1, source_target_pairs={{0,24},{8,16},{16,8},{24,0},{1,25},{9,17},{17,9},{25,1},{2,26},{10... | collective-permute-start | bytes 2359304 | tf_op jit(solution)/shard_map/ppermute | solution.py:31
  286.5 13.4 %copy-start.16 = (f32[256,768]{1,0:T(8,128)}, f32[256,768]{1,0:T(8,128)S(1)}, u32[]{:S(2)}) copy-start(f32[256,768]{1,0:T(8,128)S(1)} %collective-permute-done.26) | copy-start | bytes 2359300
  286.5 13.4 %copy-start.17 = (f32[256,768]{1,0:T(8,128)}, f32[256,768]{1,0:T(8,128)S(1)}, u32[]{:S(2)}) copy-start(f32[256,768]{1,0:T(8,128)S(1)} %collective-permute-done.27) | copy-start | bytes 2359300
  288.1 11.8 %copy-start.19 = (f32[256,768]{1,0:T(8,128)}, f32[256,768]{1,0:T(8,128)S(1)}, u32[]{:S(2)}) copy-start(f32[256,768]{1,0:T(8,128)S(1)} %collective-permute-done.28) | copy-start | bytes 2359300
  300.0 76.5 %reduce-scatter.6.cloned.1.call-start = ((), (), s32[]{:S(2)}) async-start(), calls=%async_computation.8 | async-start | bytes 3096576 | tf_op jit(solution)/shard_map/reduce_scatter | solution.py:84
  300.1 19.5 %collective-permute-start.30 = (f32[256,768]{1,0:T(8,128)}, f32[256,768]{1,0:T(8,128)S(1)}, u32[]{:S(2)}, u32[]{:S(2)}) collective-permute-start(f32[256,768]{1,0:T(8,128)} %get-tuple-element.318), channel_id=1, source_target_pairs={{0,8},{8,0},{16,24},{24,16},{1,9},{9,1},{17,25},{25,17},{2,10},{10... | collective-permute-start | bytes 2359304 | tf_op jit(solution)/shard_map/ppermute | solution.py:31
  301.0 18.5 %collective-permute-start.31 = (f32[256,768]{1,0:T(8,128)}, f32[256,768]{1,0:T(8,128)}, u32[]{:S(2)}, u32[]{:S(2)}) collective-permute-start(f32[256,768]{1,0:T(8,128)} %get-tuple-element.319), channel_id=1, source_target_pairs={{0,16},{8,24},{16,0},{24,8},{1,17},{9,25},{17,1},{25,9},{2,18},{10... | collective-permute-start | bytes 2359304 | tf_op jit(solution)/shard_map/ppermute | solution.py:31
  321.0 21.7 %collective-permute-start.36 = (f32[256,768]{1,0:T(8,128)}, f32[256,768]{1,0:T(8,128)}, u32[]{:S(2)}, u32[]{:S(2)}) collective-permute-start(f32[256,768]{1,0:T(8,128)} %get-tuple-element.348), channel_id=1, source_target_pairs={{0,24},{8,16},{16,8},{24,0},{1,25},{9,17},{17,9},{25,1},{2,26},{10... | collective-permute-start | bytes 2359304 | tf_op jit(solution)/shard_map/ppermute | solution.py:31
  322.5 36.6 %collective-permute-start.32 = (f32[256,768]{1,0:T(8,128)}, f32[256,768]{1,0:T(8,128)}, u32[]{:S(2)}, u32[]{:S(2)}) collective-permute-start(f32[256,768]{1,0:T(8,128)} %get-tuple-element.332), channel_id=1, source_target_pairs={{0,8},{8,0},{16,24},{24,16},{1,9},{9,1},{17,25},{25,17},{2,10},{10... | collective-permute-start | bytes 2359304 | tf_op jit(solution)/shard_map/ppermute | solution.py:31
  323.4 36.0 %collective-permute-start.33 = (f32[256,768]{1,0:T(8,128)}, f32[256,768]{1,0:T(8,128)}, u32[]{:S(2)}, u32[]{:S(2)}) collective-permute-start(f32[256,768]{1,0:T(8,128)} %get-tuple-element.333), channel_id=1, source_target_pairs={{0,16},{8,24},{16,0},{24,8},{1,17},{9,25},{17,1},{25,9},{2,18},{10... | collective-permute-start | bytes 2359304 | tf_op jit(solution)/shard_map/ppermute | solution.py:31
  324.5 44.1 %collective-permute-start.34 = (f32[256,768]{1,0:T(8,128)}, f32[256,768]{1,0:T(8,128)}, u32[]{:S(2)}, u32[]{:S(2)}) collective-permute-start(f32[256,768]{1,0:T(8,128)} %get-tuple-element.334), channel_id=1, source_target_pairs={{0,24},{8,16},{16,8},{24,0},{1,25},{9,17},{17,9},{25,1},{2,26},{10... | collective-permute-start | bytes 2359304 | tf_op jit(solution)/shard_map/ppermute | solution.py:31
  338.6 30.0 %collective-permute-start.35 = (f32[2,32,3,192]{3,0,1,2:T(2,128)S(1)}, f32[2,32,3,192]{3,0,1,2:T(2,128)S(1)}, u32[]{:S(2)}, u32[]{:S(2)}) collective-permute-start(f32[2,32,3,192]{3,0,1,2:T(2,128)S(1)} %rev.7), channel_id=1, source_target_pairs={{0,7},{1,6},{2,5},{3,4},{4,3},{5,2},{6,1},{7,0},{8,15},{9,14},{10,... | collective-permute-start | bytes 442376 | tf_op jit(solution)/shard_map/ppermute | solution.py:1025
  340.9 36.6 %slice-start = ((f32[96,2304]{1,0:T(8,128)}), f32[96,1536]{1,0:T(8,128)S(1)}, s32[]{:S(2)}) async-start(f32[96,2304]{1,0:T(8,128)} %reduce-scatter.4.cloned.1.call-done), calls=%async_computation.10 | async-start | bytes 1179648 | tf_op jit(solution)/shard_map/slice | solution.py:1028
  378.3 9.0 %collective-permute-start.39 = (f32[24,2176]{1,0:T(8,128)S(1)}, f32[24,2176]{1,0:T(8,128)S(1)}, u32[]{:S(2)}, u32[]{:S(2)}) collective-permute-start(f32[24,2176]{1,0:T(8,128)S(1)} %get-tuple-element.399), channel_id=1, source_target_pairs={{0,24},{8,16},{16,8},{24,0},{1,25},{9,17},{17,9},{25,1},{2,26},{10... | collective-permute-start | bytes 626696 | tf_op jit(solution)/shard_map/ppermute | solution.py:31
  380.6 7.5 %collective-permute-start.38 = (f32[24,2176]{1,0:T(8,128)S(1)}, f32[24,2176]{1,0:T(8,128)S(1)}, u32[]{:S(2)}, u32[]{:S(2)}) collective-permute-start(f32[24,2176]{1,0:T(8,128)S(1)} %get-tuple-element.400), channel_id=1, source_target_pairs={{0,16},{8,24},{16,0},{24,8},{1,17},{9,25},{17,1},{25,9},{2,18},{10... | collective-permute-start | bytes 626696 | tf_op jit(solution)/shard_map/ppermute | solution.py:31
  381.2 6.9 %collective-permute-start.37 = (f32[24,2176]{1,0:T(8,128)S(1)}, f32[24,2176]{1,0:T(8,128)S(1)}, u32[]{:S(2)}, u32[]{:S(2)}) collective-permute-start(f32[24,2176]{1,0:T(8,128)S(1)} %get-tuple-element.401), channel_id=1, source_target_pairs={{0,8},{8,0},{16,24},{24,16},{1,9},{9,1},{17,25},{25,17},{2,10},{10... | collective-permute-start | bytes 626696 | tf_op jit(solution)/shard_map/ppermute | solution.py:31
  (28 other events, 98.3 us)
Sparse Core Ops, SparseCore 0:
  19.6 44.2 all-gather.4
  66.1 26.2 all-gather.6
  94.0 51.2 all-gather.8
  146.7 30.4 all-gather.10
  214.2 79.0 reduce-scatter.3
  300.1 37.2 reduce-scatter.7
  339.8 36.6 reduce-scatter.5
